TPU v7x, 32 devices: a whole 2x2x4 slice. The times are simulated.
32 devices in a mesh: depth: 8 (over y, x, core), lat: 4 (over z).
Axes of the slice: x: 2, y: 2, z: 4, core: 2. Of those that a mesh axis runs over, the one named last changes fastest.
Arguments:
- inflow: float32 [8, 16, 128, 256], P('depth', 'lat'), may hold values from -6 to 6
- source: bfloat16 [3, 16, 128, 256], P(None, 'lat'), may hold values from -6 to 6
- operators: bfloat16 [8, 16, 6, 2, 128, 128], P('depth', 'lat'), may hold values from -0.15625 to 0.15625
- transmission: float32 [8, 16, 128], P('depth', 'lat'), may hold values from 0.5 to 1
- reflectivity: float32 [8, 16, 128], P('depth', 'lat'), may hold values from -1 to 1
- send_ids: int32 [4, 2, 2], P('lat'), may hold values from 0 to 3, as said below
- send_count: int32 [4, 2], P('lat'), may hold values from 1 to 2, as said below
- pattern: int32 [16, 6], P('lat'), may hold values from 0 to 7, as said below
Outputs:
- reflected: bfloat16 [4, 8, 16, 128, 256], P(None, 'depth', 'lat')
- transmitted: float32 [8, 16, 128, 256], P('depth', 'lat')
Inputs may be any that keep to these rules, and one draw needn't show every extreme that they name: `send_ids`: the 2 numbers of one list are distinct block numbers of the tile that holds the list. `send_count`: some list holds 2 live entries in every draw. `pattern`: entry 0 of block b names b's own local number (b modulo 4). Other entries name a local block or a live received slot: slots 4 + i for i below the lower tile's count for its upper list, slots 4 + 2 + i for i below the upper tile's count for its lower list; tile 0 names no lower slot, tile 4 - 1 no upper slot. Every live received slot of a tile is named by some entry of that tile.
All inputs are finite; a program needn't handle non-finite values.
Results may differ from a plain program's by a relative error of at most 0.0061.
Values may be sent and summed in bfloat16 or wider, within the bound.
No kernel may reach another device: no remote copies, remote signals or barrier semaphores. Data moves between devices by JAX's collectives and lax.ppermute only.
A program may use at most 64 MiB of HBM per device.

v0:
```python
import functools

import jax
import jax.numpy as jnp
from jax import lax
from jax.experimental import pallas as pl
from jax.experimental.pallas import tpu as pltpu
from jax.sharding import PartitionSpec as P

WAVE = jnp.bfloat16
SMEM_SPEC = pl.BlockSpec(memory_space=pltpu.SMEM)
VMEM_SPEC = pl.BlockSpec(memory_space=pltpu.VMEM)
ANY_SPEC = pl.BlockSpec(memory_space=pl.ANY)
VMEM_LIMIT = 8 * 1024 * 1024
LOWER, UPPER = 0, 1


def in_vmem(array):
    return pltpu.with_memory_space_constraint(array, pltpu.VMEM)


def in_hbm(array):
    return pltpu.with_memory_space_constraint(array, pltpu.HBM)


def write_lists(section, plan_ref, blocks_ref, lists):
    listed = lists[0].shape[0]
    parity = lax.rem(section, 2)
    for list_ref, side in zip(lists, (UPPER - parity, parity)):
        count = plan_ref[2 * listed + side]
        for slot in range(listed):
            live = slot < count

            @pl.when(live)
            def _():
                list_ref[slot] = blocks_ref[plan_ref[side * listed + slot]]

            @pl.when(jnp.logical_not(live))
            def _():
                list_ref[slot] = jnp.zeros(list_ref.shape[1:], list_ref.dtype)


def prepare_kernel(
    ids_hbm, count_hbm, pattern_hbm, inflow_hbm, plan_ref, wave_ref, first_ref, second_ref,
    ids, count, pattern, landed, small_sems, sems,
):
    blocks = wave_ref.shape[0]
    small = [
        pltpu.make_async_copy(source, target, small_sems.at[i])
        for i, (source, target) in enumerate(
            ((ids_hbm, ids), (count_hbm, count), (pattern_hbm, pattern))
        )
    ]
    large = [
        pltpu.make_async_copy(inflow_hbm.at[0, b], landed.at[b], sems.at[b]) for b in range(blocks)
    ]
    for copy in small + large:
        copy.start()
    for copy in small:
        copy.wait()
    _, sides, listed = ids.shape
    taken = pattern.shape[1]
    for side in range(sides):
        for slot in range(listed):
            plan_ref[side * listed + slot] = ids[0, side, slot]
        plan_ref[sides * listed + side] = count[0, side]
    for b in range(blocks):
        for k in range(taken):
            plan_ref[sides * (listed + 1) + b * taken + k] = pattern[b, k]
    for b, copy in enumerate(large):
        copy.wait()
        wave_ref[b] = landed[b].astype(wave_ref.dtype)
    write_lists(lax.axis_index("depth"), plan_ref, wave_ref, (first_ref, second_ref))


def load_kernel(
    ops_hbm, source_hbm, pass_hbm, reflect_hbm, after_ref,
    ops_ref, source_ref, pass_ref, reflect_ref, pass_rows, reflect_rows, sems,
):
    del after_ref
    copies = [
        pltpu.make_async_copy(source, target, sems.at[i])
        for i, (source, target) in enumerate(
            (
                (pass_hbm, pass_rows),
                (reflect_hbm, reflect_rows),
                (ops_hbm, ops_ref),
                (source_hbm, source_ref),
            )
        )
    ]
    for copy in copies:
        copy.start()
    for copy, rows, columns_ref in zip(copies, (pass_rows, reflect_rows), (pass_ref, reflect_ref)):
        copy.wait()
        for b in range(columns_ref.shape[0]):
            row = rows[0, pl.ds(b, 1), :]
            columns_ref[b] = jnp.broadcast_to(row, columns_ref.shape[1:]).T
    for copy in copies[2:]:
        copy.wait()


def fill_buffer(section, sections, tick, source_ref, wave_ref, first_ref, second_ref, buffer):
    blocks, listed = wave_ref.shape[0], first_ref.shape[0]
    if tick == 0:
        sender = section
        buffer[:blocks] = wave_ref[...]
    else:
        sender = lax.rem(section + sections - 1, sections)

        @pl.when(section == 0)
        def _():
            buffer[:blocks] = source_ref[tick - 1]

        @pl.when(section != 0)
        def _():
            buffer[:blocks] = wave_ref[...]
    parity = lax.rem(sender, 2)
    buffer[pl.ds(blocks + parity * listed, listed)] = first_ref[...]
    buffer[pl.ds(blocks + (1 - parity) * listed, listed)] = second_ref[...]


def extrapolate_block(plan_ref, pattern_start, ops_ref, buffer, b):
    taken = ops_ref.shape[2]
    points = ops_ref.shape[5]
    left = jnp.concatenate(
        [ops_ref[0, b, k].reshape(2 * points, points) for k in range(taken)], axis=1
    )
    right = jnp.concatenate(
        [buffer[plan_ref[pattern_start + b * taken + k]] for k in range(taken)], axis=0
    )
    products = jnp.dot(left, right, preferred_element_type=jnp.float32)
    half = products.shape[1] // 2
    real_part = products[:points, :half] - products[points:, half:]
    imag_part = products[:points, half:] + products[points:, :half]
    return real_part, imag_part


def tick_kernel(
    tick, sections, plan_ref, ops_ref, source_ref, pass_ref, reflect_ref,
    wave_ref, first_in_ref, second_in_ref, echo_ref, onward_ref, first_ref, second_ref, buffer,
):
    section = lax.axis_index("depth")
    listed = first_ref.shape[0]
    fill_buffer(
        section, sections, tick, source_ref, wave_ref, first_in_ref, second_in_ref, buffer
    )
    for b in range(wave_ref.shape[0]):
        parts = extrapolate_block(plan_ref, 2 * (listed + 1), ops_ref, buffer, b)
        for i, part in enumerate(parts):
            cols = pl.ds(i * part.shape[1], part.shape[1])
            onward_ref[b, :, cols] = (pass_ref[b] * part).astype(onward_ref.dtype)
            echo_ref[b, :, cols] = (reflect_ref[b] * part).astype(echo_ref.dtype)

    @pl.when(section != sections - 1)
    def _():
        write_lists(section, plan_ref, onward_ref, (first_ref, second_ref))

    @pl.when(section == sections - 1)
    def _():
        write_lists(section, plan_ref, source_ref.at[tick], (first_ref, second_ref))


def last_kernel(
    tick, sections, plan_ref, ops_ref, source_ref, pass_ref, reflect_ref,
    wave_ref, first_in_ref, second_in_ref, *rest,
):
    earlier = rest[:tick]
    (reflected_ref, transmitted_ref, buffer, echo, leaving,
     early_sems, echo_sems, leave_sems) = rest[tick:]
    section = lax.axis_index("depth")
    listed = first_in_ref.shape[0]
    copies = [
        pltpu.make_async_copy(earlier[t], reflected_ref.at[t, 0], early_sems.at[t])
        for t in range(tick)
    ]
    for copy in copies:
        copy.start()
    fill_buffer(
        section, sections, tick, source_ref, wave_ref, first_in_ref, second_in_ref, buffer
    )
    for b in range(wave_ref.shape[0]):
        parts = extrapolate_block(plan_ref, 2 * (listed + 1), ops_ref, buffer, b)
        for i, part in enumerate(parts):
            cols = pl.ds(i * part.shape[1], part.shape[1])
            leaving[b, :, cols] = pass_ref[b] * part
            echo[b, :, cols] = (reflect_ref[b] * part).astype(echo.dtype)
        for copy in (
            pltpu.make_async_copy(leaving.at[b], transmitted_ref.at[0, b], leave_sems.at[b]),
            pltpu.make_async_copy(echo.at[b], reflected_ref.at[tick, 0, b], echo_sems.at[b]),
        ):
            copy.start()
            copies.append(copy)
    for copy in copies:
        copy.wait()


def halo_routes(sections, tiles, deeper):
    routes = []
    for turn in (0, 1):
        route = []
        for s in range(sections):
            way = 1 if (s + turn) % 2 == 0 else -1
            to_section = (s + 1) % sections if deeper else s
            route += [
                (s * tiles + j, to_section * tiles + j + way)
                for j in range(tiles)
                if 0 <= j + way < tiles
            ]
        routes.append(route)
    return routes


def per_device(
    inflow, source, operators, transmission, reflectivity, send_ids, send_count, pattern
):
    sections, tiles = lax.axis_size("depth"), lax.axis_size("lat")
    ticks = source.shape[0] + 1
    _, blocks, points, columns = inflow.shape
    listed = send_ids.shape[-1]
    taken = operators.shape[2]
    wave_type = pltpu.VMEM((blocks, points, columns), WAVE)
    list_type = pltpu.VMEM((listed, points, columns), WAVE)
    params = pltpu.CompilerParams(vmem_limit_bytes=VMEM_LIMIT)
    tick_cost = pl.CostEstimate(
        flops=blocks * taken * 4 * points * points * columns,
        bytes_accessed=2 * operators.size + 8 * blocks * points * columns,
        transcendentals=0,
    )
    both = ("depth", "lat")
    deeper = [(s, s + 1) for s in range(sections - 1)]

    plan, wave, first, second = pl.pallas_call(
        prepare_kernel,
        out_shape=(
            pltpu.SMEM((2 * (listed + 1) + blocks * taken,), jnp.int32),
            wave_type,
            list_type,
            list_type,
        ),
        in_specs=[ANY_SPEC] * 4,
        out_specs=(SMEM_SPEC,) + (VMEM_SPEC,) * 3,
        scratch_shapes=[
            pltpu.SMEM(send_ids.shape, jnp.int32),
            pltpu.SMEM(send_count.shape, jnp.int32),
            pltpu.SMEM(pattern.shape, jnp.int32),
            pltpu.VMEM((blocks, points, columns), inflow.dtype),
            pltpu.SemaphoreType.DMA((3,)),
            pltpu.SemaphoreType.DMA((blocks,)),
        ],
        compiler_params=params,
        cost_estimate=pl.CostEstimate(
            flops=inflow.size, bytes_accessed=8 * inflow.size, transcendentals=0
        ),
        name="prepare",
    )(*map(in_hbm, (send_ids, send_count, pattern, inflow)))
    routes = halo_routes(sections, tiles, False)
    loaded_first = first
    first = lax.ppermute(first, both, routes[0])
    second = lax.ppermute(second, both, routes[1])

    column_type = pltpu.VMEM((blocks, points, columns // 2), jnp.float32)
    fixed = pl.pallas_call(
        load_kernel,
        out_shape=(
            pltpu.VMEM(operators.shape, operators.dtype),
            pltpu.VMEM(source.shape, source.dtype),
            column_type,
            column_type,
        ),
        in_specs=[ANY_SPEC] * 4 + [VMEM_SPEC],
        out_specs=(VMEM_SPEC,) * 4,
        scratch_shapes=[
            pltpu.VMEM(transmission.shape, transmission.dtype),
            pltpu.VMEM(reflectivity.shape, reflectivity.dtype),
            pltpu.SemaphoreType.DMA((4,)),
        ],
        compiler_params=params,
        cost_estimate=pl.CostEstimate(
            flops=0, bytes_accessed=4 * (operators.size + source.size), transcendentals=0
        ),
        name="load",
    )(*map(in_hbm, (operators, source, transmission, reflectivity)), in_vmem(loaded_first))
    fixed = [plan, *map(in_vmem, fixed)]

    buffer_type = pltpu.VMEM((blocks + 2 * listed, points, columns), WAVE)
    routes = halo_routes(sections, tiles, True)
    echoes = []
    for tick in range(ticks - 1):
        echo, onward, first, second = pl.pallas_call(
            functools.partial(tick_kernel, tick, sections),
            out_shape=(wave_type, wave_type, list_type, list_type),
            in_specs=[SMEM_SPEC] + [VMEM_SPEC] * 7,
            out_specs=(VMEM_SPEC,) * 4,
            scratch_shapes=[buffer_type],
            compiler_params=params,
            cost_estimate=tick_cost,
            name=f"tick{tick}",
        )(*fixed, in_vmem(wave), in_vmem(first), in_vmem(second))
        echoes.append(echo)
        wave = lax.ppermute(onward, "depth", deeper)
        first = lax.ppermute(first, both, routes[0])
        second = lax.ppermute(second, both, routes[1])

    tick = ticks - 1
    reflected, transmitted = pl.pallas_call(
        functools.partial(last_kernel, tick, sections),
        out_shape=(
            jax.ShapeDtypeStruct((ticks, 1, blocks, points, columns), WAVE),
            jax.ShapeDtypeStruct((1, blocks, points, columns), jnp.float32),
        ),
        in_specs=[SMEM_SPEC] + [VMEM_SPEC] * (7 + tick),
        out_specs=(ANY_SPEC, ANY_SPEC),
        scratch_shapes=[
            buffer_type,
            pltpu.VMEM((blocks, points, columns), WAVE),
            pltpu.VMEM((blocks, points, columns), jnp.float32),
            pltpu.SemaphoreType.DMA((tick,)),
            pltpu.SemaphoreType.DMA((blocks,)),
            pltpu.SemaphoreType.DMA((blocks,)),
        ],
        compiler_params=params,
        cost_estimate=tick_cost,
        name="last_tick",
    )(*fixed, in_vmem(wave), in_vmem(first), in_vmem(second), *map(in_vmem, echoes))
    return reflected, transmitted


def solution(mesh):
    return jax.shard_map(
        per_device,
        mesh=mesh,
        in_specs=(
            P("depth", "lat", None, None),
            P(None, "lat", None, None),
            P("depth", "lat", None, None, None, None),
            P("depth", "lat", None),
            P("depth", "lat", None),
            P("lat", None, None),
            P("lat", None),
            P("lat", None),
        ),
        out_specs=(P(None, "depth", "lat", None, None), P("depth", "lat", None, None)),
        check_vma=False,
    )
```

profile of v0, /device:TPU:1, one launch (start us, length us, event | category | flops | bytes accessed | tf_op | source)
XLA Modules:
  0.0 55.7 jit_solution(13334262907298731547)
XLA Ops:
  0.6 1.2 %prepare.1 = (s32[30]{0:T(128)S(4)}, bf16[4,128,256]{2,1,0:T(8,128)(2,1)S(1)}, bf16[2,128,256]{2,1,0:T(8,128)(2,1)S(1)}, bf16[2,128,256]{2,1,0:T(8,128)(2,1)S(1)}) custom-call(s32[1,2,2]{2,1,0:T(2,128)} %ids_hbm.1, s32[1,2]{1,0:T(1,128)} %count_hbm.1, s32[4,6]{1,0:T(4,128)} %pattern_hbm.1, f32[1,4,128,256]{3,2,1,0:T(8,128)} %inflow_hbm.1), custom_call_target="tpu_custom_call" | custom-call | flops 131072 | bytes 1048576 | tf_op jit(solution)/shard_map/prepare/pallas_call | solution.py:233
  1.8 4.0 %collective-permute-start.1 = (bf16[2,128,256]{2,1,0:T(8,128)(2,1)S(1)}, bf16[2,128,256]{2,1,0:T(8,128)(2,1)S(1)}, u32[]{:S(2)}, u32[]{:S(2)}) collective-permute-start(bf16[2,128,256]{2,1,0:T(8,128)(2,1)S(1)} %get-tuple-element.29), channel_id=1, source_target_pairs={{1,0},{2,1},{3,2},{4,5},{5,6},{6,7},{9,8},{10,9},{11,10},{12,13},{... | collective-permute-start | bytes 393224 | tf_op jit(solution)/shard_map/ppermute | solution.py:260
  5.9 1.3 %collective-permute-start = (bf16[2,128,256]{2,1,0:T(8,128)(2,1)S(1)}, bf16[2,128,256]{2,1,0:T(8,128)(2,1)S(1)}, u32[]{:S(2)}, u32[]{:S(2)}) collective-permute-start(bf16[2,128,256]{2,1,0:T(8,128)(2,1)S(1)} %get-tuple-element.23.after_ref), channel_id=1, source_target_pairs={{0,1},{1,2},{2,3},{5,4},{6,5},{7,6},{8,9},{9,10},{10,11},{13,12},{... | collective-permute-start | bytes 393224 | tf_op jit(solution)/shard_map/ppermute | solution.py:259
  7.2 1.7 %load.1 = (bf16[1,4,6,2,128,128]{5,4,3,2,1,0:T(8,128)(2,1)S(1)}, bf16[3,4,128,256]{3,2,1,0:T(8,128)(2,1)S(1)}, f32[4,128,128]{2,1,0:T(8,128)S(1)}, f32[4,128,128]{2,1,0:T(8,128)S(1)}) custom-call(bf16[1,4,6,2,128,128]{5,4,3,2,1,0:T(8,128)(2,1)} %ops_hbm.1, bf16[3,4,128,256]{3,2,1,0:T(8,128)(2,1)} %source_hbm.1, f32[1,4,128]{2,1,0:T(4,128)} %pass_hbm.1, ...), custom_call_target="tpu_custom_call" | custom-call | bytes 4718592 | tf_op jit(solution)/shard_map/load/pallas_call | solution.py:263
  8.9 0.0 collective-permute-done.1.second_in_ref
  8.9 2.7 %collective-permute-done.first_in_ref = bf16[2,128,256]{2,1,0:T(8,128)(2,1)S(1)} collective-permute-done((bf16[2,128,256]{2,1,0:T(8,128)(2,1)S(1)}, bf16[2,128,256]{2,1,0:T(8,128)(2,1)S(1)}, u32[]{:S(2)}, u32[]{:S(2)}) %collective-permute-start) | collective-permute-done | bytes 131104 | tf_op jit(solution)/shard_map/ppermute | solution.py:259
  11.6 0.7 %tick0.1 = (bf16[4,128,256]{2,1,0:T(8,128)(2,1)S(1)}, bf16[4,128,256]{2,1,0:T(8,128)(2,1)S(1)}, bf16[2,128,256]{2,1,0:T(8,128)(2,1)S(1)}, bf16[2,128,256]{2,1,0:T(8,128)(2,1)S(1)}) custom-call(s32[30]{0:T(128)S(4)} %get-tuple-element.22.plan_ref, bf16[1,4,6,2,128,128]{5,4,3,2,1,0:T(8,128)(2,1)S(1)} %get-tuple-element.24.ops_ref, ...), custom_call_target="tpu_custom_call" | custom-call | flops 402653184 | bytes 2621440 | tf_op jit(solution)/shard_map/tick0/pallas_call | solution.py:290
  12.3 3.1 %collective-permute-start.2 = (bf16[4,128,256]{2,1,0:T(8,128)(2,1)S(1)}, bf16[4,128,256]{2,1,0:T(8,128)(2,1)S(1)}, u32[]{:S(2)}, u32[]{:S(2)}) collective-permute-start(bf16[4,128,256]{2,1,0:T(8,128)(2,1)S(1)} %get-tuple-element.30), channel_id=1, source_target_pairs={{0,4},{4,8},{8,12},{12,16},{16,20},{20,24},{24,28},{1,5},{5,9},{9,... | collective-permute-start | bytes 786440 | tf_op jit(solution)/shard_map/ppermute | solution.py:301
  15.4 0.7 %collective-permute-start.3 = (bf16[2,128,256]{2,1,0:T(8,128)(2,1)S(1)}, bf16[2,128,256]{2,1,0:T(8,128)(2,1)S(1)}, u32[]{:S(2)}, u32[]{:S(2)}) collective-permute-start(bf16[2,128,256]{2,1,0:T(8,128)(2,1)S(1)} %get-tuple-element.31), channel_id=1, source_target_pairs={{0,5},{1,6},{2,7},{5,8},{6,9},{7,10},{8,13},{9,14},{10,15},{13,16}... | collective-permute-start | bytes 393224 | tf_op jit(solution)/shard_map/ppermute | solution.py:302
  16.1 7.8 %collective-permute-start.4 = (bf16[2,128,256]{2,1,0:T(8,128)(2,1)S(1)}, bf16[2,128,256]{2,1,0:T(8,128)(2,1)S(1)}, u32[]{:S(2)}, u32[]{:S(2)}) collective-permute-start(bf16[2,128,256]{2,1,0:T(8,128)(2,1)S(1)} %get-tuple-element.32), channel_id=1, source_target_pairs={{1,4},{2,5},{3,6},{4,9},{5,10},{6,11},{9,12},{10,13},{11,14},{12,1... | collective-permute-start | bytes 393224 | tf_op jit(solution)/shard_map/ppermute | solution.py:303
  23.9 0.0 collective-permute-done.3.first_in_ref
  23.9 1.9 %collective-permute-done.4.second_in_ref = bf16[2,128,256]{2,1,0:T(8,128)(2,1)S(1)} collective-permute-done((bf16[2,128,256]{2,1,0:T(8,128)(2,1)S(1)}, bf16[2,128,256]{2,1,0:T(8,128)(2,1)S(1)}, u32[]{:S(2)}, u32[]{:S(2)}) %collective-permute-start.4) | collective-permute-done | bytes 131104 | tf_op jit(solution)/shard_map/ppermute | solution.py:303
  25.9 0.0 collective-permute-done.2.wave_ref
  25.9 0.7 %tick1.1 = (bf16[4,128,256]{2,1,0:T(8,128)(2,1)S(1)}, bf16[4,128,256]{2,1,0:T(8,128)(2,1)S(1)}, bf16[2,128,256]{2,1,0:T(8,128)(2,1)S(1)}, bf16[2,128,256]{2,1,0:T(8,128)(2,1)S(1)}) custom-call(s32[30]{0:T(128)S(4)} %get-tuple-element.22.plan_ref, bf16[1,4,6,2,128,128]{5,4,3,2,1,0:T(8,128)(2,1)S(1)} %get-tuple-element.24.ops_ref, ...), custom_call_target="tpu_custom_call" | custom-call | flops 402653184 | bytes 2621440 | tf_op jit(solution)/shard_map/tick1/pallas_call | solution.py:290
  26.6 1.9 %collective-permute-start.5 = (bf16[4,128,256]{2,1,0:T(8,128)(2,1)S(1)}, bf16[4,128,256]{2,1,0:T(8,128)(2,1)S(1)}, u32[]{:S(2)}, u32[]{:S(2)}) collective-permute-start(bf16[4,128,256]{2,1,0:T(8,128)(2,1)S(1)} %get-tuple-element.33), channel_id=1, source_target_pairs={{0,4},{4,8},{8,12},{12,16},{16,20},{20,24},{24,28},{1,5},{5,9},{9,... | collective-permute-start | bytes 786440 | tf_op jit(solution)/shard_map/ppermute | solution.py:301
  28.5 0.7 %collective-permute-start.6 = (bf16[2,128,256]{2,1,0:T(8,128)(2,1)S(1)}, bf16[2,128,256]{2,1,0:T(8,128)(2,1)S(1)}, u32[]{:S(2)}, u32[]{:S(2)}) collective-permute-start(bf16[2,128,256]{2,1,0:T(8,128)(2,1)S(1)} %get-tuple-element.34), channel_id=1, source_target_pairs={{0,5},{1,6},{2,7},{5,8},{6,9},{7,10},{8,13},{9,14},{10,15},{13,16}... | collective-permute-start | bytes 393224 | tf_op jit(solution)/shard_map/ppermute | solution.py:302
  29.2 10.2 %collective-permute-start.7 = (bf16[2,128,256]{2,1,0:T(8,128)(2,1)S(1)}, bf16[2,128,256]{2,1,0:T(8,128)(2,1)S(1)}, u32[]{:S(2)}, u32[]{:S(2)}) collective-permute-start(bf16[2,128,256]{2,1,0:T(8,128)(2,1)S(1)} %get-tuple-element.35), channel_id=1, source_target_pairs={{1,4},{2,5},{3,6},{4,9},{5,10},{6,11},{9,12},{10,13},{11,14},{12,1... | collective-permute-start | bytes 393224 | tf_op jit(solution)/shard_map/ppermute | solution.py:303
  39.3 0.0 collective-permute-done.6.first_in_ref
  39.4 1.9 %collective-permute-done.7.second_in_ref = bf16[2,128,256]{2,1,0:T(8,128)(2,1)S(1)} collective-permute-done((bf16[2,128,256]{2,1,0:T(8,128)(2,1)S(1)}, bf16[2,128,256]{2,1,0:T(8,128)(2,1)S(1)}, u32[]{:S(2)}, u32[]{:S(2)}) %collective-permute-start.7) | collective-permute-done | bytes 131104 | tf_op jit(solution)/shard_map/ppermute | solution.py:303
  41.3 0.0 collective-permute-done.5.wave_ref
  41.3 0.7 %tick2.1 = (bf16[4,128,256]{2,1,0:T(8,128)(2,1)S(1)}, bf16[4,128,256]{2,1,0:T(8,128)(2,1)S(1)}, bf16[2,128,256]{2,1,0:T(8,128)(2,1)S(1)}, bf16[2,128,256]{2,1,0:T(8,128)(2,1)S(1)}) custom-call(s32[30]{0:T(128)S(4)} %get-tuple-element.22.plan_ref, bf16[1,4,6,2,128,128]{5,4,3,2,1,0:T(8,128)(2,1)S(1)} %get-tuple-element.24.ops_ref, ...), custom_call_target="tpu_custom_call" | custom-call | flops 402653184 | bytes 2621440 | tf_op jit(solution)/shard_map/tick2/pallas_call | solution.py:290
  42.0 1.9 %collective-permute-start.8 = (bf16[4,128,256]{2,1,0:T(8,128)(2,1)S(1)}, bf16[4,128,256]{2,1,0:T(8,128)(2,1)S(1)}, u32[]{:S(2)}, u32[]{:S(2)}) collective-permute-start(bf16[4,128,256]{2,1,0:T(8,128)(2,1)S(1)} %get-tuple-element.36), channel_id=1, source_target_pairs={{0,4},{4,8},{8,12},{12,16},{16,20},{20,24},{24,28},{1,5},{5,9},{9,... | collective-permute-start | bytes 786440 | tf_op jit(solution)/shard_map/ppermute | solution.py:301
  43.9 0.7 %collective-permute-start.9 = (bf16[2,128,256]{2,1,0:T(8,128)(2,1)S(1)}, bf16[2,128,256]{2,1,0:T(8,128)(2,1)S(1)}, u32[]{:S(2)}, u32[]{:S(2)}) collective-permute-start(bf16[2,128,256]{2,1,0:T(8,128)(2,1)S(1)} %get-tuple-element.37), channel_id=1, source_target_pairs={{0,5},{1,6},{2,7},{5,8},{6,9},{7,10},{8,13},{9,14},{10,15},{13,16}... | collective-permute-start | bytes 393224 | tf_op jit(solution)/shard_map/ppermute | solution.py:302
  44.6 7.7 %collective-permute-start.10 = (bf16[2,128,256]{2,1,0:T(8,128)(2,1)S(1)}, bf16[2,128,256]{2,1,0:T(8,128)(2,1)S(1)}, u32[]{:S(2)}, u32[]{:S(2)}) collective-permute-start(bf16[2,128,256]{2,1,0:T(8,128)(2,1)S(1)} %get-tuple-element.38), channel_id=1, source_target_pairs={{1,4},{2,5},{3,6},{4,9},{5,10},{6,11},{9,12},{10,13},{11,14},{12,1... | collective-permute-start | bytes 393224 | tf_op jit(solution)/shard_map/ppermute | solution.py:303
  52.3 0.0 collective-permute-done.9.first_in_ref
  52.3 1.9 %collective-permute-done.10.second_in_ref = bf16[2,128,256]{2,1,0:T(8,128)(2,1)S(1)} collective-permute-done((bf16[2,128,256]{2,1,0:T(8,128)(2,1)S(1)}, bf16[2,128,256]{2,1,0:T(8,128)(2,1)S(1)}, u32[]{:S(2)}, u32[]{:S(2)}) %collective-permute-start.10) | collective-permute-done | bytes 131104 | tf_op jit(solution)/shard_map/ppermute | solution.py:303
  54.2 0.0 collective-permute-done.8.wave_ref
  54.3 1.5 %last_tick.1 = (bf16[4,1,4,128,256]{4,3,2,1,0:T(8,128)(2,1)}, f32[1,4,128,256]{3,2,1,0:T(8,128)}) custom-call(s32[30]{0:T(128)S(4)} %get-tuple-element.22.plan_ref, bf16[1,4,6,2,128,128]{5,4,3,2,1,0:T(8,128)(2,1)S(1)} %get-tuple-element.24.ops_ref, bf16[3,4,128,256]{3,2,1,0:T(8,128)(2,1)S(1)} %get-tuple-element.25.source_ref, ...), custom_call_target="tpu_custom_call" | custom-call | flops 402653184 | bytes 2621440 | tf_op jit(solution)/shard_map/last_tick/pallas_call | solution.py:306
Async XLA Ops:
  1.8 7.0 %collective-permute-start.1 = (bf16[2,128,256]{2,1,0:T(8,128)(2,1)S(1)}, bf16[2,128,256]{2,1,0:T(8,128)(2,1)S(1)}, u32[]{:S(2)}, u32[]{:S(2)}) collective-permute-start(bf16[2,128,256]{2,1,0:T(8,128)(2,1)S(1)} %get-tuple-element.29), channel_id=1, source_target_pairs={{1,0},{2,1},{3,2},{4,5},{5,6},{6,7},{9,8},{10,9},{11,10},{12,13},{... | collective-permute-start | bytes 393224 | tf_op jit(solution)/shard_map/ppermute | solution.py:260
  5.9 5.7 %collective-permute-start = (bf16[2,128,256]{2,1,0:T(8,128)(2,1)S(1)}, bf16[2,128,256]{2,1,0:T(8,128)(2,1)S(1)}, u32[]{:S(2)}, u32[]{:S(2)}) collective-permute-start(bf16[2,128,256]{2,1,0:T(8,128)(2,1)S(1)} %get-tuple-element.23.after_ref), channel_id=1, source_target_pairs={{0,1},{1,2},{2,3},{5,4},{6,5},{7,6},{8,9},{9,10},{10,11},{13,12},{... | collective-permute-start | bytes 393224 | tf_op jit(solution)/shard_map/ppermute | solution.py:259
  12.3 13.5 %collective-permute-start.2 = (bf16[4,128,256]{2,1,0:T(8,128)(2,1)S(1)}, bf16[4,128,256]{2,1,0:T(8,128)(2,1)S(1)}, u32[]{:S(2)}, u32[]{:S(2)}) collective-permute-start(bf16[4,128,256]{2,1,0:T(8,128)(2,1)S(1)} %get-tuple-element.30), channel_id=1, source_target_pairs={{0,4},{4,8},{8,12},{12,16},{16,20},{20,24},{24,28},{1,5},{5,9},{9,... | collective-permute-start | bytes 786440 | tf_op jit(solution)/shard_map/ppermute | solution.py:301
  15.4 8.5 %collective-permute-start.3 = (bf16[2,128,256]{2,1,0:T(8,128)(2,1)S(1)}, bf16[2,128,256]{2,1,0:T(8,128)(2,1)S(1)}, u32[]{:S(2)}, u32[]{:S(2)}) collective-permute-start(bf16[2,128,256]{2,1,0:T(8,128)(2,1)S(1)} %get-tuple-element.31), channel_id=1, source_target_pairs={{0,5},{1,6},{2,7},{5,8},{6,9},{7,10},{8,13},{9,14},{10,15},{13,16}... | collective-permute-start | bytes 393224 | tf_op jit(solution)/shard_map/ppermute | solution.py:302
  16.1 9.8 %collective-permute-start.4 = (bf16[2,128,256]{2,1,0:T(8,128)(2,1)S(1)}, bf16[2,128,256]{2,1,0:T(8,128)(2,1)S(1)}, u32[]{:S(2)}, u32[]{:S(2)}) collective-permute-start(bf16[2,128,256]{2,1,0:T(8,128)(2,1)S(1)} %get-tuple-element.32), channel_id=1, source_target_pairs={{1,4},{2,5},{3,6},{4,9},{5,10},{6,11},{9,12},{10,13},{11,14},{12,1... | collective-permute-start | bytes 393224 | tf_op jit(solution)/shard_map/ppermute | solution.py:303
  26.6 14.7 %collective-permute-start.5 = (bf16[4,128,256]{2,1,0:T(8,128)(2,1)S(1)}, bf16[4,128,256]{2,1,0:T(8,128)(2,1)S(1)}, u32[]{:S(2)}, u32[]{:S(2)}) collective-permute-start(bf16[4,128,256]{2,1,0:T(8,128)(2,1)S(1)} %get-tuple-element.33), channel_id=1, source_target_pairs={{0,4},{4,8},{8,12},{12,16},{16,20},{20,24},{24,28},{1,5},{5,9},{9,... | collective-permute-start | bytes 786440 | tf_op jit(solution)/shard_map/ppermute | solution.py:301
  28.5 10.8 %collective-permute-start.6 = (bf16[2,128,256]{2,1,0:T(8,128)(2,1)S(1)}, bf16[2,128,256]{2,1,0:T(8,128)(2,1)S(1)}, u32[]{:S(2)}, u32[]{:S(2)}) collective-permute-start(bf16[2,128,256]{2,1,0:T(8,128)(2,1)S(1)} %get-tuple-element.34), channel_id=1, source_target_pairs={{0,5},{1,6},{2,7},{5,8},{6,9},{7,10},{8,13},{9,14},{10,15},{13,16}... | collective-permute-start | bytes 393224 | tf_op jit(solution)/shard_map/ppermute | solution.py:302
  29.2 12.1 %collective-permute-start.7 = (bf16[2,128,256]{2,1,0:T(8,128)(2,1)S(1)}, bf16[2,128,256]{2,1,0:T(8,128)(2,1)S(1)}, u32[]{:S(2)}, u32[]{:S(2)}) collective-permute-start(bf16[2,128,256]{2,1,0:T(8,128)(2,1)S(1)} %get-tuple-element.35), channel_id=1, source_target_pairs={{1,4},{2,5},{3,6},{4,9},{5,10},{6,11},{9,12},{10,13},{11,14},{12,1... | collective-permute-start | bytes 393224 | tf_op jit(solution)/shard_map/ppermute | solution.py:303
  42.0 12.3 %collective-permute-start.8 = (bf16[4,128,256]{2,1,0:T(8,128)(2,1)S(1)}, bf16[4,128,256]{2,1,0:T(8,128)(2,1)S(1)}, u32[]{:S(2)}, u32[]{:S(2)}) collective-permute-start(bf16[4,128,256]{2,1,0:T(8,128)(2,1)S(1)} %get-tuple-element.36), channel_id=1, source_target_pairs={{0,4},{4,8},{8,12},{12,16},{16,20},{20,24},{24,28},{1,5},{5,9},{9,... | collective-permute-start | bytes 786440 | tf_op jit(solution)/shard_map/ppermute | solution.py:301
  43.9 8.4 %collective-permute-start.9 = (bf16[2,128,256]{2,1,0:T(8,128)(2,1)S(1)}, bf16[2,128,256]{2,1,0:T(8,128)(2,1)S(1)}, u32[]{:S(2)}, u32[]{:S(2)}) collective-permute-start(bf16[2,128,256]{2,1,0:T(8,128)(2,1)S(1)} %get-tuple-element.37), channel_id=1, source_target_pairs={{0,5},{1,6},{2,7},{5,8},{6,9},{7,10},{8,13},{9,14},{10,15},{13,16}... | collective-permute-start | bytes 393224 | tf_op jit(solution)/shard_map/ppermute | solution.py:302
  44.6 9.7 %collective-permute-start.10 = (bf16[2,128,256]{2,1,0:T(8,128)(2,1)S(1)}, bf16[2,128,256]{2,1,0:T(8,128)(2,1)S(1)}, u32[]{:S(2)}, u32[]{:S(2)}) collective-permute-start(bf16[2,128,256]{2,1,0:T(8,128)(2,1)S(1)} %get-tuple-element.38), channel_id=1, source_target_pairs={{1,4},{2,5},{3,6},{4,9},{5,10},{6,11},{9,12},{10,13},{11,14},{12,1... | collective-permute-start | bytes 393224 | tf_op jit(solution)/shard_map/ppermute | solution.py:303
where the time goes:
time: 56.1 us; the launch traced here: 55.7 us
  starting transfers between devices  40 us (71%)
  waiting for transfers between devices  8.48 us (15%)
  Pallas kernels  6.44 us (11%)
  between operations  0.79 us (1%)
    ppermute x4, starting transfers between devices, per_device(): second = lax.ppermute(second, both, routes[1])  29.8 us
    ppermute x3, starting transfers between devices, per_device(): wave = lax.ppermute(onward, 'depth', deeper)  6.94 us
    ppermute x4, waiting for transfers between devices, per_device(): second = lax.ppermute(second, both, routes[1])  5.75 us
    ppermute x4, starting transfers between devices, per_device(): first = lax.ppermute(first, both, routes[0])  3.3 us
    ppermute x4, waiting for transfers between devices, per_device(): first = lax.ppermute(first, both, routes[0])  2.72 us
    pallas_call x3, Pallas kernels, per_device(): pl.pallas_call(functools.partial(tick_kernel, tick, sections), out_shape=...  2.1 us
    pallas_call x1, Pallas kernels, per_device(): pl.pallas_call(load_kernel, out_shape=(pltpu.VMEM(operators.shape, operat...  1.68 us
    pallas_call x1, Pallas kernels, per_device(): pl.pallas_call(functools.partial(last_kernel, tick, sections), out_shape=...  1.46 us
  transfers between devices with their start and end apart: 11, of which 4 were waited for; matrix products, arithmetic and copies ran while one was open for 0% of the time, Pallas kernels for 3%

commit v1 on v0

v1 whole, which is shorter than its diff:
```python
import functools

import jax
import jax.numpy as jnp
from jax import lax
from jax.experimental import pallas as pl
from jax.experimental.pallas import tpu as pltpu
from jax.sharding import PartitionSpec as P

WAVE = jnp.bfloat16
SMEM_SPEC = pl.BlockSpec(memory_space=pltpu.SMEM)
VMEM_SPEC = pl.BlockSpec(memory_space=pltpu.VMEM)
ANY_SPEC = pl.BlockSpec(memory_space=pl.ANY)
VMEM_LIMIT = 8 * 1024 * 1024
LOWER, UPPER = 0, 1
ORDER = ((1, 0), (0, 1))


def in_vmem(array):
    return pltpu.with_memory_space_constraint(array, pltpu.VMEM)


def in_hbm(array):
    return pltpu.with_memory_space_constraint(array, pltpu.HBM)


def write_list(plan_ref, side, blocks_ref, list_ref):
    listed = list_ref.shape[0]
    for slot in range(listed):
        live = slot < plan_ref[2 * listed + side]

        @pl.when(live)
        def _():
            list_ref[slot] = blocks_ref[plan_ref[side * listed + slot]]

        @pl.when(jnp.logical_not(live))
        def _():
            list_ref[slot] = jnp.zeros(list_ref.shape[1:], list_ref.dtype)


def prepare_kernel(
    ids_hbm, count_hbm, pattern_hbm, inflow_hbm, plan_ref, wave_ref, first_ref, second_ref,
    ids, count, pattern, landed, small_sems, sems,
):
    blocks = wave_ref.shape[0]
    small = [
        pltpu.make_async_copy(source, target, small_sems.at[i])
        for i, (source, target) in enumerate(
            ((ids_hbm, ids), (count_hbm, count), (pattern_hbm, pattern))
        )
    ]
    large = [
        pltpu.make_async_copy(inflow_hbm.at[0, b], landed.at[b], sems.at[b]) for b in range(blocks)
    ]
    for copy in small + large:
        copy.start()
    for copy in small:
        copy.wait()
    _, sides, listed = ids.shape
    taken = pattern.shape[1]
    for side in range(sides):
        for slot in range(listed):
            plan_ref[side * listed + slot] = ids[0, side, slot]
        plan_ref[sides * listed + side] = count[0, side]
    for b in range(blocks):
        for k in range(taken):
            plan_ref[sides * (listed + 1) + b * taken + k] = pattern[b, k]
    for b, copy in enumerate(large):
        copy.wait()
        wave_ref[b] = landed[b].astype(wave_ref.dtype)
    parity = lax.rem(lax.axis_index("depth"), 2)
    write_list(plan_ref, UPPER - parity, wave_ref, first_ref)
    write_list(plan_ref, parity, wave_ref, second_ref)


def load_kernel(
    ops_hbm, source_hbm, pass_hbm, reflect_hbm, after_ref,
    ops_ref, source_ref, pass_ref, reflect_ref, pass_rows, reflect_rows, sems,
):
    del after_ref
    copies = [
        pltpu.make_async_copy(source, target, sems.at[i])
        for i, (source, target) in enumerate(
            (
                (pass_hbm, pass_rows),
                (reflect_hbm, reflect_rows),
                (ops_hbm, ops_ref),
                (source_hbm, source_ref),
            )
        )
    ]
    for copy in copies:
        copy.start()
    for copy, rows, columns_ref in zip(copies, (pass_rows, reflect_rows), (pass_ref, reflect_ref)):
        copy.wait()
        for b in range(columns_ref.shape[0]):
            row = rows[0, pl.ds(b, 1), :]
            columns_ref[b] = jnp.broadcast_to(row, columns_ref.shape[1:]).T
    for copy in copies[2:]:
        copy.wait()


def fill_buffer(section, tick, source_ref, wave_ref, lower_ref, upper_ref, buffer):
    blocks, listed = wave_ref.shape[0], lower_ref.shape[0]
    if tick == 0:
        buffer[:blocks] = wave_ref[...]
    else:
        @pl.when(section == 0)
        def _():
            buffer[:blocks] = source_ref[tick - 1]

        @pl.when(section != 0)
        def _():
            buffer[:blocks] = wave_ref[...]
    buffer[blocks : blocks + listed] = lower_ref[...]
    buffer[blocks + listed :] = upper_ref[...]


def extrapolate_block(plan_ref, pattern_start, ops_ref, buffer, b):
    taken = ops_ref.shape[2]
    points = ops_ref.shape[5]
    left = jnp.concatenate(
        [ops_ref[0, b, k].reshape(2 * points, points) for k in range(taken)], axis=1
    )
    right = jnp.concatenate(
        [buffer[plan_ref[pattern_start + b * taken + k]] for k in range(taken)], axis=0
    )
    products = jnp.dot(left, right, preferred_element_type=jnp.float32)
    half = products.shape[1] // 2
    real_part = products[:points, :half] - products[points:, half:]
    imag_part = products[:points, half:] + products[points:, :half]
    return real_part, imag_part


def tick_kernel(
    parity, tick, sections, plan_ref, ops_ref, source_ref, pass_ref, reflect_ref,
    wave_ref, lower_ref, upper_ref, *rest,
):
    echo_ref, onward_ref, down_ref, up_ref, buffer = rest[-5:]
    section = lax.axis_index("depth")
    listed = lower_ref.shape[0]

    @pl.when(lax.rem(section, 2) == parity)
    def _():
        fill_buffer(section, tick, source_ref, wave_ref, lower_ref, upper_ref, buffer)
        for b in range(wave_ref.shape[0]):
            parts = extrapolate_block(plan_ref, 2 * (listed + 1), ops_ref, buffer, b)
            for i, part in enumerate(parts):
                cols = pl.ds(i * part.shape[1], part.shape[1])
                onward_ref[b, :, cols] = (pass_ref[b] * part).astype(onward_ref.dtype)
                echo_ref[b, :, cols] = (reflect_ref[b] * part).astype(echo_ref.dtype)

        @pl.when(section != sections - 1)
        def _():
            write_list(plan_ref, UPPER, onward_ref, up_ref)
            write_list(plan_ref, LOWER, onward_ref, down_ref)

        @pl.when(section == sections - 1)
        def _():
            write_list(plan_ref, UPPER, source_ref.at[tick], up_ref)
            write_list(plan_ref, LOWER, source_ref.at[tick], down_ref)


def last_kernel(
    parity, tick, plan_ref, ops_ref, source_ref, pass_ref, reflect_ref,
    wave_ref, lower_ref, upper_ref, *rest,
):
    earlier = rest[:tick]
    (reflected_ref, transmitted_ref, buffer, echo, leaving,
     early_sems, echo_sems, leave_sems) = rest[-8:]
    section = lax.axis_index("depth")
    listed = lower_ref.shape[0]

    @pl.when(lax.rem(section, 2) == parity)
    def _():
        copies = [
            pltpu.make_async_copy(earlier[t], reflected_ref.at[t, 0], early_sems.at[t])
            for t in range(tick)
        ]
        for copy in copies:
            copy.start()
        fill_buffer(section, tick, source_ref, wave_ref, lower_ref, upper_ref, buffer)
        for b in range(wave_ref.shape[0]):
            parts = extrapolate_block(plan_ref, 2 * (listed + 1), ops_ref, buffer, b)
            for i, part in enumerate(parts):
                cols = pl.ds(i * part.shape[1], part.shape[1])
                leaving[b, :, cols] = pass_ref[b] * part
                echo[b, :, cols] = (reflect_ref[b] * part).astype(echo.dtype)
            for copy in (
                pltpu.make_async_copy(leaving.at[b], transmitted_ref.at[0, b], leave_sems.at[b]),
                pltpu.make_async_copy(echo.at[b], reflected_ref.at[tick, 0, b], echo_sems.at[b]),
            ):
                copy.start()
                copies.append(copy)
        for copy in copies:
            copy.wait()


def beside(sections, tiles, ways, deeper):
    return [
        (s * tiles + j, ((s + 1) % sections if deeper else s) * tiles + j + ways[s % 2])
        for s in range(sections)
        if s % 2 in ways
        for j in range(tiles)
        if 0 <= j + ways[s % 2] < tiles
    ]


def per_device(
    inflow, source, operators, transmission, reflectivity, send_ids, send_count, pattern
):
    sections, tiles = lax.axis_size("depth"), lax.axis_size("lat")
    ticks = source.shape[0] + 1
    _, blocks, points, columns = inflow.shape
    listed = send_ids.shape[-1]
    taken = operators.shape[2]
    wave_type = pltpu.VMEM((blocks, points, columns), WAVE)
    list_type = pltpu.VMEM((listed, points, columns), WAVE)
    params = pltpu.CompilerParams(vmem_limit_bytes=VMEM_LIMIT)
    tick_cost = pl.CostEstimate(
        flops=blocks * taken * 4 * points * points * columns,
        bytes_accessed=2 * operators.size + 8 * blocks * points * columns,
        transcendentals=0,
    )
    both = ("depth", "lat")

    plan, wave, first, second = pl.pallas_call(
        prepare_kernel,
        out_shape=(
            pltpu.SMEM((2 * (listed + 1) + blocks * taken,), jnp.int32),
            wave_type,
            list_type,
            list_type,
        ),
        in_specs=[ANY_SPEC] * 4,
        out_specs=(SMEM_SPEC,) + (VMEM_SPEC,) * 3,
        scratch_shapes=[
            pltpu.SMEM(send_ids.shape, jnp.int32),
            pltpu.SMEM(send_count.shape, jnp.int32),
            pltpu.SMEM(pattern.shape, jnp.int32),
            pltpu.VMEM((blocks, points, columns), inflow.dtype),
            pltpu.SemaphoreType.DMA((3,)),
            pltpu.SemaphoreType.DMA((blocks,)),
        ],
        compiler_params=params,
        cost_estimate=pl.CostEstimate(
            flops=inflow.size, bytes_accessed=8 * inflow.size, transcendentals=0
        ),
        name="prepare",
    )(*map(in_hbm, (send_ids, send_count, pattern, inflow)))
    loaded_first = first
    first = lax.ppermute(first, both, beside(sections, tiles, {0: 1, 1: -1}, False))
    second = lax.ppermute(second, both, beside(sections, tiles, {0: -1, 1: 1}, False))

    column_type = pltpu.VMEM((blocks, points, columns // 2), jnp.float32)
    fixed = pl.pallas_call(
        load_kernel,
        out_shape=(
            pltpu.VMEM(operators.shape, operators.dtype),
            pltpu.VMEM(source.shape, source.dtype),
            column_type,
            column_type,
        ),
        in_specs=[ANY_SPEC] * 4 + [VMEM_SPEC],
        out_specs=(VMEM_SPEC,) * 4,
        scratch_shapes=[
            pltpu.VMEM(transmission.shape, transmission.dtype),
            pltpu.VMEM(reflectivity.shape, reflectivity.dtype),
            pltpu.SemaphoreType.DMA((4,)),
        ],
        compiler_params=params,
        cost_estimate=pl.CostEstimate(
            flops=0, bytes_accessed=4 * (operators.size + source.size), transcendentals=0
        ),
        name="load",
    )(*map(in_hbm, (operators, source, transmission, reflectivity)), in_vmem(loaded_first))
    fixed = [plan, *map(in_vmem, fixed)]
    buffer_type = pltpu.VMEM((blocks + 2 * listed, points, columns), WAVE)

    arrived = {0: (wave, first, second), 1: (wave, second, first)}
    echoes = []
    for tick in range(ticks - 1):
        leaving = {}
        echo = None
        for parity in ORDER[tick % 2]:
            known = [] if echo is None else [in_vmem(echo)]
            echo, onward, down, up = pl.pallas_call(
                functools.partial(tick_kernel, parity, tick, sections),
                out_shape=(wave_type, wave_type, list_type, list_type),
                in_specs=[SMEM_SPEC] + [VMEM_SPEC] * (7 + len(known)),
                out_specs=(VMEM_SPEC,) * 4,
                input_output_aliases={8: 0} if known else {},
                scratch_shapes=[buffer_type],
                compiler_params=params,
                cost_estimate=tick_cost,
                name=f"tick{tick}_{parity}",
            )(*fixed, *map(in_vmem, arrived[parity]), *known)
            deeper = [(s, s + 1) for s in range(parity, sections - 1, 2)]
            up = lax.ppermute(up, both, beside(sections, tiles, {parity: 1}, True))
            down = lax.ppermute(down, both, beside(sections, tiles, {parity: -1}, True))
            wave = lax.ppermute(onward, "depth", deeper)
            leaving[1 - parity] = (wave, up, down)
        arrived = leaving
        echoes.append(echo)

    tick = ticks - 1
    results = []
    result_types = (
        jax.ShapeDtypeStruct((ticks, 1, blocks, points, columns), WAVE),
        jax.ShapeDtypeStruct((1, blocks, points, columns), jnp.float32),
    )
    for parity in ORDER[tick % 2]:
        results = pl.pallas_call(
            functools.partial(last_kernel, parity, tick),
            out_shape=result_types,
            in_specs=[SMEM_SPEC] + [VMEM_SPEC] * (7 + tick) + [ANY_SPEC] * len(results),
            out_specs=(ANY_SPEC, ANY_SPEC),
            input_output_aliases={8 + tick: 0, 9 + tick: 1} if results else {},
            scratch_shapes=[
                buffer_type,
                pltpu.VMEM((blocks, points, columns), WAVE),
                pltpu.VMEM((blocks, points, columns), jnp.float32),
                pltpu.SemaphoreType.DMA((tick,)),
                pltpu.SemaphoreType.DMA((blocks,)),
                pltpu.SemaphoreType.DMA((blocks,)),
            ],
            compiler_params=params,
            cost_estimate=tick_cost,
            name=f"last_tick_{parity}",
        )(*fixed, *map(in_vmem, arrived[parity]), *map(in_vmem, echoes), *results)
    return tuple(results)


def solution(mesh):
    return jax.shard_map(
        per_device,
        mesh=mesh,
        in_specs=(
            P("depth", "lat", None, None),
            P(None, "lat", None, None),
            P("depth", "lat", None, None, None, None),
            P("depth", "lat", None),
            P("depth", "lat", None),
            P("lat", None, None),
            P("lat", None),
            P("lat", None),
        ),
        out_specs=(P(None, "depth", "lat", None, None), P("depth", "lat", None, None)),
        check_vma=False,
    )
```

time: 56.1 us -> 63.8 us (1.14)
  waiting for transfers between devices: 8.48 us -> 23 us
  starting transfers between devices: 40 us -> 32.6 us
    ppermute x8 -> x14, waiting for transfers between devices: 8.47 us -> 23 us  [the longest x6 20.2 us: per_device(): down = lax.ppermute(down, both, beside(sections, tiles, {parity: -1}, True))]
    ppermute x8 -> x14, starting transfers between devices: 33.1 us -> 23.7 us  [the longest x6 12.5 us: per_device(): up = lax.ppermute(up, both, beside(sections, tiles, {parity: 1}, True))]
    ppermute x3 -> x6, starting transfers between devices: 6.94 us -> 8.89 us  [per_device(): wave = lax.ppermute(onward, 'depth', deeper)]
    pallas_call x4 -> x8, Pallas kernels: 3.56 us -> 3.76 us  [the longest x6 2.18 us: per_device(): pl.pallas_call(functools.partial(tick_kernel, parity, tick, sections), ou...]
  transfers between devices with their start and end apart: 11 -> 20, of which waited for: 4 -> 3; matrix products, arithmetic and copies ran while one was open for 0% -> 0% of each run, Pallas kernels for 3% -> 5%
where the time goes in v1:
time: 63.8 us; the launch traced here: 63.2 us
  starting transfers between devices  32.6 us (51%)
  waiting for transfers between devices  23 us (36%)
  Pallas kernels  6.65 us (10%)
  between operations  0.98 us (2%)
    ppermute x6, waiting for transfers between devices, per_device(): down = lax.ppermute(down, both, beside(sections, tiles, {parity: -1}, True))  20.2 us
    ppermute x6, starting transfers between devices, per_device(): up = lax.ppermute(up, both, beside(sections, tiles, {parity: 1}, True))  12.5 us
    ppermute x6, starting transfers between devices, per_device(): wave = lax.ppermute(onward, 'depth', deeper)  8.89 us
    ppermute x6, starting transfers between devices, per_device(): down = lax.ppermute(down, both, beside(sections, tiles, {parity: -1}, True))  5.88 us
    ppermute x1, starting transfers between devices, per_device(): lax.ppermute(second, both, beside(sections, tiles, {0: -1, 1: 1}, False))  4.04 us
    ppermute x1, waiting for transfers between devices, per_device(): lax.ppermute(first, both, beside(sections, tiles, {0: 1, 1: -1}, False))  2.72 us
    pallas_call x6, Pallas kernels, per_device(): pl.pallas_call(functools.partial(tick_kernel, parity, tick, sections), ou...  2.18 us
    pallas_call x1, Pallas kernels, per_device(): pl.pallas_call(load_kernel, out_shape=(pltpu.VMEM(operators.shape, operat...  1.68 us
  transfers between devices with their start and end apart: 20, of which 3 were waited for; matrix products, arithmetic and copies ran while one was open for 0% of the time, Pallas kernels for 5%

profile of v1, /device:TPU:1, one launch (start us, length us, event | category | flops | bytes accessed | tf_op | source)
XLA Modules:
  0.0 63.2 jit_solution(17065206913434205732)
XLA Ops:
  0.6 1.2 %prepare.1 = (s32[30]{0:T(128)S(4)}, bf16[4,128,256]{2,1,0:T(8,128)(2,1)S(1)}, bf16[2,128,256]{2,1,0:T(8,128)(2,1)S(1)}, bf16[2,128,256]{2,1,0:T(8,128)(2,1)S(1)}) custom-call(s32[1,2,2]{2,1,0:T(2,128)} %ids_hbm.1, s32[1,2]{1,0:T(1,128)} %count_hbm.1, s32[4,6]{1,0:T(4,128)} %pattern_hbm.1, f32[1,4,128,256]{3,2,1,0:T(8,128)} %inflow_hbm.1), custom_call_target="tpu_custom_call" | custom-call | flops 131072 | bytes 1048576 | tf_op jit(solution)/shard_map/prepare/pallas_call | solution.py:227
  1.9 4.0 %collective-permute-start.1 = (bf16[2,128,256]{2,1,0:T(8,128)(2,1)S(1)}, bf16[2,128,256]{2,1,0:T(8,128)(2,1)S(1)}, u32[]{:S(2)}, u32[]{:S(2)}) collective-permute-start(bf16[2,128,256]{2,1,0:T(8,128)(2,1)S(1)} %get-tuple-element.43), channel_id=1, source_target_pairs={{1,0},{2,1},{3,2},{4,5},{5,6},{6,7},{9,8},{10,9},{11,10},{12,13},{... | collective-permute-start | bytes 393224 | tf_op jit(solution)/shard_map/ppermute | solution.py:253
  5.9 1.3 %collective-permute-start = (bf16[2,128,256]{2,1,0:T(8,128)(2,1)S(1)}, bf16[2,128,256]{2,1,0:T(8,128)(2,1)S(1)}, u32[]{:S(2)}, u32[]{:S(2)}) collective-permute-start(bf16[2,128,256]{2,1,0:T(8,128)(2,1)S(1)} %get-tuple-element.37.after_ref), channel_id=1, source_target_pairs={{0,1},{1,2},{2,3},{5,4},{6,5},{7,6},{8,9},{9,10},{10,11},{13,12},{... | collective-permute-start | bytes 393224 | tf_op jit(solution)/shard_map/ppermute | solution.py:252
  7.2 1.7 %load.1 = (bf16[1,4,6,2,128,128]{5,4,3,2,1,0:T(8,128)(2,1)S(1)}, bf16[3,4,128,256]{3,2,1,0:T(8,128)(2,1)S(1)}, f32[4,128,128]{2,1,0:T(8,128)S(1)}, f32[4,128,128]{2,1,0:T(8,128)S(1)}) custom-call(bf16[1,4,6,2,128,128]{5,4,3,2,1,0:T(8,128)(2,1)} %ops_hbm.1, bf16[3,4,128,256]{3,2,1,0:T(8,128)(2,1)} %source_hbm.1, f32[1,4,128]{2,1,0:T(4,128)} %pass_hbm.1, ...), custom_call_target="tpu_custom_call" | custom-call | bytes 4718592 | tf_op jit(solution)/shard_map/load/pallas_call | solution.py:256
  8.9 0.0 collective-permute-done.1.lower_ref.upper_ref
  8.9 2.7 %collective-permute-done.upper_ref.lower_ref = bf16[2,128,256]{2,1,0:T(8,128)(2,1)S(1)} collective-permute-done((bf16[2,128,256]{2,1,0:T(8,128)(2,1)S(1)}, bf16[2,128,256]{2,1,0:T(8,128)(2,1)S(1)}, u32[]{:S(2)}, u32[]{:S(2)}) %collective-permute-start) | collective-permute-done | bytes 131104 | tf_op jit(solution)/shard_map/ppermute | solution.py:252
  11.6 0.7 %tick0_1.1 = (bf16[4,128,256]{2,1,0:T(8,128)(2,1)S(1)}, bf16[4,128,256]{2,1,0:T(8,128)(2,1)S(1)}, bf16[2,128,256]{2,1,0:T(8,128)(2,1)S(1)}, bf16[2,128,256]{2,1,0:T(8,128)(2,1)S(1)}) custom-call(s32[30]{0:T(128)S(4)} %get-tuple-element.36.plan_ref, bf16[1,4,6,2,128,128]{5,4,3,2,1,0:T(8,128)(2,1)S(1)} %get-tuple-element.38.ops_ref, ...), custom_call_target="tpu_custom_call" | custom-call | flops 402653184 | bytes 2621440 | tf_op jit(solution)/shard_map/tick0_1/pallas_call | solution.py:287
  12.3 2.4 %collective-permute-start.5 = (bf16[4,128,256]{2,1,0:T(8,128)(2,1)S(1)}, bf16[4,128,256]{2,1,0:T(8,128)(2,1)S(1)}, u32[]{:S(2)}, u32[]{:S(2)}) collective-permute-start(bf16[4,128,256]{2,1,0:T(8,128)(2,1)S(1)} %get-tuple-element.48), channel_id=1, source_target_pairs={{4,8},{12,16},{20,24},{5,9},{13,17},{21,25},{6,10},{14,18},{22,26}... | collective-permute-start | bytes 786440 | tf_op jit(solution)/shard_map/ppermute | solution.py:301
  14.7 3.2 %collective-permute-start.6 = (bf16[2,128,256]{2,1,0:T(8,128)(2,1)S(1)}, bf16[2,128,256]{2,1,0:T(8,128)(2,1)S(1)}, u32[]{:S(2)}, u32[]{:S(2)}) collective-permute-start(bf16[2,128,256]{2,1,0:T(8,128)(2,1)S(1)} %get-tuple-element.49), channel_id=1, source_target_pairs={{4,9},{5,10},{6,11},{12,17},{13,18},{14,19},{20,25},{21,26},{22,27... | collective-permute-start | bytes 393224 | tf_op jit(solution)/shard_map/ppermute | solution.py:299
  17.9 1.3 %collective-permute-start.2 = (bf16[4,128,256]{2,1,0:T(8,128)(2,1)S(1)}, bf16[4,128,256]{2,1,0:T(8,128)(2,1)S(1)}, u32[]{:S(2)}, u32[]{:S(2)}) collective-permute-start(bf16[4,128,256]{2,1,0:T(8,128)(2,1)S(1)} %get-tuple-element.45), channel_id=1, source_target_pairs={{0,4},{8,12},{16,20},{24,28},{1,5},{9,13},{17,21},{25,29},{2,6},{1... | collective-permute-start | bytes 786440 | tf_op jit(solution)/shard_map/ppermute | solution.py:301
  19.2 0.7 %collective-permute-start.7 = (bf16[2,128,256]{2,1,0:T(8,128)(2,1)S(1)}, bf16[2,128,256]{2,1,0:T(8,128)(2,1)S(1)}, u32[]{:S(2)}, u32[]{:S(2)}) collective-permute-start(bf16[2,128,256]{2,1,0:T(8,128)(2,1)S(1)} %get-tuple-element.50), channel_id=1, source_target_pairs={{5,8},{6,9},{7,10},{13,16},{14,17},{15,18},{21,24},{22,25},{23,26}... | collective-permute-start | bytes 393224 | tf_op jit(solution)/shard_map/ppermute | solution.py:300
  19.9 0.7 %collective-permute-start.3 = (bf16[2,128,256]{2,1,0:T(8,128)(2,1)S(1)}, bf16[2,128,256]{2,1,0:T(8,128)(2,1)S(1)}, u32[]{:S(2)}, u32[]{:S(2)}) collective-permute-start(bf16[2,128,256]{2,1,0:T(8,128)(2,1)S(1)} %get-tuple-element.46), channel_id=1, source_target_pairs={{0,5},{1,6},{2,7},{8,13},{9,14},{10,15},{16,21},{17,22},{18,23},{2... | collective-permute-start | bytes 393224 | tf_op jit(solution)/shard_map/ppermute | solution.py:299
  20.6 0.0 collective-permute-done.6.lower_ref
  20.6 1.3 %collective-permute-start.4 = (bf16[2,128,256]{2,1,0:T(8,128)(2,1)S(1)}, bf16[2,128,256]{2,1,0:T(8,128)(2,1)S(1)}, u32[]{:S(2)}, u32[]{:S(2)}) collective-permute-start(bf16[2,128,256]{2,1,0:T(8,128)(2,1)S(1)} %get-tuple-element.47), channel_id=1, source_target_pairs={{1,4},{2,5},{3,6},{9,12},{10,13},{11,14},{17,20},{18,21},{19,22},{... | collective-permute-start | bytes 393224 | tf_op jit(solution)/shard_map/ppermute | solution.py:300
  21.9 0.0 collective-permute-done.7.upper_ref
  21.9 0.0 collective-permute-done.5.wave_ref
  21.9 1.3 %collective-permute-start.11 = (bf16[4,128,256]{2,1,0:T(8,128)(2,1)S(1)}, bf16[4,128,256]{2,1,0:T(8,128)(2,1)S(1)}, u32[]{:S(2)}, u32[]{:S(2)}) collective-permute-start(bf16[4,128,256]{2,1,0:T(8,128)(2,1)S(1)} %get-tuple-element.55), channel_id=1, source_target_pairs={{0,4},{8,12},{16,20},{24,28},{1,5},{9,13},{17,21},{25,29},{2,6},{1... | collective-permute-start | bytes 786440 | tf_op jit(solution)/shard_map/ppermute | solution.py:301
  23.2 0.7 %collective-permute-start.12 = (bf16[2,128,256]{2,1,0:T(8,128)(2,1)S(1)}, bf16[2,128,256]{2,1,0:T(8,128)(2,1)S(1)}, u32[]{:S(2)}, u32[]{:S(2)}) collective-permute-start(bf16[2,128,256]{2,1,0:T(8,128)(2,1)S(1)} %get-tuple-element.56), channel_id=1, source_target_pairs={{0,5},{1,6},{2,7},{8,13},{9,14},{10,15},{16,21},{17,22},{18,23},{2... | collective-permute-start | bytes 393224 | tf_op jit(solution)/shard_map/ppermute | solution.py:299
  23.9 0.0 collective-permute-done.3.lower_ref
  23.9 8.1 %collective-permute-done.4.upper_ref = bf16[2,128,256]{2,1,0:T(8,128)(2,1)S(1)} collective-permute-done((bf16[2,128,256]{2,1,0:T(8,128)(2,1)S(1)}, bf16[2,128,256]{2,1,0:T(8,128)(2,1)S(1)}, u32[]{:S(2)}, u32[]{:S(2)}) %collective-permute-start.4) | collective-permute-done | bytes 131104 | tf_op jit(solution)/shard_map/ppermute | solution.py:300
  32.0 0.0 collective-permute-done.2.wave_ref
  32.0 0.7 %tick1_1.1 = (bf16[4,128,256]{2,1,0:T(8,128)(2,1)S(1)}, bf16[4,128,256]{2,1,0:T(8,128)(2,1)S(1)}, bf16[2,128,256]{2,1,0:T(8,128)(2,1)S(1)}, bf16[2,128,256]{2,1,0:T(8,128)(2,1)S(1)}) custom-call(s32[30]{0:T(128)S(4)} %get-tuple-element.36.plan_ref, bf16[1,4,6,2,128,128]{5,4,3,2,1,0:T(8,128)(2,1)S(1)} %get-tuple-element.38.ops_ref, ...), custom_call_target="tpu_custom_call", output_to_operand_aliasing={{0}: (8, {})} | custom-call | flops 402653184 | bytes 2621440 | tf_op jit(solution)/shard_map/tick1_1/pallas_call | solution.py:287
  32.7 1.3 %collective-permute-start.8 = (bf16[4,128,256]{2,1,0:T(8,128)(2,1)S(1)}, bf16[4,128,256]{2,1,0:T(8,128)(2,1)S(1)}, u32[]{:S(2)}, u32[]{:S(2)}) collective-permute-start(bf16[4,128,256]{2,1,0:T(8,128)(2,1)S(1)} %get-tuple-element.52), channel_id=1, source_target_pairs={{4,8},{12,16},{20,24},{5,9},{13,17},{21,25},{6,10},{14,18},{22,26}... | collective-permute-start | bytes 786440 | tf_op jit(solution)/shard_map/ppermute | solution.py:301
  34.0 1.3 %collective-permute-start.13 = (bf16[2,128,256]{2,1,0:T(8,128)(2,1)S(1)}, bf16[2,128,256]{2,1,0:T(8,128)(2,1)S(1)}, u32[]{:S(2)}, u32[]{:S(2)}) collective-permute-start(bf16[2,128,256]{2,1,0:T(8,128)(2,1)S(1)} %get-tuple-element.57), channel_id=1, source_target_pairs={{1,4},{2,5},{3,6},{9,12},{10,13},{11,14},{17,20},{18,21},{19,22},{... | collective-permute-start | bytes 393224 | tf_op jit(solution)/shard_map/ppermute | solution.py:300
  35.3 6.0 %collective-permute-start.9 = (bf16[2,128,256]{2,1,0:T(8,128)(2,1)S(1)}, bf16[2,128,256]{2,1,0:T(8,128)(2,1)S(1)}, u32[]{:S(2)}, u32[]{:S(2)}) collective-permute-start(bf16[2,128,256]{2,1,0:T(8,128)(2,1)S(1)} %get-tuple-element.53), channel_id=1, source_target_pairs={{4,9},{5,10},{6,11},{12,17},{13,18},{14,19},{20,25},{21,26},{22,27... | collective-permute-start | bytes 393224 | tf_op jit(solution)/shard_map/ppermute | solution.py:299
  41.4 0.0 collective-permute-done.12.lower_ref
  41.4 0.7 %collective-permute-start.10 = (bf16[2,128,256]{2,1,0:T(8,128)(2,1)S(1)}, bf16[2,128,256]{2,1,0:T(8,128)(2,1)S(1)}, u32[]{:S(2)}, u32[]{:S(2)}) collective-permute-start(bf16[2,128,256]{2,1,0:T(8,128)(2,1)S(1)} %get-tuple-element.54), channel_id=1, source_target_pairs={{5,8},{6,9},{7,10},{13,16},{14,17},{15,18},{21,24},{22,25},{23,26}... | collective-permute-start | bytes 393224 | tf_op jit(solution)/shard_map/ppermute | solution.py:300
  42.1 0.0 collective-permute-done.13.upper_ref
  42.1 0.0 collective-permute-done.11.wave_ref
  42.1 0.7 %tick2_1.1 = (bf16[4,128,256]{2,1,0:T(8,128)(2,1)S(1)}, bf16[4,128,256]{2,1,0:T(8,128)(2,1)S(1)}, bf16[2,128,256]{2,1,0:T(8,128)(2,1)S(1)}, bf16[2,128,256]{2,1,0:T(8,128)(2,1)S(1)}) custom-call(s32[30]{0:T(128)S(4)} %get-tuple-element.36.plan_ref, bf16[1,4,6,2,128,128]{5,4,3,2,1,0:T(8,128)(2,1)S(1)} %get-tuple-element.38.ops_ref, ...), custom_call_target="tpu_custom_call" | custom-call | flops 402653184 | bytes 2621440 | tf_op jit(solution)/shard_map/tick2_1/pallas_call | solution.py:287
  42.8 1.3 %collective-permute-start.18 = (bf16[2,128,256]{2,1,0:T(8,128)(2,1)S(1)}, bf16[2,128,256]{2,1,0:T(8,128)(2,1)S(1)}, u32[]{:S(2)}, u32[]{:S(2)}) collective-permute-start(bf16[2,128,256]{2,1,0:T(8,128)(2,1)S(1)} %get-tuple-element.66), channel_id=1, source_target_pairs={{4,9},{5,10},{6,11},{12,17},{13,18},{14,19},{20,25},{21,26},{22,27... | collective-permute-start | bytes 393224 | tf_op jit(solution)/shard_map/ppermute | solution.py:299
  44.1 1.3 %collective-permute-start.17 = (bf16[4,128,256]{2,1,0:T(8,128)(2,1)S(1)}, bf16[4,128,256]{2,1,0:T(8,128)(2,1)S(1)}, u32[]{:S(2)}, u32[]{:S(2)}) collective-permute-start(bf16[4,128,256]{2,1,0:T(8,128)(2,1)S(1)} %get-tuple-element.65), channel_id=1, source_target_pairs={{4,8},{12,16},{20,24},{5,9},{13,17},{21,25},{6,10},{14,18},{22,26}... | collective-permute-start | bytes 786440 | tf_op jit(solution)/shard_map/ppermute | solution.py:301
  45.4 0.0 collective-permute-done.9.lower_ref
  45.5 0.0 collective-permute-done.10.upper_ref
  45.5 0.0 collective-permute-done.8.wave_ref
  45.5 1.3 %collective-permute-start.14 = (bf16[4,128,256]{2,1,0:T(8,128)(2,1)S(1)}, bf16[4,128,256]{2,1,0:T(8,128)(2,1)S(1)}, u32[]{:S(2)}, u32[]{:S(2)}) collective-permute-start(bf16[4,128,256]{2,1,0:T(8,128)(2,1)S(1)} %get-tuple-element.59), channel_id=1, source_target_pairs={{0,4},{8,12},{16,20},{24,28},{1,5},{9,13},{17,21},{25,29},{2,6},{1... | collective-permute-start | bytes 786440 | tf_op jit(solution)/shard_map/ppermute | solution.py:301
  46.8 0.7 %collective-permute-start.19 = (bf16[2,128,256]{2,1,0:T(8,128)(2,1)S(1)}, bf16[2,128,256]{2,1,0:T(8,128)(2,1)S(1)}, u32[]{:S(2)}, u32[]{:S(2)}) collective-permute-start(bf16[2,128,256]{2,1,0:T(8,128)(2,1)S(1)} %get-tuple-element.67), channel_id=1, source_target_pairs={{5,8},{6,9},{7,10},{13,16},{14,17},{15,18},{21,24},{22,25},{23,26}... | collective-permute-start | bytes 393224 | tf_op jit(solution)/shard_map/ppermute | solution.py:300
  47.5 0.7 %collective-permute-start.15 = (bf16[2,128,256]{2,1,0:T(8,128)(2,1)S(1)}, bf16[2,128,256]{2,1,0:T(8,128)(2,1)S(1)}, u32[]{:S(2)}, u32[]{:S(2)}) collective-permute-start(bf16[2,128,256]{2,1,0:T(8,128)(2,1)S(1)} %get-tuple-element.60), channel_id=1, source_target_pairs={{0,5},{1,6},{2,7},{8,13},{9,14},{10,15},{16,21},{17,22},{18,23},{2... | collective-permute-start | bytes 393224 | tf_op jit(solution)/shard_map/ppermute | solution.py:299
  48.2 0.0 collective-permute-done.18.lower_ref
  48.2 1.3 %collective-permute-start.16 = (bf16[2,128,256]{2,1,0:T(8,128)(2,1)S(1)}, bf16[2,128,256]{2,1,0:T(8,128)(2,1)S(1)}, u32[]{:S(2)}, u32[]{:S(2)}) collective-permute-start(bf16[2,128,256]{2,1,0:T(8,128)(2,1)S(1)} %get-tuple-element.61), channel_id=1, source_target_pairs={{1,4},{2,5},{3,6},{9,12},{10,13},{11,14},{17,20},{18,21},{19,22},{... | collective-permute-start | bytes 393224 | tf_op jit(solution)/shard_map/ppermute | solution.py:300
  49.5 0.0 collective-permute-done.19.upper_ref
  49.5 0.0 collective-permute-done.17.wave_ref
  49.5 0.1 last_tick_0.1
  49.6 0.0 collective-permute-done.15.lower_ref
  49.6 12.2 %collective-permute-done.16.upper_ref = bf16[2,128,256]{2,1,0:T(8,128)(2,1)S(1)} collective-permute-done((bf16[2,128,256]{2,1,0:T(8,128)(2,1)S(1)}, bf16[2,128,256]{2,1,0:T(8,128)(2,1)S(1)}, u32[]{:S(2)}, u32[]{:S(2)}) %collective-permute-start.16) | collective-permute-done | bytes 131104 | tf_op jit(solution)/shard_map/ppermute | solution.py:300
  61.8 0.0 collective-permute-done.14.wave_ref
  61.8 1.5 %last_tick_1.1 = (bf16[4,1,4,128,256]{4,3,2,1,0:T(8,128)(2,1)}, f32[1,4,128,256]{3,2,1,0:T(8,128)}) custom-call(s32[30]{0:T(128)S(4)} %get-tuple-element.36.plan_ref, bf16[1,4,6,2,128,128]{5,4,3,2,1,0:T(8,128)(2,1)S(1)} %get-tuple-element.38.ops_ref, ...), custom_call_target="tpu_custom_call", output_to_operand_aliasing={{0}: (11, {}), {1}: (12, {})} | custom-call | flops 402653184 | bytes 2621440 | tf_op jit(solution)/shard_map/last_tick_1/pallas_call | solution.py:313
  (3 shorter events, 0.1 us)
Async XLA Ops:
  1.9 7.0 %collective-permute-start.1 = (bf16[2,128,256]{2,1,0:T(8,128)(2,1)S(1)}, bf16[2,128,256]{2,1,0:T(8,128)(2,1)S(1)}, u32[]{:S(2)}, u32[]{:S(2)}) collective-permute-start(bf16[2,128,256]{2,1,0:T(8,128)(2,1)S(1)} %get-tuple-element.43), channel_id=1, source_target_pairs={{1,0},{2,1},{3,2},{4,5},{5,6},{6,7},{9,8},{10,9},{11,10},{12,13},{... | collective-permute-start | bytes 393224 | tf_op jit(solution)/shard_map/ppermute | solution.py:253
  5.9 5.7 %collective-permute-start = (bf16[2,128,256]{2,1,0:T(8,128)(2,1)S(1)}, bf16[2,128,256]{2,1,0:T(8,128)(2,1)S(1)}, u32[]{:S(2)}, u32[]{:S(2)}) collective-permute-start(bf16[2,128,256]{2,1,0:T(8,128)(2,1)S(1)} %get-tuple-element.37.after_ref), channel_id=1, source_target_pairs={{0,1},{1,2},{2,3},{5,4},{6,5},{7,6},{8,9},{9,10},{10,11},{13,12},{... | collective-permute-start | bytes 393224 | tf_op jit(solution)/shard_map/ppermute | solution.py:252
  12.3 9.6 %collective-permute-start.5 = (bf16[4,128,256]{2,1,0:T(8,128)(2,1)S(1)}, bf16[4,128,256]{2,1,0:T(8,128)(2,1)S(1)}, u32[]{:S(2)}, u32[]{:S(2)}) collective-permute-start(bf16[4,128,256]{2,1,0:T(8,128)(2,1)S(1)} %get-tuple-element.48), channel_id=1, source_target_pairs={{4,8},{12,16},{20,24},{5,9},{13,17},{21,25},{6,10},{14,18},{22,26}... | collective-permute-start | bytes 786440 | tf_op jit(solution)/shard_map/ppermute | solution.py:301
  14.7 5.9 %collective-permute-start.6 = (bf16[2,128,256]{2,1,0:T(8,128)(2,1)S(1)}, bf16[2,128,256]{2,1,0:T(8,128)(2,1)S(1)}, u32[]{:S(2)}, u32[]{:S(2)}) collective-permute-start(bf16[2,128,256]{2,1,0:T(8,128)(2,1)S(1)} %get-tuple-element.49), channel_id=1, source_target_pairs={{4,9},{5,10},{6,11},{12,17},{13,18},{14,19},{20,25},{21,26},{22,27... | collective-permute-start | bytes 393224 | tf_op jit(solution)/shard_map/ppermute | solution.py:299
  17.9 14.1 %collective-permute-start.2 = (bf16[4,128,256]{2,1,0:T(8,128)(2,1)S(1)}, bf16[4,128,256]{2,1,0:T(8,128)(2,1)S(1)}, u32[]{:S(2)}, u32[]{:S(2)}) collective-permute-start(bf16[4,128,256]{2,1,0:T(8,128)(2,1)S(1)} %get-tuple-element.45), channel_id=1, source_target_pairs={{0,4},{8,12},{16,20},{24,28},{1,5},{9,13},{17,21},{25,29},{2,6},{1... | collective-permute-start | bytes 786440 | tf_op jit(solution)/shard_map/ppermute | solution.py:301
  19.2 2.7 %collective-permute-start.7 = (bf16[2,128,256]{2,1,0:T(8,128)(2,1)S(1)}, bf16[2,128,256]{2,1,0:T(8,128)(2,1)S(1)}, u32[]{:S(2)}, u32[]{:S(2)}) collective-permute-start(bf16[2,128,256]{2,1,0:T(8,128)(2,1)S(1)} %get-tuple-element.50), channel_id=1, source_target_pairs={{5,8},{6,9},{7,10},{13,16},{14,17},{15,18},{21,24},{22,25},{23,26}... | collective-permute-start | bytes 393224 | tf_op jit(solution)/shard_map/ppermute | solution.py:300
  19.9 4.0 %collective-permute-start.3 = (bf16[2,128,256]{2,1,0:T(8,128)(2,1)S(1)}, bf16[2,128,256]{2,1,0:T(8,128)(2,1)S(1)}, u32[]{:S(2)}, u32[]{:S(2)}) collective-permute-start(bf16[2,128,256]{2,1,0:T(8,128)(2,1)S(1)} %get-tuple-element.46), channel_id=1, source_target_pairs={{0,5},{1,6},{2,7},{8,13},{9,14},{10,15},{16,21},{17,22},{18,23},{2... | collective-permute-start | bytes 393224 | tf_op jit(solution)/shard_map/ppermute | solution.py:299
  20.6 11.4 %collective-permute-start.4 = (bf16[2,128,256]{2,1,0:T(8,128)(2,1)S(1)}, bf16[2,128,256]{2,1,0:T(8,128)(2,1)S(1)}, u32[]{:S(2)}, u32[]{:S(2)}) collective-permute-start(bf16[2,128,256]{2,1,0:T(8,128)(2,1)S(1)} %get-tuple-element.47), channel_id=1, source_target_pairs={{1,4},{2,5},{3,6},{9,12},{10,13},{11,14},{17,20},{18,21},{19,22},{... | collective-permute-start | bytes 393224 | tf_op jit(solution)/shard_map/ppermute | solution.py:300
  21.9 20.1 %collective-permute-start.11 = (bf16[4,128,256]{2,1,0:T(8,128)(2,1)S(1)}, bf16[4,128,256]{2,1,0:T(8,128)(2,1)S(1)}, u32[]{:S(2)}, u32[]{:S(2)}) collective-permute-start(bf16[4,128,256]{2,1,0:T(8,128)(2,1)S(1)} %get-tuple-element.55), channel_id=1, source_target_pairs={{0,4},{8,12},{16,20},{24,28},{1,5},{9,13},{17,21},{25,29},{2,6},{1... | collective-permute-start | bytes 786440 | tf_op jit(solution)/shard_map/ppermute | solution.py:301
  23.2 18.1 %collective-permute-start.12 = (bf16[2,128,256]{2,1,0:T(8,128)(2,1)S(1)}, bf16[2,128,256]{2,1,0:T(8,128)(2,1)S(1)}, u32[]{:S(2)}, u32[]{:S(2)}) collective-permute-start(bf16[2,128,256]{2,1,0:T(8,128)(2,1)S(1)} %get-tuple-element.56), channel_id=1, source_target_pairs={{0,5},{1,6},{2,7},{8,13},{9,14},{10,15},{16,21},{17,22},{18,23},{2... | collective-permute-start | bytes 393224 | tf_op jit(solution)/shard_map/ppermute | solution.py:299
  32.7 12.8 %collective-permute-start.8 = (bf16[4,128,256]{2,1,0:T(8,128)(2,1)S(1)}, bf16[4,128,256]{2,1,0:T(8,128)(2,1)S(1)}, u32[]{:S(2)}, u32[]{:S(2)}) collective-permute-start(bf16[4,128,256]{2,1,0:T(8,128)(2,1)S(1)} %get-tuple-element.52), channel_id=1, source_target_pairs={{4,8},{12,16},{20,24},{5,9},{13,17},{21,25},{6,10},{14,18},{22,26}... | collective-permute-start | bytes 786440 | tf_op jit(solution)/shard_map/ppermute | solution.py:301
  34.0 8.0 %collective-permute-start.13 = (bf16[2,128,256]{2,1,0:T(8,128)(2,1)S(1)}, bf16[2,128,256]{2,1,0:T(8,128)(2,1)S(1)}, u32[]{:S(2)}, u32[]{:S(2)}) collective-permute-start(bf16[2,128,256]{2,1,0:T(8,128)(2,1)S(1)} %get-tuple-element.57), channel_id=1, source_target_pairs={{1,4},{2,5},{3,6},{9,12},{10,13},{11,14},{17,20},{18,21},{19,22},{... | collective-permute-start | bytes 393224 | tf_op jit(solution)/shard_map/ppermute | solution.py:300
  35.3 10.1 %collective-permute-start.9 = (bf16[2,128,256]{2,1,0:T(8,128)(2,1)S(1)}, bf16[2,128,256]{2,1,0:T(8,128)(2,1)S(1)}, u32[]{:S(2)}, u32[]{:S(2)}) collective-permute-start(bf16[2,128,256]{2,1,0:T(8,128)(2,1)S(1)} %get-tuple-element.53), channel_id=1, source_target_pairs={{4,9},{5,10},{6,11},{12,17},{13,18},{14,19},{20,25},{21,26},{22,27... | collective-permute-start | bytes 393224 | tf_op jit(solution)/shard_map/ppermute | solution.py:299
  41.4 4.1 %collective-permute-start.10 = (bf16[2,128,256]{2,1,0:T(8,128)(2,1)S(1)}, bf16[2,128,256]{2,1,0:T(8,128)(2,1)S(1)}, u32[]{:S(2)}, u32[]{:S(2)}) collective-permute-start(bf16[2,128,256]{2,1,0:T(8,128)(2,1)S(1)} %get-tuple-element.54), channel_id=1, source_target_pairs={{5,8},{6,9},{7,10},{13,16},{14,17},{15,18},{21,24},{22,25},{23,26}... | collective-permute-start | bytes 393224 | tf_op jit(solution)/shard_map/ppermute | solution.py:300
  42.8 5.3 %collective-permute-start.18 = (bf16[2,128,256]{2,1,0:T(8,128)(2,1)S(1)}, bf16[2,128,256]{2,1,0:T(8,128)(2,1)S(1)}, u32[]{:S(2)}, u32[]{:S(2)}) collective-permute-start(bf16[2,128,256]{2,1,0:T(8,128)(2,1)S(1)} %get-tuple-element.66), channel_id=1, source_target_pairs={{4,9},{5,10},{6,11},{12,17},{13,18},{14,19},{20,25},{21,26},{22,27... | collective-permute-start | bytes 393224 | tf_op jit(solution)/shard_map/ppermute | solution.py:299
  44.1 5.4 %collective-permute-start.17 = (bf16[4,128,256]{2,1,0:T(8,128)(2,1)S(1)}, bf16[4,128,256]{2,1,0:T(8,128)(2,1)S(1)}, u32[]{:S(2)}, u32[]{:S(2)}) collective-permute-start(bf16[4,128,256]{2,1,0:T(8,128)(2,1)S(1)} %get-tuple-element.65), channel_id=1, source_target_pairs={{4,8},{12,16},{20,24},{5,9},{13,17},{21,25},{6,10},{14,18},{22,26}... | collective-permute-start | bytes 786440 | tf_op jit(solution)/shard_map/ppermute | solution.py:301
  45.5 16.3 %collective-permute-start.14 = (bf16[4,128,256]{2,1,0:T(8,128)(2,1)S(1)}, bf16[4,128,256]{2,1,0:T(8,128)(2,1)S(1)}, u32[]{:S(2)}, u32[]{:S(2)}) collective-permute-start(bf16[4,128,256]{2,1,0:T(8,128)(2,1)S(1)} %get-tuple-element.59), channel_id=1, source_target_pairs={{0,4},{8,12},{16,20},{24,28},{1,5},{9,13},{17,21},{25,29},{2,6},{1... | collective-permute-start | bytes 786440 | tf_op jit(solution)/shard_map/ppermute | solution.py:301
  46.8 2.7 %collective-permute-start.19 = (bf16[2,128,256]{2,1,0:T(8,128)(2,1)S(1)}, bf16[2,128,256]{2,1,0:T(8,128)(2,1)S(1)}, u32[]{:S(2)}, u32[]{:S(2)}) collective-permute-start(bf16[2,128,256]{2,1,0:T(8,128)(2,1)S(1)} %get-tuple-element.67), channel_id=1, source_target_pairs={{5,8},{6,9},{7,10},{13,16},{14,17},{15,18},{21,24},{22,25},{23,26}... | collective-permute-start | bytes 393224 | tf_op jit(solution)/shard_map/ppermute | solution.py:300
  47.5 2.1 %collective-permute-start.15 = (bf16[2,128,256]{2,1,0:T(8,128)(2,1)S(1)}, bf16[2,128,256]{2,1,0:T(8,128)(2,1)S(1)}, u32[]{:S(2)}, u32[]{:S(2)}) collective-permute-start(bf16[2,128,256]{2,1,0:T(8,128)(2,1)S(1)} %get-tuple-element.60), channel_id=1, source_target_pairs={{0,5},{1,6},{2,7},{8,13},{9,14},{10,15},{16,21},{17,22},{18,23},{2... | collective-permute-start | bytes 393224 | tf_op jit(solution)/shard_map/ppermute | solution.py:299
  48.2 13.6 %collective-permute-start.16 = (bf16[2,128,256]{2,1,0:T(8,128)(2,1)S(1)}, bf16[2,128,256]{2,1,0:T(8,128)(2,1)S(1)}, u32[]{:S(2)}, u32[]{:S(2)}) collective-permute-start(bf16[2,128,256]{2,1,0:T(8,128)(2,1)S(1)} %get-tuple-element.61), channel_id=1, source_target_pairs={{1,4},{2,5},{3,6},{9,12},{10,13},{11,14},{17,20},{18,21},{19,22},{... | collective-permute-start | bytes 393224 | tf_op jit(solution)/shard_map/ppermute | solution.py:300

commit v2 on v0

--- a/solution.py
+++ b/solution.py
@@ -23,9 +23,9 @@
     return pltpu.with_memory_space_constraint(array, pltpu.HBM)
 
 
-def write_lists(section, plan_ref, blocks_ref, lists):
+def write_lists(tile, plan_ref, blocks_ref, lists):
     listed = lists[0].shape[0]
-    parity = lax.rem(section, 2)
+    parity = lax.rem(tile, 2)
     for list_ref, side in zip(lists, (UPPER - parity, parity)):
         count = plan_ref[2 * listed + side]
         for slot in range(listed):
@@ -70,7 +70,7 @@
     for b, copy in enumerate(large):
         copy.wait()
         wave_ref[b] = landed[b].astype(wave_ref.dtype)
-    write_lists(lax.axis_index("depth"), plan_ref, wave_ref, (first_ref, second_ref))
+    write_lists(lax.axis_index("lat"), plan_ref, wave_ref, (first_ref, second_ref))
 
 
 def load_kernel(
@@ -100,14 +100,11 @@
         copy.wait()
 
 
-def fill_buffer(section, sections, tick, source_ref, wave_ref, first_ref, second_ref, buffer):
+def fill_buffer(section, tick, source_ref, wave_ref, first_ref, second_ref, buffer):
     blocks, listed = wave_ref.shape[0], first_ref.shape[0]
     if tick == 0:
-        sender = section
         buffer[:blocks] = wave_ref[...]
     else:
-        sender = lax.rem(section + sections - 1, sections)
-
         @pl.when(section == 0)
         def _():
             buffer[:blocks] = source_ref[tick - 1]
@@ -115,9 +112,9 @@
         @pl.when(section != 0)
         def _():
             buffer[:blocks] = wave_ref[...]
-    parity = lax.rem(sender, 2)
-    buffer[pl.ds(blocks + parity * listed, listed)] = first_ref[...]
-    buffer[pl.ds(blocks + (1 - parity) * listed, listed)] = second_ref[...]
+    parity = lax.rem(lax.axis_index("lat"), 2)
+    buffer[pl.ds(blocks + (1 - parity) * listed, listed)] = first_ref[...]
+    buffer[pl.ds(blocks + parity * listed, listed)] = second_ref[...]
 
 
 def extrapolate_block(plan_ref, pattern_start, ops_ref, buffer, b):
@@ -141,10 +138,9 @@
     wave_ref, first_in_ref, second_in_ref, echo_ref, onward_ref, first_ref, second_ref, buffer,
 ):
     section = lax.axis_index("depth")
+    tile = lax.axis_index("lat")
     listed = first_ref.shape[0]
-    fill_buffer(
-        section, sections, tick, source_ref, wave_ref, first_in_ref, second_in_ref, buffer
-    )
+    fill_buffer(section, tick, source_ref, wave_ref, first_in_ref, second_in_ref, buffer)
     for b in range(wave_ref.shape[0]):
         parts = extrapolate_block(plan_ref, 2 * (listed + 1), ops_ref, buffer, b)
         for i, part in enumerate(parts):
@@ -154,15 +150,15 @@
 
     @pl.when(section != sections - 1)
     def _():
-        write_lists(section, plan_ref, onward_ref, (first_ref, second_ref))
+        write_lists(tile, plan_ref, onward_ref, (first_ref, second_ref))
 
     @pl.when(section == sections - 1)
     def _():
-        write_lists(section, plan_ref, source_ref.at[tick], (first_ref, second_ref))
+        write_lists(tile, plan_ref, source_ref.at[tick], (first_ref, second_ref))
 
 
 def last_kernel(
-    tick, sections, plan_ref, ops_ref, source_ref, pass_ref, reflect_ref,
+    tick, plan_ref, ops_ref, source_ref, pass_ref, reflect_ref,
     wave_ref, first_in_ref, second_in_ref, *rest,
 ):
     earlier = rest[:tick]
@@ -176,9 +172,7 @@
     ]
     for copy in copies:
         copy.start()
-    fill_buffer(
-        section, sections, tick, source_ref, wave_ref, first_in_ref, second_in_ref, buffer
-    )
+    fill_buffer(section, tick, source_ref, wave_ref, first_in_ref, second_in_ref, buffer)
     for b in range(wave_ref.shape[0]):
         parts = extrapolate_block(plan_ref, 2 * (listed + 1), ops_ref, buffer, b)
         for i, part in enumerate(parts):
@@ -195,18 +189,33 @@
         copy.wait()
 
 
-def halo_routes(sections, tiles, deeper):
+def neighbour(j, turn, tiles):
+    to = j + (1 if (j + turn) % 2 == 0 else -1)
+    return to if 0 <= to < tiles else None
+
+
+def swap_routes(sections, tiles):
     routes = []
     for turn in (0, 1):
         route = []
         for s in range(sections):
-            way = 1 if (s + turn) % 2 == 0 else -1
-            to_section = (s + 1) % sections if deeper else s
-            route += [
-                (s * tiles + j, to_section * tiles + j + way)
-                for j in range(tiles)
-                if 0 <= j + way < tiles
-            ]
+            for j in range(tiles):
+                to = neighbour(j, turn, tiles)
+                end = ((s ^ 1) * tiles + j) if to is None else (s * tiles + to)
+                route.append((s * tiles + j, end))
+        routes.append(route)
+    return routes
+
+
+def halo_routes(sections, tiles):
+    routes = []
+    for turn in (0, 1):
+        route = []
+        for s in range(sections):
+            for j in range(tiles):
+                to = neighbour(j, turn, tiles)
+                to = j if to is None else to
+                route.append((s * tiles + j, (s + 1) % sections * tiles + to))
         routes.append(route)
     return routes
 
@@ -228,7 +237,7 @@
         transcendentals=0,
     )
     both = ("depth", "lat")
-    deeper = [(s, s + 1) for s in range(sections - 1)]
+    deeper = [(s, (s + 1) % sections) for s in range(sections)]
 
     plan, wave, first, second = pl.pallas_call(
         prepare_kernel,
@@ -254,8 +263,8 @@
         ),
         name="prepare",
     )(*map(in_hbm, (send_ids, send_count, pattern, inflow)))
-    routes = halo_routes(sections, tiles, False)
     loaded_first = first
+    routes = swap_routes(sections, tiles)
     first = lax.ppermute(first, both, routes[0])
     second = lax.ppermute(second, both, routes[1])
 
@@ -284,7 +293,7 @@
     fixed = [plan, *map(in_vmem, fixed)]
 
     buffer_type = pltpu.VMEM((blocks + 2 * listed, points, columns), WAVE)
-    routes = halo_routes(sections, tiles, True)
+    routes = halo_routes(sections, tiles)
     echoes = []
     for tick in range(ticks - 1):
         echo, onward, first, second = pl.pallas_call(
@@ -304,7 +313,7 @@
 
     tick = ticks - 1
     reflected, transmitted = pl.pallas_call(
-        functools.partial(last_kernel, tick, sections),
+        functools.partial(last_kernel, tick),
         out_shape=(
             jax.ShapeDtypeStruct((ticks, 1, blocks, points, columns), WAVE),
             jax.ShapeDtypeStruct((1, blocks, points, columns), jnp.float32),

time: 56.1 us -> 42.2 us (0.75)
  the two profiles are of different devices: /device:TPU:1 before, /device:TPU:0 now
where the time goes in v2:
time: 42.2 us; the launch traced here: 42 us
  waiting for transfers between devices  23.9 us (57%)
  starting transfers between devices  11 us (26%)
  Pallas kernels  6.47 us (15%)
  between operations  0.71 us (2%)
    ppermute x4, waiting for transfers between devices, per_device(): first = lax.ppermute(first, both, routes[0])  17.4 us
    ppermute x4, starting transfers between devices, per_device(): first = lax.ppermute(first, both, routes[0])  10.3 us
    ppermute x4, waiting for transfers between devices, per_device(): second = lax.ppermute(second, both, routes[1])  6.44 us
    pallas_call x3, Pallas kernels, per_device(): pl.pallas_call(functools.partial(tick_kernel, tick, sections), out_shape=...  2.11 us
    pallas_call x1, Pallas kernels, per_device(): pl.pallas_call(load_kernel, out_shape=(pltpu.VMEM(operators.shape, operat...  1.67 us
    pallas_call x1, Pallas kernels, per_device(): pl.pallas_call(functools.partial(last_kernel, tick), out_shape=(jax.Shape...  1.47 us
    pallas_call x1, Pallas kernels, per_device(): pl.pallas_call(prepare_kernel, out_shape=(pltpu.SMEM((2 * (listed + 1) +...  1.22 us
  transfers between devices with their start and end apart: 11, of which 7 were waited for; matrix products, arithmetic and copies ran while one was open for 0% of the time, Pallas kernels for 4%

profile of v2, /device:TPU:0, one launch (start us, length us, event | category | flops | bytes accessed | tf_op | source)
XLA Modules:
  0.0 42.0 jit_solution(7402144563022161168)
XLA Ops:
  0.6 1.2 %prepare.1 = (s32[30]{0:T(128)S(4)}, bf16[4,128,256]{2,1,0:T(8,128)(2,1)S(1)}, bf16[2,128,256]{2,1,0:T(8,128)(2,1)S(1)}, bf16[2,128,256]{2,1,0:T(8,128)(2,1)S(1)}) custom-call(s32[1,2,2]{2,1,0:T(2,128)} %ids_hbm.1, s32[1,2]{1,0:T(1,128)} %count_hbm.1, s32[4,6]{1,0:T(4,128)} %pattern_hbm.1, f32[1,4,128,256]{3,2,1,0:T(8,128)} %inflow_hbm.1), custom_call_target="tpu_custom_call" | custom-call | flops 131072 | bytes 1048576 | tf_op jit(solution)/shard_map/prepare/pallas_call | solution.py:242
  1.9 0.5 %collective-permute-start.1 = (bf16[2,128,256]{2,1,0:T(8,128)(2,1)S(1)}, bf16[2,128,256]{2,1,0:T(8,128)(2,1)S(1)}, u32[]{:S(2)}, u32[]{:S(2)}) collective-permute-start(bf16[2,128,256]{2,1,0:T(8,128)(2,1)S(1)} %get-tuple-element.29), channel_id=1, source_target_pairs={{0,4},{1,2},{2,1},{3,7},{4,0},{5,6},{6,5},{7,3},{8,12},{9,10},{10,... | collective-permute-start | bytes 393224 | tf_op jit(solution)/shard_map/ppermute | solution.py:269
  2.4 4.1 %collective-permute-start = (bf16[2,128,256]{2,1,0:T(8,128)(2,1)S(1)}, bf16[2,128,256]{2,1,0:T(8,128)(2,1)S(1)}, u32[]{:S(2)}, u32[]{:S(2)}) collective-permute-start(bf16[2,128,256]{2,1,0:T(8,128)(2,1)S(1)} %get-tuple-element.23.after_ref), channel_id=1, source_target_pairs={{0,1},{1,0},{2,3},{3,2},{4,5},{5,4},{6,7},{7,6},{8,9},{9,8},{10,11... | collective-permute-start | bytes 393224 | tf_op jit(solution)/shard_map/ppermute | solution.py:268
  6.5 1.7 %load.1 = (bf16[1,4,6,2,128,128]{5,4,3,2,1,0:T(8,128)(2,1)S(1)}, bf16[3,4,128,256]{3,2,1,0:T(8,128)(2,1)S(1)}, f32[4,128,128]{2,1,0:T(8,128)S(1)}, f32[4,128,128]{2,1,0:T(8,128)S(1)}) custom-call(bf16[1,4,6,2,128,128]{5,4,3,2,1,0:T(8,128)(2,1)} %ops_hbm.1, bf16[3,4,128,256]{3,2,1,0:T(8,128)(2,1)} %source_hbm.1, f32[1,4,128]{2,1,0:T(4,128)} %pass_hbm.1, ...), custom_call_target="tpu_custom_call" | custom-call | bytes 4718592 | tf_op jit(solution)/shard_map/load/pallas_call | solution.py:272
  8.2 0.0 collective-permute-done.1.second_in_ref
  8.2 1.5 %collective-permute-done.first_in_ref = bf16[2,128,256]{2,1,0:T(8,128)(2,1)S(1)} collective-permute-done((bf16[2,128,256]{2,1,0:T(8,128)(2,1)S(1)}, bf16[2,128,256]{2,1,0:T(8,128)(2,1)S(1)}, u32[]{:S(2)}, u32[]{:S(2)}) %collective-permute-start) | collective-permute-done | bytes 131104 | tf_op jit(solution)/shard_map/ppermute | solution.py:268
  9.7 0.7 %tick0.1 = (bf16[4,128,256]{2,1,0:T(8,128)(2,1)S(1)}, bf16[4,128,256]{2,1,0:T(8,128)(2,1)S(1)}, bf16[2,128,256]{2,1,0:T(8,128)(2,1)S(1)}, bf16[2,128,256]{2,1,0:T(8,128)(2,1)S(1)}) custom-call(s32[30]{0:T(128)S(4)} %get-tuple-element.22.plan_ref, bf16[1,4,6,2,128,128]{5,4,3,2,1,0:T(8,128)(2,1)S(1)} %get-tuple-element.24.ops_ref, ...), custom_call_target="tpu_custom_call" | custom-call | flops 402653184 | bytes 2621440 | tf_op jit(solution)/shard_map/tick0/pallas_call | solution.py:299
  10.4 0.1 collective-permute-start.2
  10.5 2.9 %collective-permute-start.3 = (bf16[2,128,256]{2,1,0:T(8,128)(2,1)S(1)}, bf16[2,128,256]{2,1,0:T(8,128)(2,1)S(1)}, u32[]{:S(2)}, u32[]{:S(2)}) collective-permute-start(bf16[2,128,256]{2,1,0:T(8,128)(2,1)S(1)} %get-tuple-element.31), channel_id=1, source_target_pairs={{0,5},{1,4},{2,7},{3,6},{4,9},{5,8},{6,11},{7,10},{8,13},{9,12},{1... | collective-permute-start | bytes 393224 | tf_op jit(solution)/shard_map/ppermute | solution.py:311
  13.4 0.0 collective-permute-start.4
  13.5 4.4 %collective-permute-done.3.first_in_ref = bf16[2,128,256]{2,1,0:T(8,128)(2,1)S(1)} collective-permute-done((bf16[2,128,256]{2,1,0:T(8,128)(2,1)S(1)}, bf16[2,128,256]{2,1,0:T(8,128)(2,1)S(1)}, u32[]{:S(2)}, u32[]{:S(2)}) %collective-permute-start.3) | collective-permute-done | bytes 131104 | tf_op jit(solution)/shard_map/ppermute | solution.py:311
  17.9 2.1 %collective-permute-done.4.second_in_ref = bf16[2,128,256]{2,1,0:T(8,128)(2,1)S(1)} collective-permute-done((bf16[2,128,256]{2,1,0:T(8,128)(2,1)S(1)}, bf16[2,128,256]{2,1,0:T(8,128)(2,1)S(1)}, u32[]{:S(2)}, u32[]{:S(2)}) %collective-permute-start.4) | collective-permute-done | bytes 131104 | tf_op jit(solution)/shard_map/ppermute | solution.py:312
  20.0 0.0 collective-permute-done.2.wave_ref
  20.0 0.7 %tick1.1 = (bf16[4,128,256]{2,1,0:T(8,128)(2,1)S(1)}, bf16[4,128,256]{2,1,0:T(8,128)(2,1)S(1)}, bf16[2,128,256]{2,1,0:T(8,128)(2,1)S(1)}, bf16[2,128,256]{2,1,0:T(8,128)(2,1)S(1)}) custom-call(s32[30]{0:T(128)S(4)} %get-tuple-element.22.plan_ref, bf16[1,4,6,2,128,128]{5,4,3,2,1,0:T(8,128)(2,1)S(1)} %get-tuple-element.24.ops_ref, ...), custom_call_target="tpu_custom_call" | custom-call | flops 402653184 | bytes 2621440 | tf_op jit(solution)/shard_map/tick1/pallas_call | solution.py:299
  20.7 0.1 collective-permute-start.5
  20.8 2.0 %collective-permute-start.6 = (bf16[2,128,256]{2,1,0:T(8,128)(2,1)S(1)}, bf16[2,128,256]{2,1,0:T(8,128)(2,1)S(1)}, u32[]{:S(2)}, u32[]{:S(2)}) collective-permute-start(bf16[2,128,256]{2,1,0:T(8,128)(2,1)S(1)} %get-tuple-element.34), channel_id=1, source_target_pairs={{0,5},{1,4},{2,7},{3,6},{4,9},{5,8},{6,11},{7,10},{8,13},{9,12},{1... | collective-permute-start | bytes 393224 | tf_op jit(solution)/shard_map/ppermute | solution.py:311
  22.8 0.0 collective-permute-start.7
  22.8 5.3 %collective-permute-done.6.first_in_ref = bf16[2,128,256]{2,1,0:T(8,128)(2,1)S(1)} collective-permute-done((bf16[2,128,256]{2,1,0:T(8,128)(2,1)S(1)}, bf16[2,128,256]{2,1,0:T(8,128)(2,1)S(1)}, u32[]{:S(2)}, u32[]{:S(2)}) %collective-permute-start.6) | collective-permute-done | bytes 131104 | tf_op jit(solution)/shard_map/ppermute | solution.py:311
  28.1 2.1 %collective-permute-done.7.second_in_ref = bf16[2,128,256]{2,1,0:T(8,128)(2,1)S(1)} collective-permute-done((bf16[2,128,256]{2,1,0:T(8,128)(2,1)S(1)}, bf16[2,128,256]{2,1,0:T(8,128)(2,1)S(1)}, u32[]{:S(2)}, u32[]{:S(2)}) %collective-permute-start.7) | collective-permute-done | bytes 131104 | tf_op jit(solution)/shard_map/ppermute | solution.py:312
  30.3 0.0 collective-permute-done.5.wave_ref
  30.3 0.7 %tick2.1 = (bf16[4,128,256]{2,1,0:T(8,128)(2,1)S(1)}, bf16[4,128,256]{2,1,0:T(8,128)(2,1)S(1)}, bf16[2,128,256]{2,1,0:T(8,128)(2,1)S(1)}, bf16[2,128,256]{2,1,0:T(8,128)(2,1)S(1)}) custom-call(s32[30]{0:T(128)S(4)} %get-tuple-element.22.plan_ref, bf16[1,4,6,2,128,128]{5,4,3,2,1,0:T(8,128)(2,1)S(1)} %get-tuple-element.24.ops_ref, ...), custom_call_target="tpu_custom_call" | custom-call | flops 402653184 | bytes 2621440 | tf_op jit(solution)/shard_map/tick2/pallas_call | solution.py:299
  31.0 0.1 collective-permute-start.8
  31.1 1.1 %collective-permute-start.9 = (bf16[2,128,256]{2,1,0:T(8,128)(2,1)S(1)}, bf16[2,128,256]{2,1,0:T(8,128)(2,1)S(1)}, u32[]{:S(2)}, u32[]{:S(2)}) collective-permute-start(bf16[2,128,256]{2,1,0:T(8,128)(2,1)S(1)} %get-tuple-element.37), channel_id=1, source_target_pairs={{0,5},{1,4},{2,7},{3,6},{4,9},{5,8},{6,11},{7,10},{8,13},{9,12},{1... | collective-permute-start | bytes 393224 | tf_op jit(solution)/shard_map/ppermute | solution.py:311
  32.2 0.0 collective-permute-start.10
  32.2 6.2 %collective-permute-done.9.first_in_ref = bf16[2,128,256]{2,1,0:T(8,128)(2,1)S(1)} collective-permute-done((bf16[2,128,256]{2,1,0:T(8,128)(2,1)S(1)}, bf16[2,128,256]{2,1,0:T(8,128)(2,1)S(1)}, u32[]{:S(2)}, u32[]{:S(2)}) %collective-permute-start.9) | collective-permute-done | bytes 131104 | tf_op jit(solution)/shard_map/ppermute | solution.py:311
  38.4 2.2 %collective-permute-done.10.second_in_ref = bf16[2,128,256]{2,1,0:T(8,128)(2,1)S(1)} collective-permute-done((bf16[2,128,256]{2,1,0:T(8,128)(2,1)S(1)}, bf16[2,128,256]{2,1,0:T(8,128)(2,1)S(1)}, u32[]{:S(2)}, u32[]{:S(2)}) %collective-permute-start.10) | collective-permute-done | bytes 131104 | tf_op jit(solution)/shard_map/ppermute | solution.py:312
  40.5 0.0 collective-permute-done.8.wave_ref
  40.5 1.5 %last_tick.1 = (bf16[4,1,4,128,256]{4,3,2,1,0:T(8,128)(2,1)}, f32[1,4,128,256]{3,2,1,0:T(8,128)}) custom-call(s32[30]{0:T(128)S(4)} %get-tuple-element.22.plan_ref, bf16[1,4,6,2,128,128]{5,4,3,2,1,0:T(8,128)(2,1)S(1)} %get-tuple-element.24.ops_ref, bf16[3,4,128,256]{3,2,1,0:T(8,128)(2,1)S(1)} %get-tuple-element.25.source_ref, ...), custom_call_target="tpu_custom_call" | custom-call | flops 402653184 | bytes 2621440 | tf_op jit(solution)/shard_map/last_tick/pallas_call | solution.py:315
Async XLA Ops:
  1.9 6.3 %collective-permute-start.1 = (bf16[2,128,256]{2,1,0:T(8,128)(2,1)S(1)}, bf16[2,128,256]{2,1,0:T(8,128)(2,1)S(1)}, u32[]{:S(2)}, u32[]{:S(2)}) collective-permute-start(bf16[2,128,256]{2,1,0:T(8,128)(2,1)S(1)} %get-tuple-element.29), channel_id=1, source_target_pairs={{0,4},{1,2},{2,1},{3,7},{4,0},{5,6},{6,5},{7,3},{8,12},{9,10},{10,... | collective-permute-start | bytes 393224 | tf_op jit(solution)/shard_map/ppermute | solution.py:269
  2.4 7.4 %collective-permute-start = (bf16[2,128,256]{2,1,0:T(8,128)(2,1)S(1)}, bf16[2,128,256]{2,1,0:T(8,128)(2,1)S(1)}, u32[]{:S(2)}, u32[]{:S(2)}) collective-permute-start(bf16[2,128,256]{2,1,0:T(8,128)(2,1)S(1)} %get-tuple-element.23.after_ref), channel_id=1, source_target_pairs={{0,1},{1,0},{2,3},{3,2},{4,5},{5,4},{6,7},{7,6},{8,9},{9,8},{10,11... | collective-permute-start | bytes 393224 | tf_op jit(solution)/shard_map/ppermute | solution.py:268
  10.4 9.6 %collective-permute-start.2 = (bf16[4,128,256]{2,1,0:T(8,128)(2,1)S(1)}, bf16[4,128,256]{2,1,0:T(8,128)(2,1)S(1)}, u32[]{:S(2)}, u32[]{:S(2)}) collective-permute-start(bf16[4,128,256]{2,1,0:T(8,128)(2,1)S(1)} %get-tuple-element.30), channel_id=1, source_target_pairs={{0,4},{4,8},{8,12},{12,16},{16,20},{20,24},{24,28},{28,0},{1,5},{5... | collective-permute-start | bytes 786440 | tf_op jit(solution)/shard_map/ppermute | solution.py:310
  10.5 7.4 %collective-permute-start.3 = (bf16[2,128,256]{2,1,0:T(8,128)(2,1)S(1)}, bf16[2,128,256]{2,1,0:T(8,128)(2,1)S(1)}, u32[]{:S(2)}, u32[]{:S(2)}) collective-permute-start(bf16[2,128,256]{2,1,0:T(8,128)(2,1)S(1)} %get-tuple-element.31), channel_id=1, source_target_pairs={{0,5},{1,4},{2,7},{3,6},{4,9},{5,8},{6,11},{7,10},{8,13},{9,12},{1... | collective-permute-start | bytes 393224 | tf_op jit(solution)/shard_map/ppermute | solution.py:311
  13.4 6.5 %collective-permute-start.4 = (bf16[2,128,256]{2,1,0:T(8,128)(2,1)S(1)}, bf16[2,128,256]{2,1,0:T(8,128)(2,1)S(1)}, u32[]{:S(2)}, u32[]{:S(2)}) collective-permute-start(bf16[2,128,256]{2,1,0:T(8,128)(2,1)S(1)} %get-tuple-element.32), channel_id=1, source_target_pairs={{0,4},{1,6},{2,5},{3,7},{4,8},{5,10},{6,9},{7,11},{8,12},{9,14},{1... | collective-permute-start | bytes 393224 | tf_op jit(solution)/shard_map/ppermute | solution.py:312
  20.7 9.6 %collective-permute-start.5 = (bf16[4,128,256]{2,1,0:T(8,128)(2,1)S(1)}, bf16[4,128,256]{2,1,0:T(8,128)(2,1)S(1)}, u32[]{:S(2)}, u32[]{:S(2)}) collective-permute-start(bf16[4,128,256]{2,1,0:T(8,128)(2,1)S(1)} %get-tuple-element.33), channel_id=1, source_target_pairs={{0,4},{4,8},{8,12},{12,16},{16,20},{20,24},{24,28},{28,0},{1,5},{5... | collective-permute-start | bytes 786440 | tf_op jit(solution)/shard_map/ppermute | solution.py:310
  20.8 7.3 %collective-permute-start.6 = (bf16[2,128,256]{2,1,0:T(8,128)(2,1)S(1)}, bf16[2,128,256]{2,1,0:T(8,128)(2,1)S(1)}, u32[]{:S(2)}, u32[]{:S(2)}) collective-permute-start(bf16[2,128,256]{2,1,0:T(8,128)(2,1)S(1)} %get-tuple-element.34), channel_id=1, source_target_pairs={{0,5},{1,4},{2,7},{3,6},{4,9},{5,8},{6,11},{7,10},{8,13},{9,12},{1... | collective-permute-start | bytes 393224 | tf_op jit(solution)/shard_map/ppermute | solution.py:311
  22.8 7.5 %collective-permute-start.7 = (bf16[2,128,256]{2,1,0:T(8,128)(2,1)S(1)}, bf16[2,128,256]{2,1,0:T(8,128)(2,1)S(1)}, u32[]{:S(2)}, u32[]{:S(2)}) collective-permute-start(bf16[2,128,256]{2,1,0:T(8,128)(2,1)S(1)} %get-tuple-element.35), channel_id=1, source_target_pairs={{0,4},{1,6},{2,5},{3,7},{4,8},{5,10},{6,9},{7,11},{8,12},{9,14},{1... | collective-permute-start | bytes 393224 | tf_op jit(solution)/shard_map/ppermute | solution.py:312
  31.0 9.6 %collective-permute-start.8 = (bf16[4,128,256]{2,1,0:T(8,128)(2,1)S(1)}, bf16[4,128,256]{2,1,0:T(8,128)(2,1)S(1)}, u32[]{:S(2)}, u32[]{:S(2)}) collective-permute-start(bf16[4,128,256]{2,1,0:T(8,128)(2,1)S(1)} %get-tuple-element.36), channel_id=1, source_target_pairs={{0,4},{4,8},{8,12},{12,16},{16,20},{20,24},{24,28},{28,0},{1,5},{5... | collective-permute-start | bytes 786440 | tf_op jit(solution)/shard_map/ppermute | solution.py:310
  31.1 7.3 %collective-permute-start.9 = (bf16[2,128,256]{2,1,0:T(8,128)(2,1)S(1)}, bf16[2,128,256]{2,1,0:T(8,128)(2,1)S(1)}, u32[]{:S(2)}, u32[]{:S(2)}) collective-permute-start(bf16[2,128,256]{2,1,0:T(8,128)(2,1)S(1)} %get-tuple-element.37), channel_id=1, source_target_pairs={{0,5},{1,4},{2,7},{3,6},{4,9},{5,8},{6,11},{7,10},{8,13},{9,12},{1... | collective-permute-start | bytes 393224 | tf_op jit(solution)/shard_map/ppermute | solution.py:311
  32.2 8.4 %collective-permute-start.10 = (bf16[2,128,256]{2,1,0:T(8,128)(2,1)S(1)}, bf16[2,128,256]{2,1,0:T(8,128)(2,1)S(1)}, u32[]{:S(2)}, u32[]{:S(2)}) collective-permute-start(bf16[2,128,256]{2,1,0:T(8,128)(2,1)S(1)} %get-tuple-element.38), channel_id=1, source_target_pairs={{0,4},{1,6},{2,5},{3,7},{4,8},{5,10},{6,9},{7,11},{8,12},{9,14},{1... | collective-permute-start | bytes 393224 | tf_op jit(solution)/shard_map/ppermute | solution.py:312

commit v3 on v1

--- a/solution.py
+++ b/solution.py
@@ -13,7 +13,6 @@
 ANY_SPEC = pl.BlockSpec(memory_space=pl.ANY)
 VMEM_LIMIT = 8 * 1024 * 1024
 LOWER, UPPER = 0, 1
-ORDER = ((1, 0), (0, 1))
 
 
 def in_vmem(array):
@@ -24,18 +23,21 @@
     return pltpu.with_memory_space_constraint(array, pltpu.HBM)
 
 
-def write_list(plan_ref, side, blocks_ref, list_ref):
-    listed = list_ref.shape[0]
-    for slot in range(listed):
-        live = slot < plan_ref[2 * listed + side]
-
-        @pl.when(live)
-        def _():
-            list_ref[slot] = blocks_ref[plan_ref[side * listed + slot]]
-
-        @pl.when(jnp.logical_not(live))
-        def _():
-            list_ref[slot] = jnp.zeros(list_ref.shape[1:], list_ref.dtype)
+def write_lists(tile, plan_ref, blocks_ref, lists):
+    listed = lists[0].shape[0]
+    parity = lax.rem(tile, 2)
+    for list_ref, side in zip(lists, (UPPER - parity, parity)):
+        count = plan_ref[2 * listed + side]
+        for slot in range(listed):
+            live = slot < count
+
+            @pl.when(live)
+            def _():
+                list_ref[slot] = blocks_ref[plan_ref[side * listed + slot]]
+
+            @pl.when(jnp.logical_not(live))
+            def _():
+                list_ref[slot] = jnp.zeros(list_ref.shape[1:], list_ref.dtype)
 
 
 def prepare_kernel(
@@ -68,9 +70,7 @@
     for b, copy in enumerate(large):
         copy.wait()
         wave_ref[b] = landed[b].astype(wave_ref.dtype)
-    parity = lax.rem(lax.axis_index("depth"), 2)
-    write_list(plan_ref, UPPER - parity, wave_ref, first_ref)
-    write_list(plan_ref, parity, wave_ref, second_ref)
+    write_lists(lax.axis_index("lat"), plan_ref, wave_ref, (first_ref, second_ref))
 
 
 def load_kernel(
@@ -100,20 +100,27 @@
         copy.wait()
 
 
-def fill_buffer(section, tick, source_ref, wave_ref, lower_ref, upper_ref, buffer):
-    blocks, listed = wave_ref.shape[0], lower_ref.shape[0]
+def fill_buffer(section, tick, source_ref, wave_refs, first_ref, second_ref, buffer):
+    blocks, listed = source_ref.shape[1], first_ref.shape[0]
+
+    def fill_wave():
+        start = 0
+        for wave_ref in wave_refs:
+            buffer[start : start + wave_ref.shape[0]] = wave_ref[...]
+            start += wave_ref.shape[0]
+
     if tick == 0:
-        buffer[:blocks] = wave_ref[...]
+        fill_wave()
     else:
+        pl.when(section != 0)(fill_wave)
+
         @pl.when(section == 0)
         def _():
             buffer[:blocks] = source_ref[tick - 1]
 
-        @pl.when(section != 0)
-        def _():
-            buffer[:blocks] = wave_ref[...]
-    buffer[blocks : blocks + listed] = lower_ref[...]
-    buffer[blocks + listed :] = upper_ref[...]
+    parity = lax.rem(lax.axis_index("lat"), 2)
+    buffer[pl.ds(blocks + (1 - parity) * listed, listed)] = first_ref[...]
+    buffer[pl.ds(blocks + parity * listed, listed)] = second_ref[...]
 
 
 def extrapolate_block(plan_ref, pattern_start, ops_ref, buffer, b):
@@ -132,46 +139,56 @@
     return real_part, imag_part
 
 
+def acts(section, parity):
+    return True if parity is None else lax.rem(section, 2) == parity
+
+
 def tick_kernel(
     parity, tick, sections, plan_ref, ops_ref, source_ref, pass_ref, reflect_ref,
-    wave_ref, lower_ref, upper_ref, *rest,
+    wave_refs, first_in_ref, second_in_ref, known_refs, out_refs, buffer, onward,
 ):
-    echo_ref, onward_ref, down_ref, up_ref, buffer = rest[-5:]
+    del known_refs
+    echo_ref, first_ref, second_ref, *onward_refs = out_refs
     section = lax.axis_index("depth")
-    listed = lower_ref.shape[0]
-
-    @pl.when(lax.rem(section, 2) == parity)
+    tile = lax.axis_index("lat")
+    listed = first_ref.shape[0]
+
+    @pl.when(acts(section, parity))
     def _():
-        fill_buffer(section, tick, source_ref, wave_ref, lower_ref, upper_ref, buffer)
-        for b in range(wave_ref.shape[0]):
+        fill_buffer(section, tick, source_ref, wave_refs, first_in_ref, second_in_ref, buffer)
+        for b in range(echo_ref.shape[0]):
             parts = extrapolate_block(plan_ref, 2 * (listed + 1), ops_ref, buffer, b)
             for i, part in enumerate(parts):
                 cols = pl.ds(i * part.shape[1], part.shape[1])
-                onward_ref[b, :, cols] = (pass_ref[b] * part).astype(onward_ref.dtype)
+                onward[b, :, cols] = (pass_ref[b] * part).astype(onward.dtype)
                 echo_ref[b, :, cols] = (reflect_ref[b] * part).astype(echo_ref.dtype)
+        start = 0
+        for onward_ref in onward_refs:
+            if start == onward.shape[0]:
+                start = 0
+            onward_ref[...] = onward[start : start + onward_ref.shape[0]]
+            start += onward_ref.shape[0]
 
         @pl.when(section != sections - 1)
         def _():
-            write_list(plan_ref, UPPER, onward_ref, up_ref)
-            write_list(plan_ref, LOWER, onward_ref, down_ref)
+            write_lists(tile, plan_ref, onward, (first_ref, second_ref))
 
         @pl.when(section == sections - 1)
         def _():
-            write_list(plan_ref, UPPER, source_ref.at[tick], up_ref)
-            write_list(plan_ref, LOWER, source_ref.at[tick], down_ref)
+            write_lists(tile, plan_ref, source_ref.at[tick], (first_ref, second_ref))
 
 
 def last_kernel(
     parity, tick, plan_ref, ops_ref, source_ref, pass_ref, reflect_ref,
-    wave_ref, lower_ref, upper_ref, *rest,
+    wave_refs, first_in_ref, second_in_ref, earlier, known_refs, out_refs,
+    buffer, echo, leaving, early_sems, echo_sems, leave_sems,
 ):
-    earlier = rest[:tick]
-    (reflected_ref, transmitted_ref, buffer, echo, leaving,
-     early_sems, echo_sems, leave_sems) = rest[-8:]
+    del known_refs
+    reflected_ref, transmitted_ref = out_refs
     section = lax.axis_index("depth")
-    listed = lower_ref.shape[0]
-
-    @pl.when(lax.rem(section, 2) == parity)
+    listed = first_in_ref.shape[0]
+
+    @pl.when(acts(section, parity))
     def _():
         copies = [
             pltpu.make_async_copy(earlier[t], reflected_ref.at[t, 0], early_sems.at[t])
@@ -179,8 +196,8 @@
         ]
         for copy in copies:
             copy.start()
-        fill_buffer(section, tick, source_ref, wave_ref, lower_ref, upper_ref, buffer)
-        for b in range(wave_ref.shape[0]):
+        fill_buffer(section, tick, source_ref, wave_refs, first_in_ref, second_in_ref, buffer)
+        for b in range(echo.shape[0]):
             parts = extrapolate_block(plan_ref, 2 * (listed + 1), ops_ref, buffer, b)
             for i, part in enumerate(parts):
                 cols = pl.ds(i * part.shape[1], part.shape[1])
@@ -196,14 +213,54 @@
             copy.wait()
 
 
-def beside(sections, tiles, ways, deeper):
-    return [
-        (s * tiles + j, ((s + 1) % sections if deeper else s) * tiles + j + ways[s % 2])
-        for s in range(sections)
-        if s % 2 in ways
-        for j in range(tiles)
-        if 0 <= j + ways[s % 2] < tiles
-    ]
+def grouped_call(kernel, groups, outs, out_specs, known, **options):
+    flat = [array for group in groups for array in (group if isinstance(group, list) else [group])]
+
+    def body(*refs):
+        refs = list(refs)
+        take = lambda count: [refs.pop(0) for _ in range(count)]
+        inputs = [take(len(g)) if isinstance(g, list) else refs.pop(0) for g in groups]
+        kernel(*inputs, take(len(known)), take(len(outs)), *refs)
+
+    return pl.pallas_call(
+        body,
+        out_shape=tuple(outs),
+        in_specs=[SMEM_SPEC] + [VMEM_SPEC] * (len(flat) - 1) + list(out_specs[: len(known)]),
+        out_specs=tuple(out_specs),
+        input_output_aliases={len(flat) + i: i for i in range(len(known))},
+        **options,
+    )(flat[0], *map(in_vmem, flat[1:]), *known)
+
+
+def neighbour(j, turn, tiles):
+    to = j + (1 if (j + turn) % 2 == 0 else -1)
+    return to if 0 <= to < tiles else None
+
+
+def swap_routes(sections, tiles):
+    routes = []
+    for turn in (0, 1):
+        route = []
+        for s in range(sections):
+            for j in range(tiles):
+                to = neighbour(j, turn, tiles)
+                end = ((s ^ 1) * tiles + j) if to is None else (s * tiles + to)
+                route.append((s * tiles + j, end))
+        routes.append(route)
+    return routes
+
+
+def halo_routes(sections, tiles):
+    routes = []
+    for turn in (0, 1):
+        route = []
+        for s in range(sections):
+            for j in range(tiles):
+                to = neighbour(j, turn, tiles)
+                end = (s ^ 1) * tiles + j if to is None else (s + 1) % sections * tiles + to
+                route.append((s * tiles + j, end))
+        routes.append(route)
+    return routes
 
 
 def per_device(
@@ -223,6 +280,7 @@
         transcendentals=0,
     )
     both = ("depth", "lat")
+    deeper = [(s, (s + 1) % sections) for s in range(sections)]
 
     plan, wave, first, second = pl.pallas_call(
         prepare_kernel,
@@ -249,8 +307,9 @@
         name="prepare",
     )(*map(in_hbm, (send_ids, send_count, pattern, inflow)))
     loaded_first = first
-    first = lax.ppermute(first, both, beside(sections, tiles, {0: 1, 1: -1}, False))
-    second = lax.ppermute(second, both, beside(sections, tiles, {0: -1, 1: 1}, False))
+    routes = swap_routes(sections, tiles)
+    first = lax.ppermute(first, both, routes[0])
+    second = lax.ppermute(second, both, routes[1])
 
     column_type = pltpu.VMEM((blocks, points, columns // 2), jnp.float32)
     fixed = pl.pallas_call(
@@ -274,33 +333,44 @@
         ),
         name="load",
     )(*map(in_hbm, (operators, source, transmission, reflectivity)), in_vmem(loaded_first))
-    fixed = [plan, *map(in_vmem, fixed)]
+    fixed = [plan, *fixed]
+
     buffer_type = pltpu.VMEM((blocks + 2 * listed, points, columns), WAVE)
 
-    arrived = {0: (wave, first, second), 1: (wave, second, first)}
+    ODD, EVEN = 1, 0
+    halves = [blocks // 2, blocks - blocks // 2]
+    half_types = [pltpu.VMEM((n, points, columns), WAVE) for n in halves]
+    crossing = [(s, (s + 1) % sections) for s in range(sections)]
+    inside = [(s, s ^ 1) for s in range(sections)]
+    routes = halo_routes(sections, tiles)
+
+    waves = {None: [wave]}
     echoes = []
     for tick in range(ticks - 1):
-        leaving = {}
-        echo = None
-        for parity in ORDER[tick % 2]:
-            known = [] if echo is None else [in_vmem(echo)]
-            echo, onward, down, up = pl.pallas_call(
+        known = []
+        sent = {}
+        for parity in (None,) if tick == 0 else (ODD, EVEN):
+            to_next = ([wave_type] if parity != EVEN else []) + (half_types if parity != ODD else [])
+            outs = [wave_type, list_type, list_type] + to_next
+            known = grouped_call(
                 functools.partial(tick_kernel, parity, tick, sections),
-                out_shape=(wave_type, wave_type, list_type, list_type),
-                in_specs=[SMEM_SPEC] + [VMEM_SPEC] * (7 + len(known)),
-                out_specs=(VMEM_SPEC,) * 4,
-                input_output_aliases={8: 0} if known else {},
-                scratch_shapes=[buffer_type],
+                [*fixed, waves[parity], first, second],
+                outs,
+                [VMEM_SPEC] * len(outs),
+                known[:3] and [in_vmem(a) for a in known[:3]],
+                scratch_shapes=[buffer_type, pltpu.VMEM(wave_type.shape, WAVE)],
                 compiler_params=params,
                 cost_estimate=tick_cost,
-                name=f"tick{tick}_{parity}",
-            )(*fixed, *map(in_vmem, arrived[parity]), *known)
-            deeper = [(s, s + 1) for s in range(parity, sections - 1, 2)]
-            up = lax.ppermute(up, both, beside(sections, tiles, {parity: 1}, True))
-            down = lax.ppermute(down, both, beside(sections, tiles, {parity: -1}, True))
-            wave = lax.ppermute(onward, "depth", deeper)
-            leaving[1 - parity] = (wave, up, down)
-        arrived = leaving
+                name=f"tick{tick}" + ("" if parity is None else "_odd" if parity else "_even"),
+            )
+            if parity != EVEN:
+                sent[EVEN] = [lax.ppermute(known[3], "depth", crossing)]
+            if parity != ODD:
+                sent[ODD] = [lax.ppermute(a, "depth", inside) for a in known[-2:]]
+        waves = sent
+        echo, first, second = known[:3]
+        first = lax.ppermute(first, both, routes[0])
+        second = lax.ppermute(second, both, routes[1])
         echoes.append(echo)
 
     tick = ticks - 1
@@ -309,13 +379,13 @@
         jax.ShapeDtypeStruct((ticks, 1, blocks, points, columns), WAVE),
         jax.ShapeDtypeStruct((1, blocks, points, columns), jnp.float32),
     )
-    for parity in ORDER[tick % 2]:
-        results = pl.pallas_call(
+    for parity in (ODD, EVEN):
+        results = grouped_call(
             functools.partial(last_kernel, parity, tick),
-            out_shape=result_types,
-            in_specs=[SMEM_SPEC] + [VMEM_SPEC] * (7 + tick) + [ANY_SPEC] * len(results),
-            out_specs=(ANY_SPEC, ANY_SPEC),
-            input_output_aliases={8 + tick: 0, 9 + tick: 1} if results else {},
+            [*fixed, waves[parity], first, second, echoes],
+            result_types,
+            [ANY_SPEC] * 2,
+            list(results),
             scratch_shapes=[
                 buffer_type,
                 pltpu.VMEM((blocks, points, columns), WAVE),
@@ -326,8 +396,8 @@
             ],
             compiler_params=params,
             cost_estimate=tick_cost,
-            name=f"last_tick_{parity}",
-        )(*fixed, *map(in_vmem, arrived[parity]), *map(in_vmem, echoes), *results)
+            name="last_tick" + ("_odd" if parity else "_even"),
+        )
     return tuple(results)
 
 

time: 63.8 us -> 38.9 us (0.61)
  the two profiles are of different devices: /device:TPU:1 before, /device:TPU:12 now
where the time goes in v3:
time: 38.9 us; the launch traced here: 38.8 us
  waiting for transfers between devices  23 us (59%)
  starting transfers between devices  8.31 us (21%)
  Pallas kernels  6.7 us (17%)
  between operations  0.73 us (2%)
    ppermute x4, waiting for transfers between devices, per_device(): first = lax.ppermute(first, both, routes[0])  17.4 us
    ppermute x4, starting transfers between devices, per_device(): second = lax.ppermute(second, both, routes[1])  4.59 us
    ppermute x4, waiting for transfers between devices, per_device(): second = lax.ppermute(second, both, routes[1])  4.09 us
    pallas_call x7, Pallas kernels, grouped_call(): pl.pallas_call(body, out_shape=tuple(outs), in_specs=[SMEM_SPEC] + [VMEM_...  3.82 us
    ppermute x6, starting transfers between devices, per_device(): sent[ODD] = [lax.ppermute(a, 'depth', inside) for a in known[-2:]]  2.07 us
    pallas_call x1, Pallas kernels, per_device(): pl.pallas_call(load_kernel, out_shape=(pltpu.VMEM(operators.shape, operat...  1.67 us
    ppermute x4, starting transfers between devices, per_device(): first = lax.ppermute(first, both, routes[0])  1.53 us
    ppermute x3, waiting for transfers between devices, per_device(): sent[EVEN] = [lax.ppermute(known[3], 'depth', crossing)]  1.34 us
  transfers between devices with their start and end apart: 17, of which 9 were waited for; matrix products, arithmetic and copies ran while one was open for 0% of the time, Pallas kernels for 8%

profile of v3, /device:TPU:12, one launch (start us, length us, event | category | flops | bytes accessed | tf_op | source)
XLA Modules:
  0.0 38.8 jit_solution(16470047031150568402)
XLA Ops:
  0.6 1.2 %prepare.1 = (s32[30]{0:T(128)S(4)}, bf16[4,128,256]{2,1,0:T(8,128)(2,1)S(1)}, bf16[2,128,256]{2,1,0:T(8,128)(2,1)S(1)}, bf16[2,128,256]{2,1,0:T(8,128)(2,1)S(1)}) custom-call(s32[1,2,2]{2,1,0:T(2,128)} %ids_hbm.1, s32[1,2]{1,0:T(1,128)} %count_hbm.1, s32[4,6]{1,0:T(4,128)} %pattern_hbm.1, f32[1,4,128,256]{3,2,1,0:T(8,128)} %inflow_hbm.1), custom_call_target="tpu_custom_call" | custom-call | flops 131072 | bytes 1048576 | tf_op jit(solution)/shard_map/prepare/pallas_call | solution.py:285
  1.8 1.6 %collective-permute-start.1 = (bf16[2,128,256]{2,1,0:T(8,128)(2,1)S(1)}, bf16[2,128,256]{2,1,0:T(8,128)(2,1)S(1)}, u32[]{:S(2)}, u32[]{:S(2)}) collective-permute-start(bf16[2,128,256]{2,1,0:T(8,128)(2,1)S(1)} %get-tuple-element.43), channel_id=1, source_target_pairs={{0,4},{1,2},{2,1},{3,7},{4,0},{5,6},{6,5},{7,3},{8,12},{9,10},{10,... | collective-permute-start | bytes 393224 | tf_op jit(solution)/shard_map/ppermute | solution.py:312
  3.5 0.0 collective-permute-start
  3.5 1.7 %load.1 = (bf16[1,4,6,2,128,128]{5,4,3,2,1,0:T(8,128)(2,1)S(1)}, bf16[3,4,128,256]{3,2,1,0:T(8,128)(2,1)S(1)}, f32[4,128,128]{2,1,0:T(8,128)S(1)}, f32[4,128,128]{2,1,0:T(8,128)S(1)}) custom-call(bf16[1,4,6,2,128,128]{5,4,3,2,1,0:T(8,128)(2,1)} %ops_hbm.1, bf16[3,4,128,256]{3,2,1,0:T(8,128)(2,1)} %source_hbm.1, f32[1,4,128]{2,1,0:T(4,128)} %pass_hbm.1, ...), custom_call_target="tpu_custom_call" | custom-call | bytes 4718592 | tf_op jit(solution)/shard_map/load/pallas_call | solution.py:315
  5.2 2.0 %collective-permute-done.1.refs_7_ = bf16[2,128,256]{2,1,0:T(8,128)(2,1)S(1)} collective-permute-done((bf16[2,128,256]{2,1,0:T(8,128)(2,1)S(1)}, bf16[2,128,256]{2,1,0:T(8,128)(2,1)S(1)}, u32[]{:S(2)}, u32[]{:S(2)}) %collective-permute-start.1) | collective-permute-done | bytes 131104 | tf_op jit(solution)/shard_map/ppermute | solution.py:312
  7.2 1.3 %collective-permute-done.refs_6_ = bf16[2,128,256]{2,1,0:T(8,128)(2,1)S(1)} collective-permute-done((bf16[2,128,256]{2,1,0:T(8,128)(2,1)S(1)}, bf16[2,128,256]{2,1,0:T(8,128)(2,1)S(1)}, u32[]{:S(2)}, u32[]{:S(2)}) %collective-permute-start) | collective-permute-done | bytes 131104 | tf_op jit(solution)/shard_map/ppermute | solution.py:311
  8.5 0.7 %tick0.1 = (bf16[4,128,256]{2,1,0:T(8,128)(2,1)S(1)}, bf16[2,128,256]{2,1,0:T(8,128)(2,1)S(1)}, bf16[2,128,256]{2,1,0:T(8,128)(2,1)S(1)}, bf16[4,128,256]{2,1,0:...) custom-call(s32[30]{0:T(128)S(4)} %get-tuple-element.36.refs_0_, ...), custom_call_target="tpu_custom_call" | custom-call | flops 402653184 | bytes 2621440 | tf_op jit(solution)/shard_map/tick0/pallas_call | solution.py:225
  9.2 0.1 collective-permute-start.2
  9.3 1.5 %collective-permute-start.3 = (bf16[2,128,256]{2,1,0:T(8,128)(2,1)S(1)}, bf16[2,128,256]{2,1,0:T(8,128)(2,1)S(1)}, u32[]{:S(2)}, u32[]{:S(2)}) collective-permute-start(bf16[2,128,256]{2,1,0:T(8,128)(2,1)S(1)} %get-tuple-element.45), channel_id=1, source_target_pairs={{0,5},{1,4},{2,7},{3,6},{4,9},{5,8},{6,11},{7,10},{8,13},{9,12},{1... | collective-permute-start | bytes 393224 | tf_op jit(solution)/shard_map/ppermute | solution.py:372
  10.8 1.8 %collective-permute-start.4 = (bf16[2,128,256]{2,1,0:T(8,128)(2,1)S(1)}, bf16[2,128,256]{2,1,0:T(8,128)(2,1)S(1)}, u32[]{:S(2)}, u32[]{:S(2)}) collective-permute-start(bf16[2,128,256]{2,1,0:T(8,128)(2,1)S(1)} %get-tuple-element.46), channel_id=1, source_target_pairs={{0,4},{1,6},{2,5},{3,7},{4,0},{5,10},{6,9},{7,3},{8,12},{9,14},{10... | collective-permute-start | bytes 393224 | tf_op jit(solution)/shard_map/ppermute | solution.py:373
  12.5 0.5 %collective-permute-start.5 = (bf16[2,128,256]{2,1,0:T(8,128)(2,1)S(1)}, bf16[2,128,256]{2,1,0:T(8,128)(2,1)S(1)}, u32[]{:S(2)}, u32[]{:S(2)}) collective-permute-start(bf16[2,128,256]{2,1,0:T(8,128)(2,1)S(1)} %get-tuple-element.47), channel_id=1, source_target_pairs={{0,4},{4,0},{8,12},{12,8},{16,20},{20,16},{24,28},{28,24},{1,5},{5... | collective-permute-start | bytes 393224 | tf_op jit(solution)/shard_map/ppermute | solution.py:369
  13.0 0.0 collective-permute-start.6
  13.0 3.1 %collective-permute-done.3.refs_7_.refs_6_ = bf16[2,128,256]{2,1,0:T(8,128)(2,1)S(1)} collective-permute-done((bf16[2,128,256]{2,1,0:T(8,128)(2,1)S(1)}, bf16[2,128,256]{2,1,0:T(8,128)(2,1)S(1)}, u32[]{:S(2)}, u32[]{:S(2)}) %collective-permute-start.3) | collective-permute-done | bytes 131104 | tf_op jit(solution)/shard_map/ppermute | solution.py:372
  16.2 2.1 %collective-permute-done.4.refs_8_.refs_7_ = bf16[2,128,256]{2,1,0:T(8,128)(2,1)S(1)} collective-permute-done((bf16[2,128,256]{2,1,0:T(8,128)(2,1)S(1)}, bf16[2,128,256]{2,1,0:T(8,128)(2,1)S(1)}, u32[]{:S(2)}, u32[]{:S(2)}) %collective-permute-start.4) | collective-permute-done | bytes 131104 | tf_op jit(solution)/shard_map/ppermute | solution.py:373
  18.2 0.0 collective-permute-done.5.refs_5_
  18.2 0.0 collective-permute-done.6.refs_6_
  18.2 0.1 collective-permute-start.12
  18.3 0.5 %collective-permute-done.2.refs_5_ = bf16[4,128,256]{2,1,0:T(8,128)(2,1)S(1)} collective-permute-done((bf16[4,128,256]{2,1,0:T(8,128)(2,1)S(1)}, bf16[4,128,256]{2,1,0:T(8,128)(2,1)S(1)}, u32[]{:S(2)}, u32[]{:S(2)}) %collective-permute-start.2) | collective-permute-done | bytes 262176 | tf_op jit(solution)/shard_map/ppermute | solution.py:367
  18.8 0.7 %tick1_even.1 = (bf16[4,128,256]{2,1,0:T(8,128)(2,1)S(1)}, bf16[2,128,256]{2,1,0:T(8,128)(2,1)S(1)}, bf16[2,128,256]{2,1,0:T(8,128)(2,1)S(1)}, bf16[2,128,256]{2,1,0:T(8,128)(2,1)S(1)}, bf16[2,128,256]{2,1,0:T(8,128)(2,1)S(1)}) custom-call(s32[30]{0:T(128)S(4)} %get-tuple-element.36.refs_0_, ...), custom_call_target="tpu_custom_call", output_to_operand_aliasing={{0}: (8, {}), {1}: (9, {}), {2}: (10, {})} | custom-call | flops 402653184 | bytes 2621440 | tf_op jit(solution)/shard_map/tick1_even/pallas_call | solution.py:225
  19.5 0.1 collective-permute-start.7
  19.6 0.5 %collective-permute-start.8 = (bf16[2,128,256]{2,1,0:T(8,128)(2,1)S(1)}, bf16[2,128,256]{2,1,0:T(8,128)(2,1)S(1)}, u32[]{:S(2)}, u32[]{:S(2)}) collective-permute-start(bf16[2,128,256]{2,1,0:T(8,128)(2,1)S(1)} %get-tuple-element.53), channel_id=1, source_target_pairs={{0,4},{4,0},{8,12},{12,8},{16,20},{20,16},{24,28},{28,24},{1,5},{5... | collective-permute-start | bytes 393224 | tf_op jit(solution)/shard_map/ppermute | solution.py:369
  20.1 0.0 collective-permute-start.9
  20.1 0.9 %collective-permute-start.10 = (bf16[2,128,256]{2,1,0:T(8,128)(2,1)S(1)}, bf16[2,128,256]{2,1,0:T(8,128)(2,1)S(1)}, u32[]{:S(2)}, u32[]{:S(2)}) collective-permute-start(bf16[2,128,256]{2,1,0:T(8,128)(2,1)S(1)} %get-tuple-element.55), channel_id=1, source_target_pairs={{0,4},{1,6},{2,5},{3,7},{4,0},{5,10},{6,9},{7,3},{8,12},{9,14},{10... | collective-permute-start | bytes 393224 | tf_op jit(solution)/shard_map/ppermute | solution.py:373
  21.0 0.0 collective-permute-done.7.refs_5_
  21.0 0.1 collective-permute-done.8.refs_6_
  21.1 6.7 %collective-permute-done.9.refs_7_.refs_6_ = bf16[2,128,256]{2,1,0:T(8,128)(2,1)S(1)} collective-permute-done((bf16[2,128,256]{2,1,0:T(8,128)(2,1)S(1)}, bf16[2,128,256]{2,1,0:T(8,128)(2,1)S(1)}, u32[]{:S(2)}, u32[]{:S(2)}) %collective-permute-start.9) | collective-permute-done | bytes 131104 | tf_op jit(solution)/shard_map/ppermute | solution.py:372
  27.8 0.0 collective-permute-done.10.refs_8_.refs_7_
  27.8 0.0 collective-permute-start.11
  27.8 0.0 collective-permute-done.12.refs_5_
  27.8 0.8 %tick2_even.1 = (bf16[4,128,256]{2,1,0:T(8,128)(2,1)S(1)}, bf16[2,128,256]{2,1,0:T(8,128)(2,1)S(1)}, bf16[2,128,256]{2,1,0:T(8,128)(2,1)S(1)}, bf16[2,128,256]{2,1,0:T(8,128)(2,1)S(1)}, bf16[2,128,256]{2,1,0:T(8,128)(2,1)S(1)}) custom-call(s32[30]{0:T(128)S(4)} %get-tuple-element.36.refs_0_, ...), custom_call_target="tpu_custom_call", output_to_operand_aliasing={{0}: (8, {}), {1}: (9, {}), {2}: (10, {})} | custom-call | flops 402653184 | bytes 2621440 | tf_op jit(solution)/shard_map/tick2_even/pallas_call | solution.py:225
  28.6 0.1 collective-permute-start.13
  28.6 0.3 collective-permute-start.14
  29.0 1.0 %collective-permute-start.15 = (bf16[2,128,256]{2,1,0:T(8,128)(2,1)S(1)}, bf16[2,128,256]{2,1,0:T(8,128)(2,1)S(1)}, u32[]{:S(2)}, u32[]{:S(2)}) collective-permute-start(bf16[2,128,256]{2,1,0:T(8,128)(2,1)S(1)} %get-tuple-element.66), channel_id=1, source_target_pairs={{0,4},{4,0},{8,12},{12,8},{16,20},{20,16},{24,28},{28,24},{1,5},{5... | collective-permute-start | bytes 393224 | tf_op jit(solution)/shard_map/ppermute | solution.py:369
  29.9 0.0 collective-permute-start.16
  29.9 6.3 %collective-permute-done.13.refs_7_.refs_6_ = bf16[2,128,256]{2,1,0:T(8,128)(2,1)S(1)} collective-permute-done((bf16[2,128,256]{2,1,0:T(8,128)(2,1)S(1)}, bf16[2,128,256]{2,1,0:T(8,128)(2,1)S(1)}, u32[]{:S(2)}, u32[]{:S(2)}) %collective-permute-start.13) | collective-permute-done | bytes 131104 | tf_op jit(solution)/shard_map/ppermute | solution.py:372
  36.3 0.0 collective-permute-done.14.refs_8_.refs_7_
  36.3 0.0 collective-permute-done.15.refs_5_
  36.3 0.0 collective-permute-done.16.refs_6_
  36.3 0.1 last_tick_odd.1
  36.4 0.9 %collective-permute-done.11.refs_5_ = bf16[4,128,256]{2,1,0:T(8,128)(2,1)S(1)} collective-permute-done((bf16[4,128,256]{2,1,0:T(8,128)(2,1)S(1)}, bf16[4,128,256]{2,1,0:T(8,128)(2,1)S(1)}, u32[]{:S(2)}, u32[]{:S(2)}) %collective-permute-start.11) | collective-permute-done | bytes 262176 | tf_op jit(solution)/shard_map/ppermute | solution.py:367
  37.3 1.5 %last_tick_even.1 = (bf16[4,1,4,128,256]{4,3,2,1,0:T(8,128)(2,1)}, f32[1,4,128,256]{3,2,1,0:T(8,128)}) custom-call(s32[30]{0:T(128)S(4)} %get-tuple-element.36.refs_0_, bf16[1,4,6,2,128,128]{5,4,3,2,1,0:T(8,128)(2,1)S(1)} %get-tuple-element.38.refs_1_, ...), custom_call_target="tpu_custom_call", output_to_operand_aliasing={{0}: (11, {}), {1}: (12, {})} | custom-call | flops 402653184 | bytes 2621440 | tf_op jit(solution)/shard_map/last_tick_even/pallas_call | solution.py:225
  (2 shorter events, 0.0 us)
Async XLA Ops:
  1.8 5.3 %collective-permute-start.1 = (bf16[2,128,256]{2,1,0:T(8,128)(2,1)S(1)}, bf16[2,128,256]{2,1,0:T(8,128)(2,1)S(1)}, u32[]{:S(2)}, u32[]{:S(2)}) collective-permute-start(bf16[2,128,256]{2,1,0:T(8,128)(2,1)S(1)} %get-tuple-element.43), channel_id=1, source_target_pairs={{0,4},{1,2},{2,1},{3,7},{4,0},{5,6},{6,5},{7,3},{8,12},{9,10},{10,... | collective-permute-start | bytes 393224 | tf_op jit(solution)/shard_map/ppermute | solution.py:312
  3.5 5.0 %collective-permute-start = (bf16[2,128,256]{2,1,0:T(8,128)(2,1)S(1)}, bf16[2,128,256]{2,1,0:T(8,128)(2,1)S(1)}, u32[]{:S(2)}, u32[]{:S(2)}) collective-permute-start(bf16[2,128,256]{2,1,0:T(8,128)(2,1)S(1)} %get-tuple-element.37.after_ref), channel_id=1, source_target_pairs={{0,1},{1,0},{2,3},{3,2},{4,5},{5,4},{6,7},{7,6},{8,9},{9,8},{10,11... | collective-permute-start | bytes 393224 | tf_op jit(solution)/shard_map/ppermute | solution.py:311
  9.2 9.6 %collective-permute-start.2 = (bf16[4,128,256]{2,1,0:T(8,128)(2,1)S(1)}, bf16[4,128,256]{2,1,0:T(8,128)(2,1)S(1)}, u32[]{:S(2)}, u32[]{:S(2)}) collective-permute-start(bf16[4,128,256]{2,1,0:T(8,128)(2,1)S(1)} %get-tuple-element.44), channel_id=1, source_target_pairs={{0,4},{4,8},{8,12},{12,16},{16,20},{20,24},{24,28},{28,0},{1,5},{5... | collective-permute-start | bytes 786440 | tf_op jit(solution)/shard_map/ppermute | solution.py:367
  9.3 6.9 %collective-permute-start.3 = (bf16[2,128,256]{2,1,0:T(8,128)(2,1)S(1)}, bf16[2,128,256]{2,1,0:T(8,128)(2,1)S(1)}, u32[]{:S(2)}, u32[]{:S(2)}) collective-permute-start(bf16[2,128,256]{2,1,0:T(8,128)(2,1)S(1)} %get-tuple-element.45), channel_id=1, source_target_pairs={{0,5},{1,4},{2,7},{3,6},{4,9},{5,8},{6,11},{7,10},{8,13},{9,12},{1... | collective-permute-start | bytes 393224 | tf_op jit(solution)/shard_map/ppermute | solution.py:372
  10.8 7.5 %collective-permute-start.4 = (bf16[2,128,256]{2,1,0:T(8,128)(2,1)S(1)}, bf16[2,128,256]{2,1,0:T(8,128)(2,1)S(1)}, u32[]{:S(2)}, u32[]{:S(2)}) collective-permute-start(bf16[2,128,256]{2,1,0:T(8,128)(2,1)S(1)} %get-tuple-element.46), channel_id=1, source_target_pairs={{0,4},{1,6},{2,5},{3,7},{4,0},{5,10},{6,9},{7,3},{8,12},{9,14},{10... | collective-permute-start | bytes 393224 | tf_op jit(solution)/shard_map/ppermute | solution.py:373
  12.5 5.7 %collective-permute-start.5 = (bf16[2,128,256]{2,1,0:T(8,128)(2,1)S(1)}, bf16[2,128,256]{2,1,0:T(8,128)(2,1)S(1)}, u32[]{:S(2)}, u32[]{:S(2)}) collective-permute-start(bf16[2,128,256]{2,1,0:T(8,128)(2,1)S(1)} %get-tuple-element.47), channel_id=1, source_target_pairs={{0,4},{4,0},{8,12},{12,8},{16,20},{20,16},{24,28},{28,24},{1,5},{5... | collective-permute-start | bytes 393224 | tf_op jit(solution)/shard_map/ppermute | solution.py:369
  13.0 5.2 %collective-permute-start.6 = (bf16[2,128,256]{2,1,0:T(8,128)(2,1)S(1)}, bf16[2,128,256]{2,1,0:T(8,128)(2,1)S(1)}, u32[]{:S(2)}, u32[]{:S(2)}) collective-permute-start(bf16[2,128,256]{2,1,0:T(8,128)(2,1)S(1)} %get-tuple-element.48), channel_id=1, source_target_pairs={{0,4},{4,0},{8,12},{12,8},{16,20},{20,16},{24,28},{28,24},{1,5},{5... | collective-permute-start | bytes 393224 | tf_op jit(solution)/shard_map/ppermute | solution.py:369
  18.2 9.6 %collective-permute-start.12 = (bf16[4,128,256]{2,1,0:T(8,128)(2,1)S(1)}, bf16[4,128,256]{2,1,0:T(8,128)(2,1)S(1)}, u32[]{:S(2)}, u32[]{:S(2)}) collective-permute-start(bf16[4,128,256]{2,1,0:T(8,128)(2,1)S(1)} %get-tuple-element.57), channel_id=1, source_target_pairs={{0,4},{4,8},{8,12},{12,16},{16,20},{20,24},{24,28},{28,0},{1,5},{5... | collective-permute-start | bytes 786440 | tf_op jit(solution)/shard_map/ppermute | solution.py:367
  19.5 1.5 %collective-permute-start.7 = (bf16[2,128,256]{2,1,0:T(8,128)(2,1)S(1)}, bf16[2,128,256]{2,1,0:T(8,128)(2,1)S(1)}, u32[]{:S(2)}, u32[]{:S(2)}) collective-permute-start(bf16[2,128,256]{2,1,0:T(8,128)(2,1)S(1)} %get-tuple-element.52), channel_id=1, source_target_pairs={{0,4},{4,0},{8,12},{12,8},{16,20},{20,16},{24,28},{28,24},{1,5},{5... | collective-permute-start | bytes 393224 | tf_op jit(solution)/shard_map/ppermute | solution.py:369
  19.6 1.5 %collective-permute-start.8 = (bf16[2,128,256]{2,1,0:T(8,128)(2,1)S(1)}, bf16[2,128,256]{2,1,0:T(8,128)(2,1)S(1)}, u32[]{:S(2)}, u32[]{:S(2)}) collective-permute-start(bf16[2,128,256]{2,1,0:T(8,128)(2,1)S(1)} %get-tuple-element.53), channel_id=1, source_target_pairs={{0,4},{4,0},{8,12},{12,8},{16,20},{20,16},{24,28},{28,24},{1,5},{5... | collective-permute-start | bytes 393224 | tf_op jit(solution)/shard_map/ppermute | solution.py:369
  20.1 7.7 %collective-permute-start.9 = (bf16[2,128,256]{2,1,0:T(8,128)(2,1)S(1)}, bf16[2,128,256]{2,1,0:T(8,128)(2,1)S(1)}, u32[]{:S(2)}, u32[]{:S(2)}) collective-permute-start(bf16[2,128,256]{2,1,0:T(8,128)(2,1)S(1)} %get-tuple-element.54), channel_id=1, source_target_pairs={{0,5},{1,4},{2,7},{3,6},{4,9},{5,8},{6,11},{7,10},{8,13},{9,12},{1... | collective-permute-start | bytes 393224 | tf_op jit(solution)/shard_map/ppermute | solution.py:372
  20.1 7.7 %collective-permute-start.10 = (bf16[2,128,256]{2,1,0:T(8,128)(2,1)S(1)}, bf16[2,128,256]{2,1,0:T(8,128)(2,1)S(1)}, u32[]{:S(2)}, u32[]{:S(2)}) collective-permute-start(bf16[2,128,256]{2,1,0:T(8,128)(2,1)S(1)} %get-tuple-element.55), channel_id=1, source_target_pairs={{0,4},{1,6},{2,5},{3,7},{4,0},{5,10},{6,9},{7,3},{8,12},{9,14},{10... | collective-permute-start | bytes 393224 | tf_op jit(solution)/shard_map/ppermute | solution.py:373
  27.8 9.5 %collective-permute-start.11 = (bf16[4,128,256]{2,1,0:T(8,128)(2,1)S(1)}, bf16[4,128,256]{2,1,0:T(8,128)(2,1)S(1)}, u32[]{:S(2)}, u32[]{:S(2)}) collective-permute-start(bf16[4,128,256]{2,1,0:T(8,128)(2,1)S(1)} %get-tuple-element.56), channel_id=1, source_target_pairs={{0,4},{4,8},{8,12},{12,16},{16,20},{20,24},{24,28},{28,0},{1,5},{5... | collective-permute-start | bytes 786440 | tf_op jit(solution)/shard_map/ppermute | solution.py:367
  28.6 7.7 %collective-permute-start.13 = (bf16[2,128,256]{2,1,0:T(8,128)(2,1)S(1)}, bf16[2,128,256]{2,1,0:T(8,128)(2,1)S(1)}, u32[]{:S(2)}, u32[]{:S(2)}) collective-permute-start(bf16[2,128,256]{2,1,0:T(8,128)(2,1)S(1)} %get-tuple-element.61), channel_id=1, source_target_pairs={{0,5},{1,4},{2,7},{3,6},{4,9},{5,8},{6,11},{7,10},{8,13},{9,12},{1... | collective-permute-start | bytes 393224 | tf_op jit(solution)/shard_map/ppermute | solution.py:372
  28.6 7.7 %collective-permute-start.14 = (bf16[2,128,256]{2,1,0:T(8,128)(2,1)S(1)}, bf16[2,128,256]{2,1,0:T(8,128)(2,1)S(1)}, u32[]{:S(2)}, u32[]{:S(2)}) collective-permute-start(bf16[2,128,256]{2,1,0:T(8,128)(2,1)S(1)} %get-tuple-element.62), channel_id=1, source_target_pairs={{0,4},{1,6},{2,5},{3,7},{4,0},{5,10},{6,9},{7,3},{8,12},{9,14},{10... | collective-permute-start | bytes 393224 | tf_op jit(solution)/shard_map/ppermute | solution.py:373
  29.0 7.4 %collective-permute-start.15 = (bf16[2,128,256]{2,1,0:T(8,128)(2,1)S(1)}, bf16[2,128,256]{2,1,0:T(8,128)(2,1)S(1)}, u32[]{:S(2)}, u32[]{:S(2)}) collective-permute-start(bf16[2,128,256]{2,1,0:T(8,128)(2,1)S(1)} %get-tuple-element.66), channel_id=1, source_target_pairs={{0,4},{4,0},{8,12},{12,8},{16,20},{20,16},{24,28},{28,24},{1,5},{5... | collective-permute-start | bytes 393224 | tf_op jit(solution)/shard_map/ppermute | solution.py:369
  29.9 6.4 %collective-permute-start.16 = (bf16[2,128,256]{2,1,0:T(8,128)(2,1)S(1)}, bf16[2,128,256]{2,1,0:T(8,128)(2,1)S(1)}, u32[]{:S(2)}, u32[]{:S(2)}) collective-permute-start(bf16[2,128,256]{2,1,0:T(8,128)(2,1)S(1)} %get-tuple-element.67), channel_id=1, source_target_pairs={{0,4},{4,0},{8,12},{12,8},{16,20},{20,16},{24,28},{28,24},{1,5},{5... | collective-permute-start | bytes 393224 | tf_op jit(solution)/shard_map/ppermute | solution.py:369

commit v4 on v3

--- a/solution.py
+++ b/solution.py
@@ -363,9 +363,12 @@
                 cost_estimate=tick_cost,
                 name=f"tick{tick}" + ("" if parity is None else "_odd" if parity else "_even"),
             )
-            if parity != EVEN:
+            if parity is None:
+                sent[EVEN] = [lax.ppermute(a, "depth", crossing) for a in known[-2:]]
+                sent[ODD] = [lax.ppermute(known[3], "depth", inside)]
+            elif parity == ODD:
                 sent[EVEN] = [lax.ppermute(known[3], "depth", crossing)]
-            if parity != ODD:
+            else:
                 sent[ODD] = [lax.ppermute(a, "depth", inside) for a in known[-2:]]
         waves = sent
         echo, first, second = known[:3]

time: 38.9 us -> 40.1 us (1.031)
  the two profiles are of different devices: /device:TPU:12 before, /device:TPU:0 now
where the time goes in v4:
time: 40.1 us; the launch traced here: 39.3 us
  starting transfers between devices  16.6 us (41%)
  waiting for transfers between devices  15.2 us (38%)
  Pallas kernels  6.75 us (17%)
  between operations  0.74 us (2%)
    ppermute x4, waiting for transfers between devices, per_device(): first = lax.ppermute(first, both, routes[0])  12.7 us
    ppermute x4, starting transfers between devices, per_device(): first = lax.ppermute(first, both, routes[0])  9.67 us
    ppermute x4, starting transfers between devices, per_device(): second = lax.ppermute(second, both, routes[1])  4.1 us
    pallas_call x7, Pallas kernels, grouped_call(): pl.pallas_call(body, out_shape=tuple(outs), in_specs=[SMEM_SPEC] + [VMEM_...  3.87 us
    ppermute x2, waiting for transfers between devices, per_device(): sent[EVEN] = [lax.ppermute(a, 'depth', crossing) for a in known[-2:]]  2.46 us
    pallas_call x1, Pallas kernels, per_device(): pl.pallas_call(load_kernel, out_shape=(pltpu.VMEM(operators.shape, operat...  1.67 us
    ppermute x2, starting transfers between devices, per_device(): sent[EVEN] = [lax.ppermute(a, 'depth', crossing) for a in known[-2:]]  1.61 us
    pallas_call x1, Pallas kernels, per_device(): pl.pallas_call(prepare_kernel, out_shape=(pltpu.SMEM((2 * (listed + 1) +...  1.21 us
  transfers between devices with their start and end apart: 17, of which 6 were waited for; matrix products, arithmetic and copies ran while one was open for 0% of the time, Pallas kernels for 8%

profile of v4, /device:TPU:0, one launch (start us, length us, event | category | flops | bytes accessed | tf_op | source)
XLA Modules:
  0.0 39.3 jit_solution(12355483030320558692)
XLA Ops:
  0.6 1.2 %prepare.1 = (s32[30]{0:T(128)S(4)}, bf16[4,128,256]{2,1,0:T(8,128)(2,1)S(1)}, bf16[2,128,256]{2,1,0:T(8,128)(2,1)S(1)}, bf16[2,128,256]{2,1,0:T(8,128)(2,1)S(1)}) custom-call(s32[1,2,2]{2,1,0:T(2,128)} %ids_hbm.1, s32[1,2]{1,0:T(1,128)} %count_hbm.1, s32[4,6]{1,0:T(4,128)} %pattern_hbm.1, f32[1,4,128,256]{3,2,1,0:T(8,128)} %inflow_hbm.1), custom_call_target="tpu_custom_call" | custom-call | flops 131072 | bytes 1048576 | tf_op jit(solution)/shard_map/prepare/pallas_call | solution.py:285
  1.8 0.5 %collective-permute-start.1 = (bf16[2,128,256]{2,1,0:T(8,128)(2,1)S(1)}, bf16[2,128,256]{2,1,0:T(8,128)(2,1)S(1)}, u32[]{:S(2)}, u32[]{:S(2)}) collective-permute-start(bf16[2,128,256]{2,1,0:T(8,128)(2,1)S(1)} %get-tuple-element.43), channel_id=1, source_target_pairs={{0,4},{1,2},{2,1},{3,7},{4,0},{5,6},{6,5},{7,3},{8,12},{9,10},{10,... | collective-permute-start | bytes 393224 | tf_op jit(solution)/shard_map/ppermute | solution.py:312
  2.4 4.1 %collective-permute-start = (bf16[2,128,256]{2,1,0:T(8,128)(2,1)S(1)}, bf16[2,128,256]{2,1,0:T(8,128)(2,1)S(1)}, u32[]{:S(2)}, u32[]{:S(2)}) collective-permute-start(bf16[2,128,256]{2,1,0:T(8,128)(2,1)S(1)} %get-tuple-element.37.after_ref), channel_id=1, source_target_pairs={{0,1},{1,0},{2,3},{3,2},{4,5},{5,4},{6,7},{7,6},{8,9},{9,8},{10,11... | collective-permute-start | bytes 393224 | tf_op jit(solution)/shard_map/ppermute | solution.py:311
  6.5 1.7 %load.1 = (bf16[1,4,6,2,128,128]{5,4,3,2,1,0:T(8,128)(2,1)S(1)}, bf16[3,4,128,256]{3,2,1,0:T(8,128)(2,1)S(1)}, f32[4,128,128]{2,1,0:T(8,128)S(1)}, f32[4,128,128]{2,1,0:T(8,128)S(1)}) custom-call(bf16[1,4,6,2,128,128]{5,4,3,2,1,0:T(8,128)(2,1)} %ops_hbm.1, bf16[3,4,128,256]{3,2,1,0:T(8,128)(2,1)} %source_hbm.1, f32[1,4,128]{2,1,0:T(4,128)} %pass_hbm.1, ...), custom_call_target="tpu_custom_call" | custom-call | bytes 4718592 | tf_op jit(solution)/shard_map/load/pallas_call | solution.py:315
  8.2 0.0 collective-permute-done.1.refs_7_
  8.2 1.5 %collective-permute-done.refs_6_ = bf16[2,128,256]{2,1,0:T(8,128)(2,1)S(1)} collective-permute-done((bf16[2,128,256]{2,1,0:T(8,128)(2,1)S(1)}, bf16[2,128,256]{2,1,0:T(8,128)(2,1)S(1)}, u32[]{:S(2)}, u32[]{:S(2)}) %collective-permute-start) | collective-permute-done | bytes 131104 | tf_op jit(solution)/shard_map/ppermute | solution.py:311
  9.7 0.7 %tick0.1 = (bf16[4,128,256]{2,1,0:T(8,128)(2,1)S(1)}, bf16[2,128,256]{2,1,0:T(8,128)(2,1)S(1)}, bf16[2,128,256]{2,1,0:T(8,128)(2,1)S(1)}, bf16[4,128,256]{2,1,0:...) custom-call(s32[30]{0:T(128)S(4)} %get-tuple-element.36.refs_0_, ...), custom_call_target="tpu_custom_call" | custom-call | flops 402653184 | bytes 2621440 | tf_op jit(solution)/shard_map/tick0/pallas_call | solution.py:225
  10.5 0.1 collective-permute-start.6
  10.6 1.9 %collective-permute-start.4 = (bf16[2,128,256]{2,1,0:T(8,128)(2,1)S(1)}, bf16[2,128,256]{2,1,0:T(8,128)(2,1)S(1)}, u32[]{:S(2)}, u32[]{:S(2)}) collective-permute-start(bf16[2,128,256]{2,1,0:T(8,128)(2,1)S(1)} %get-tuple-element.46), channel_id=1, source_target_pairs={{0,5},{1,4},{2,7},{3,6},{4,9},{5,8},{6,11},{7,10},{8,13},{9,12},{1... | collective-permute-start | bytes 393224 | tf_op jit(solution)/shard_map/ppermute | solution.py:375
  12.4 1.0 %collective-permute-start.5 = (bf16[2,128,256]{2,1,0:T(8,128)(2,1)S(1)}, bf16[2,128,256]{2,1,0:T(8,128)(2,1)S(1)}, u32[]{:S(2)}, u32[]{:S(2)}) collective-permute-start(bf16[2,128,256]{2,1,0:T(8,128)(2,1)S(1)} %get-tuple-element.47), channel_id=1, source_target_pairs={{0,4},{1,6},{2,5},{3,7},{4,0},{5,10},{6,9},{7,3},{8,12},{9,14},{10... | collective-permute-start | bytes 393224 | tf_op jit(solution)/shard_map/ppermute | solution.py:376
  13.4 0.0 collective-permute-start.2
  13.4 1.6 %collective-permute-start.3 = (bf16[2,128,256]{2,1,0:T(8,128)(2,1)S(1)}, bf16[2,128,256]{2,1,0:T(8,128)(2,1)S(1)}, u32[]{:S(2)}, u32[]{:S(2)}) collective-permute-start(bf16[2,128,256]{2,1,0:T(8,128)(2,1)S(1)} %get-tuple-element.45), channel_id=1, source_target_pairs={{0,4},{4,8},{8,12},{12,16},{16,20},{20,24},{24,28},{28,0},{1,5},{5... | collective-permute-start | bytes 393224 | tf_op jit(solution)/shard_map/ppermute | solution.py:367
  15.0 2.8 %collective-permute-done.4.refs_6_.refs_7_ = bf16[2,128,256]{2,1,0:T(8,128)(2,1)S(1)} collective-permute-done((bf16[2,128,256]{2,1,0:T(8,128)(2,1)S(1)}, bf16[2,128,256]{2,1,0:T(8,128)(2,1)S(1)}, u32[]{:S(2)}, u32[]{:S(2)}) %collective-permute-start.4) | collective-permute-done | bytes 131104 | tf_op jit(solution)/shard_map/ppermute | solution.py:375
  17.9 0.0 collective-permute-done.5.refs_7_.refs_8_
  17.9 0.0 collective-permute-done.6.refs_5_
  17.9 0.1 collective-permute-start.12
  17.9 1.1 %collective-permute-done.2.refs_5_ = bf16[2,128,256]{2,1,0:T(8,128)(2,1)S(1)} collective-permute-done((bf16[2,128,256]{2,1,0:T(8,128)(2,1)S(1)}, bf16[2,128,256]{2,1,0:T(8,128)(2,1)S(1)}, u32[]{:S(2)}, u32[]{:S(2)}) %collective-permute-start.2) | collective-permute-done | bytes 131104 | tf_op jit(solution)/shard_map/ppermute | solution.py:367
  19.0 1.4 %collective-permute-done.3.refs_6_ = bf16[2,128,256]{2,1,0:T(8,128)(2,1)S(1)} collective-permute-done((bf16[2,128,256]{2,1,0:T(8,128)(2,1)S(1)}, bf16[2,128,256]{2,1,0:T(8,128)(2,1)S(1)}, u32[]{:S(2)}, u32[]{:S(2)}) %collective-permute-start.3) | collective-permute-done | bytes 131104 | tf_op jit(solution)/shard_map/ppermute | solution.py:367
  20.4 0.7 %tick1_even.1 = (bf16[4,128,256]{2,1,0:T(8,128)(2,1)S(1)}, bf16[2,128,256]{2,1,0:T(8,128)(2,1)S(1)}, bf16[2,128,256]{2,1,0:T(8,128)(2,1)S(1)}, bf16[2,128,256]{2,1,0:T(8,128)(2,1)S(1)}, bf16[2,128,256]{2,1,0:T(8,128)(2,1)S(1)}) custom-call(s32[30]{0:T(128)S(4)} %get-tuple-element.36.refs_0_, ...), custom_call_target="tpu_custom_call", output_to_operand_aliasing={{0}: (9, {}), {1}: (10, {}), {2}: (11, {})} | custom-call | flops 402653184 | bytes 2621440 | tf_op jit(solution)/shard_map/tick1_even/pallas_call | solution.py:225
  21.2 0.1 collective-permute-start.7
  21.2 0.5 %collective-permute-start.8 = (bf16[2,128,256]{2,1,0:T(8,128)(2,1)S(1)}, bf16[2,128,256]{2,1,0:T(8,128)(2,1)S(1)}, u32[]{:S(2)}, u32[]{:S(2)}) collective-permute-start(bf16[2,128,256]{2,1,0:T(8,128)(2,1)S(1)} %get-tuple-element.53), channel_id=1, source_target_pairs={{0,4},{4,0},{8,12},{12,8},{16,20},{20,16},{24,28},{28,24},{1,5},{5... | collective-permute-start | bytes 393224 | tf_op jit(solution)/shard_map/ppermute | solution.py:372
  21.7 2.1 %collective-permute-start.9 = (bf16[2,128,256]{2,1,0:T(8,128)(2,1)S(1)}, bf16[2,128,256]{2,1,0:T(8,128)(2,1)S(1)}, u32[]{:S(2)}, u32[]{:S(2)}) collective-permute-start(bf16[2,128,256]{2,1,0:T(8,128)(2,1)S(1)} %get-tuple-element.54), channel_id=1, source_target_pairs={{0,5},{1,4},{2,7},{3,6},{4,9},{5,8},{6,11},{7,10},{8,13},{9,12},{1... | collective-permute-start | bytes 393224 | tf_op jit(solution)/shard_map/ppermute | solution.py:375
  23.8 0.7 %collective-permute-start.10 = (bf16[2,128,256]{2,1,0:T(8,128)(2,1)S(1)}, bf16[2,128,256]{2,1,0:T(8,128)(2,1)S(1)}, u32[]{:S(2)}, u32[]{:S(2)}) collective-permute-start(bf16[2,128,256]{2,1,0:T(8,128)(2,1)S(1)} %get-tuple-element.55), channel_id=1, source_target_pairs={{0,4},{1,6},{2,5},{3,7},{4,0},{5,10},{6,9},{7,3},{8,12},{9,14},{10... | collective-permute-start | bytes 393224 | tf_op jit(solution)/shard_map/ppermute | solution.py:376
  24.5 0.0 collective-permute-done.7.refs_5_
  24.5 0.0 collective-permute-done.8.refs_6_
  24.5 4.5 %collective-permute-done.9.refs_7_.refs_6_ = bf16[2,128,256]{2,1,0:T(8,128)(2,1)S(1)} collective-permute-done((bf16[2,128,256]{2,1,0:T(8,128)(2,1)S(1)}, bf16[2,128,256]{2,1,0:T(8,128)(2,1)S(1)}, u32[]{:S(2)}, u32[]{:S(2)}) %collective-permute-start.9) | collective-permute-done | bytes 131104 | tf_op jit(solution)/shard_map/ppermute | solution.py:375
  29.0 0.0 collective-permute-done.10.refs_8_.refs_7_
  29.0 0.0 collective-permute-start.11
  29.0 0.0 collective-permute-done.12.refs_5_
  29.0 0.8 %tick2_even.1 = (bf16[4,128,256]{2,1,0:T(8,128)(2,1)S(1)}, bf16[2,128,256]{2,1,0:T(8,128)(2,1)S(1)}, bf16[2,128,256]{2,1,0:T(8,128)(2,1)S(1)}, bf16[2,128,256]{2,1,0:T(8,128)(2,1)S(1)}, bf16[2,128,256]{2,1,0:T(8,128)(2,1)S(1)}) custom-call(s32[30]{0:T(128)S(4)} %get-tuple-element.36.refs_0_, ...), custom_call_target="tpu_custom_call", output_to_operand_aliasing={{0}: (8, {}), {1}: (9, {}), {2}: (10, {})} | custom-call | flops 402653184 | bytes 2621440 | tf_op jit(solution)/shard_map/tick2_even/pallas_call | solution.py:225
  29.8 1.6 %collective-permute-start.13 = (bf16[2,128,256]{2,1,0:T(8,128)(2,1)S(1)}, bf16[2,128,256]{2,1,0:T(8,128)(2,1)S(1)}, u32[]{:S(2)}, u32[]{:S(2)}) collective-permute-start(bf16[2,128,256]{2,1,0:T(8,128)(2,1)S(1)} %get-tuple-element.61), channel_id=1, source_target_pairs={{0,5},{1,4},{2,7},{3,6},{4,9},{5,8},{6,11},{7,10},{8,13},{9,12},{1... | collective-permute-start | bytes 393224 | tf_op jit(solution)/shard_map/ppermute | solution.py:375
  31.4 1.9 %collective-permute-start.14 = (bf16[2,128,256]{2,1,0:T(8,128)(2,1)S(1)}, bf16[2,128,256]{2,1,0:T(8,128)(2,1)S(1)}, u32[]{:S(2)}, u32[]{:S(2)}) collective-permute-start(bf16[2,128,256]{2,1,0:T(8,128)(2,1)S(1)} %get-tuple-element.62), channel_id=1, source_target_pairs={{0,4},{1,6},{2,5},{3,7},{4,0},{5,10},{6,9},{7,3},{8,12},{9,14},{10... | collective-permute-start | bytes 393224 | tf_op jit(solution)/shard_map/ppermute | solution.py:376
  33.3 0.0 collective-permute-start.15
  33.3 0.5 %collective-permute-start.16 = (bf16[2,128,256]{2,1,0:T(8,128)(2,1)S(1)}, bf16[2,128,256]{2,1,0:T(8,128)(2,1)S(1)}, u32[]{:S(2)}, u32[]{:S(2)}) collective-permute-start(bf16[2,128,256]{2,1,0:T(8,128)(2,1)S(1)} %get-tuple-element.67), channel_id=1, source_target_pairs={{0,4},{4,0},{8,12},{12,8},{16,20},{20,16},{24,28},{28,24},{1,5},{5... | collective-permute-start | bytes 393224 | tf_op jit(solution)/shard_map/ppermute | solution.py:372
  33.8 3.9 %collective-permute-done.13.refs_7_.refs_6_ = bf16[2,128,256]{2,1,0:T(8,128)(2,1)S(1)} collective-permute-done((bf16[2,128,256]{2,1,0:T(8,128)(2,1)S(1)}, bf16[2,128,256]{2,1,0:T(8,128)(2,1)S(1)}, u32[]{:S(2)}, u32[]{:S(2)}) %collective-permute-start.13) | collective-permute-done | bytes 131104 | tf_op jit(solution)/shard_map/ppermute | solution.py:375
  37.7 0.0 collective-permute-done.14.refs_8_.refs_7_
  37.7 0.0 collective-permute-done.15.refs_5_
  37.7 0.0 collective-permute-done.16.refs_6_
  37.7 0.1 last_tick_odd.1
  37.8 0.0 collective-permute-done.11.refs_5_
  37.8 1.5 %last_tick_even.1 = (bf16[4,1,4,128,256]{4,3,2,1,0:T(8,128)(2,1)}, f32[1,4,128,256]{3,2,1,0:T(8,128)}) custom-call(s32[30]{0:T(128)S(4)} %get-tuple-element.36.refs_0_, bf16[1,4,6,2,128,128]{5,4,3,2,1,0:T(8,128)(2,1)S(1)} %get-tuple-element.38.refs_1_, ...), custom_call_target="tpu_custom_call", output_to_operand_aliasing={{0}: (11, {}), {1}: (12, {})} | custom-call | flops 402653184 | bytes 2621440 | tf_op jit(solution)/shard_map/last_tick_even/pallas_call | solution.py:225
  (2 shorter events, 0.0 us)
Async XLA Ops:
  1.8 6.3 %collective-permute-start.1 = (bf16[2,128,256]{2,1,0:T(8,128)(2,1)S(1)}, bf16[2,128,256]{2,1,0:T(8,128)(2,1)S(1)}, u32[]{:S(2)}, u32[]{:S(2)}) collective-permute-start(bf16[2,128,256]{2,1,0:T(8,128)(2,1)S(1)} %get-tuple-element.43), channel_id=1, source_target_pairs={{0,4},{1,2},{2,1},{3,7},{4,0},{5,6},{6,5},{7,3},{8,12},{9,10},{10,... | collective-permute-start | bytes 393224 | tf_op jit(solution)/shard_map/ppermute | solution.py:312
  2.4 7.4 %collective-permute-start = (bf16[2,128,256]{2,1,0:T(8,128)(2,1)S(1)}, bf16[2,128,256]{2,1,0:T(8,128)(2,1)S(1)}, u32[]{:S(2)}, u32[]{:S(2)}) collective-permute-start(bf16[2,128,256]{2,1,0:T(8,128)(2,1)S(1)} %get-tuple-element.37.after_ref), channel_id=1, source_target_pairs={{0,1},{1,0},{2,3},{3,2},{4,5},{5,4},{6,7},{7,6},{8,9},{9,8},{10,11... | collective-permute-start | bytes 393224 | tf_op jit(solution)/shard_map/ppermute | solution.py:311
  10.5 7.4 %collective-permute-start.6 = (bf16[4,128,256]{2,1,0:T(8,128)(2,1)S(1)}, bf16[4,128,256]{2,1,0:T(8,128)(2,1)S(1)}, u32[]{:S(2)}, u32[]{:S(2)}) collective-permute-start(bf16[4,128,256]{2,1,0:T(8,128)(2,1)S(1)} %get-tuple-element.48), channel_id=1, source_target_pairs={{0,4},{4,0},{8,12},{12,8},{16,20},{20,16},{24,28},{28,24},{1,5},{5... | collective-permute-start | bytes 786440 | tf_op jit(solution)/shard_map/ppermute | solution.py:368
  10.6 7.3 %collective-permute-start.4 = (bf16[2,128,256]{2,1,0:T(8,128)(2,1)S(1)}, bf16[2,128,256]{2,1,0:T(8,128)(2,1)S(1)}, u32[]{:S(2)}, u32[]{:S(2)}) collective-permute-start(bf16[2,128,256]{2,1,0:T(8,128)(2,1)S(1)} %get-tuple-element.46), channel_id=1, source_target_pairs={{0,5},{1,4},{2,7},{3,6},{4,9},{5,8},{6,11},{7,10},{8,13},{9,12},{1... | collective-permute-start | bytes 393224 | tf_op jit(solution)/shard_map/ppermute | solution.py:375
  12.4 5.4 %collective-permute-start.5 = (bf16[2,128,256]{2,1,0:T(8,128)(2,1)S(1)}, bf16[2,128,256]{2,1,0:T(8,128)(2,1)S(1)}, u32[]{:S(2)}, u32[]{:S(2)}) collective-permute-start(bf16[2,128,256]{2,1,0:T(8,128)(2,1)S(1)} %get-tuple-element.47), channel_id=1, source_target_pairs={{0,4},{1,6},{2,5},{3,7},{4,0},{5,10},{6,9},{7,3},{8,12},{9,14},{10... | collective-permute-start | bytes 393224 | tf_op jit(solution)/shard_map/ppermute | solution.py:376
  13.4 5.6 %collective-permute-start.2 = (bf16[2,128,256]{2,1,0:T(8,128)(2,1)S(1)}, bf16[2,128,256]{2,1,0:T(8,128)(2,1)S(1)}, u32[]{:S(2)}, u32[]{:S(2)}) collective-permute-start(bf16[2,128,256]{2,1,0:T(8,128)(2,1)S(1)} %get-tuple-element.44), channel_id=1, source_target_pairs={{0,4},{4,8},{8,12},{12,16},{16,20},{20,24},{24,28},{28,0},{1,5},{5... | collective-permute-start | bytes 393224 | tf_op jit(solution)/shard_map/ppermute | solution.py:367
  13.4 7.0 %collective-permute-start.3 = (bf16[2,128,256]{2,1,0:T(8,128)(2,1)S(1)}, bf16[2,128,256]{2,1,0:T(8,128)(2,1)S(1)}, u32[]{:S(2)}, u32[]{:S(2)}) collective-permute-start(bf16[2,128,256]{2,1,0:T(8,128)(2,1)S(1)} %get-tuple-element.45), channel_id=1, source_target_pairs={{0,4},{4,8},{8,12},{12,16},{16,20},{20,24},{24,28},{28,0},{1,5},{5... | collective-permute-start | bytes 393224 | tf_op jit(solution)/shard_map/ppermute | solution.py:367
  17.9 11.2 %collective-permute-start.12 = (bf16[4,128,256]{2,1,0:T(8,128)(2,1)S(1)}, bf16[4,128,256]{2,1,0:T(8,128)(2,1)S(1)}, u32[]{:S(2)}, u32[]{:S(2)}) collective-permute-start(bf16[4,128,256]{2,1,0:T(8,128)(2,1)S(1)} %get-tuple-element.57), channel_id=1, source_target_pairs={{0,4},{4,8},{8,12},{12,16},{16,20},{20,24},{24,28},{28,0},{1,5},{5... | collective-permute-start | bytes 786440 | tf_op jit(solution)/shard_map/ppermute | solution.py:370
  21.2 3.4 %collective-permute-start.7 = (bf16[2,128,256]{2,1,0:T(8,128)(2,1)S(1)}, bf16[2,128,256]{2,1,0:T(8,128)(2,1)S(1)}, u32[]{:S(2)}, u32[]{:S(2)}) collective-permute-start(bf16[2,128,256]{2,1,0:T(8,128)(2,1)S(1)} %get-tuple-element.52), channel_id=1, source_target_pairs={{0,4},{4,0},{8,12},{12,8},{16,20},{20,16},{24,28},{28,24},{1,5},{5... | collective-permute-start | bytes 393224 | tf_op jit(solution)/shard_map/ppermute | solution.py:372
  21.2 3.3 %collective-permute-start.8 = (bf16[2,128,256]{2,1,0:T(8,128)(2,1)S(1)}, bf16[2,128,256]{2,1,0:T(8,128)(2,1)S(1)}, u32[]{:S(2)}, u32[]{:S(2)}) collective-permute-start(bf16[2,128,256]{2,1,0:T(8,128)(2,1)S(1)} %get-tuple-element.53), channel_id=1, source_target_pairs={{0,4},{4,0},{8,12},{12,8},{16,20},{20,16},{24,28},{28,24},{1,5},{5... | collective-permute-start | bytes 393224 | tf_op jit(solution)/shard_map/ppermute | solution.py:372
  21.7 7.3 %collective-permute-start.9 = (bf16[2,128,256]{2,1,0:T(8,128)(2,1)S(1)}, bf16[2,128,256]{2,1,0:T(8,128)(2,1)S(1)}, u32[]{:S(2)}, u32[]{:S(2)}) collective-permute-start(bf16[2,128,256]{2,1,0:T(8,128)(2,1)S(1)} %get-tuple-element.54), channel_id=1, source_target_pairs={{0,5},{1,4},{2,7},{3,6},{4,9},{5,8},{6,11},{7,10},{8,13},{9,12},{1... | collective-permute-start | bytes 393224 | tf_op jit(solution)/shard_map/ppermute | solution.py:375
  23.8 5.2 %collective-permute-start.10 = (bf16[2,128,256]{2,1,0:T(8,128)(2,1)S(1)}, bf16[2,128,256]{2,1,0:T(8,128)(2,1)S(1)}, u32[]{:S(2)}, u32[]{:S(2)}) collective-permute-start(bf16[2,128,256]{2,1,0:T(8,128)(2,1)S(1)} %get-tuple-element.55), channel_id=1, source_target_pairs={{0,4},{1,6},{2,5},{3,7},{4,0},{5,10},{6,9},{7,3},{8,12},{9,14},{10... | collective-permute-start | bytes 393224 | tf_op jit(solution)/shard_map/ppermute | solution.py:376
  29.0 8.8 %collective-permute-start.11 = (bf16[4,128,256]{2,1,0:T(8,128)(2,1)S(1)}, bf16[4,128,256]{2,1,0:T(8,128)(2,1)S(1)}, u32[]{:S(2)}, u32[]{:S(2)}) collective-permute-start(bf16[4,128,256]{2,1,0:T(8,128)(2,1)S(1)} %get-tuple-element.56), channel_id=1, source_target_pairs={{0,4},{4,8},{8,12},{12,16},{16,20},{20,24},{24,28},{28,0},{1,5},{5... | collective-permute-start | bytes 786440 | tf_op jit(solution)/shard_map/ppermute | solution.py:370
  29.8 7.8 %collective-permute-start.13 = (bf16[2,128,256]{2,1,0:T(8,128)(2,1)S(1)}, bf16[2,128,256]{2,1,0:T(8,128)(2,1)S(1)}, u32[]{:S(2)}, u32[]{:S(2)}) collective-permute-start(bf16[2,128,256]{2,1,0:T(8,128)(2,1)S(1)} %get-tuple-element.61), channel_id=1, source_target_pairs={{0,5},{1,4},{2,7},{3,6},{4,9},{5,8},{6,11},{7,10},{8,13},{9,12},{1... | collective-permute-start | bytes 393224 | tf_op jit(solution)/shard_map/ppermute | solution.py:375
  31.4 6.3 %collective-permute-start.14 = (bf16[2,128,256]{2,1,0:T(8,128)(2,1)S(1)}, bf16[2,128,256]{2,1,0:T(8,128)(2,1)S(1)}, u32[]{:S(2)}, u32[]{:S(2)}) collective-permute-start(bf16[2,128,256]{2,1,0:T(8,128)(2,1)S(1)} %get-tuple-element.62), channel_id=1, source_target_pairs={{0,4},{1,6},{2,5},{3,7},{4,0},{5,10},{6,9},{7,3},{8,12},{9,14},{10... | collective-permute-start | bytes 393224 | tf_op jit(solution)/shard_map/ppermute | solution.py:376
  33.3 4.4 %collective-permute-start.15 = (bf16[2,128,256]{2,1,0:T(8,128)(2,1)S(1)}, bf16[2,128,256]{2,1,0:T(8,128)(2,1)S(1)}, u32[]{:S(2)}, u32[]{:S(2)}) collective-permute-start(bf16[2,128,256]{2,1,0:T(8,128)(2,1)S(1)} %get-tuple-element.66), channel_id=1, source_target_pairs={{0,4},{4,0},{8,12},{12,8},{16,20},{20,16},{24,28},{28,24},{1,5},{5... | collective-permute-start | bytes 393224 | tf_op jit(solution)/shard_map/ppermute | solution.py:372
  33.3 4.4 %collective-permute-start.16 = (bf16[2,128,256]{2,1,0:T(8,128)(2,1)S(1)}, bf16[2,128,256]{2,1,0:T(8,128)(2,1)S(1)}, u32[]{:S(2)}, u32[]{:S(2)}) collective-permute-start(bf16[2,128,256]{2,1,0:T(8,128)(2,1)S(1)} %get-tuple-element.67), channel_id=1, source_target_pairs={{0,4},{4,0},{8,12},{12,8},{16,20},{20,16},{24,28},{28,24},{1,5},{5... | collective-permute-start | bytes 393224 | tf_op jit(solution)/shard_map/ppermute | solution.py:372

commit v5 on v3

--- a/solution.py
+++ b/solution.py
@@ -40,9 +40,31 @@
                 list_ref[slot] = jnp.zeros(list_ref.shape[1:], list_ref.dtype)
 
 
+def start_load(hbm_refs, refs, rows, sems):
+    ops_hbm, source_hbm, pass_hbm, reflect_hbm = hbm_refs
+    pairs = ((pass_hbm, rows[0]), (reflect_hbm, rows[1]), (ops_hbm, refs[0]), (source_hbm, refs[1]))
+    copies = [
+        pltpu.make_async_copy(source, target, sems.at[i]) for i, (source, target) in enumerate(pairs)
+    ]
+    for copy in copies:
+        copy.start()
+    return copies
+
+
+def finish_load(copies, refs, rows):
+    for copy, coefficient, columns_ref in zip(copies, rows, refs[2:]):
+        copy.wait()
+        for b in range(columns_ref.shape[0]):
+            row = coefficient[0, pl.ds(b, 1), :]
+            columns_ref[b] = jnp.broadcast_to(row, columns_ref.shape[1:]).T
+    for copy in copies[2:]:
+        copy.wait()
+
+
 def prepare_kernel(
-    ids_hbm, count_hbm, pattern_hbm, inflow_hbm, plan_ref, wave_ref, first_ref, second_ref,
-    ids, count, pattern, landed, small_sems, sems,
+    ids_hbm, count_hbm, pattern_hbm, inflow_hbm, ops_hbm, source_hbm, pass_hbm, reflect_hbm,
+    plan_ref, wave_ref, first_ref, second_ref, ops_ref, source_ref, pass_ref, reflect_ref,
+    ids, count, pattern, landed, small_sems, sems, pass_rows, reflect_rows, load_sems,
 ):
     blocks = wave_ref.shape[0]
     small = [
@@ -72,32 +94,22 @@
         wave_ref[b] = landed[b].astype(wave_ref.dtype)
     write_lists(lax.axis_index("lat"), plan_ref, wave_ref, (first_ref, second_ref))
 
-
-def load_kernel(
-    ops_hbm, source_hbm, pass_hbm, reflect_hbm, after_ref,
-    ops_ref, source_ref, pass_ref, reflect_ref, pass_rows, reflect_rows, sems,
-):
-    del after_ref
-    copies = [
-        pltpu.make_async_copy(source, target, sems.at[i])
-        for i, (source, target) in enumerate(
-            (
-                (pass_hbm, pass_rows),
-                (reflect_hbm, reflect_rows),
-                (ops_hbm, ops_ref),
-                (source_hbm, source_ref),
-            )
-        )
-    ]
-    for copy in copies:
-        copy.start()
-    for copy, rows, columns_ref in zip(copies, (pass_rows, reflect_rows), (pass_ref, reflect_ref)):
-        copy.wait()
-        for b in range(columns_ref.shape[0]):
-            row = rows[0, pl.ds(b, 1), :]
-            columns_ref[b] = jnp.broadcast_to(row, columns_ref.shape[1:]).T
-    for copy in copies[2:]:
-        copy.wait()
+    @pl.when(lax.rem(lax.axis_index("depth"), 2) == 1)
+    def _():
+        refs = (ops_ref, source_ref, pass_ref, reflect_ref)
+        rows = (pass_rows, reflect_rows)
+        copies = start_load((ops_hbm, source_hbm, pass_hbm, reflect_hbm), refs, rows, load_sems)
+        finish_load(copies, refs, rows)
+
+
+def load_kernel(ops_hbm, source_hbm, pass_hbm, reflect_hbm, *rest):
+    refs, (pass_rows, reflect_rows, sems) = rest[4:8], rest[8:]
+
+    @pl.when(lax.rem(lax.axis_index("depth"), 2) == 0)
+    def _():
+        rows = (pass_rows, reflect_rows)
+        copies = start_load((ops_hbm, source_hbm, pass_hbm, reflect_hbm), refs, rows, sems)
+        finish_load(copies, refs, rows)
 
 
 def fill_buffer(section, tick, source_ref, wave_refs, first_ref, second_ref, buffer):
@@ -282,16 +294,33 @@
     both = ("depth", "lat")
     deeper = [(s, (s + 1) % sections) for s in range(sections)]
 
-    plan, wave, first, second = pl.pallas_call(
+    column_type = pltpu.VMEM((blocks, points, columns // 2), jnp.float32)
+    fixed_types = (
+        pltpu.VMEM(operators.shape, operators.dtype),
+        pltpu.VMEM(source.shape, source.dtype),
+        column_type,
+        column_type,
+    )
+    load_scratch = [
+        pltpu.VMEM(transmission.shape, transmission.dtype),
+        pltpu.VMEM(reflectivity.shape, reflectivity.dtype),
+        pltpu.SemaphoreType.DMA((4,)),
+    ]
+    load_cost = pl.CostEstimate(
+        flops=0, bytes_accessed=4 * (operators.size + source.size), transcendentals=0
+    )
+    stored = [in_hbm(a) for a in (operators, source, transmission, reflectivity)]
+    plan, wave, first, second, *fixed = pl.pallas_call(
         prepare_kernel,
         out_shape=(
             pltpu.SMEM((2 * (listed + 1) + blocks * taken,), jnp.int32),
             wave_type,
             list_type,
             list_type,
+            *fixed_types,
         ),
-        in_specs=[ANY_SPEC] * 4,
-        out_specs=(SMEM_SPEC,) + (VMEM_SPEC,) * 3,
+        in_specs=[ANY_SPEC] * 8,
+        out_specs=(SMEM_SPEC,) + (VMEM_SPEC,) * 7,
         scratch_shapes=[
             pltpu.SMEM(send_ids.shape, jnp.int32),
             pltpu.SMEM(send_count.shape, jnp.int32),
@@ -299,40 +328,29 @@
             pltpu.VMEM((blocks, points, columns), inflow.dtype),
             pltpu.SemaphoreType.DMA((3,)),
             pltpu.SemaphoreType.DMA((blocks,)),
+            *load_scratch,
         ],
         compiler_params=params,
         cost_estimate=pl.CostEstimate(
             flops=inflow.size, bytes_accessed=8 * inflow.size, transcendentals=0
         ),
         name="prepare",
-    )(*map(in_hbm, (send_ids, send_count, pattern, inflow)))
-    loaded_first = first
+    )(*map(in_hbm, (send_ids, send_count, pattern, inflow)), *stored)
     routes = swap_routes(sections, tiles)
     first = lax.ppermute(first, both, routes[0])
     second = lax.ppermute(second, both, routes[1])
 
-    column_type = pltpu.VMEM((blocks, points, columns // 2), jnp.float32)
     fixed = pl.pallas_call(
         load_kernel,
-        out_shape=(
-            pltpu.VMEM(operators.shape, operators.dtype),
-            pltpu.VMEM(source.shape, source.dtype),
-            column_type,
-            column_type,
-        ),
-        in_specs=[ANY_SPEC] * 4 + [VMEM_SPEC],
+        out_shape=fixed_types,
+        in_specs=[ANY_SPEC] * 4 + [VMEM_SPEC] * 4,
         out_specs=(VMEM_SPEC,) * 4,
-        scratch_shapes=[
-            pltpu.VMEM(transmission.shape, transmission.dtype),
-            pltpu.VMEM(reflectivity.shape, reflectivity.dtype),
-            pltpu.SemaphoreType.DMA((4,)),
-        ],
+        input_output_aliases={4: 0, 5: 1, 6: 2, 7: 3},
+        scratch_shapes=load_scratch,
         compiler_params=params,
-        cost_estimate=pl.CostEstimate(
-            flops=0, bytes_accessed=4 * (operators.size + source.size), transcendentals=0
-        ),
+        cost_estimate=load_cost,
         name="load",
-    )(*map(in_hbm, (operators, source, transmission, reflectivity)), in_vmem(loaded_first))
+    )(*stored, *map(in_vmem, fixed))
     fixed = [plan, *fixed]
 
     buffer_type = pltpu.VMEM((blocks + 2 * listed, points, columns), WAVE)
@@ -366,11 +384,11 @@
             if parity != EVEN:
                 sent[EVEN] = [lax.ppermute(known[3], "depth", crossing)]
             if parity != ODD:
+                echo, first, second = known[:3]
+                first = lax.ppermute(first, both, routes[0])
+                second = lax.ppermute(second, both, routes[1])
                 sent[ODD] = [lax.ppermute(a, "depth", inside) for a in known[-2:]]
         waves = sent
-        echo, first, second = known[:3]
-        first = lax.ppermute(first, both, routes[0])
-        second = lax.ppermute(second, both, routes[1])
         echoes.append(echo)
 
     tick = ticks - 1

time: 38.9 us -> 40.1 us (1.031)
  the two profiles are of different devices: /device:TPU:12 before, /device:TPU:20 now
where the time goes in v5:
time: 40.1 us; the launch traced here: 39.9 us
  waiting for transfers between devices  27.7 us (69%)
  Pallas kernels  6.76 us (17%)
  starting transfers between devices  4.7 us (12%)
  between operations  0.74 us (2%)
    ppermute x4, waiting for transfers between devices, per_device(): first = lax.ppermute(first, both, routes[0])  21.6 us
    pallas_call x7, Pallas kernels, grouped_call(): pl.pallas_call(body, out_shape=tuple(outs), in_specs=[SMEM_SPEC] + [VMEM_...  3.82 us
    ppermute x4, waiting for transfers between devices, per_device(): second = lax.ppermute(second, both, routes[1])  3.3 us
    ppermute x4, starting transfers between devices, per_device(): first = lax.ppermute(first, both, routes[0])  2.61 us
    ppermute x3, waiting for transfers between devices, per_device(): sent[EVEN] = [lax.ppermute(known[3], 'depth', crossing)]  1.84 us
    ppermute x6, starting transfers between devices, per_device(): sent[ODD] = [lax.ppermute(a, 'depth', inside) for a in known[-2:]]  1.8 us
    pallas_call x1, Pallas kernels, per_device(): pl.pallas_call(load_kernel, out_shape=fixed_types, in_specs=[ANY_SPEC] *...  1.67 us
    pallas_call x1, Pallas kernels, per_device(): pl.pallas_call(prepare_kernel, out_shape=(pltpu.SMEM((2 * (listed + 1) +...  1.26 us
  transfers between devices with their start and end apart: 17, of which 10 were waited for; matrix products, arithmetic and copies ran while one was open for 0% of the time, Pallas kernels for 8%

profile of v5, /device:TPU:20, one launch (start us, length us, event | category | flops | bytes accessed | tf_op | source)
XLA Modules:
  0.0 39.9 jit_solution(10193639845130363531)
XLA Ops:
  0.6 1.3 %prepare.1 = (s32[30]{0:T(128)S(4)}, bf16[4,128,256]{2,1,0:T(8,128)(2,1)S(1)}, bf16[2,128,256]{2,1,0:T(8,128)(2,1)S(1)}, bf16[2,128,256]{2,1,0:T(8,128)(2,1)S(1)...) custom-call(s32[1,2,2]{2,1,0:T(2,128)} %ids_hbm.1, ...), custom_call_target="tpu_custom_call" | custom-call | flops 131072 | bytes 1048576 | tf_op jit(solution)/shard_map/prepare/pallas_call | solution.py:313
  1.9 1.7 %collective-permute-start = (bf16[2,128,256]{2,1,0:T(8,128)(2,1)S(1)}, bf16[2,128,256]{2,1,0:T(8,128)(2,1)S(1)}, u32[]{:S(2)}, u32[]{:S(2)}) collective-permute-start(bf16[2,128,256]{2,1,0:T(8,128)(2,1)S(1)} %get-tuple-element.50), channel_id=1, source_target_pairs={{0,1},{1,0},{2,3},{3,2},{4,5},{5,4},{6,7},{7,6},{8,9},{9,8},{10,11... | collective-permute-start | bytes 393224 | tf_op jit(solution)/shard_map/ppermute | solution.py:340
  3.6 0.0 collective-permute-start.1
  3.6 1.7 %load.1 = (bf16[1,4,6,2,128,128]{5,4,3,2,1,0:T(8,128)(2,1)S(1)}, bf16[3,4,128,256]{3,2,1,0:T(8,128)(2,1)S(1)}, f32[4,128,128]{2,1,0:T(8,128)S(1)}, f32[4,128,128]{2,1,0:T(8,128)S(1)}) custom-call(bf16[1,4,6,2,128,128]{5,4,3,2,1,0:T(8,128)(2,1)} %ops_hbm.3, ...), custom_call_target="tpu_custom_call", output_to_operand_aliasing={{0}: (4, {}), {1}: (5, {}), {2}: (6, {}), {3}: (7, {})} | custom-call | bytes 4718592 | tf_op jit(solution)/shard_map/load/pallas_call | solution.py:343
  5.2 2.7 %collective-permute-done.refs_6_ = bf16[2,128,256]{2,1,0:T(8,128)(2,1)S(1)} collective-permute-done((bf16[2,128,256]{2,1,0:T(8,128)(2,1)S(1)}, bf16[2,128,256]{2,1,0:T(8,128)(2,1)S(1)}, u32[]{:S(2)}, u32[]{:S(2)}) %collective-permute-start) | collective-permute-done | bytes 131104 | tf_op jit(solution)/shard_map/ppermute | solution.py:340
  7.9 1.8 %collective-permute-done.1.refs_7_ = bf16[2,128,256]{2,1,0:T(8,128)(2,1)S(1)} collective-permute-done((bf16[2,128,256]{2,1,0:T(8,128)(2,1)S(1)}, bf16[2,128,256]{2,1,0:T(8,128)(2,1)S(1)}, u32[]{:S(2)}, u32[]{:S(2)}) %collective-permute-start.1) | collective-permute-done | bytes 131104 | tf_op jit(solution)/shard_map/ppermute | solution.py:341
  9.7 0.7 %tick0.1 = (bf16[4,128,256]{2,1,0:T(8,128)(2,1)S(1)}, bf16[2,128,256]{2,1,0:T(8,128)(2,1)S(1)}, bf16[2,128,256]{2,1,0:T(8,128)(2,1)S(1)}, bf16[4,128,256]{2,1,0:...) custom-call(s32[30]{0:T(128)S(4)} %get-tuple-element.40.refs_0_, ...), custom_call_target="tpu_custom_call" | custom-call | flops 402653184 | bytes 2621440 | tf_op jit(solution)/shard_map/tick0/pallas_call | solution.py:237
  10.5 0.2 collective-permute-start.2
  10.6 0.9 %collective-permute-start.3 = (bf16[2,128,256]{2,1,0:T(8,128)(2,1)S(1)}, bf16[2,128,256]{2,1,0:T(8,128)(2,1)S(1)}, u32[]{:S(2)}, u32[]{:S(2)}) collective-permute-start(bf16[2,128,256]{2,1,0:T(8,128)(2,1)S(1)} %get-tuple-element.53), channel_id=1, source_target_pairs={{0,5},{1,4},{2,7},{3,6},{4,9},{5,8},{6,11},{7,10},{8,13},{9,12},{1... | collective-permute-start | bytes 393224 | tf_op jit(solution)/shard_map/ppermute | solution.py:388
  11.5 0.0 collective-permute-start.4
  11.5 0.6 %collective-permute-start.5 = (bf16[2,128,256]{2,1,0:T(8,128)(2,1)S(1)}, bf16[2,128,256]{2,1,0:T(8,128)(2,1)S(1)}, u32[]{:S(2)}, u32[]{:S(2)}) collective-permute-start(bf16[2,128,256]{2,1,0:T(8,128)(2,1)S(1)} %get-tuple-element.55), channel_id=1, source_target_pairs={{0,4},{4,0},{8,12},{12,8},{16,20},{20,16},{24,28},{28,24},{1,5},{5... | collective-permute-start | bytes 393224 | tf_op jit(solution)/shard_map/ppermute | solution.py:390
  12.1 0.1 collective-permute-start.6
  12.2 5.3 %collective-permute-done.3.refs_7_.refs_6_ = bf16[2,128,256]{2,1,0:T(8,128)(2,1)S(1)} collective-permute-done((bf16[2,128,256]{2,1,0:T(8,128)(2,1)S(1)}, bf16[2,128,256]{2,1,0:T(8,128)(2,1)S(1)}, u32[]{:S(2)}, u32[]{:S(2)}) %collective-permute-start.3) | collective-permute-done | bytes 131104 | tf_op jit(solution)/shard_map/ppermute | solution.py:388
  17.5 1.5 %collective-permute-done.4.refs_8_.refs_7_ = bf16[2,128,256]{2,1,0:T(8,128)(2,1)S(1)} collective-permute-done((bf16[2,128,256]{2,1,0:T(8,128)(2,1)S(1)}, bf16[2,128,256]{2,1,0:T(8,128)(2,1)S(1)}, u32[]{:S(2)}, u32[]{:S(2)}) %collective-permute-start.4) | collective-permute-done | bytes 131104 | tf_op jit(solution)/shard_map/ppermute | solution.py:389
  19.0 0.0 collective-permute-done.5.refs_5_
  19.0 0.0 collective-permute-done.6.refs_6_
  19.0 0.1 collective-permute-start.12
  19.0 1.0 %collective-permute-done.2.refs_5_ = bf16[4,128,256]{2,1,0:T(8,128)(2,1)S(1)} collective-permute-done((bf16[4,128,256]{2,1,0:T(8,128)(2,1)S(1)}, bf16[4,128,256]{2,1,0:T(8,128)(2,1)S(1)}, u32[]{:S(2)}, u32[]{:S(2)}) %collective-permute-start.2) | collective-permute-done | bytes 262176 | tf_op jit(solution)/shard_map/ppermute | solution.py:385
  20.0 0.7 %tick1_even.1 = (bf16[4,128,256]{2,1,0:T(8,128)(2,1)S(1)}, bf16[2,128,256]{2,1,0:T(8,128)(2,1)S(1)}, bf16[2,128,256]{2,1,0:T(8,128)(2,1)S(1)}, bf16[2,128,256]{2,1,0:T(8,128)(2,1)S(1)}, bf16[2,128,256]{2,1,0:T(8,128)(2,1)S(1)}) custom-call(s32[30]{0:T(128)S(4)} %get-tuple-element.40.refs_0_, ...), custom_call_target="tpu_custom_call", output_to_operand_aliasing={{0}: (8, {}), {1}: (9, {}), {2}: (10, {})} | custom-call | flops 402653184 | bytes 2621440 | tf_op jit(solution)/shard_map/tick1_even/pallas_call | solution.py:237
  20.8 0.1 collective-permute-start.7
  20.8 0.5 %collective-permute-start.8 = (bf16[2,128,256]{2,1,0:T(8,128)(2,1)S(1)}, bf16[2,128,256]{2,1,0:T(8,128)(2,1)S(1)}, u32[]{:S(2)}, u32[]{:S(2)}) collective-permute-start(bf16[2,128,256]{2,1,0:T(8,128)(2,1)S(1)} %get-tuple-element.61), channel_id=1, source_target_pairs={{0,4},{4,0},{8,12},{12,8},{16,20},{20,16},{24,28},{28,24},{1,5},{5... | collective-permute-start | bytes 393224 | tf_op jit(solution)/shard_map/ppermute | solution.py:390
  21.3 0.0 collective-permute-start.9
  21.4 0.0 collective-permute-start.10
  21.4 0.8 %collective-permute-done.7.refs_5_ = bf16[2,128,256]{2,1,0:T(8,128)(2,1)S(1)} collective-permute-done((bf16[2,128,256]{2,1,0:T(8,128)(2,1)S(1)}, bf16[2,128,256]{2,1,0:T(8,128)(2,1)S(1)}, u32[]{:S(2)}, u32[]{:S(2)}) %collective-permute-start.7) | collective-permute-done | bytes 131104 | tf_op jit(solution)/shard_map/ppermute | solution.py:390
  22.2 0.2 collective-permute-done.8.refs_6_
  22.4 6.6 %collective-permute-done.9.refs_7_.refs_6_ = bf16[2,128,256]{2,1,0:T(8,128)(2,1)S(1)} collective-permute-done((bf16[2,128,256]{2,1,0:T(8,128)(2,1)S(1)}, bf16[2,128,256]{2,1,0:T(8,128)(2,1)S(1)}, u32[]{:S(2)}, u32[]{:S(2)}) %collective-permute-start.9) | collective-permute-done | bytes 131104 | tf_op jit(solution)/shard_map/ppermute | solution.py:388
  28.9 0.0 collective-permute-done.10.refs_8_.refs_7_
  28.9 0.0 collective-permute-start.11
  29.0 0.0 collective-permute-done.12.refs_5_
  29.0 0.8 %tick2_even.1 = (bf16[4,128,256]{2,1,0:T(8,128)(2,1)S(1)}, bf16[2,128,256]{2,1,0:T(8,128)(2,1)S(1)}, bf16[2,128,256]{2,1,0:T(8,128)(2,1)S(1)}, bf16[2,128,256]{2,1,0:T(8,128)(2,1)S(1)}, bf16[2,128,256]{2,1,0:T(8,128)(2,1)S(1)}) custom-call(s32[30]{0:T(128)S(4)} %get-tuple-element.40.refs_0_, ...), custom_call_target="tpu_custom_call", output_to_operand_aliasing={{0}: (8, {}), {1}: (9, {}), {2}: (10, {})} | custom-call | flops 402653184 | bytes 2621440 | tf_op jit(solution)/shard_map/tick2_even/pallas_call | solution.py:237
  29.7 0.1 collective-permute-start.13
  29.8 0.1 collective-permute-start.14
  29.9 0.1 collective-permute-start.15
  29.9 0.5 %collective-permute-start.16 = (bf16[2,128,256]{2,1,0:T(8,128)(2,1)S(1)}, bf16[2,128,256]{2,1,0:T(8,128)(2,1)S(1)}, u32[]{:S(2)}, u32[]{:S(2)}) collective-permute-start(bf16[2,128,256]{2,1,0:T(8,128)(2,1)S(1)} %get-tuple-element.75), channel_id=1, source_target_pairs={{0,4},{4,0},{8,12},{12,8},{16,20},{20,16},{24,28},{28,24},{1,5},{5... | collective-permute-start | bytes 393224 | tf_op jit(solution)/shard_map/ppermute | solution.py:390
  30.4 7.0 %collective-permute-done.13.refs_7_.refs_6_ = bf16[2,128,256]{2,1,0:T(8,128)(2,1)S(1)} collective-permute-done((bf16[2,128,256]{2,1,0:T(8,128)(2,1)S(1)}, bf16[2,128,256]{2,1,0:T(8,128)(2,1)S(1)}, u32[]{:S(2)}, u32[]{:S(2)}) %collective-permute-start.13) | collective-permute-done | bytes 131104 | tf_op jit(solution)/shard_map/ppermute | solution.py:388
  37.4 0.0 collective-permute-done.14.refs_8_.refs_7_
  37.5 0.0 collective-permute-done.15.refs_5_
  37.5 0.0 collective-permute-done.16.refs_6_
  37.5 0.1 last_tick_odd.1
  37.6 0.9 %collective-permute-done.11.refs_5_ = bf16[4,128,256]{2,1,0:T(8,128)(2,1)S(1)} collective-permute-done((bf16[4,128,256]{2,1,0:T(8,128)(2,1)S(1)}, bf16[4,128,256]{2,1,0:T(8,128)(2,1)S(1)}, u32[]{:S(2)}, u32[]{:S(2)}) %collective-permute-start.11) | collective-permute-done | bytes 262176 | tf_op jit(solution)/shard_map/ppermute | solution.py:385
  38.5 1.5 %last_tick_even.1 = (bf16[4,1,4,128,256]{4,3,2,1,0:T(8,128)(2,1)}, f32[1,4,128,256]{3,2,1,0:T(8,128)}) custom-call(s32[30]{0:T(128)S(4)} %get-tuple-element.40.refs_0_, bf16[1,4,6,2,128,128]{5,4,3,2,1,0:T(8,128)(2,1)S(1)} %get-tuple-element.45.refs_1_, ...), custom_call_target="tpu_custom_call", output_to_operand_aliasing={{0}: (11, {}), {1}: (12, {})} | custom-call | flops 402653184 | bytes 2621440 | tf_op jit(solution)/shard_map/last_tick_even/pallas_call | solution.py:237
  (2 shorter events, 0.0 us)
Async XLA Ops:
  1.9 6.0 %collective-permute-start = (bf16[2,128,256]{2,1,0:T(8,128)(2,1)S(1)}, bf16[2,128,256]{2,1,0:T(8,128)(2,1)S(1)}, u32[]{:S(2)}, u32[]{:S(2)}) collective-permute-start(bf16[2,128,256]{2,1,0:T(8,128)(2,1)S(1)} %get-tuple-element.50), channel_id=1, source_target_pairs={{0,1},{1,0},{2,3},{3,2},{4,5},{5,4},{6,7},{7,6},{8,9},{9,8},{10,11... | collective-permute-start | bytes 393224 | tf_op jit(solution)/shard_map/ppermute | solution.py:340
  3.6 6.2 %collective-permute-start.1 = (bf16[2,128,256]{2,1,0:T(8,128)(2,1)S(1)}, bf16[2,128,256]{2,1,0:T(8,128)(2,1)S(1)}, u32[]{:S(2)}, u32[]{:S(2)}) collective-permute-start(bf16[2,128,256]{2,1,0:T(8,128)(2,1)S(1)} %get-tuple-element.51), channel_id=1, source_target_pairs={{0,4},{1,2},{2,1},{3,7},{4,0},{5,6},{6,5},{7,3},{8,12},{9,10},{10,... | collective-permute-start | bytes 393224 | tf_op jit(solution)/shard_map/ppermute | solution.py:341
  10.5 9.6 %collective-permute-start.2 = (bf16[4,128,256]{2,1,0:T(8,128)(2,1)S(1)}, bf16[4,128,256]{2,1,0:T(8,128)(2,1)S(1)}, u32[]{:S(2)}, u32[]{:S(2)}) collective-permute-start(bf16[4,128,256]{2,1,0:T(8,128)(2,1)S(1)} %get-tuple-element.52), channel_id=1, source_target_pairs={{0,4},{4,8},{8,12},{12,16},{16,20},{20,24},{24,28},{28,0},{1,5},{5... | collective-permute-start | bytes 786440 | tf_op jit(solution)/shard_map/ppermute | solution.py:385
  10.6 6.9 %collective-permute-start.3 = (bf16[2,128,256]{2,1,0:T(8,128)(2,1)S(1)}, bf16[2,128,256]{2,1,0:T(8,128)(2,1)S(1)}, u32[]{:S(2)}, u32[]{:S(2)}) collective-permute-start(bf16[2,128,256]{2,1,0:T(8,128)(2,1)S(1)} %get-tuple-element.53), channel_id=1, source_target_pairs={{0,5},{1,4},{2,7},{3,6},{4,9},{5,8},{6,11},{7,10},{8,13},{9,12},{1... | collective-permute-start | bytes 393224 | tf_op jit(solution)/shard_map/ppermute | solution.py:388
  11.5 7.4 %collective-permute-start.4 = (bf16[2,128,256]{2,1,0:T(8,128)(2,1)S(1)}, bf16[2,128,256]{2,1,0:T(8,128)(2,1)S(1)}, u32[]{:S(2)}, u32[]{:S(2)}) collective-permute-start(bf16[2,128,256]{2,1,0:T(8,128)(2,1)S(1)} %get-tuple-element.54), channel_id=1, source_target_pairs={{0,4},{1,6},{2,5},{3,7},{4,0},{5,10},{6,9},{7,3},{8,12},{9,14},{10... | collective-permute-start | bytes 393224 | tf_op jit(solution)/shard_map/ppermute | solution.py:389
  11.5 7.4 %collective-permute-start.5 = (bf16[2,128,256]{2,1,0:T(8,128)(2,1)S(1)}, bf16[2,128,256]{2,1,0:T(8,128)(2,1)S(1)}, u32[]{:S(2)}, u32[]{:S(2)}) collective-permute-start(bf16[2,128,256]{2,1,0:T(8,128)(2,1)S(1)} %get-tuple-element.55), channel_id=1, source_target_pairs={{0,4},{4,0},{8,12},{12,8},{16,20},{20,16},{24,28},{28,24},{1,5},{5... | collective-permute-start | bytes 393224 | tf_op jit(solution)/shard_map/ppermute | solution.py:390
  12.1 6.9 %collective-permute-start.6 = (bf16[2,128,256]{2,1,0:T(8,128)(2,1)S(1)}, bf16[2,128,256]{2,1,0:T(8,128)(2,1)S(1)}, u32[]{:S(2)}, u32[]{:S(2)}) collective-permute-start(bf16[2,128,256]{2,1,0:T(8,128)(2,1)S(1)} %get-tuple-element.56), channel_id=1, source_target_pairs={{0,4},{4,0},{8,12},{12,8},{16,20},{20,16},{24,28},{28,24},{1,5},{5... | collective-permute-start | bytes 393224 | tf_op jit(solution)/shard_map/ppermute | solution.py:390
  19.0 10.0 %collective-permute-start.12 = (bf16[4,128,256]{2,1,0:T(8,128)(2,1)S(1)}, bf16[4,128,256]{2,1,0:T(8,128)(2,1)S(1)}, u32[]{:S(2)}, u32[]{:S(2)}) collective-permute-start(bf16[4,128,256]{2,1,0:T(8,128)(2,1)S(1)} %get-tuple-element.65), channel_id=1, source_target_pairs={{0,4},{4,8},{8,12},{12,16},{16,20},{20,24},{24,28},{28,0},{1,5},{5... | collective-permute-start | bytes 786440 | tf_op jit(solution)/shard_map/ppermute | solution.py:385
  20.8 1.4 %collective-permute-start.7 = (bf16[2,128,256]{2,1,0:T(8,128)(2,1)S(1)}, bf16[2,128,256]{2,1,0:T(8,128)(2,1)S(1)}, u32[]{:S(2)}, u32[]{:S(2)}) collective-permute-start(bf16[2,128,256]{2,1,0:T(8,128)(2,1)S(1)} %get-tuple-element.60), channel_id=1, source_target_pairs={{0,4},{4,0},{8,12},{12,8},{16,20},{20,16},{24,28},{28,24},{1,5},{5... | collective-permute-start | bytes 393224 | tf_op jit(solution)/shard_map/ppermute | solution.py:390
  20.8 1.5 %collective-permute-start.8 = (bf16[2,128,256]{2,1,0:T(8,128)(2,1)S(1)}, bf16[2,128,256]{2,1,0:T(8,128)(2,1)S(1)}, u32[]{:S(2)}, u32[]{:S(2)}) collective-permute-start(bf16[2,128,256]{2,1,0:T(8,128)(2,1)S(1)} %get-tuple-element.61), channel_id=1, source_target_pairs={{0,4},{4,0},{8,12},{12,8},{16,20},{20,16},{24,28},{28,24},{1,5},{5... | collective-permute-start | bytes 393224 | tf_op jit(solution)/shard_map/ppermute | solution.py:390
  21.3 7.6 %collective-permute-start.9 = (bf16[2,128,256]{2,1,0:T(8,128)(2,1)S(1)}, bf16[2,128,256]{2,1,0:T(8,128)(2,1)S(1)}, u32[]{:S(2)}, u32[]{:S(2)}) collective-permute-start(bf16[2,128,256]{2,1,0:T(8,128)(2,1)S(1)} %get-tuple-element.62), channel_id=1, source_target_pairs={{0,5},{1,4},{2,7},{3,6},{4,9},{5,8},{6,11},{7,10},{8,13},{9,12},{1... | collective-permute-start | bytes 393224 | tf_op jit(solution)/shard_map/ppermute | solution.py:388
  21.4 7.6 %collective-permute-start.10 = (bf16[2,128,256]{2,1,0:T(8,128)(2,1)S(1)}, bf16[2,128,256]{2,1,0:T(8,128)(2,1)S(1)}, u32[]{:S(2)}, u32[]{:S(2)}) collective-permute-start(bf16[2,128,256]{2,1,0:T(8,128)(2,1)S(1)} %get-tuple-element.63), channel_id=1, source_target_pairs={{0,4},{1,6},{2,5},{3,7},{4,0},{5,10},{6,9},{7,3},{8,12},{9,14},{10... | collective-permute-start | bytes 393224 | tf_op jit(solution)/shard_map/ppermute | solution.py:389
  28.9 9.5 %collective-permute-start.11 = (bf16[4,128,256]{2,1,0:T(8,128)(2,1)S(1)}, bf16[4,128,256]{2,1,0:T(8,128)(2,1)S(1)}, u32[]{:S(2)}, u32[]{:S(2)}) collective-permute-start(bf16[4,128,256]{2,1,0:T(8,128)(2,1)S(1)} %get-tuple-element.64), channel_id=1, source_target_pairs={{0,4},{4,8},{8,12},{12,16},{16,20},{20,24},{24,28},{28,0},{1,5},{5... | collective-permute-start | bytes 786440 | tf_op jit(solution)/shard_map/ppermute | solution.py:385
  29.7 7.7 %collective-permute-start.13 = (bf16[2,128,256]{2,1,0:T(8,128)(2,1)S(1)}, bf16[2,128,256]{2,1,0:T(8,128)(2,1)S(1)}, u32[]{:S(2)}, u32[]{:S(2)}) collective-permute-start(bf16[2,128,256]{2,1,0:T(8,128)(2,1)S(1)} %get-tuple-element.69), channel_id=1, source_target_pairs={{0,5},{1,4},{2,7},{3,6},{4,9},{5,8},{6,11},{7,10},{8,13},{9,12},{1... | collective-permute-start | bytes 393224 | tf_op jit(solution)/shard_map/ppermute | solution.py:388
  29.8 7.7 %collective-permute-start.14 = (bf16[2,128,256]{2,1,0:T(8,128)(2,1)S(1)}, bf16[2,128,256]{2,1,0:T(8,128)(2,1)S(1)}, u32[]{:S(2)}, u32[]{:S(2)}) collective-permute-start(bf16[2,128,256]{2,1,0:T(8,128)(2,1)S(1)} %get-tuple-element.70), channel_id=1, source_target_pairs={{0,4},{1,6},{2,5},{3,7},{4,0},{5,10},{6,9},{7,3},{8,12},{9,14},{10... | collective-permute-start | bytes 393224 | tf_op jit(solution)/shard_map/ppermute | solution.py:389
  29.9 7.6 %collective-permute-start.15 = (bf16[2,128,256]{2,1,0:T(8,128)(2,1)S(1)}, bf16[2,128,256]{2,1,0:T(8,128)(2,1)S(1)}, u32[]{:S(2)}, u32[]{:S(2)}) collective-permute-start(bf16[2,128,256]{2,1,0:T(8,128)(2,1)S(1)} %get-tuple-element.74), channel_id=1, source_target_pairs={{0,4},{4,0},{8,12},{12,8},{16,20},{20,16},{24,28},{28,24},{1,5},{5... | collective-permute-start | bytes 393224 | tf_op jit(solution)/shard_map/ppermute | solution.py:390
  29.9 7.5 %collective-permute-start.16 = (bf16[2,128,256]{2,1,0:T(8,128)(2,1)S(1)}, bf16[2,128,256]{2,1,0:T(8,128)(2,1)S(1)}, u32[]{:S(2)}, u32[]{:S(2)}) collective-permute-start(bf16[2,128,256]{2,1,0:T(8,128)(2,1)S(1)} %get-tuple-element.75), channel_id=1, source_target_pairs={{0,4},{4,0},{8,12},{12,8},{16,20},{20,16},{24,28},{28,24},{1,5},{5... | collective-permute-start | bytes 393224 | tf_op jit(solution)/shard_map/ppermute | solution.py:390

commit v6 on v3

--- a/solution.py
+++ b/solution.py
@@ -23,9 +23,9 @@
     return pltpu.with_memory_space_constraint(array, pltpu.HBM)
 
 
-def write_lists(tile, plan_ref, blocks_ref, lists):
+def write_lists(section, plan_ref, blocks_ref, lists):
     listed = lists[0].shape[0]
-    parity = lax.rem(tile, 2)
+    parity = lax.rem(section + lax.axis_index("lat"), 2)
     for list_ref, side in zip(lists, (UPPER - parity, parity)):
         count = plan_ref[2 * listed + side]
         for slot in range(listed):
@@ -70,7 +70,7 @@
     for b, copy in enumerate(large):
         copy.wait()
         wave_ref[b] = landed[b].astype(wave_ref.dtype)
-    write_lists(lax.axis_index("lat"), plan_ref, wave_ref, (first_ref, second_ref))
+    write_lists(lax.axis_index("depth"), plan_ref, wave_ref, (first_ref, second_ref))
 
 
 def load_kernel(
@@ -118,7 +118,8 @@
         def _():
             buffer[:blocks] = source_ref[tick - 1]
 
-    parity = lax.rem(lax.axis_index("lat"), 2)
+    sender = section if tick == 0 else section + 1
+    parity = lax.rem(sender + lax.axis_index("lat"), 2)
     buffer[pl.ds(blocks + (1 - parity) * listed, listed)] = first_ref[...]
     buffer[pl.ds(blocks + parity * listed, listed)] = second_ref[...]
 
@@ -150,7 +151,6 @@
     del known_refs
     echo_ref, first_ref, second_ref, *onward_refs = out_refs
     section = lax.axis_index("depth")
-    tile = lax.axis_index("lat")
     listed = first_ref.shape[0]
 
     @pl.when(acts(section, parity))
@@ -171,11 +171,11 @@
 
         @pl.when(section != sections - 1)
         def _():
-            write_lists(tile, plan_ref, onward, (first_ref, second_ref))
+            write_lists(section, plan_ref, onward, (first_ref, second_ref))
 
         @pl.when(section == sections - 1)
         def _():
-            write_lists(tile, plan_ref, source_ref.at[tick], (first_ref, second_ref))
+            write_lists(section, plan_ref, source_ref.at[tick], (first_ref, second_ref))
 
 
 def last_kernel(
@@ -232,8 +232,8 @@
     )(flat[0], *map(in_vmem, flat[1:]), *known)
 
 
-def neighbour(j, turn, tiles):
-    to = j + (1 if (j + turn) % 2 == 0 else -1)
+def neighbour(s, j, turn, tiles):
+    to = j + (1 if (s + j + turn) % 2 == 0 else -1)
     return to if 0 <= to < tiles else None
 
 
@@ -243,8 +243,8 @@
         route = []
         for s in range(sections):
             for j in range(tiles):
-                to = neighbour(j, turn, tiles)
-                end = ((s ^ 1) * tiles + j) if to is None else (s * tiles + to)
+                to = neighbour(s, j, turn, tiles)
+                end = (s + 2) % sections * tiles + j if to is None else s * tiles + to
                 route.append((s * tiles + j, end))
         routes.append(route)
     return routes
@@ -256,7 +256,7 @@
         route = []
         for s in range(sections):
             for j in range(tiles):
-                to = neighbour(j, turn, tiles)
+                to = neighbour(s, j, turn, tiles)
                 end = (s ^ 1) * tiles + j if to is None else (s + 1) % sections * tiles + to
                 route.append((s * tiles + j, end))
         routes.append(route)

time: 38.9 us -> 39.2 us (level)
  the two profiles are of different devices: /device:TPU:12 before, /device:TPU:0 now
where the time goes in v6:
time: 39.2 us; the launch traced here: 39.1 us
  waiting for transfers between devices  16.1 us (41%)
  starting transfers between devices  15.4 us (39%)
  Pallas kernels  6.81 us (17%)
  between operations  0.73 us (2%)
    ppermute x4, waiting for transfers between devices, per_device(): second = lax.ppermute(second, both, routes[1])  12.7 us
    ppermute x4, starting transfers between devices, per_device(): first = lax.ppermute(first, both, routes[0])  6.6 us
    ppermute x6, starting transfers between devices, per_device(): sent[ODD] = [lax.ppermute(a, 'depth', inside) for a in known[-2:]]  5.57 us
    pallas_call x7, Pallas kernels, grouped_call(): pl.pallas_call(body, out_shape=tuple(outs), in_specs=[SMEM_SPEC] + [VMEM_...  3.91 us
    ppermute x4, waiting for transfers between devices, per_device(): first = lax.ppermute(first, both, routes[0])  3.42 us
    ppermute x4, starting transfers between devices, per_device(): second = lax.ppermute(second, both, routes[1])  3 us
    pallas_call x1, Pallas kernels, per_device(): pl.pallas_call(load_kernel, out_shape=(pltpu.VMEM(operators.shape, operat...  1.67 us
    pallas_call x1, Pallas kernels, per_device(): pl.pallas_call(prepare_kernel, out_shape=(pltpu.SMEM((2 * (listed + 1) +...  1.22 us
  transfers between devices with their start and end apart: 17, of which 7 were waited for; matrix products, arithmetic and copies ran while one was open for 0% of the time, Pallas kernels for 9%

profile of v6, /device:TPU:0, one launch (start us, length us, event | category | flops | bytes accessed | tf_op | source)
XLA Modules:
  0.0 39.1 jit_solution(13251990366182695344)
XLA Ops:
  0.6 1.2 %prepare.1 = (s32[30]{0:T(128)S(4)}, bf16[4,128,256]{2,1,0:T(8,128)(2,1)S(1)}, bf16[2,128,256]{2,1,0:T(8,128)(2,1)S(1)}, bf16[2,128,256]{2,1,0:T(8,128)(2,1)S(1)}) custom-call(s32[1,2,2]{2,1,0:T(2,128)} %ids_hbm.1, s32[1,2]{1,0:T(1,128)} %count_hbm.1, s32[4,6]{1,0:T(4,128)} %pattern_hbm.1, f32[1,4,128,256]{3,2,1,0:T(8,128)} %inflow_hbm.1), custom_call_target="tpu_custom_call" | custom-call | flops 131072 | bytes 1048576 | tf_op jit(solution)/shard_map/prepare/pallas_call | solution.py:285
  1.9 3.0 %collective-permute-start.1 = (bf16[2,128,256]{2,1,0:T(8,128)(2,1)S(1)}, bf16[2,128,256]{2,1,0:T(8,128)(2,1)S(1)}, u32[]{:S(2)}, u32[]{:S(2)}) collective-permute-start(bf16[2,128,256]{2,1,0:T(8,128)(2,1)S(1)} %get-tuple-element.43), channel_id=1, source_target_pairs={{0,8},{1,2},{2,1},{3,11},{4,5},{5,4},{6,7},{7,6},{8,16},{9,10},{10... | collective-permute-start | bytes 393224 | tf_op jit(solution)/shard_map/ppermute | solution.py:312
  4.8 1.7 %collective-permute-start = (bf16[2,128,256]{2,1,0:T(8,128)(2,1)S(1)}, bf16[2,128,256]{2,1,0:T(8,128)(2,1)S(1)}, u32[]{:S(2)}, u32[]{:S(2)}) collective-permute-start(bf16[2,128,256]{2,1,0:T(8,128)(2,1)S(1)} %get-tuple-element.37.after_ref), channel_id=1, source_target_pairs={{0,1},{1,0},{2,3},{3,2},{4,12},{5,6},{6,5},{7,15},{8,9},{9,8},{10,... | collective-permute-start | bytes 393224 | tf_op jit(solution)/shard_map/ppermute | solution.py:311
  6.5 1.7 %load.1 = (bf16[1,4,6,2,128,128]{5,4,3,2,1,0:T(8,128)(2,1)S(1)}, bf16[3,4,128,256]{3,2,1,0:T(8,128)(2,1)S(1)}, f32[4,128,128]{2,1,0:T(8,128)S(1)}, f32[4,128,128]{2,1,0:T(8,128)S(1)}) custom-call(bf16[1,4,6,2,128,128]{5,4,3,2,1,0:T(8,128)(2,1)} %ops_hbm.1, bf16[3,4,128,256]{3,2,1,0:T(8,128)(2,1)} %source_hbm.1, f32[1,4,128]{2,1,0:T(4,128)} %pass_hbm.1, ...), custom_call_target="tpu_custom_call" | custom-call | bytes 4718592 | tf_op jit(solution)/shard_map/load/pallas_call | solution.py:315
  8.2 1.4 %collective-permute-done.1.refs_7_ = bf16[2,128,256]{2,1,0:T(8,128)(2,1)S(1)} collective-permute-done((bf16[2,128,256]{2,1,0:T(8,128)(2,1)S(1)}, bf16[2,128,256]{2,1,0:T(8,128)(2,1)S(1)}, u32[]{:S(2)}, u32[]{:S(2)}) %collective-permute-start.1) | collective-permute-done | bytes 131104 | tf_op jit(solution)/shard_map/ppermute | solution.py:312
  9.6 0.2 collective-permute-done.refs_6_
  9.8 0.8 %tick0.1 = (bf16[4,128,256]{2,1,0:T(8,128)(2,1)S(1)}, bf16[2,128,256]{2,1,0:T(8,128)(2,1)S(1)}, bf16[2,128,256]{2,1,0:T(8,128)(2,1)S(1)}, bf16[4,128,256]{2,1,0:...) custom-call(s32[30]{0:T(128)S(4)} %get-tuple-element.36.refs_0_, ...), custom_call_target="tpu_custom_call" | custom-call | flops 402653184 | bytes 2621440 | tf_op jit(solution)/shard_map/tick0/pallas_call | solution.py:225
  10.6 0.2 collective-permute-start.2
  10.8 2.7 %collective-permute-start.3 = (bf16[2,128,256]{2,1,0:T(8,128)(2,1)S(1)}, bf16[2,128,256]{2,1,0:T(8,128)(2,1)S(1)}, u32[]{:S(2)}, u32[]{:S(2)}) collective-permute-start(bf16[2,128,256]{2,1,0:T(8,128)(2,1)S(1)} %get-tuple-element.45), channel_id=1, source_target_pairs={{0,5},{1,4},{2,7},{3,6},{4,0},{5,10},{6,9},{7,3},{8,13},{9,12},{10... | collective-permute-start | bytes 393224 | tf_op jit(solution)/shard_map/ppermute | solution.py:372
  13.5 0.0 collective-permute-start.4
  13.5 2.1 %collective-permute-start.5 = (bf16[2,128,256]{2,1,0:T(8,128)(2,1)S(1)}, bf16[2,128,256]{2,1,0:T(8,128)(2,1)S(1)}, u32[]{:S(2)}, u32[]{:S(2)}) collective-permute-start(bf16[2,128,256]{2,1,0:T(8,128)(2,1)S(1)} %get-tuple-element.47), channel_id=1, source_target_pairs={{0,4},{4,0},{8,12},{12,8},{16,20},{20,16},{24,28},{28,24},{1,5},{5... | collective-permute-start | bytes 393224 | tf_op jit(solution)/shard_map/ppermute | solution.py:369
  15.6 0.0 collective-permute-start.6
  15.6 0.4 %collective-permute-done.3.refs_7_.refs_6_ = bf16[2,128,256]{2,1,0:T(8,128)(2,1)S(1)} collective-permute-done((bf16[2,128,256]{2,1,0:T(8,128)(2,1)S(1)}, bf16[2,128,256]{2,1,0:T(8,128)(2,1)S(1)}, u32[]{:S(2)}, u32[]{:S(2)}) %collective-permute-start.3) | collective-permute-done | bytes 131104 | tf_op jit(solution)/shard_map/ppermute | solution.py:372
  16.0 3.7 %collective-permute-done.4.refs_8_.refs_7_ = bf16[2,128,256]{2,1,0:T(8,128)(2,1)S(1)} collective-permute-done((bf16[2,128,256]{2,1,0:T(8,128)(2,1)S(1)}, bf16[2,128,256]{2,1,0:T(8,128)(2,1)S(1)}, u32[]{:S(2)}, u32[]{:S(2)}) %collective-permute-start.4) | collective-permute-done | bytes 131104 | tf_op jit(solution)/shard_map/ppermute | solution.py:373
  19.7 0.0 collective-permute-done.5.refs_5_
  19.7 0.0 collective-permute-done.6.refs_6_
  19.7 0.1 collective-permute-start.12
  19.7 0.0 collective-permute-done.2.refs_5_
  19.8 0.8 %tick1_even.1 = (bf16[4,128,256]{2,1,0:T(8,128)(2,1)S(1)}, bf16[2,128,256]{2,1,0:T(8,128)(2,1)S(1)}, bf16[2,128,256]{2,1,0:T(8,128)(2,1)S(1)}, bf16[2,128,256]{2,1,0:T(8,128)(2,1)S(1)}, bf16[2,128,256]{2,1,0:T(8,128)(2,1)S(1)}) custom-call(s32[30]{0:T(128)S(4)} %get-tuple-element.36.refs_0_, ...), custom_call_target="tpu_custom_call", output_to_operand_aliasing={{0}: (8, {}), {1}: (9, {}), {2}: (10, {})} | custom-call | flops 402653184 | bytes 2621440 | tf_op jit(solution)/shard_map/tick1_even/pallas_call | solution.py:225
  20.6 0.1 collective-permute-start.7
  20.6 0.5 %collective-permute-start.8 = (bf16[2,128,256]{2,1,0:T(8,128)(2,1)S(1)}, bf16[2,128,256]{2,1,0:T(8,128)(2,1)S(1)}, u32[]{:S(2)}, u32[]{:S(2)}) collective-permute-start(bf16[2,128,256]{2,1,0:T(8,128)(2,1)S(1)} %get-tuple-element.53), channel_id=1, source_target_pairs={{0,4},{4,0},{8,12},{12,8},{16,20},{20,16},{24,28},{28,24},{1,5},{5... | collective-permute-start | bytes 393224 | tf_op jit(solution)/shard_map/ppermute | solution.py:369
  21.1 1.7 %collective-permute-start.9 = (bf16[2,128,256]{2,1,0:T(8,128)(2,1)S(1)}, bf16[2,128,256]{2,1,0:T(8,128)(2,1)S(1)}, u32[]{:S(2)}, u32[]{:S(2)}) collective-permute-start(bf16[2,128,256]{2,1,0:T(8,128)(2,1)S(1)} %get-tuple-element.54), channel_id=1, source_target_pairs={{0,5},{1,4},{2,7},{3,6},{4,0},{5,10},{6,9},{7,3},{8,13},{9,12},{10... | collective-permute-start | bytes 393224 | tf_op jit(solution)/shard_map/ppermute | solution.py:372
  22.8 0.0 collective-permute-start.10
  22.8 0.0 collective-permute-done.7.refs_5_
  22.8 0.0 collective-permute-done.8.refs_6_
  22.8 2.8 %collective-permute-done.9.refs_7_.refs_6_ = bf16[2,128,256]{2,1,0:T(8,128)(2,1)S(1)} collective-permute-done((bf16[2,128,256]{2,1,0:T(8,128)(2,1)S(1)}, bf16[2,128,256]{2,1,0:T(8,128)(2,1)S(1)}, u32[]{:S(2)}, u32[]{:S(2)}) %collective-permute-start.9) | collective-permute-done | bytes 131104 | tf_op jit(solution)/shard_map/ppermute | solution.py:372
  25.6 3.4 %collective-permute-done.10.refs_8_.refs_7_ = bf16[2,128,256]{2,1,0:T(8,128)(2,1)S(1)} collective-permute-done((bf16[2,128,256]{2,1,0:T(8,128)(2,1)S(1)}, bf16[2,128,256]{2,1,0:T(8,128)(2,1)S(1)}, u32[]{:S(2)}, u32[]{:S(2)}) %collective-permute-start.10) | collective-permute-done | bytes 131104 | tf_op jit(solution)/shard_map/ppermute | solution.py:373
  29.0 0.0 collective-permute-start.11
  29.0 0.0 collective-permute-done.12.refs_5_
  29.0 0.8 %tick2_even.1 = (bf16[4,128,256]{2,1,0:T(8,128)(2,1)S(1)}, bf16[2,128,256]{2,1,0:T(8,128)(2,1)S(1)}, bf16[2,128,256]{2,1,0:T(8,128)(2,1)S(1)}, bf16[2,128,256]{2,1,0:T(8,128)(2,1)S(1)}, bf16[2,128,256]{2,1,0:T(8,128)(2,1)S(1)}) custom-call(s32[30]{0:T(128)S(4)} %get-tuple-element.36.refs_0_, ...), custom_call_target="tpu_custom_call", output_to_operand_aliasing={{0}: (8, {}), {1}: (9, {}), {2}: (10, {})} | custom-call | flops 402653184 | bytes 2621440 | tf_op jit(solution)/shard_map/tick2_even/pallas_call | solution.py:225
  29.8 0.6 %collective-permute-start.13 = (bf16[2,128,256]{2,1,0:T(8,128)(2,1)S(1)}, bf16[2,128,256]{2,1,0:T(8,128)(2,1)S(1)}, u32[]{:S(2)}, u32[]{:S(2)}) collective-permute-start(bf16[2,128,256]{2,1,0:T(8,128)(2,1)S(1)} %get-tuple-element.61), channel_id=1, source_target_pairs={{0,5},{1,4},{2,7},{3,6},{4,0},{5,10},{6,9},{7,3},{8,13},{9,12},{10... | collective-permute-start | bytes 393224 | tf_op jit(solution)/shard_map/ppermute | solution.py:372
  30.4 0.0 collective-permute-start.14
  30.4 2.9 %collective-permute-start.15 = (bf16[2,128,256]{2,1,0:T(8,128)(2,1)S(1)}, bf16[2,128,256]{2,1,0:T(8,128)(2,1)S(1)}, u32[]{:S(2)}, u32[]{:S(2)}) collective-permute-start(bf16[2,128,256]{2,1,0:T(8,128)(2,1)S(1)} %get-tuple-element.66), channel_id=1, source_target_pairs={{0,4},{4,0},{8,12},{12,8},{16,20},{20,16},{24,28},{28,24},{1,5},{5... | collective-permute-start | bytes 393224 | tf_op jit(solution)/shard_map/ppermute | solution.py:369
  33.3 0.0 collective-permute-start.16
  33.3 0.0 collective-permute-done.13.refs_7_.refs_6_
  33.3 4.2 %collective-permute-done.14.refs_8_.refs_7_ = bf16[2,128,256]{2,1,0:T(8,128)(2,1)S(1)} collective-permute-done((bf16[2,128,256]{2,1,0:T(8,128)(2,1)S(1)}, bf16[2,128,256]{2,1,0:T(8,128)(2,1)S(1)}, u32[]{:S(2)}, u32[]{:S(2)}) %collective-permute-start.14) | collective-permute-done | bytes 131104 | tf_op jit(solution)/shard_map/ppermute | solution.py:373
  37.5 0.0 collective-permute-done.15.refs_5_
  37.5 0.0 collective-permute-done.16.refs_6_
  37.5 0.1 last_tick_odd.1
  37.6 0.0 collective-permute-done.11.refs_5_
  37.6 1.5 %last_tick_even.1 = (bf16[4,1,4,128,256]{4,3,2,1,0:T(8,128)(2,1)}, f32[1,4,128,256]{3,2,1,0:T(8,128)}) custom-call(s32[30]{0:T(128)S(4)} %get-tuple-element.36.refs_0_, bf16[1,4,6,2,128,128]{5,4,3,2,1,0:T(8,128)(2,1)S(1)} %get-tuple-element.38.refs_1_, ...), custom_call_target="tpu_custom_call", output_to_operand_aliasing={{0}: (11, {}), {1}: (12, {})} | custom-call | flops 402653184 | bytes 2621440 | tf_op jit(solution)/shard_map/last_tick_even/pallas_call | solution.py:225
  (2 shorter events, 0.0 us)
Async XLA Ops:
  1.9 7.7 %collective-permute-start.1 = (bf16[2,128,256]{2,1,0:T(8,128)(2,1)S(1)}, bf16[2,128,256]{2,1,0:T(8,128)(2,1)S(1)}, u32[]{:S(2)}, u32[]{:S(2)}) collective-permute-start(bf16[2,128,256]{2,1,0:T(8,128)(2,1)S(1)} %get-tuple-element.43), channel_id=1, source_target_pairs={{0,8},{1,2},{2,1},{3,11},{4,5},{5,4},{6,7},{7,6},{8,16},{9,10},{10... | collective-permute-start | bytes 393224 | tf_op jit(solution)/shard_map/ppermute | solution.py:312
  4.8 5.0 %collective-permute-start = (bf16[2,128,256]{2,1,0:T(8,128)(2,1)S(1)}, bf16[2,128,256]{2,1,0:T(8,128)(2,1)S(1)}, u32[]{:S(2)}, u32[]{:S(2)}) collective-permute-start(bf16[2,128,256]{2,1,0:T(8,128)(2,1)S(1)} %get-tuple-element.37.after_ref), channel_id=1, source_target_pairs={{0,1},{1,0},{2,3},{3,2},{4,12},{5,6},{6,5},{7,15},{8,9},{9,8},{10,... | collective-permute-start | bytes 393224 | tf_op jit(solution)/shard_map/ppermute | solution.py:311
  10.6 9.2 %collective-permute-start.2 = (bf16[4,128,256]{2,1,0:T(8,128)(2,1)S(1)}, bf16[4,128,256]{2,1,0:T(8,128)(2,1)S(1)}, u32[]{:S(2)}, u32[]{:S(2)}) collective-permute-start(bf16[4,128,256]{2,1,0:T(8,128)(2,1)S(1)} %get-tuple-element.44), channel_id=1, source_target_pairs={{0,4},{4,8},{8,12},{12,16},{16,20},{20,24},{24,28},{28,0},{1,5},{5... | collective-permute-start | bytes 786440 | tf_op jit(solution)/shard_map/ppermute | solution.py:367
  10.8 5.2 %collective-permute-start.3 = (bf16[2,128,256]{2,1,0:T(8,128)(2,1)S(1)}, bf16[2,128,256]{2,1,0:T(8,128)(2,1)S(1)}, u32[]{:S(2)}, u32[]{:S(2)}) collective-permute-start(bf16[2,128,256]{2,1,0:T(8,128)(2,1)S(1)} %get-tuple-element.45), channel_id=1, source_target_pairs={{0,5},{1,4},{2,7},{3,6},{4,0},{5,10},{6,9},{7,3},{8,13},{9,12},{10... | collective-permute-start | bytes 393224 | tf_op jit(solution)/shard_map/ppermute | solution.py:372
  13.5 6.2 %collective-permute-start.4 = (bf16[2,128,256]{2,1,0:T(8,128)(2,1)S(1)}, bf16[2,128,256]{2,1,0:T(8,128)(2,1)S(1)}, u32[]{:S(2)}, u32[]{:S(2)}) collective-permute-start(bf16[2,128,256]{2,1,0:T(8,128)(2,1)S(1)} %get-tuple-element.46), channel_id=1, source_target_pairs={{0,4},{1,6},{2,5},{3,7},{4,9},{5,8},{6,11},{7,10},{8,12},{9,14},{1... | collective-permute-start | bytes 393224 | tf_op jit(solution)/shard_map/ppermute | solution.py:373
  13.5 6.2 %collective-permute-start.5 = (bf16[2,128,256]{2,1,0:T(8,128)(2,1)S(1)}, bf16[2,128,256]{2,1,0:T(8,128)(2,1)S(1)}, u32[]{:S(2)}, u32[]{:S(2)}) collective-permute-start(bf16[2,128,256]{2,1,0:T(8,128)(2,1)S(1)} %get-tuple-element.47), channel_id=1, source_target_pairs={{0,4},{4,0},{8,12},{12,8},{16,20},{20,16},{24,28},{28,24},{1,5},{5... | collective-permute-start | bytes 393224 | tf_op jit(solution)/shard_map/ppermute | solution.py:369
  15.6 4.1 %collective-permute-start.6 = (bf16[2,128,256]{2,1,0:T(8,128)(2,1)S(1)}, bf16[2,128,256]{2,1,0:T(8,128)(2,1)S(1)}, u32[]{:S(2)}, u32[]{:S(2)}) collective-permute-start(bf16[2,128,256]{2,1,0:T(8,128)(2,1)S(1)} %get-tuple-element.48), channel_id=1, source_target_pairs={{0,4},{4,0},{8,12},{12,8},{16,20},{20,16},{24,28},{28,24},{1,5},{5... | collective-permute-start | bytes 393224 | tf_op jit(solution)/shard_map/ppermute | solution.py:369
  19.7 9.3 %collective-permute-start.12 = (bf16[4,128,256]{2,1,0:T(8,128)(2,1)S(1)}, bf16[4,128,256]{2,1,0:T(8,128)(2,1)S(1)}, u32[]{:S(2)}, u32[]{:S(2)}) collective-permute-start(bf16[4,128,256]{2,1,0:T(8,128)(2,1)S(1)} %get-tuple-element.57), channel_id=1, source_target_pairs={{0,4},{4,8},{8,12},{12,16},{16,20},{20,24},{24,28},{28,0},{1,5},{5... | collective-permute-start | bytes 786440 | tf_op jit(solution)/shard_map/ppermute | solution.py:367
  20.6 2.3 %collective-permute-start.7 = (bf16[2,128,256]{2,1,0:T(8,128)(2,1)S(1)}, bf16[2,128,256]{2,1,0:T(8,128)(2,1)S(1)}, u32[]{:S(2)}, u32[]{:S(2)}) collective-permute-start(bf16[2,128,256]{2,1,0:T(8,128)(2,1)S(1)} %get-tuple-element.52), channel_id=1, source_target_pairs={{0,4},{4,0},{8,12},{12,8},{16,20},{20,16},{24,28},{28,24},{1,5},{5... | collective-permute-start | bytes 393224 | tf_op jit(solution)/shard_map/ppermute | solution.py:369
  20.6 2.2 %collective-permute-start.8 = (bf16[2,128,256]{2,1,0:T(8,128)(2,1)S(1)}, bf16[2,128,256]{2,1,0:T(8,128)(2,1)S(1)}, u32[]{:S(2)}, u32[]{:S(2)}) collective-permute-start(bf16[2,128,256]{2,1,0:T(8,128)(2,1)S(1)} %get-tuple-element.53), channel_id=1, source_target_pairs={{0,4},{4,0},{8,12},{12,8},{16,20},{20,16},{24,28},{28,24},{1,5},{5... | collective-permute-start | bytes 393224 | tf_op jit(solution)/shard_map/ppermute | solution.py:369
  21.1 4.4 %collective-permute-start.9 = (bf16[2,128,256]{2,1,0:T(8,128)(2,1)S(1)}, bf16[2,128,256]{2,1,0:T(8,128)(2,1)S(1)}, u32[]{:S(2)}, u32[]{:S(2)}) collective-permute-start(bf16[2,128,256]{2,1,0:T(8,128)(2,1)S(1)} %get-tuple-element.54), channel_id=1, source_target_pairs={{0,5},{1,4},{2,7},{3,6},{4,0},{5,10},{6,9},{7,3},{8,13},{9,12},{10... | collective-permute-start | bytes 393224 | tf_op jit(solution)/shard_map/ppermute | solution.py:372
  22.8 6.2 %collective-permute-start.10 = (bf16[2,128,256]{2,1,0:T(8,128)(2,1)S(1)}, bf16[2,128,256]{2,1,0:T(8,128)(2,1)S(1)}, u32[]{:S(2)}, u32[]{:S(2)}) collective-permute-start(bf16[2,128,256]{2,1,0:T(8,128)(2,1)S(1)} %get-tuple-element.55), channel_id=1, source_target_pairs={{0,4},{1,6},{2,5},{3,7},{4,9},{5,8},{6,11},{7,10},{8,12},{9,14},{1... | collective-permute-start | bytes 393224 | tf_op jit(solution)/shard_map/ppermute | solution.py:373
  29.0 8.6 %collective-permute-start.11 = (bf16[4,128,256]{2,1,0:T(8,128)(2,1)S(1)}, bf16[4,128,256]{2,1,0:T(8,128)(2,1)S(1)}, u32[]{:S(2)}, u32[]{:S(2)}) collective-permute-start(bf16[4,128,256]{2,1,0:T(8,128)(2,1)S(1)} %get-tuple-element.56), channel_id=1, source_target_pairs={{0,4},{4,8},{8,12},{12,16},{16,20},{20,24},{24,28},{28,0},{1,5},{5... | collective-permute-start | bytes 786440 | tf_op jit(solution)/shard_map/ppermute | solution.py:367
  29.8 3.5 %collective-permute-start.13 = (bf16[2,128,256]{2,1,0:T(8,128)(2,1)S(1)}, bf16[2,128,256]{2,1,0:T(8,128)(2,1)S(1)}, u32[]{:S(2)}, u32[]{:S(2)}) collective-permute-start(bf16[2,128,256]{2,1,0:T(8,128)(2,1)S(1)} %get-tuple-element.61), channel_id=1, source_target_pairs={{0,5},{1,4},{2,7},{3,6},{4,0},{5,10},{6,9},{7,3},{8,13},{9,12},{10... | collective-permute-start | bytes 393224 | tf_op jit(solution)/shard_map/ppermute | solution.py:372
  30.4 7.1 %collective-permute-start.14 = (bf16[2,128,256]{2,1,0:T(8,128)(2,1)S(1)}, bf16[2,128,256]{2,1,0:T(8,128)(2,1)S(1)}, u32[]{:S(2)}, u32[]{:S(2)}) collective-permute-start(bf16[2,128,256]{2,1,0:T(8,128)(2,1)S(1)} %get-tuple-element.62), channel_id=1, source_target_pairs={{0,4},{1,6},{2,5},{3,7},{4,9},{5,8},{6,11},{7,10},{8,12},{9,14},{1... | collective-permute-start | bytes 393224 | tf_op jit(solution)/shard_map/ppermute | solution.py:373
  30.4 7.1 %collective-permute-start.15 = (bf16[2,128,256]{2,1,0:T(8,128)(2,1)S(1)}, bf16[2,128,256]{2,1,0:T(8,128)(2,1)S(1)}, u32[]{:S(2)}, u32[]{:S(2)}) collective-permute-start(bf16[2,128,256]{2,1,0:T(8,128)(2,1)S(1)} %get-tuple-element.66), channel_id=1, source_target_pairs={{0,4},{4,0},{8,12},{12,8},{16,20},{20,16},{24,28},{28,24},{1,5},{5... | collective-permute-start | bytes 393224 | tf_op jit(solution)/shard_map/ppermute | solution.py:369
  33.3 4.2 %collective-permute-start.16 = (bf16[2,128,256]{2,1,0:T(8,128)(2,1)S(1)}, bf16[2,128,256]{2,1,0:T(8,128)(2,1)S(1)}, u32[]{:S(2)}, u32[]{:S(2)}) collective-permute-start(bf16[2,128,256]{2,1,0:T(8,128)(2,1)S(1)} %get-tuple-element.67), channel_id=1, source_target_pairs={{0,4},{4,0},{8,12},{12,8},{16,20},{20,16},{24,28},{28,24},{1,5},{5... | collective-permute-start | bytes 393224 | tf_op jit(solution)/shard_map/ppermute | solution.py:369

commit v7 on v3

--- a/solution.py
+++ b/solution.py
@@ -140,7 +140,7 @@
 
 
 def acts(section, parity):
-    return True if parity is None else lax.rem(section, 2) == parity
+    return lax.rem(section, 2) == parity
 
 
 def tick_kernel(
@@ -164,8 +164,6 @@
                 echo_ref[b, :, cols] = (reflect_ref[b] * part).astype(echo_ref.dtype)
         start = 0
         for onward_ref in onward_refs:
-            if start == onward.shape[0]:
-                start = 0
             onward_ref[...] = onward[start : start + onward_ref.shape[0]]
             start += onward_ref.shape[0]
 
@@ -344,13 +342,13 @@
     inside = [(s, s ^ 1) for s in range(sections)]
     routes = halo_routes(sections, tiles)
 
-    waves = {None: [wave]}
+    waves = {ODD: [wave], EVEN: [wave]}
     echoes = []
     for tick in range(ticks - 1):
         known = []
         sent = {}
-        for parity in (None,) if tick == 0 else (ODD, EVEN):
-            to_next = ([wave_type] if parity != EVEN else []) + (half_types if parity != ODD else [])
+        for parity in (ODD, EVEN):
+            to_next = [wave_type] if parity == ODD else half_types
             outs = [wave_type, list_type, list_type] + to_next
             known = grouped_call(
                 functools.partial(tick_kernel, parity, tick, sections),
@@ -361,11 +359,11 @@
                 scratch_shapes=[buffer_type, pltpu.VMEM(wave_type.shape, WAVE)],
                 compiler_params=params,
                 cost_estimate=tick_cost,
-                name=f"tick{tick}" + ("" if parity is None else "_odd" if parity else "_even"),
+                name=f"tick{tick}" + ("_odd" if parity else "_even"),
             )
-            if parity != EVEN:
+            if parity == ODD:
                 sent[EVEN] = [lax.ppermute(known[3], "depth", crossing)]
-            if parity != ODD:
+            else:
                 sent[ODD] = [lax.ppermute(a, "depth", inside) for a in known[-2:]]
         waves = sent
         echo, first, second = known[:3]

time: 38.9 us -> 38.5 us (0.990)
  the two profiles are of different devices: /device:TPU:12 before, /device:TPU:16 now
where the time goes in v7:
time: 38.5 us; the launch traced here: 38.3 us
  waiting for transfers between devices  23.9 us (62%)
  starting transfers between devices  6.98 us (18%)
  Pallas kernels  6.69 us (17%)
  between operations  0.72 us (2%)
    ppermute x4, waiting for transfers between devices, per_device(): first = lax.ppermute(first, both, routes[0])  17.6 us
    ppermute x4, waiting for transfers between devices, per_device(): second = lax.ppermute(second, both, routes[1])  4.7 us
    pallas_call x8, Pallas kernels, grouped_call(): pl.pallas_call(body, out_shape=tuple(outs), in_specs=[SMEM_SPEC] + [VMEM_...  3.8 us
    ppermute x4, starting transfers between devices, per_device(): first = lax.ppermute(first, both, routes[0])  3.49 us
    ppermute x6, starting transfers between devices, per_device(): sent[ODD] = [lax.ppermute(a, 'depth', inside) for a in known[-2:]]  2.24 us
    pallas_call x1, Pallas kernels, per_device(): pl.pallas_call(load_kernel, out_shape=(pltpu.VMEM(operators.shape, operat...  1.67 us
    pallas_call x1, Pallas kernels, per_device(): pl.pallas_call(prepare_kernel, out_shape=(pltpu.SMEM((2 * (listed + 1) +...  1.21 us
    ppermute x4, starting transfers between devices, per_device(): second = lax.ppermute(second, both, routes[1])  0.83 us
  transfers between devices with their start and end apart: 17, of which 11 were waited for; matrix products, arithmetic and copies ran while one was open for 0% of the time, Pallas kernels for 10%

profile of v7, /device:TPU:16, one launch (start us, length us, event | category | flops | bytes accessed | tf_op | source)
XLA Modules:
  0.0 38.3 jit_solution(11982522191238211308)
XLA Ops:
  0.6 1.2 %prepare.1 = (s32[30]{0:T(128)S(4)}, bf16[4,128,256]{2,1,0:T(8,128)(2,1)S(1)}, bf16[2,128,256]{2,1,0:T(8,128)(2,1)S(1)}, bf16[2,128,256]{2,1,0:T(8,128)(2,1)S(1)}) custom-call(s32[1,2,2]{2,1,0:T(2,128)} %ids_hbm.1, s32[1,2]{1,0:T(1,128)} %count_hbm.1, s32[4,6]{1,0:T(4,128)} %pattern_hbm.1, f32[1,4,128,256]{3,2,1,0:T(8,128)} %inflow_hbm.1), custom_call_target="tpu_custom_call" | custom-call | flops 131072 | bytes 1048576 | tf_op jit(solution)/shard_map/prepare/pallas_call | solution.py:283
  1.8 0.5 %collective-permute-start.1 = (bf16[2,128,256]{2,1,0:T(8,128)(2,1)S(1)}, bf16[2,128,256]{2,1,0:T(8,128)(2,1)S(1)}, u32[]{:S(2)}, u32[]{:S(2)}) collective-permute-start(bf16[2,128,256]{2,1,0:T(8,128)(2,1)S(1)} %get-tuple-element.46), channel_id=1, source_target_pairs={{0,4},{1,2},{2,1},{3,7},{4,0},{5,6},{6,5},{7,3},{8,12},{9,10},{10,... | collective-permute-start | bytes 393224 | tf_op jit(solution)/shard_map/ppermute | solution.py:310
  2.4 1.2 %collective-permute-start = (bf16[2,128,256]{2,1,0:T(8,128)(2,1)S(1)}, bf16[2,128,256]{2,1,0:T(8,128)(2,1)S(1)}, u32[]{:S(2)}, u32[]{:S(2)}) collective-permute-start(bf16[2,128,256]{2,1,0:T(8,128)(2,1)S(1)} %get-tuple-element.40.after_ref), channel_id=1, source_target_pairs={{0,1},{1,0},{2,3},{3,2},{4,5},{5,4},{6,7},{7,6},{8,9},{9,8},{10,11... | collective-permute-start | bytes 393224 | tf_op jit(solution)/shard_map/ppermute | solution.py:309
  3.6 1.7 %load.1 = (bf16[1,4,6,2,128,128]{5,4,3,2,1,0:T(8,128)(2,1)S(1)}, bf16[3,4,128,256]{3,2,1,0:T(8,128)(2,1)S(1)}, f32[4,128,128]{2,1,0:T(8,128)S(1)}, f32[4,128,128]{2,1,0:T(8,128)S(1)}) custom-call(bf16[1,4,6,2,128,128]{5,4,3,2,1,0:T(8,128)(2,1)} %ops_hbm.1, bf16[3,4,128,256]{3,2,1,0:T(8,128)(2,1)} %source_hbm.1, f32[1,4,128]{2,1,0:T(4,128)} %pass_hbm.1, ...), custom_call_target="tpu_custom_call" | custom-call | bytes 4718592 | tf_op jit(solution)/shard_map/load/pallas_call | solution.py:313
  5.3 1.9 %collective-permute-done.1.refs_7_ = bf16[2,128,256]{2,1,0:T(8,128)(2,1)S(1)} collective-permute-done((bf16[2,128,256]{2,1,0:T(8,128)(2,1)S(1)}, bf16[2,128,256]{2,1,0:T(8,128)(2,1)S(1)}, u32[]{:S(2)}, u32[]{:S(2)}) %collective-permute-start.1) | collective-permute-done | bytes 131104 | tf_op jit(solution)/shard_map/ppermute | solution.py:310
  7.2 0.5 %collective-permute-done.refs_6_ = bf16[2,128,256]{2,1,0:T(8,128)(2,1)S(1)} collective-permute-done((bf16[2,128,256]{2,1,0:T(8,128)(2,1)S(1)}, bf16[2,128,256]{2,1,0:T(8,128)(2,1)S(1)}, u32[]{:S(2)}, u32[]{:S(2)}) %collective-permute-start) | collective-permute-done | bytes 131104 | tf_op jit(solution)/shard_map/ppermute | solution.py:309
  7.7 0.0 collective-permute-start.2
  7.7 0.7 %tick0_even.1 = (bf16[4,128,256]{2,1,0:T(8,128)(2,1)S(1)}, bf16[2,128,256]{2,1,0:T(8,128)(2,1)S(1)}, bf16[2,128,256]{2,1,0:T(8,128)(2,1)S(1)}, bf16[2,128,256]{2,1,0:T(8,128)(2,1)S(1)}, bf16[2,128,256]{2,1,0:T(8,128)(2,1)S(1)}) custom-call(s32[30]{0:T(128)S(4)} %get-tuple-element.39.refs_0_, ...), custom_call_target="tpu_custom_call", output_to_operand_aliasing={{0}: (8, {}), {1}: (9, {}), {2}: (10, {})} | custom-call | flops 402653184 | bytes 2621440 | tf_op jit(solution)/shard_map/tick0_even/pallas_call | solution.py:223
  8.4 2.2 %collective-permute-start.3 = (bf16[2,128,256]{2,1,0:T(8,128)(2,1)S(1)}, bf16[2,128,256]{2,1,0:T(8,128)(2,1)S(1)}, u32[]{:S(2)}, u32[]{:S(2)}) collective-permute-start(bf16[2,128,256]{2,1,0:T(8,128)(2,1)S(1)} %get-tuple-element.51), channel_id=1, source_target_pairs={{0,5},{1,4},{2,7},{3,6},{4,9},{5,8},{6,11},{7,10},{8,13},{9,12},{1... | collective-permute-start | bytes 393224 | tf_op jit(solution)/shard_map/ppermute | solution.py:370
  10.6 0.0 collective-permute-start.4
  10.6 1.1 %collective-permute-start.5 = (bf16[2,128,256]{2,1,0:T(8,128)(2,1)S(1)}, bf16[2,128,256]{2,1,0:T(8,128)(2,1)S(1)}, u32[]{:S(2)}, u32[]{:S(2)}) collective-permute-start(bf16[2,128,256]{2,1,0:T(8,128)(2,1)S(1)} %get-tuple-element.53), channel_id=1, source_target_pairs={{0,4},{4,0},{8,12},{12,8},{16,20},{20,16},{24,28},{28,24},{1,5},{5... | collective-permute-start | bytes 393224 | tf_op jit(solution)/shard_map/ppermute | solution.py:367
  11.7 0.0 collective-permute-start.6
  11.7 3.5 %collective-permute-done.3.refs_7_.refs_6_ = bf16[2,128,256]{2,1,0:T(8,128)(2,1)S(1)} collective-permute-done((bf16[2,128,256]{2,1,0:T(8,128)(2,1)S(1)}, bf16[2,128,256]{2,1,0:T(8,128)(2,1)S(1)}, u32[]{:S(2)}, u32[]{:S(2)}) %collective-permute-start.3) | collective-permute-done | bytes 131104 | tf_op jit(solution)/shard_map/ppermute | solution.py:370
  15.2 2.7 %collective-permute-done.4.refs_8_.refs_7_ = bf16[2,128,256]{2,1,0:T(8,128)(2,1)S(1)} collective-permute-done((bf16[2,128,256]{2,1,0:T(8,128)(2,1)S(1)}, bf16[2,128,256]{2,1,0:T(8,128)(2,1)S(1)}, u32[]{:S(2)}, u32[]{:S(2)}) %collective-permute-start.4) | collective-permute-done | bytes 131104 | tf_op jit(solution)/shard_map/ppermute | solution.py:371
  17.9 0.0 collective-permute-done.5.refs_5_
  17.9 0.0 collective-permute-done.6.refs_6_
  17.9 0.4 %collective-permute-start.12 = (bf16[4,128,256]{2,1,0:T(8,128)(2,1)S(1)}, bf16[4,128,256]{2,1,0:T(8,128)(2,1)S(1)}, u32[]{:S(2)}, u32[]{:S(2)}) collective-permute-start(bf16[4,128,256]{2,1,0:T(8,128)(2,1)S(1)} %get-tuple-element.63), channel_id=1, source_target_pairs={{0,4},{4,8},{8,12},{12,16},{16,20},{20,24},{24,28},{28,0},{1,5},{5... | collective-permute-start | bytes 786440 | tf_op jit(solution)/shard_map/ppermute | solution.py:365
  18.3 0.0 collective-permute-done.2.refs_5_
  18.3 0.7 %tick1_even.1 = (bf16[4,128,256]{2,1,0:T(8,128)(2,1)S(1)}, bf16[2,128,256]{2,1,0:T(8,128)(2,1)S(1)}, bf16[2,128,256]{2,1,0:T(8,128)(2,1)S(1)}, bf16[2,128,256]{2,1,0:T(8,128)(2,1)S(1)}, bf16[2,128,256]{2,1,0:T(8,128)(2,1)S(1)}) custom-call(s32[30]{0:T(128)S(4)} %get-tuple-element.39.refs_0_, ...), custom_call_target="tpu_custom_call", output_to_operand_aliasing={{0}: (8, {}), {1}: (9, {}), {2}: (10, {})} | custom-call | flops 402653184 | bytes 2621440 | tf_op jit(solution)/shard_map/tick1_even/pallas_call | solution.py:223
  19.0 0.1 collective-permute-start.7
  19.1 0.5 %collective-permute-start.8 = (bf16[2,128,256]{2,1,0:T(8,128)(2,1)S(1)}, bf16[2,128,256]{2,1,0:T(8,128)(2,1)S(1)}, u32[]{:S(2)}, u32[]{:S(2)}) collective-permute-start(bf16[2,128,256]{2,1,0:T(8,128)(2,1)S(1)} %get-tuple-element.59), channel_id=1, source_target_pairs={{0,4},{4,0},{8,12},{12,8},{16,20},{20,16},{24,28},{28,24},{1,5},{5... | collective-permute-start | bytes 393224 | tf_op jit(solution)/shard_map/ppermute | solution.py:367
  19.6 0.0 collective-permute-start.9
  19.6 0.3 collective-permute-start.10
  19.9 0.6 %collective-permute-done.7.refs_5_ = bf16[2,128,256]{2,1,0:T(8,128)(2,1)S(1)} collective-permute-done((bf16[2,128,256]{2,1,0:T(8,128)(2,1)S(1)}, bf16[2,128,256]{2,1,0:T(8,128)(2,1)S(1)}, u32[]{:S(2)}, u32[]{:S(2)}) %collective-permute-start.7) | collective-permute-done | bytes 131104 | tf_op jit(solution)/shard_map/ppermute | solution.py:367
  20.5 0.2 collective-permute-done.8.refs_6_
  20.6 6.5 %collective-permute-done.9.refs_7_.refs_6_ = bf16[2,128,256]{2,1,0:T(8,128)(2,1)S(1)} collective-permute-done((bf16[2,128,256]{2,1,0:T(8,128)(2,1)S(1)}, bf16[2,128,256]{2,1,0:T(8,128)(2,1)S(1)}, u32[]{:S(2)}, u32[]{:S(2)}) %collective-permute-start.9) | collective-permute-done | bytes 131104 | tf_op jit(solution)/shard_map/ppermute | solution.py:370
  27.2 0.1 collective-permute-done.10.refs_8_.refs_7_
  27.3 0.0 collective-permute-start.11
  27.3 0.1 collective-permute-done.12.refs_5_
  27.4 0.7 %tick2_even.1 = (bf16[4,128,256]{2,1,0:T(8,128)(2,1)S(1)}, bf16[2,128,256]{2,1,0:T(8,128)(2,1)S(1)}, bf16[2,128,256]{2,1,0:T(8,128)(2,1)S(1)}, bf16[2,128,256]{2,1,0:T(8,128)(2,1)S(1)}, bf16[2,128,256]{2,1,0:T(8,128)(2,1)S(1)}) custom-call(s32[30]{0:T(128)S(4)} %get-tuple-element.39.refs_0_, ...), custom_call_target="tpu_custom_call", output_to_operand_aliasing={{0}: (8, {}), {1}: (9, {}), {2}: (10, {})} | custom-call | flops 402653184 | bytes 2621440 | tf_op jit(solution)/shard_map/tick2_even/pallas_call | solution.py:223
  28.2 0.1 collective-permute-start.13
  28.3 0.1 collective-permute-start.14
  28.3 0.4 %collective-permute-start.15 = (bf16[2,128,256]{2,1,0:T(8,128)(2,1)S(1)}, bf16[2,128,256]{2,1,0:T(8,128)(2,1)S(1)}, u32[]{:S(2)}, u32[]{:S(2)}) collective-permute-start(bf16[2,128,256]{2,1,0:T(8,128)(2,1)S(1)} %get-tuple-element.72), channel_id=1, source_target_pairs={{0,4},{4,0},{8,12},{12,8},{16,20},{20,16},{24,28},{28,24},{1,5},{5... | collective-permute-start | bytes 393224 | tf_op jit(solution)/shard_map/ppermute | solution.py:367
  28.8 0.2 collective-permute-start.16
  28.9 7.1 %collective-permute-done.13.refs_7_.refs_6_ = bf16[2,128,256]{2,1,0:T(8,128)(2,1)S(1)} collective-permute-done((bf16[2,128,256]{2,1,0:T(8,128)(2,1)S(1)}, bf16[2,128,256]{2,1,0:T(8,128)(2,1)S(1)}, u32[]{:S(2)}, u32[]{:S(2)}) %collective-permute-start.13) | collective-permute-done | bytes 131104 | tf_op jit(solution)/shard_map/ppermute | solution.py:370
  36.0 0.0 collective-permute-done.14.refs_8_.refs_7_
  36.0 0.0 collective-permute-done.15.refs_5_
  36.0 0.0 collective-permute-done.16.refs_6_
  36.0 0.1 last_tick_odd.1
  36.1 0.7 %collective-permute-done.11.refs_5_ = bf16[4,128,256]{2,1,0:T(8,128)(2,1)S(1)} collective-permute-done((bf16[4,128,256]{2,1,0:T(8,128)(2,1)S(1)}, bf16[4,128,256]{2,1,0:T(8,128)(2,1)S(1)}, u32[]{:S(2)}, u32[]{:S(2)}) %collective-permute-start.11) | collective-permute-done | bytes 262176 | tf_op jit(solution)/shard_map/ppermute | solution.py:365
  36.8 1.5 %last_tick_even.1 = (bf16[4,1,4,128,256]{4,3,2,1,0:T(8,128)(2,1)}, f32[1,4,128,256]{3,2,1,0:T(8,128)}) custom-call(s32[30]{0:T(128)S(4)} %get-tuple-element.39.refs_0_, bf16[1,4,6,2,128,128]{5,4,3,2,1,0:T(8,128)(2,1)S(1)} %get-tuple-element.41.refs_1_, ...), custom_call_target="tpu_custom_call", output_to_operand_aliasing={{0}: (11, {}), {1}: (12, {})} | custom-call | flops 402653184 | bytes 2621440 | tf_op jit(solution)/shard_map/last_tick_even/pallas_call | solution.py:223
  (3 shorter events, 0.0 us)
Async XLA Ops:
  1.8 5.3 %collective-permute-start.1 = (bf16[2,128,256]{2,1,0:T(8,128)(2,1)S(1)}, bf16[2,128,256]{2,1,0:T(8,128)(2,1)S(1)}, u32[]{:S(2)}, u32[]{:S(2)}) collective-permute-start(bf16[2,128,256]{2,1,0:T(8,128)(2,1)S(1)} %get-tuple-element.46), channel_id=1, source_target_pairs={{0,4},{1,2},{2,1},{3,7},{4,0},{5,6},{6,5},{7,3},{8,12},{9,10},{10,... | collective-permute-start | bytes 393224 | tf_op jit(solution)/shard_map/ppermute | solution.py:310
  2.4 5.3 %collective-permute-start = (bf16[2,128,256]{2,1,0:T(8,128)(2,1)S(1)}, bf16[2,128,256]{2,1,0:T(8,128)(2,1)S(1)}, u32[]{:S(2)}, u32[]{:S(2)}) collective-permute-start(bf16[2,128,256]{2,1,0:T(8,128)(2,1)S(1)} %get-tuple-element.40.after_ref), channel_id=1, source_target_pairs={{0,1},{1,0},{2,3},{3,2},{4,5},{5,4},{6,7},{7,6},{8,9},{9,8},{10,11... | collective-permute-start | bytes 393224 | tf_op jit(solution)/shard_map/ppermute | solution.py:309
  7.7 10.6 %collective-permute-start.2 = (bf16[4,128,256]{2,1,0:T(8,128)(2,1)S(1)}, bf16[4,128,256]{2,1,0:T(8,128)(2,1)S(1)}, u32[]{:S(2)}, u32[]{:S(2)}) collective-permute-start(bf16[4,128,256]{2,1,0:T(8,128)(2,1)S(1)} %get-tuple-element.47), channel_id=1, source_target_pairs={{0,4},{4,8},{8,12},{12,16},{16,20},{20,24},{24,28},{28,0},{1,5},{5... | collective-permute-start | bytes 786440 | tf_op jit(solution)/shard_map/ppermute | solution.py:365
  8.4 6.8 %collective-permute-start.3 = (bf16[2,128,256]{2,1,0:T(8,128)(2,1)S(1)}, bf16[2,128,256]{2,1,0:T(8,128)(2,1)S(1)}, u32[]{:S(2)}, u32[]{:S(2)}) collective-permute-start(bf16[2,128,256]{2,1,0:T(8,128)(2,1)S(1)} %get-tuple-element.51), channel_id=1, source_target_pairs={{0,5},{1,4},{2,7},{3,6},{4,9},{5,8},{6,11},{7,10},{8,13},{9,12},{1... | collective-permute-start | bytes 393224 | tf_op jit(solution)/shard_map/ppermute | solution.py:370
  10.6 7.2 %collective-permute-start.4 = (bf16[2,128,256]{2,1,0:T(8,128)(2,1)S(1)}, bf16[2,128,256]{2,1,0:T(8,128)(2,1)S(1)}, u32[]{:S(2)}, u32[]{:S(2)}) collective-permute-start(bf16[2,128,256]{2,1,0:T(8,128)(2,1)S(1)} %get-tuple-element.52), channel_id=1, source_target_pairs={{0,4},{1,6},{2,5},{3,7},{4,0},{5,10},{6,9},{7,3},{8,12},{9,14},{10... | collective-permute-start | bytes 393224 | tf_op jit(solution)/shard_map/ppermute | solution.py:371
  10.6 7.2 %collective-permute-start.5 = (bf16[2,128,256]{2,1,0:T(8,128)(2,1)S(1)}, bf16[2,128,256]{2,1,0:T(8,128)(2,1)S(1)}, u32[]{:S(2)}, u32[]{:S(2)}) collective-permute-start(bf16[2,128,256]{2,1,0:T(8,128)(2,1)S(1)} %get-tuple-element.53), channel_id=1, source_target_pairs={{0,4},{4,0},{8,12},{12,8},{16,20},{20,16},{24,28},{28,24},{1,5},{5... | collective-permute-start | bytes 393224 | tf_op jit(solution)/shard_map/ppermute | solution.py:367
  11.7 6.2 %collective-permute-start.6 = (bf16[2,128,256]{2,1,0:T(8,128)(2,1)S(1)}, bf16[2,128,256]{2,1,0:T(8,128)(2,1)S(1)}, u32[]{:S(2)}, u32[]{:S(2)}) collective-permute-start(bf16[2,128,256]{2,1,0:T(8,128)(2,1)S(1)} %get-tuple-element.54), channel_id=1, source_target_pairs={{0,4},{4,0},{8,12},{12,8},{16,20},{20,16},{24,28},{28,24},{1,5},{5... | collective-permute-start | bytes 393224 | tf_op jit(solution)/shard_map/ppermute | solution.py:367
  17.9 9.6 %collective-permute-start.12 = (bf16[4,128,256]{2,1,0:T(8,128)(2,1)S(1)}, bf16[4,128,256]{2,1,0:T(8,128)(2,1)S(1)}, u32[]{:S(2)}, u32[]{:S(2)}) collective-permute-start(bf16[4,128,256]{2,1,0:T(8,128)(2,1)S(1)} %get-tuple-element.63), channel_id=1, source_target_pairs={{0,4},{4,8},{8,12},{12,16},{16,20},{20,24},{24,28},{28,0},{1,5},{5... | collective-permute-start | bytes 786440 | tf_op jit(solution)/shard_map/ppermute | solution.py:365
  19.0 1.4 %collective-permute-start.7 = (bf16[2,128,256]{2,1,0:T(8,128)(2,1)S(1)}, bf16[2,128,256]{2,1,0:T(8,128)(2,1)S(1)}, u32[]{:S(2)}, u32[]{:S(2)}) collective-permute-start(bf16[2,128,256]{2,1,0:T(8,128)(2,1)S(1)} %get-tuple-element.58), channel_id=1, source_target_pairs={{0,4},{4,0},{8,12},{12,8},{16,20},{20,16},{24,28},{28,24},{1,5},{5... | collective-permute-start | bytes 393224 | tf_op jit(solution)/shard_map/ppermute | solution.py:367
  19.1 1.5 %collective-permute-start.8 = (bf16[2,128,256]{2,1,0:T(8,128)(2,1)S(1)}, bf16[2,128,256]{2,1,0:T(8,128)(2,1)S(1)}, u32[]{:S(2)}, u32[]{:S(2)}) collective-permute-start(bf16[2,128,256]{2,1,0:T(8,128)(2,1)S(1)} %get-tuple-element.59), channel_id=1, source_target_pairs={{0,4},{4,0},{8,12},{12,8},{16,20},{20,16},{24,28},{28,24},{1,5},{5... | collective-permute-start | bytes 393224 | tf_op jit(solution)/shard_map/ppermute | solution.py:367
  19.6 7.6 %collective-permute-start.9 = (bf16[2,128,256]{2,1,0:T(8,128)(2,1)S(1)}, bf16[2,128,256]{2,1,0:T(8,128)(2,1)S(1)}, u32[]{:S(2)}, u32[]{:S(2)}) collective-permute-start(bf16[2,128,256]{2,1,0:T(8,128)(2,1)S(1)} %get-tuple-element.60), channel_id=1, source_target_pairs={{0,5},{1,4},{2,7},{3,6},{4,9},{5,8},{6,11},{7,10},{8,13},{9,12},{1... | collective-permute-start | bytes 393224 | tf_op jit(solution)/shard_map/ppermute | solution.py:370
  19.6 7.7 %collective-permute-start.10 = (bf16[2,128,256]{2,1,0:T(8,128)(2,1)S(1)}, bf16[2,128,256]{2,1,0:T(8,128)(2,1)S(1)}, u32[]{:S(2)}, u32[]{:S(2)}) collective-permute-start(bf16[2,128,256]{2,1,0:T(8,128)(2,1)S(1)} %get-tuple-element.61), channel_id=1, source_target_pairs={{0,4},{1,6},{2,5},{3,7},{4,0},{5,10},{6,9},{7,3},{8,12},{9,14},{10... | collective-permute-start | bytes 393224 | tf_op jit(solution)/shard_map/ppermute | solution.py:371
  27.3 9.5 %collective-permute-start.11 = (bf16[4,128,256]{2,1,0:T(8,128)(2,1)S(1)}, bf16[4,128,256]{2,1,0:T(8,128)(2,1)S(1)}, u32[]{:S(2)}, u32[]{:S(2)}) collective-permute-start(bf16[4,128,256]{2,1,0:T(8,128)(2,1)S(1)} %get-tuple-element.62), channel_id=1, source_target_pairs={{0,4},{4,8},{8,12},{12,16},{16,20},{20,24},{24,28},{28,0},{1,5},{5... | collective-permute-start | bytes 786440 | tf_op jit(solution)/shard_map/ppermute | solution.py:365
  28.2 7.8 %collective-permute-start.13 = (bf16[2,128,256]{2,1,0:T(8,128)(2,1)S(1)}, bf16[2,128,256]{2,1,0:T(8,128)(2,1)S(1)}, u32[]{:S(2)}, u32[]{:S(2)}) collective-permute-start(bf16[2,128,256]{2,1,0:T(8,128)(2,1)S(1)} %get-tuple-element.67), channel_id=1, source_target_pairs={{0,5},{1,4},{2,7},{3,6},{4,9},{5,8},{6,11},{7,10},{8,13},{9,12},{1... | collective-permute-start | bytes 393224 | tf_op jit(solution)/shard_map/ppermute | solution.py:370
  28.3 7.7 %collective-permute-start.14 = (bf16[2,128,256]{2,1,0:T(8,128)(2,1)S(1)}, bf16[2,128,256]{2,1,0:T(8,128)(2,1)S(1)}, u32[]{:S(2)}, u32[]{:S(2)}) collective-permute-start(bf16[2,128,256]{2,1,0:T(8,128)(2,1)S(1)} %get-tuple-element.68), channel_id=1, source_target_pairs={{0,4},{1,6},{2,5},{3,7},{4,0},{5,10},{6,9},{7,3},{8,12},{9,14},{10... | collective-permute-start | bytes 393224 | tf_op jit(solution)/shard_map/ppermute | solution.py:371
  28.3 7.7 %collective-permute-start.15 = (bf16[2,128,256]{2,1,0:T(8,128)(2,1)S(1)}, bf16[2,128,256]{2,1,0:T(8,128)(2,1)S(1)}, u32[]{:S(2)}, u32[]{:S(2)}) collective-permute-start(bf16[2,128,256]{2,1,0:T(8,128)(2,1)S(1)} %get-tuple-element.72), channel_id=1, source_target_pairs={{0,4},{4,0},{8,12},{12,8},{16,20},{20,16},{24,28},{28,24},{1,5},{5... | collective-permute-start | bytes 393224 | tf_op jit(solution)/shard_map/ppermute | solution.py:367
  28.8 7.2 %collective-permute-start.16 = (bf16[2,128,256]{2,1,0:T(8,128)(2,1)S(1)}, bf16[2,128,256]{2,1,0:T(8,128)(2,1)S(1)}, u32[]{:S(2)}, u32[]{:S(2)}) collective-permute-start(bf16[2,128,256]{2,1,0:T(8,128)(2,1)S(1)} %get-tuple-element.73), channel_id=1, source_target_pairs={{0,4},{4,0},{8,12},{12,8},{16,20},{20,16},{24,28},{28,24},{1,5},{5... | collective-permute-start | bytes 393224 | tf_op jit(solution)/shard_map/ppermute | solution.py:367

commit v8 on v7

--- a/solution.py
+++ b/solution.py
@@ -25,6 +25,7 @@
 
 def write_lists(tile, plan_ref, blocks_ref, lists):
     listed = lists[0].shape[0]
+    points = blocks_ref.shape[1]
     parity = lax.rem(tile, 2)
     for list_ref, side in zip(lists, (UPPER - parity, parity)):
         count = plan_ref[2 * listed + side]
@@ -33,11 +34,11 @@
 
             @pl.when(live)
             def _():
-                list_ref[slot] = blocks_ref[plan_ref[side * listed + slot]]
+                list_ref[slot, :points] = blocks_ref[plan_ref[side * listed + slot]]
 
             @pl.when(jnp.logical_not(live))
             def _():
-                list_ref[slot] = jnp.zeros(list_ref.shape[1:], list_ref.dtype)
+                list_ref[slot, :points] = jnp.zeros(blocks_ref.shape[1:], list_ref.dtype)
 
 
 def prepare_kernel(
@@ -104,10 +105,8 @@
     blocks, listed = source_ref.shape[1], first_ref.shape[0]
 
     def fill_wave():
-        start = 0
         for wave_ref in wave_refs:
-            buffer[start : start + wave_ref.shape[0]] = wave_ref[...]
-            start += wave_ref.shape[0]
+            buffer[:blocks] = wave_ref[...] if len(wave_ref.shape) == 3 else wave_ref[0]
 
     if tick == 0:
         fill_wave()
@@ -119,8 +118,9 @@
             buffer[:blocks] = source_ref[tick - 1]
 
     parity = lax.rem(lax.axis_index("lat"), 2)
-    buffer[pl.ds(blocks + (1 - parity) * listed, listed)] = first_ref[...]
-    buffer[pl.ds(blocks + parity * listed, listed)] = second_ref[...]
+    points = buffer.shape[1]
+    buffer[pl.ds(blocks + (1 - parity) * listed, listed)] = first_ref[:, :points]
+    buffer[pl.ds(blocks + parity * listed, listed)] = second_ref[:, :points]
 
 
 def extrapolate_block(plan_ref, pattern_start, ops_ref, buffer, b):
@@ -162,10 +162,9 @@
                 cols = pl.ds(i * part.shape[1], part.shape[1])
                 onward[b, :, cols] = (pass_ref[b] * part).astype(onward.dtype)
                 echo_ref[b, :, cols] = (reflect_ref[b] * part).astype(echo_ref.dtype)
-        start = 0
         for onward_ref in onward_refs:
-            onward_ref[...] = onward[start : start + onward_ref.shape[0]]
-            start += onward_ref.shape[0]
+            slot = onward_ref if len(onward_ref.shape) == 3 else onward_ref.at[1]
+            slot[...] = onward[...]
 
         @pl.when(section != sections - 1)
         def _():
@@ -248,14 +247,15 @@
     return routes
 
 
-def halo_routes(sections, tiles):
+def halo_routes(sections, tiles, parity):
     routes = []
     for turn in (0, 1):
         route = []
         for s in range(sections):
             for j in range(tiles):
                 to = neighbour(j, turn, tiles)
-                end = (s ^ 1) * tiles + j if to is None else (s + 1) % sections * tiles + to
+                real = to is not None and s % 2 == parity
+                end = (s + 1) % sections * tiles + to if real else (s ^ 1) * tiles + j
                 route.append((s * tiles + j, end))
         routes.append(route)
     return routes
@@ -273,8 +273,8 @@
     list_type = pltpu.VMEM((listed, points, columns), WAVE)
     params = pltpu.CompilerParams(vmem_limit_bytes=VMEM_LIMIT)
     tick_cost = pl.CostEstimate(
-        flops=blocks * taken * 4 * points * points * columns,
-        bytes_accessed=2 * operators.size + 8 * blocks * points * columns,
+        flops=0,
+        bytes_accessed=0,
         transcendentals=0,
     )
     both = ("depth", "lat")
@@ -336,40 +336,43 @@
     buffer_type = pltpu.VMEM((blocks + 2 * listed, points, columns), WAVE)
 
     ODD, EVEN = 1, 0
-    halves = [blocks // 2, blocks - blocks // 2]
-    half_types = [pltpu.VMEM((n, points, columns), WAVE) for n in halves]
     crossing = [(s, (s + 1) % sections) for s in range(sections)]
-    inside = [(s, s ^ 1) for s in range(sections)]
-    routes = halo_routes(sections, tiles)
-
-    waves = {ODD: [wave], EVEN: [wave]}
+    pairs = [[s, s + 1] for s in range(0, sections, 2)]
+    far_list_type = pltpu.VMEM((listed, points + 16, columns), WAVE)
+    pair_type = pltpu.VMEM((2, blocks, points, columns), WAVE)
+    routes = {parity: halo_routes(sections, tiles, parity) for parity in (ODD, EVEN)}
+
+    arrived = {parity: ([wave], first, second) for parity in (ODD, EVEN)}
     echoes = []
     for tick in range(ticks - 1):
-        known = []
+        echo = []
         sent = {}
         for parity in (ODD, EVEN):
-            to_next = [wave_type] if parity == ODD else half_types
-            outs = [wave_type, list_type, list_type] + to_next
-            known = grouped_call(
+            kind = list_type if parity == EVEN else far_list_type
+            outs = [wave_type, kind, kind, wave_type if parity == ODD else pair_type]
+            echo, first, second, onward = grouped_call(
                 functools.partial(tick_kernel, parity, tick, sections),
-                [*fixed, waves[parity], first, second],
+                [*fixed, *arrived[parity]],
                 outs,
                 [VMEM_SPEC] * len(outs),
-                known[:3] and [in_vmem(a) for a in known[:3]],
+                [in_vmem(a) for a in echo],
                 scratch_shapes=[buffer_type, pltpu.VMEM(wave_type.shape, WAVE)],
                 compiler_params=params,
                 cost_estimate=tick_cost,
                 name=f"tick{tick}" + ("_odd" if parity else "_even"),
             )
+            echo = [echo]
             if parity == ODD:
-                sent[EVEN] = [lax.ppermute(known[3], "depth", crossing)]
+                onward = lax.ppermute(onward, "depth", crossing)
             else:
-                sent[ODD] = [lax.ppermute(a, "depth", inside) for a in known[-2:]]
-        waves = sent
-        echo, first, second = known[:3]
-        first = lax.ppermute(first, both, routes[0])
-        second = lax.ppermute(second, both, routes[1])
-        echoes.append(echo)
+                onward = lax.all_to_all(onward, "depth", 0, 0, axis_index_groups=pairs)
+            sent[1 - parity] = (
+                [onward],
+                lax.ppermute(first, both, routes[parity][0]),
+                lax.ppermute(second, both, routes[parity][1]),
+            )
+        arrived = sent
+        echoes += echo
 
     tick = ticks - 1
     results = []
@@ -380,7 +383,7 @@
     for parity in (ODD, EVEN):
         results = grouped_call(
             functools.partial(last_kernel, parity, tick),
-            [*fixed, waves[parity], first, second, echoes],
+            [*fixed, *arrived[parity], echoes],
             result_types,
             [ANY_SPEC] * 2,
             list(results),

time: 38.5 us -> 38.6 us (level)
  the two profiles are of different devices: /device:TPU:16 before, /device:TPU:0 now
where the time goes in v8:
time: 38.6 us; the launch traced here: 38.3 us
  starting transfers between devices  16.8 us (44%)
  blocking collectives  12.4 us (32%)
  Pallas kernels  6.72 us (17%)
  waiting for transfers between devices  1.57 us (4%)
  between operations  0.73 us (2%)
    all_to_all x3, blocking collectives, per_device(): onward = lax.all_to_all(onward, 'depth', 0, 0, axis_index_groups=pairs)  12.4 us
    ppermute x6, starting transfers between devices, per_device(): lax.ppermute(first, both, routes[parity][0])  6.08 us
    ppermute x6, starting transfers between devices, per_device(): lax.ppermute(second, both, routes[parity][1])  4.21 us
    ppermute x1, starting transfers between devices, per_device(): first = lax.ppermute(first, both, routes[0])  4.15 us
    pallas_call x8, Pallas kernels, grouped_call(): pl.pallas_call(body, out_shape=tuple(outs), in_specs=[SMEM_SPEC] + [VMEM_...  3.84 us
    ppermute x3, starting transfers between devices, per_device(): onward = lax.ppermute(onward, 'depth', crossing)  1.88 us
    pallas_call x1, Pallas kernels, per_device(): pl.pallas_call(load_kernel, out_shape=(pltpu.VMEM(operators.shape, operat...  1.67 us
    ppermute x1, waiting for transfers between devices, per_device(): first = lax.ppermute(first, both, routes[0])  1.52 us
  transfers between devices with their start and end apart: 17, of which 1 were waited for; matrix products, arithmetic and copies ran while one was open for 0% of the time, Pallas kernels for 10%

profile of v8, /device:TPU:0, one launch (start us, length us, event | category | flops | bytes accessed | tf_op | source)
XLA Modules:
  0.0 38.3 jit_solution(2387527259316210022)
XLA Ops:
  0.6 1.2 %prepare.1 = (s32[30]{0:T(128)S(4)}, bf16[4,128,256]{2,1,0:T(8,128)(2,1)S(1)}, bf16[2,128,256]{2,1,0:T(8,128)(2,1)S(1)}, bf16[2,128,256]{2,1,0:T(8,128)(2,1)S(1)}) custom-call(s32[1,2,2]{2,1,0:T(2,128)} %ids_hbm.1, s32[1,2]{1,0:T(1,128)} %count_hbm.1, s32[4,6]{1,0:T(4,128)} %pattern_hbm.1, f32[1,4,128,256]{3,2,1,0:T(8,128)} %inflow_hbm.1), custom_call_target="tpu_custom_call" | custom-call | flops 131072 | bytes 1048576 | tf_op jit(solution)/shard_map/prepare/pallas_call | solution.py:283
  1.8 0.5 %collective-permute-start.1 = (bf16[2,128,256]{2,1,0:T(8,128)(2,1)S(1)}, bf16[2,128,256]{2,1,0:T(8,128)(2,1)S(1)}, u32[]{:S(2)}, u32[]{:S(2)}) collective-permute-start(bf16[2,128,256]{2,1,0:T(8,128)(2,1)S(1)} %get-tuple-element.43), channel_id=1, source_target_pairs={{0,4},{1,2},{2,1},{3,7},{4,0},{5,6},{6,5},{7,3},{8,12},{9,10},{10,... | collective-permute-start | bytes 393224 | tf_op jit(solution)/shard_map/ppermute | solution.py:310
  2.4 4.2 %collective-permute-start = (bf16[2,128,256]{2,1,0:T(8,128)(2,1)S(1)}, bf16[2,128,256]{2,1,0:T(8,128)(2,1)S(1)}, u32[]{:S(2)}, u32[]{:S(2)}) collective-permute-start(bf16[2,128,256]{2,1,0:T(8,128)(2,1)S(1)} %get-tuple-element.37.after_ref), channel_id=1, source_target_pairs={{0,1},{1,0},{2,3},{3,2},{4,5},{5,4},{6,7},{7,6},{8,9},{9,8},{10,11... | collective-permute-start | bytes 393224 | tf_op jit(solution)/shard_map/ppermute | solution.py:309
  6.5 1.7 %load.1 = (bf16[1,4,6,2,128,128]{5,4,3,2,1,0:T(8,128)(2,1)S(1)}, bf16[3,4,128,256]{3,2,1,0:T(8,128)(2,1)S(1)}, f32[4,128,128]{2,1,0:T(8,128)S(1)}, f32[4,128,128]{2,1,0:T(8,128)S(1)}) custom-call(bf16[1,4,6,2,128,128]{5,4,3,2,1,0:T(8,128)(2,1)} %ops_hbm.1, bf16[3,4,128,256]{3,2,1,0:T(8,128)(2,1)} %source_hbm.1, f32[1,4,128]{2,1,0:T(4,128)} %pass_hbm.1, ...), custom_call_target="tpu_custom_call" | custom-call | bytes 4718592 | tf_op jit(solution)/shard_map/load/pallas_call | solution.py:313
  8.2 0.0 collective-permute-done.1.refs_7_
  8.2 1.5 %collective-permute-done.refs_6_ = bf16[2,128,256]{2,1,0:T(8,128)(2,1)S(1)} collective-permute-done((bf16[2,128,256]{2,1,0:T(8,128)(2,1)S(1)}, bf16[2,128,256]{2,1,0:T(8,128)(2,1)S(1)}, u32[]{:S(2)}, u32[]{:S(2)}) %collective-permute-start) | collective-permute-done | bytes 131104 | tf_op jit(solution)/shard_map/ppermute | solution.py:309
  9.7 0.0 collective-permute-start.2
  9.7 1.6 %collective-permute-start.3 = (bf16[2,144,256]{2,1,0:T(8,128)(2,1)S(1)}, bf16[2,144,256]{2,1,0:T(8,128)(2,1)S(1)}, u32[]{:S(2)}, u32[]{:S(2)}) collective-permute-start(bf16[2,144,256]{2,1,0:T(8,128)(2,1)S(1)} %get-tuple-element.45), channel_id=1, source_target_pairs={{0,4},{1,5},{2,6},{3,7},{4,9},{5,8},{6,11},{7,10},{8,12},{9,13},{1... | collective-permute-start | bytes 442376 | tf_op jit(solution)/shard_map/ppermute | solution.py:371
  11.3 1.2 %collective-permute-start.4 = (bf16[2,144,256]{2,1,0:T(8,128)(2,1)S(1)}, bf16[2,144,256]{2,1,0:T(8,128)(2,1)S(1)}, u32[]{:S(2)}, u32[]{:S(2)}) collective-permute-start(bf16[2,144,256]{2,1,0:T(8,128)(2,1)S(1)} %get-tuple-element.46), channel_id=1, source_target_pairs={{0,4},{1,5},{2,6},{3,7},{4,0},{5,10},{6,9},{7,3},{8,12},{9,13},{10... | collective-permute-start | bytes 442376 | tf_op jit(solution)/shard_map/ppermute | solution.py:372
  12.5 0.7 %tick0_even.1 = (bf16[4,128,256]{2,1,0:T(8,128)(2,1)S(1)}, bf16[2,128,256]{2,1,0:T(8,128)(2,1)S(1)}, bf16[2,128,256]{2,1,0:T(8,128)(2,1)S(1)}, bf16[2,4,128,256]{3,2,1,0:T(8,128)(2,1)S(1)}) custom-call(s32[30]{0:T(128)S(4)} %get-tuple-element.36.refs_0_, ...), custom_call_target="tpu_custom_call", output_to_operand_aliasing={{0}: (8, {})} | custom-call | tf_op jit(solution)/shard_map/tick0_even/pallas_call | solution.py:222
  13.3 1.2 %collective-permute-start.5 = (bf16[2,128,256]{2,1,0:T(8,128)(2,1)S(1)}, bf16[2,128,256]{2,1,0:T(8,128)(2,1)S(1)}, u32[]{:S(2)}, u32[]{:S(2)}) collective-permute-start(bf16[2,128,256]{2,1,0:T(8,128)(2,1)S(1)} %get-tuple-element.49), channel_id=1, source_target_pairs={{0,5},{1,4},{2,7},{3,6},{4,0},{5,1},{6,2},{7,3},{8,13},{9,12},{10,... | collective-permute-start | bytes 393224 | tf_op jit(solution)/shard_map/ppermute | solution.py:371
  14.5 0.0 collective-permute-start.6
  14.5 4.1 %all_to_all.15.refs_5_ = bf16[2,4,128,256]{3,2,1,0:T(8,128)(2,1)S(1)} all-to-all(bf16[2,4,128,256]{3,2,1,0:T(8,128)(2,1)S(1)} %get-tuple-element.48), channel_id=1, replica_groups={{0,4},{8,12},{16,20},{24,28},{1,5},{9,13},{17,21},{25,29},{2,6},{10,14}..., dimensions={0} | all-to-all | bytes 1048576 | tf_op jit(solution)/shard_map/all_to_all | solution.py:368
  18.7 0.0 collective-permute-done.5.refs_6_
  18.7 0.0 collective-permute-done.6.refs_7_
  18.7 0.9 %collective-permute-start.12 = (bf16[4,128,256]{2,1,0:T(8,128)(2,1)S(1)}, bf16[4,128,256]{2,1,0:T(8,128)(2,1)S(1)}, u32[]{:S(2)}, u32[]{:S(2)}) collective-permute-start(bf16[4,128,256]{2,1,0:T(8,128)(2,1)S(1)} %get-tuple-element.60), channel_id=1, source_target_pairs={{0,4},{4,8},{8,12},{12,16},{16,20},{20,24},{24,28},{28,0},{1,5},{5... | collective-permute-start | bytes 786440 | tf_op jit(solution)/shard_map/ppermute | solution.py:366
  19.6 0.0 collective-permute-done.3.refs_6_
  19.6 0.0 collective-permute-done.4.refs_7_
  19.6 0.0 collective-permute-done.2.refs_5_
  19.6 0.8 %tick1_even.1 = (bf16[4,128,256]{2,1,0:T(8,128)(2,1)S(1)}, bf16[2,128,256]{2,1,0:T(8,128)(2,1)S(1)}, bf16[2,128,256]{2,1,0:T(8,128)(2,1)S(1)}, bf16[2,4,128,256]{3,2,1,0:T(8,128)(2,1)S(1)}) custom-call(s32[30]{0:T(128)S(4)} %get-tuple-element.36.refs_0_, ...), custom_call_target="tpu_custom_call", output_to_operand_aliasing={{0}: (8, {})} | custom-call | tf_op jit(solution)/shard_map/tick1_even/pallas_call | solution.py:222
  20.4 1.5 %collective-permute-start.7 = (bf16[2,128,256]{2,1,0:T(8,128)(2,1)S(1)}, bf16[2,128,256]{2,1,0:T(8,128)(2,1)S(1)}, u32[]{:S(2)}, u32[]{:S(2)}) collective-permute-start(bf16[2,128,256]{2,1,0:T(8,128)(2,1)S(1)} %get-tuple-element.53), channel_id=1, source_target_pairs={{0,5},{1,4},{2,7},{3,6},{4,0},{5,1},{6,2},{7,3},{8,13},{9,12},{10,... | collective-permute-start | bytes 393224 | tf_op jit(solution)/shard_map/ppermute | solution.py:371
  21.9 0.0 collective-permute-start.8
  21.9 0.5 %collective-permute-start.13 = (bf16[2,144,256]{2,1,0:T(8,128)(2,1)S(1)}, bf16[2,144,256]{2,1,0:T(8,128)(2,1)S(1)}, u32[]{:S(2)}, u32[]{:S(2)}) collective-permute-start(bf16[2,144,256]{2,1,0:T(8,128)(2,1)S(1)} %get-tuple-element.61), channel_id=1, source_target_pairs={{0,4},{1,5},{2,6},{3,7},{4,9},{5,8},{6,11},{7,10},{8,12},{9,13},{1... | collective-permute-start | bytes 442376 | tf_op jit(solution)/shard_map/ppermute | solution.py:371
  22.4 1.7 %collective-permute-start.14 = (bf16[2,144,256]{2,1,0:T(8,128)(2,1)S(1)}, bf16[2,144,256]{2,1,0:T(8,128)(2,1)S(1)}, u32[]{:S(2)}, u32[]{:S(2)}) collective-permute-start(bf16[2,144,256]{2,1,0:T(8,128)(2,1)S(1)} %get-tuple-element.62), channel_id=1, source_target_pairs={{0,4},{1,5},{2,6},{3,7},{4,0},{5,10},{6,9},{7,3},{8,12},{9,13},{10... | collective-permute-start | bytes 442376 | tf_op jit(solution)/shard_map/ppermute | solution.py:372
  24.1 4.1 %all_to_all.16.refs_5_ = bf16[2,4,128,256]{3,2,1,0:T(8,128)(2,1)S(1)} all-to-all(bf16[2,4,128,256]{3,2,1,0:T(8,128)(2,1)S(1)} %get-tuple-element.52), channel_id=1, replica_groups={{0,4},{8,12},{16,20},{24,28},{1,5},{9,13},{17,21},{25,29},{2,6},{10,14}..., dimensions={0} | all-to-all | bytes 1048576 | tf_op jit(solution)/shard_map/all_to_all | solution.py:368
  28.3 0.0 collective-permute-done.7.refs_6_
  28.3 0.0 collective-permute-done.8.refs_7_
  28.3 0.9 %collective-permute-start.9 = (bf16[4,128,256]{2,1,0:T(8,128)(2,1)S(1)}, bf16[4,128,256]{2,1,0:T(8,128)(2,1)S(1)}, u32[]{:S(2)}, u32[]{:S(2)}) collective-permute-start(bf16[4,128,256]{2,1,0:T(8,128)(2,1)S(1)} %get-tuple-element.55), channel_id=1, source_target_pairs={{0,4},{4,8},{8,12},{12,16},{16,20},{20,24},{24,28},{28,0},{1,5},{5... | collective-permute-start | bytes 786440 | tf_op jit(solution)/shard_map/ppermute | solution.py:366
  29.2 0.9 %collective-permute-start.10 = (bf16[2,144,256]{2,1,0:T(8,128)(2,1)S(1)}, bf16[2,144,256]{2,1,0:T(8,128)(2,1)S(1)}, u32[]{:S(2)}, u32[]{:S(2)}) collective-permute-start(bf16[2,144,256]{2,1,0:T(8,128)(2,1)S(1)} %get-tuple-element.56), channel_id=1, source_target_pairs={{0,4},{1,5},{2,6},{3,7},{4,9},{5,8},{6,11},{7,10},{8,12},{9,13},{1... | collective-permute-start | bytes 442376 | tf_op jit(solution)/shard_map/ppermute | solution.py:371
  30.1 0.0 collective-permute-done.13.refs_6_
  30.1 1.0 %collective-permute-start.11 = (bf16[2,144,256]{2,1,0:T(8,128)(2,1)S(1)}, bf16[2,144,256]{2,1,0:T(8,128)(2,1)S(1)}, u32[]{:S(2)}, u32[]{:S(2)}) collective-permute-start(bf16[2,144,256]{2,1,0:T(8,128)(2,1)S(1)} %get-tuple-element.57), channel_id=1, source_target_pairs={{0,4},{1,5},{2,6},{3,7},{4,0},{5,10},{6,9},{7,3},{8,12},{9,13},{10... | collective-permute-start | bytes 442376 | tf_op jit(solution)/shard_map/ppermute | solution.py:372
  31.2 0.0 collective-permute-done.14.refs_7_
  31.2 0.0 collective-permute-done.12.refs_5_
  31.2 0.7 %tick2_even.1 = (bf16[4,128,256]{2,1,0:T(8,128)(2,1)S(1)}, bf16[2,128,256]{2,1,0:T(8,128)(2,1)S(1)}, bf16[2,128,256]{2,1,0:T(8,128)(2,1)S(1)}, bf16[2,4,128,256]{3,2,1,0:T(8,128)(2,1)S(1)}) custom-call(s32[30]{0:T(128)S(4)} %get-tuple-element.36.refs_0_, ...), custom_call_target="tpu_custom_call", output_to_operand_aliasing={{0}: (8, {})} | custom-call | tf_op jit(solution)/shard_map/tick2_even/pallas_call | solution.py:222
  31.9 0.3 collective-permute-start.15
  32.2 0.3 collective-permute-start.16
  32.5 4.1 %all_to_all.17.refs_5_ = bf16[2,4,128,256]{3,2,1,0:T(8,128)(2,1)S(1)} all-to-all(bf16[2,4,128,256]{3,2,1,0:T(8,128)(2,1)S(1)} %get-tuple-element.65), channel_id=1, replica_groups={{0,4},{8,12},{16,20},{24,28},{1,5},{9,13},{17,21},{25,29},{2,6},{10,14}..., dimensions={0} | all-to-all | bytes 1048576 | tf_op jit(solution)/shard_map/all_to_all | solution.py:368
  36.6 0.0 collective-permute-done.15.refs_6_
  36.7 0.0 collective-permute-done.16.refs_7_
  36.7 0.1 last_tick_odd.1
  36.8 0.0 collective-permute-done.10.refs_6_
  36.8 0.0 collective-permute-done.11.refs_7_
  36.8 0.0 collective-permute-done.9.refs_5_
  36.8 1.5 %last_tick_even.1 = (bf16[4,1,4,128,256]{4,3,2,1,0:T(8,128)(2,1)}, f32[1,4,128,256]{3,2,1,0:T(8,128)}) custom-call(s32[30]{0:T(128)S(4)} %get-tuple-element.36.refs_0_, bf16[1,4,6,2,128,128]{5,4,3,2,1,0:T(8,128)(2,1)S(1)} %get-tuple-element.38.refs_1_, ...), custom_call_target="tpu_custom_call", output_to_operand_aliasing={{0}: (11, {}), {1}: (12, {})} | custom-call | tf_op jit(solution)/shard_map/last_tick_even/pallas_call | solution.py:222
  (3 shorter events, 0.0 us)
Async XLA Ops:
  1.8 6.4 %collective-permute-start.1 = (bf16[2,128,256]{2,1,0:T(8,128)(2,1)S(1)}, bf16[2,128,256]{2,1,0:T(8,128)(2,1)S(1)}, u32[]{:S(2)}, u32[]{:S(2)}) collective-permute-start(bf16[2,128,256]{2,1,0:T(8,128)(2,1)S(1)} %get-tuple-element.43), channel_id=1, source_target_pairs={{0,4},{1,2},{2,1},{3,7},{4,0},{5,6},{6,5},{7,3},{8,12},{9,10},{10,... | collective-permute-start | bytes 393224 | tf_op jit(solution)/shard_map/ppermute | solution.py:310
  2.4 7.4 %collective-permute-start = (bf16[2,128,256]{2,1,0:T(8,128)(2,1)S(1)}, bf16[2,128,256]{2,1,0:T(8,128)(2,1)S(1)}, u32[]{:S(2)}, u32[]{:S(2)}) collective-permute-start(bf16[2,128,256]{2,1,0:T(8,128)(2,1)S(1)} %get-tuple-element.37.after_ref), channel_id=1, source_target_pairs={{0,1},{1,0},{2,3},{3,2},{4,5},{5,4},{6,7},{7,6},{8,9},{9,8},{10,11... | collective-permute-start | bytes 393224 | tf_op jit(solution)/shard_map/ppermute | solution.py:309
  9.7 9.9 %collective-permute-start.2 = (bf16[4,128,256]{2,1,0:T(8,128)(2,1)S(1)}, bf16[4,128,256]{2,1,0:T(8,128)(2,1)S(1)}, u32[]{:S(2)}, u32[]{:S(2)}) collective-permute-start(bf16[4,128,256]{2,1,0:T(8,128)(2,1)S(1)} %get-tuple-element.44), channel_id=1, source_target_pairs={{0,4},{4,8},{8,12},{12,16},{16,20},{20,24},{24,28},{28,0},{1,5},{5... | collective-permute-start | bytes 786440 | tf_op jit(solution)/shard_map/ppermute | solution.py:366
  9.7 9.9 %collective-permute-start.3 = (bf16[2,144,256]{2,1,0:T(8,128)(2,1)S(1)}, bf16[2,144,256]{2,1,0:T(8,128)(2,1)S(1)}, u32[]{:S(2)}, u32[]{:S(2)}) collective-permute-start(bf16[2,144,256]{2,1,0:T(8,128)(2,1)S(1)} %get-tuple-element.45), channel_id=1, source_target_pairs={{0,4},{1,5},{2,6},{3,7},{4,9},{5,8},{6,11},{7,10},{8,12},{9,13},{1... | collective-permute-start | bytes 442376 | tf_op jit(solution)/shard_map/ppermute | solution.py:371
  11.3 8.3 %collective-permute-start.4 = (bf16[2,144,256]{2,1,0:T(8,128)(2,1)S(1)}, bf16[2,144,256]{2,1,0:T(8,128)(2,1)S(1)}, u32[]{:S(2)}, u32[]{:S(2)}) collective-permute-start(bf16[2,144,256]{2,1,0:T(8,128)(2,1)S(1)} %get-tuple-element.46), channel_id=1, source_target_pairs={{0,4},{1,5},{2,6},{3,7},{4,0},{5,10},{6,9},{7,3},{8,12},{9,13},{10... | collective-permute-start | bytes 442376 | tf_op jit(solution)/shard_map/ppermute | solution.py:372
  13.3 5.4 %collective-permute-start.5 = (bf16[2,128,256]{2,1,0:T(8,128)(2,1)S(1)}, bf16[2,128,256]{2,1,0:T(8,128)(2,1)S(1)}, u32[]{:S(2)}, u32[]{:S(2)}) collective-permute-start(bf16[2,128,256]{2,1,0:T(8,128)(2,1)S(1)} %get-tuple-element.49), channel_id=1, source_target_pairs={{0,5},{1,4},{2,7},{3,6},{4,0},{5,1},{6,2},{7,3},{8,13},{9,12},{10,... | collective-permute-start | bytes 393224 | tf_op jit(solution)/shard_map/ppermute | solution.py:371
  14.5 4.2 %collective-permute-start.6 = (bf16[2,128,256]{2,1,0:T(8,128)(2,1)S(1)}, bf16[2,128,256]{2,1,0:T(8,128)(2,1)S(1)}, u32[]{:S(2)}, u32[]{:S(2)}) collective-permute-start(bf16[2,128,256]{2,1,0:T(8,128)(2,1)S(1)} %get-tuple-element.50), channel_id=1, source_target_pairs={{0,4},{1,6},{2,5},{3,7},{4,0},{5,1},{6,2},{7,3},{8,12},{9,14},{10,... | collective-permute-start | bytes 393224 | tf_op jit(solution)/shard_map/ppermute | solution.py:372
  18.7 12.5 %collective-permute-start.12 = (bf16[4,128,256]{2,1,0:T(8,128)(2,1)S(1)}, bf16[4,128,256]{2,1,0:T(8,128)(2,1)S(1)}, u32[]{:S(2)}, u32[]{:S(2)}) collective-permute-start(bf16[4,128,256]{2,1,0:T(8,128)(2,1)S(1)} %get-tuple-element.60), channel_id=1, source_target_pairs={{0,4},{4,8},{8,12},{12,16},{16,20},{20,24},{24,28},{28,0},{1,5},{5... | collective-permute-start | bytes 786440 | tf_op jit(solution)/shard_map/ppermute | solution.py:366
  20.4 7.9 %collective-permute-start.7 = (bf16[2,128,256]{2,1,0:T(8,128)(2,1)S(1)}, bf16[2,128,256]{2,1,0:T(8,128)(2,1)S(1)}, u32[]{:S(2)}, u32[]{:S(2)}) collective-permute-start(bf16[2,128,256]{2,1,0:T(8,128)(2,1)S(1)} %get-tuple-element.53), channel_id=1, source_target_pairs={{0,5},{1,4},{2,7},{3,6},{4,0},{5,1},{6,2},{7,3},{8,13},{9,12},{10,... | collective-permute-start | bytes 393224 | tf_op jit(solution)/shard_map/ppermute | solution.py:371
  21.9 6.4 %collective-permute-start.8 = (bf16[2,128,256]{2,1,0:T(8,128)(2,1)S(1)}, bf16[2,128,256]{2,1,0:T(8,128)(2,1)S(1)}, u32[]{:S(2)}, u32[]{:S(2)}) collective-permute-start(bf16[2,128,256]{2,1,0:T(8,128)(2,1)S(1)} %get-tuple-element.54), channel_id=1, source_target_pairs={{0,4},{1,6},{2,5},{3,7},{4,0},{5,1},{6,2},{7,3},{8,12},{9,14},{10,... | collective-permute-start | bytes 393224 | tf_op jit(solution)/shard_map/ppermute | solution.py:372
  21.9 8.2 %collective-permute-start.13 = (bf16[2,144,256]{2,1,0:T(8,128)(2,1)S(1)}, bf16[2,144,256]{2,1,0:T(8,128)(2,1)S(1)}, u32[]{:S(2)}, u32[]{:S(2)}) collective-permute-start(bf16[2,144,256]{2,1,0:T(8,128)(2,1)S(1)} %get-tuple-element.61), channel_id=1, source_target_pairs={{0,4},{1,5},{2,6},{3,7},{4,9},{5,8},{6,11},{7,10},{8,12},{9,13},{1... | collective-permute-start | bytes 442376 | tf_op jit(solution)/shard_map/ppermute | solution.py:371
  22.4 8.7 %collective-permute-start.14 = (bf16[2,144,256]{2,1,0:T(8,128)(2,1)S(1)}, bf16[2,144,256]{2,1,0:T(8,128)(2,1)S(1)}, u32[]{:S(2)}, u32[]{:S(2)}) collective-permute-start(bf16[2,144,256]{2,1,0:T(8,128)(2,1)S(1)} %get-tuple-element.62), channel_id=1, source_target_pairs={{0,4},{1,5},{2,6},{3,7},{4,0},{5,10},{6,9},{7,3},{8,12},{9,13},{10... | collective-permute-start | bytes 442376 | tf_op jit(solution)/shard_map/ppermute | solution.py:372
  28.3 8.5 %collective-permute-start.9 = (bf16[4,128,256]{2,1,0:T(8,128)(2,1)S(1)}, bf16[4,128,256]{2,1,0:T(8,128)(2,1)S(1)}, u32[]{:S(2)}, u32[]{:S(2)}) collective-permute-start(bf16[4,128,256]{2,1,0:T(8,128)(2,1)S(1)} %get-tuple-element.55), channel_id=1, source_target_pairs={{0,4},{4,8},{8,12},{12,16},{16,20},{20,24},{24,28},{28,0},{1,5},{5... | collective-permute-start | bytes 786440 | tf_op jit(solution)/shard_map/ppermute | solution.py:366
  29.2 7.5 %collective-permute-start.10 = (bf16[2,144,256]{2,1,0:T(8,128)(2,1)S(1)}, bf16[2,144,256]{2,1,0:T(8,128)(2,1)S(1)}, u32[]{:S(2)}, u32[]{:S(2)}) collective-permute-start(bf16[2,144,256]{2,1,0:T(8,128)(2,1)S(1)} %get-tuple-element.56), channel_id=1, source_target_pairs={{0,4},{1,5},{2,6},{3,7},{4,9},{5,8},{6,11},{7,10},{8,12},{9,13},{1... | collective-permute-start | bytes 442376 | tf_op jit(solution)/shard_map/ppermute | solution.py:371
  30.1 6.6 %collective-permute-start.11 = (bf16[2,144,256]{2,1,0:T(8,128)(2,1)S(1)}, bf16[2,144,256]{2,1,0:T(8,128)(2,1)S(1)}, u32[]{:S(2)}, u32[]{:S(2)}) collective-permute-start(bf16[2,144,256]{2,1,0:T(8,128)(2,1)S(1)} %get-tuple-element.57), channel_id=1, source_target_pairs={{0,4},{1,5},{2,6},{3,7},{4,0},{5,10},{6,9},{7,3},{8,12},{9,13},{10... | collective-permute-start | bytes 442376 | tf_op jit(solution)/shard_map/ppermute | solution.py:372
  31.9 4.7 %collective-permute-start.15 = (bf16[2,128,256]{2,1,0:T(8,128)(2,1)S(1)}, bf16[2,128,256]{2,1,0:T(8,128)(2,1)S(1)}, u32[]{:S(2)}, u32[]{:S(2)}) collective-permute-start(bf16[2,128,256]{2,1,0:T(8,128)(2,1)S(1)} %get-tuple-element.66), channel_id=1, source_target_pairs={{0,5},{1,4},{2,7},{3,6},{4,0},{5,1},{6,2},{7,3},{8,13},{9,12},{10,... | collective-permute-start | bytes 393224 | tf_op jit(solution)/shard_map/ppermute | solution.py:371
  32.2 4.4 %collective-permute-start.16 = (bf16[2,128,256]{2,1,0:T(8,128)(2,1)S(1)}, bf16[2,128,256]{2,1,0:T(8,128)(2,1)S(1)}, u32[]{:S(2)}, u32[]{:S(2)}) collective-permute-start(bf16[2,128,256]{2,1,0:T(8,128)(2,1)S(1)} %get-tuple-element.67), channel_id=1, source_target_pairs={{0,4},{1,6},{2,5},{3,7},{4,0},{5,1},{6,2},{7,3},{8,12},{9,14},{10,... | collective-permute-start | bytes 393224 | tf_op jit(solution)/shard_map/ppermute | solution.py:372

commit v9 on v8

--- a/solution.py
+++ b/solution.py
@@ -105,8 +105,11 @@
     blocks, listed = source_ref.shape[1], first_ref.shape[0]
 
     def fill_wave():
+        start = 0
         for wave_ref in wave_refs:
-            buffer[:blocks] = wave_ref[...] if len(wave_ref.shape) == 3 else wave_ref[0]
+            part = wave_ref[:, : buffer.shape[1]] if len(wave_ref.shape) == 3 else wave_ref[0]
+            buffer[start : start + part.shape[0]] = part
+            start += part.shape[0]
 
     if tick == 0:
         fill_wave()
@@ -162,9 +165,11 @@
                 cols = pl.ds(i * part.shape[1], part.shape[1])
                 onward[b, :, cols] = (pass_ref[b] * part).astype(onward.dtype)
                 echo_ref[b, :, cols] = (reflect_ref[b] * part).astype(echo_ref.dtype)
+        start = 0
         for onward_ref in onward_refs:
             slot = onward_ref if len(onward_ref.shape) == 3 else onward_ref.at[1]
-            slot[...] = onward[...]
+            slot[:, : onward.shape[1]] = onward[start : start + slot.shape[0]]
+            start += slot.shape[0]
 
         @pl.when(section != sections - 1)
         def _():
@@ -247,14 +252,14 @@
     return routes
 
 
-def halo_routes(sections, tiles, parity):
+def halo_routes(sections, tiles, senders):
     routes = []
     for turn in (0, 1):
         route = []
         for s in range(sections):
             for j in range(tiles):
                 to = neighbour(j, turn, tiles)
-                real = to is not None and s % 2 == parity
+                real = to is not None and s % 2 in senders
                 end = (s + 1) % sections * tiles + to if real else (s ^ 1) * tiles + j
                 route.append((s * tiles + j, end))
         routes.append(route)
@@ -337,42 +342,63 @@
 
     ODD, EVEN = 1, 0
     crossing = [(s, (s + 1) % sections) for s in range(sections)]
+    inside = [(s, s ^ 1) for s in range(sections)]
     pairs = [[s, s + 1] for s in range(0, sections, 2)]
-    far_list_type = pltpu.VMEM((listed, points + 16, columns), WAVE)
     pair_type = pltpu.VMEM((2, blocks, points, columns), WAVE)
-    routes = {parity: halo_routes(sections, tiles, parity) for parity in (ODD, EVEN)}
+    part_types = [pltpu.VMEM((blocks // 2, points, columns), WAVE)] * 2
+    half_types = [pltpu.VMEM((n, points, columns), WAVE) for n in (blocks // 2, blocks - blocks // 2)]
+
+    def lists_of(extra):
+        return [pltpu.VMEM((listed, points + extra, columns), WAVE)] * 2
+
+    def exchange(lists, senders):
+        routes = halo_routes(sections, tiles, senders)
+        return [lax.ppermute(a, both, route) for a, route in zip(lists, routes)]
 
     arrived = {parity: ([wave], first, second) for parity in (ODD, EVEN)}
     echoes = []
     for tick in range(ticks - 1):
-        echo = []
-        sent = {}
+        first_step, last_step = tick == 0, tick == ticks - 2
+        known = []
+        waves, halos = {}, {}
         for parity in (ODD, EVEN):
-            kind = list_type if parity == EVEN else far_list_type
-            outs = [wave_type, kind, kind, wave_type if parity == ODD else pair_type]
-            echo, first, second, onward = grouped_call(
+            if first_step:
+                extra = 0
+            elif last_step:
+                extra = 16 if parity == ODD else 0
+            else:
+                extra = 0 if parity == ODD else 16
+            if parity == ODD:
+                long = 0 if first_step or last_step else 16
+                to_next = [pltpu.VMEM((blocks, points + long, columns), WAVE)]
+            else:
+                to_next = [pair_type] if last_step else half_types if first_step else part_types
+            outs = [wave_type, *lists_of(extra), *to_next]
+            echo, *lists = grouped_call(
                 functools.partial(tick_kernel, parity, tick, sections),
                 [*fixed, *arrived[parity]],
                 outs,
                 [VMEM_SPEC] * len(outs),
-                [in_vmem(a) for a in echo],
+                [in_vmem(a) for a in known],
                 scratch_shapes=[buffer_type, pltpu.VMEM(wave_type.shape, WAVE)],
                 compiler_params=params,
                 cost_estimate=tick_cost,
                 name=f"tick{tick}" + ("_odd" if parity else "_even"),
             )
-            echo = [echo]
+            lists, onward = lists[:2], lists[2:]
+            known = [echo, *lists] if first_step else [echo]
             if parity == ODD:
-                onward = lax.ppermute(onward, "depth", crossing)
+                waves[EVEN] = [lax.ppermute(onward[0], "depth", crossing)]
+            elif last_step:
+                waves[ODD] = [lax.all_to_all(onward[0], "depth", 0, 0, axis_index_groups=pairs)]
             else:
-                onward = lax.all_to_all(onward, "depth", 0, 0, axis_index_groups=pairs)
-            sent[1 - parity] = (
-                [onward],
-                lax.ppermute(first, both, routes[parity][0]),
-                lax.ppermute(second, both, routes[parity][1]),
-            )
-        arrived = sent
-        echoes += echo
+                waves[ODD] = [lax.ppermute(a, "depth", inside) for a in onward]
+            if not first_step:
+                halos[1 - parity] = exchange(lists, (parity,))
+        if first_step:
+            halos[ODD] = halos[EVEN] = exchange(lists, (ODD, EVEN))
+        arrived = {parity: (waves[parity], *halos[parity]) for parity in (ODD, EVEN)}
+        echoes.append(echo)
 
     tick = ticks - 1
     results = []

time: 38.6 us -> 37.7 us (0.977)
  blocking collectives: 12.4 us -> 4.15 us
  waiting for transfers between devices: 1.57 us -> 8.96 us
    all_to_all x3 -> x1, blocking collectives: 12.4 us -> 4.15 us  [per_device(): lax.all_to_all(onward[0], 'depth', 0, 0, axis_index_groups=pairs)]
    ppermute x15 -> x17, waiting for transfers between devices: 0.04 us -> 7.43 us  [the longest x10 6.37 us: exchange(): return [lax.ppermute(a, both, route) for a, route in zip(lists, routes)]]
    ppermute x15 -> x17, starting transfers between devices: 12.2 us -> 12.2 us  [the longest x10 9.96 us: exchange(): return [lax.ppermute(a, both, route) for a, route in zip(lists, routes)]]
  transfers between devices with their start and end apart: 17 -> 19, of which waited for: 1 -> 4; matrix products, arithmetic and copies ran while one was open for 0% -> 0% of each run, Pallas kernels for 10% -> 11%
where the time goes in v9:
time: 37.7 us; the launch traced here: 37.5 us
  starting transfers between devices  16.9 us (45%)
  waiting for transfers between devices  8.96 us (24%)
  Pallas kernels  6.74 us (18%)
  blocking collectives  4.15 us (11%)
  between operations  0.75 us (2%)
    ppermute x10, starting transfers between devices, exchange(): return [lax.ppermute(a, both, route) for a, route in zip(lists, routes)]  9.96 us
    ppermute x10, waiting for transfers between devices, exchange(): return [lax.ppermute(a, both, route) for a, route in zip(lists, routes)]  6.37 us
    all_to_all x1, blocking collectives, per_device(): lax.all_to_all(onward[0], 'depth', 0, 0, axis_index_groups=pairs)  4.15 us
    ppermute x1, starting transfers between devices, per_device(): first = lax.ppermute(first, both, routes[0])  4.15 us
    pallas_call x8, Pallas kernels, grouped_call(): pl.pallas_call(body, out_shape=tuple(outs), in_specs=[SMEM_SPEC] + [VMEM_...  3.85 us
    pallas_call x1, Pallas kernels, per_device(): pl.pallas_call(load_kernel, out_shape=(pltpu.VMEM(operators.shape, operat...  1.67 us
    ppermute x1, waiting for transfers between devices, per_device(): first = lax.ppermute(first, both, routes[0])  1.52 us
    pallas_call x1, Pallas kernels, per_device(): pl.pallas_call(prepare_kernel, out_shape=(pltpu.SMEM((2 * (listed + 1) +...  1.22 us
  transfers between devices with their start and end apart: 19, of which 4 were waited for; matrix products, arithmetic and copies ran while one was open for 0% of the time, Pallas kernels for 11%

profile of v9, /device:TPU:0, one launch (start us, length us, event | category | flops | bytes accessed | tf_op | source)
XLA Modules:
  0.0 37.5 jit_solution(18213885463797680207)
XLA Ops:
  0.6 1.2 %prepare.1 = (s32[30]{0:T(128)S(4)}, bf16[4,128,256]{2,1,0:T(8,128)(2,1)S(1)}, bf16[2,128,256]{2,1,0:T(8,128)(2,1)S(1)}, bf16[2,128,256]{2,1,0:T(8,128)(2,1)S(1)}) custom-call(s32[1,2,2]{2,1,0:T(2,128)} %ids_hbm.1, s32[1,2]{1,0:T(1,128)} %count_hbm.1, s32[4,6]{1,0:T(4,128)} %pattern_hbm.1, f32[1,4,128,256]{3,2,1,0:T(8,128)} %inflow_hbm.1), custom_call_target="tpu_custom_call" | custom-call | flops 131072 | bytes 1048576 | tf_op jit(solution)/shard_map/prepare/pallas_call | solution.py:288
  1.9 0.5 %collective-permute-start.1 = (bf16[2,128,256]{2,1,0:T(8,128)(2,1)S(1)}, bf16[2,128,256]{2,1,0:T(8,128)(2,1)S(1)}, u32[]{:S(2)}, u32[]{:S(2)}) collective-permute-start(bf16[2,128,256]{2,1,0:T(8,128)(2,1)S(1)} %get-tuple-element.45), channel_id=1, source_target_pairs={{0,4},{1,2},{2,1},{3,7},{4,0},{5,6},{6,5},{7,3},{8,12},{9,10},{10,... | collective-permute-start | bytes 393224 | tf_op jit(solution)/shard_map/ppermute | solution.py:315
  2.4 4.1 %collective-permute-start = (bf16[2,128,256]{2,1,0:T(8,128)(2,1)S(1)}, bf16[2,128,256]{2,1,0:T(8,128)(2,1)S(1)}, u32[]{:S(2)}, u32[]{:S(2)}) collective-permute-start(bf16[2,128,256]{2,1,0:T(8,128)(2,1)S(1)} %get-tuple-element.39.after_ref), channel_id=1, source_target_pairs={{0,1},{1,0},{2,3},{3,2},{4,5},{5,4},{6,7},{7,6},{8,9},{9,8},{10,11... | collective-permute-start | bytes 393224 | tf_op jit(solution)/shard_map/ppermute | solution.py:314
  6.5 1.7 %load.1 = (bf16[1,4,6,2,128,128]{5,4,3,2,1,0:T(8,128)(2,1)S(1)}, bf16[3,4,128,256]{3,2,1,0:T(8,128)(2,1)S(1)}, f32[4,128,128]{2,1,0:T(8,128)S(1)}, f32[4,128,128]{2,1,0:T(8,128)S(1)}) custom-call(bf16[1,4,6,2,128,128]{5,4,3,2,1,0:T(8,128)(2,1)} %ops_hbm.1, bf16[3,4,128,256]{3,2,1,0:T(8,128)(2,1)} %source_hbm.1, f32[1,4,128]{2,1,0:T(4,128)} %pass_hbm.1, ...), custom_call_target="tpu_custom_call" | custom-call | bytes 4718592 | tf_op jit(solution)/shard_map/load/pallas_call | solution.py:318
  8.2 0.0 collective-permute-done.1.refs_7_
  8.2 1.5 %collective-permute-done.refs_6_ = bf16[2,128,256]{2,1,0:T(8,128)(2,1)S(1)} collective-permute-done((bf16[2,128,256]{2,1,0:T(8,128)(2,1)S(1)}, bf16[2,128,256]{2,1,0:T(8,128)(2,1)S(1)}, u32[]{:S(2)}, u32[]{:S(2)}) %collective-permute-start) | collective-permute-done | bytes 131104 | tf_op jit(solution)/shard_map/ppermute | solution.py:314
  9.7 0.0 collective-permute-start.2
  9.7 0.7 %tick0_even.1 = (bf16[4,128,256]{2,1,0:T(8,128)(2,1)S(1)}, bf16[2,128,256]{2,1,0:T(8,128)(2,1)S(1)}, bf16[2,128,256]{2,1,0:T(8,128)(2,1)S(1)}, bf16[2,128,256]{2,1,0:T(8,128)(2,1)S(1)}, bf16[2,128,256]{2,1,0:T(8,128)(2,1)S(1)}) custom-call(s32[30]{0:T(128)S(4)} %get-tuple-element.38.refs_0_, ...), custom_call_target="tpu_custom_call", output_to_operand_aliasing={{0}: (8, {}), {1}: (9, {}), {2}: (10, {})} | custom-call | tf_op jit(solution)/shard_map/tick0_even/pallas_call | solution.py:227
  10.5 2.2 %collective-permute-start.3 = (bf16[2,128,256]{2,1,0:T(8,128)(2,1)S(1)}, bf16[2,128,256]{2,1,0:T(8,128)(2,1)S(1)}, u32[]{:S(2)}, u32[]{:S(2)}) collective-permute-start(bf16[2,128,256]{2,1,0:T(8,128)(2,1)S(1)} %get-tuple-element.50), channel_id=1, source_target_pairs={{0,5},{1,4},{2,7},{3,6},{4,9},{5,8},{6,11},{7,10},{8,13},{9,12},{1... | collective-permute-start | bytes 393224 | tf_op jit(solution)/shard_map/ppermute | solution.py:356
  12.7 0.6 %collective-permute-start.4 = (bf16[2,128,256]{2,1,0:T(8,128)(2,1)S(1)}, bf16[2,128,256]{2,1,0:T(8,128)(2,1)S(1)}, u32[]{:S(2)}, u32[]{:S(2)}) collective-permute-start(bf16[2,128,256]{2,1,0:T(8,128)(2,1)S(1)} %get-tuple-element.51), channel_id=1, source_target_pairs={{0,4},{1,6},{2,5},{3,7},{4,0},{5,10},{6,9},{7,3},{8,12},{9,14},{10... | collective-permute-start | bytes 393224 | tf_op jit(solution)/shard_map/ppermute | solution.py:356
  13.3 0.0 collective-permute-start.5
  13.3 0.5 %collective-permute-start.6 = (bf16[2,128,256]{2,1,0:T(8,128)(2,1)S(1)}, bf16[2,128,256]{2,1,0:T(8,128)(2,1)S(1)}, u32[]{:S(2)}, u32[]{:S(2)}) collective-permute-start(bf16[2,128,256]{2,1,0:T(8,128)(2,1)S(1)} %get-tuple-element.53), channel_id=1, source_target_pairs={{0,4},{4,0},{8,12},{12,8},{16,20},{20,16},{24,28},{28,24},{1,5},{5... | collective-permute-start | bytes 393224 | tf_op jit(solution)/shard_map/ppermute | solution.py:395
  13.8 4.0 %collective-permute-done.3.refs_7_.refs_6_ = bf16[2,128,256]{2,1,0:T(8,128)(2,1)S(1)} collective-permute-done((bf16[2,128,256]{2,1,0:T(8,128)(2,1)S(1)}, bf16[2,128,256]{2,1,0:T(8,128)(2,1)S(1)}, u32[]{:S(2)}, u32[]{:S(2)}) %collective-permute-start.3) | collective-permute-done | bytes 131104 | tf_op jit(solution)/shard_map/ppermute | solution.py:356
  17.8 0.0 collective-permute-done.4.refs_8_.refs_7_
  17.8 0.0 collective-permute-done.5.refs_5_
  17.8 0.0 collective-permute-done.6.refs_6_
  17.9 0.4 collective-permute-start.14
  18.2 0.0 collective-permute-done.2.refs_5_
  18.2 0.7 %tick1_even.1 = (bf16[4,128,256]{2,1,0:T(8,128)(2,1)S(1)}, bf16[2,144,256]{2,1,0:T(8,128)(2,1)S(1)}, bf16[2,144,256]{2,1,0:T(8,128)(2,1)S(1)}, bf16[2,128,256]{2,1,0:T(8,128)(2,1)S(1)}, bf16[2,128,256]{2,1,0:T(8,128)(2,1)S(1)}) custom-call(s32[30]{0:T(128)S(4)} %get-tuple-element.38.refs_0_, ...), custom_call_target="tpu_custom_call", output_to_operand_aliasing={{0}: (8, {})} | custom-call | tf_op jit(solution)/shard_map/tick1_even/pallas_call | solution.py:227
  19.0 0.1 collective-permute-start.7
  19.1 2.9 %collective-permute-start.9 = (bf16[2,144,256]{2,1,0:T(8,128)(2,1)S(1)}, bf16[2,144,256]{2,1,0:T(8,128)(2,1)S(1)}, u32[]{:S(2)}, u32[]{:S(2)}) collective-permute-start(bf16[2,144,256]{2,1,0:T(8,128)(2,1)S(1)} %get-tuple-element.57), channel_id=1, source_target_pairs={{0,5},{1,4},{2,7},{3,6},{4,0},{5,1},{6,2},{7,3},{8,13},{9,12},{10,... | collective-permute-start | bytes 442376 | tf_op jit(solution)/shard_map/ppermute | solution.py:356
  21.9 0.0 collective-permute-start.10
  21.9 0.5 %collective-permute-start.8 = (bf16[2,128,256]{2,1,0:T(8,128)(2,1)S(1)}, bf16[2,128,256]{2,1,0:T(8,128)(2,1)S(1)}, u32[]{:S(2)}, u32[]{:S(2)}) collective-permute-start(bf16[2,128,256]{2,1,0:T(8,128)(2,1)S(1)} %get-tuple-element.56), channel_id=1, source_target_pairs={{0,4},{4,0},{8,12},{12,8},{16,20},{20,16},{24,28},{28,24},{1,5},{5... | collective-permute-start | bytes 393224 | tf_op jit(solution)/shard_map/ppermute | solution.py:395
  22.4 0.0 collective-permute-done.7.refs_5_
  22.4 0.0 collective-permute-start.15
  22.4 1.0 %collective-permute-done.8.refs_6_ = bf16[2,128,256]{2,1,0:T(8,128)(2,1)S(1)} collective-permute-done((bf16[2,128,256]{2,1,0:T(8,128)(2,1)S(1)}, bf16[2,128,256]{2,1,0:T(8,128)(2,1)S(1)}, u32[]{:S(2)}, u32[]{:S(2)}) %collective-permute-start.8) | collective-permute-done | bytes 131104 | tf_op jit(solution)/shard_map/ppermute | solution.py:395
  23.5 1.8 %collective-permute-start.16 = (bf16[2,128,256]{2,1,0:T(8,128)(2,1)S(1)}, bf16[2,128,256]{2,1,0:T(8,128)(2,1)S(1)}, u32[]{:S(2)}, u32[]{:S(2)}) collective-permute-start(bf16[2,128,256]{2,1,0:T(8,128)(2,1)S(1)} %get-tuple-element.66), channel_id=1, source_target_pairs={{0,4},{1,5},{2,6},{3,7},{4,0},{5,10},{6,9},{7,3},{8,12},{9,13},{10... | collective-permute-start | bytes 393224 | tf_op jit(solution)/shard_map/ppermute | solution.py:356
  25.3 0.0 collective-permute-done.9.refs_7_
  25.3 0.0 collective-permute-done.10.refs_8_
  25.3 0.8 %collective-permute-start.11 = (bf16[4,128,256]{2,1,0:T(8,128)(2,1)S(1)}, bf16[4,128,256]{2,1,0:T(8,128)(2,1)S(1)}, u32[]{:S(2)}, u32[]{:S(2)}) collective-permute-start(bf16[4,128,256]{2,1,0:T(8,128)(2,1)S(1)} %get-tuple-element.59), channel_id=1, source_target_pairs={{0,4},{4,8},{8,12},{12,16},{16,20},{20,24},{24,28},{28,0},{1,5},{5... | collective-permute-start | bytes 786440 | tf_op jit(solution)/shard_map/ppermute | solution.py:391
  26.2 0.1 collective-permute-start.12
  26.3 2.4 %collective-permute-done.15.refs_6_ = bf16[2,128,256]{2,1,0:T(8,128)(2,1)S(1)} collective-permute-done((bf16[2,128,256]{2,1,0:T(8,128)(2,1)S(1)}, bf16[2,128,256]{2,1,0:T(8,128)(2,1)S(1)}, u32[]{:S(2)}, u32[]{:S(2)}) %collective-permute-start.15) | collective-permute-done | bytes 131104 | tf_op jit(solution)/shard_map/ppermute | solution.py:356
  28.6 0.4 %collective-permute-start.13 = (bf16[2,144,256]{2,1,0:T(8,128)(2,1)S(1)}, bf16[2,144,256]{2,1,0:T(8,128)(2,1)S(1)}, u32[]{:S(2)}, u32[]{:S(2)}) collective-permute-start(bf16[2,144,256]{2,1,0:T(8,128)(2,1)S(1)} %get-tuple-element.61), channel_id=1, source_target_pairs={{0,4},{1,5},{2,6},{3,7},{4,0},{5,10},{6,9},{7,3},{8,12},{9,13},{10... | collective-permute-start | bytes 442376 | tf_op jit(solution)/shard_map/ppermute | solution.py:356
  29.1 0.0 collective-permute-done.16.refs_7_
  29.1 0.0 collective-permute-done.14.refs_5_
  29.1 0.7 %tick2_even.1 = (bf16[4,128,256]{2,1,0:T(8,128)(2,1)S(1)}, bf16[2,128,256]{2,1,0:T(8,128)(2,1)S(1)}, bf16[2,128,256]{2,1,0:T(8,128)(2,1)S(1)}, bf16[2,4,128,256]{3,2,1,0:T(8,128)(2,1)S(1)}) custom-call(s32[30]{0:T(128)S(4)} %get-tuple-element.38.refs_0_, ...), custom_call_target="tpu_custom_call", output_to_operand_aliasing={{0}: (8, {})} | custom-call | tf_op jit(solution)/shard_map/tick2_even/pallas_call | solution.py:227
  29.8 1.9 %collective-permute-start.17 = (bf16[2,128,256]{2,1,0:T(8,128)(2,1)S(1)}, bf16[2,128,256]{2,1,0:T(8,128)(2,1)S(1)}, u32[]{:S(2)}, u32[]{:S(2)}) collective-permute-start(bf16[2,128,256]{2,1,0:T(8,128)(2,1)S(1)} %get-tuple-element.70), channel_id=1, source_target_pairs={{0,5},{1,4},{2,7},{3,6},{4,0},{5,1},{6,2},{7,3},{8,13},{9,12},{10,... | collective-permute-start | bytes 393224 | tf_op jit(solution)/shard_map/ppermute | solution.py:356
  31.7 0.0 collective-permute-start.18
  31.7 4.1 %all_to_all.5.refs_5_ = bf16[2,4,128,256]{3,2,1,0:T(8,128)(2,1)S(1)} all-to-all(bf16[2,4,128,256]{3,2,1,0:T(8,128)(2,1)S(1)} %get-tuple-element.69), channel_id=1, replica_groups={{0,4},{8,12},{16,20},{24,28},{1,5},{9,13},{17,21},{25,29},{2,6},{10,14}..., dimensions={0} | all-to-all | bytes 1048576 | tf_op jit(solution)/shard_map/all_to_all | solution.py:393
  35.9 0.0 collective-permute-done.17.refs_6_
  35.9 0.0 collective-permute-done.18.refs_7_
  35.9 0.1 last_tick_odd.1
  36.0 0.0 collective-permute-done.12.refs_6_
  36.0 0.0 collective-permute-done.13.refs_7_
  36.0 0.0 collective-permute-done.11.refs_5_
  36.0 1.5 %last_tick_even.1 = (bf16[4,1,4,128,256]{4,3,2,1,0:T(8,128)(2,1)}, f32[1,4,128,256]{3,2,1,0:T(8,128)}) custom-call(s32[30]{0:T(128)S(4)} %get-tuple-element.38.refs_0_, bf16[1,4,6,2,128,128]{5,4,3,2,1,0:T(8,128)(2,1)S(1)} %get-tuple-element.40.refs_1_, ...), custom_call_target="tpu_custom_call", output_to_operand_aliasing={{0}: (11, {}), {1}: (12, {})} | custom-call | tf_op jit(solution)/shard_map/last_tick_even/pallas_call | solution.py:227
  (3 shorter events, 0.0 us)
Async XLA Ops:
  1.9 6.3 %collective-permute-start.1 = (bf16[2,128,256]{2,1,0:T(8,128)(2,1)S(1)}, bf16[2,128,256]{2,1,0:T(8,128)(2,1)S(1)}, u32[]{:S(2)}, u32[]{:S(2)}) collective-permute-start(bf16[2,128,256]{2,1,0:T(8,128)(2,1)S(1)} %get-tuple-element.45), channel_id=1, source_target_pairs={{0,4},{1,2},{2,1},{3,7},{4,0},{5,6},{6,5},{7,3},{8,12},{9,10},{10,... | collective-permute-start | bytes 393224 | tf_op jit(solution)/shard_map/ppermute | solution.py:315
  2.4 7.4 %collective-permute-start = (bf16[2,128,256]{2,1,0:T(8,128)(2,1)S(1)}, bf16[2,128,256]{2,1,0:T(8,128)(2,1)S(1)}, u32[]{:S(2)}, u32[]{:S(2)}) collective-permute-start(bf16[2,128,256]{2,1,0:T(8,128)(2,1)S(1)} %get-tuple-element.39.after_ref), channel_id=1, source_target_pairs={{0,1},{1,0},{2,3},{3,2},{4,5},{5,4},{6,7},{7,6},{8,9},{9,8},{10,11... | collective-permute-start | bytes 393224 | tf_op jit(solution)/shard_map/ppermute | solution.py:314
  9.7 8.5 %collective-permute-start.2 = (bf16[4,128,256]{2,1,0:T(8,128)(2,1)S(1)}, bf16[4,128,256]{2,1,0:T(8,128)(2,1)S(1)}, u32[]{:S(2)}, u32[]{:S(2)}) collective-permute-start(bf16[4,128,256]{2,1,0:T(8,128)(2,1)S(1)} %get-tuple-element.46), channel_id=1, source_target_pairs={{0,4},{4,8},{8,12},{12,16},{16,20},{20,24},{24,28},{28,0},{1,5},{5... | collective-permute-start | bytes 786440 | tf_op jit(solution)/shard_map/ppermute | solution.py:391
  10.5 7.3 %collective-permute-start.3 = (bf16[2,128,256]{2,1,0:T(8,128)(2,1)S(1)}, bf16[2,128,256]{2,1,0:T(8,128)(2,1)S(1)}, u32[]{:S(2)}, u32[]{:S(2)}) collective-permute-start(bf16[2,128,256]{2,1,0:T(8,128)(2,1)S(1)} %get-tuple-element.50), channel_id=1, source_target_pairs={{0,5},{1,4},{2,7},{3,6},{4,9},{5,8},{6,11},{7,10},{8,13},{9,12},{1... | collective-permute-start | bytes 393224 | tf_op jit(solution)/shard_map/ppermute | solution.py:356
  12.7 5.1 %collective-permute-start.4 = (bf16[2,128,256]{2,1,0:T(8,128)(2,1)S(1)}, bf16[2,128,256]{2,1,0:T(8,128)(2,1)S(1)}, u32[]{:S(2)}, u32[]{:S(2)}) collective-permute-start(bf16[2,128,256]{2,1,0:T(8,128)(2,1)S(1)} %get-tuple-element.51), channel_id=1, source_target_pairs={{0,4},{1,6},{2,5},{3,7},{4,0},{5,10},{6,9},{7,3},{8,12},{9,14},{10... | collective-permute-start | bytes 393224 | tf_op jit(solution)/shard_map/ppermute | solution.py:356
  13.3 4.5 %collective-permute-start.5 = (bf16[2,128,256]{2,1,0:T(8,128)(2,1)S(1)}, bf16[2,128,256]{2,1,0:T(8,128)(2,1)S(1)}, u32[]{:S(2)}, u32[]{:S(2)}) collective-permute-start(bf16[2,128,256]{2,1,0:T(8,128)(2,1)S(1)} %get-tuple-element.52), channel_id=1, source_target_pairs={{0,4},{4,0},{8,12},{12,8},{16,20},{20,16},{24,28},{28,24},{1,5},{5... | collective-permute-start | bytes 393224 | tf_op jit(solution)/shard_map/ppermute | solution.py:395
  13.3 4.5 %collective-permute-start.6 = (bf16[2,128,256]{2,1,0:T(8,128)(2,1)S(1)}, bf16[2,128,256]{2,1,0:T(8,128)(2,1)S(1)}, u32[]{:S(2)}, u32[]{:S(2)}) collective-permute-start(bf16[2,128,256]{2,1,0:T(8,128)(2,1)S(1)} %get-tuple-element.53), channel_id=1, source_target_pairs={{0,4},{4,0},{8,12},{12,8},{16,20},{20,16},{24,28},{28,24},{1,5},{5... | collective-permute-start | bytes 393224 | tf_op jit(solution)/shard_map/ppermute | solution.py:395
  17.9 11.2 %collective-permute-start.14 = (bf16[4,144,256]{2,1,0:T(8,128)(2,1)S(1)}, bf16[4,144,256]{2,1,0:T(8,128)(2,1)S(1)}, u32[]{:S(2)}, u32[]{:S(2)}) collective-permute-start(bf16[4,144,256]{2,1,0:T(8,128)(2,1)S(1)} %get-tuple-element.64), channel_id=1, source_target_pairs={{0,4},{4,8},{8,12},{12,16},{16,20},{20,24},{24,28},{28,0},{1,5},{5... | collective-permute-start | bytes 884744 | tf_op jit(solution)/shard_map/ppermute | solution.py:391
  19.0 3.5 %collective-permute-start.7 = (bf16[2,128,256]{2,1,0:T(8,128)(2,1)S(1)}, bf16[2,128,256]{2,1,0:T(8,128)(2,1)S(1)}, u32[]{:S(2)}, u32[]{:S(2)}) collective-permute-start(bf16[2,128,256]{2,1,0:T(8,128)(2,1)S(1)} %get-tuple-element.55), channel_id=1, source_target_pairs={{0,4},{4,0},{8,12},{12,8},{16,20},{20,16},{24,28},{28,24},{1,5},{5... | collective-permute-start | bytes 393224 | tf_op jit(solution)/shard_map/ppermute | solution.py:395
  19.1 6.3 %collective-permute-start.9 = (bf16[2,144,256]{2,1,0:T(8,128)(2,1)S(1)}, bf16[2,144,256]{2,1,0:T(8,128)(2,1)S(1)}, u32[]{:S(2)}, u32[]{:S(2)}) collective-permute-start(bf16[2,144,256]{2,1,0:T(8,128)(2,1)S(1)} %get-tuple-element.57), channel_id=1, source_target_pairs={{0,5},{1,4},{2,7},{3,6},{4,0},{5,1},{6,2},{7,3},{8,13},{9,12},{10,... | collective-permute-start | bytes 442376 | tf_op jit(solution)/shard_map/ppermute | solution.py:356
  21.9 3.4 %collective-permute-start.10 = (bf16[2,144,256]{2,1,0:T(8,128)(2,1)S(1)}, bf16[2,144,256]{2,1,0:T(8,128)(2,1)S(1)}, u32[]{:S(2)}, u32[]{:S(2)}) collective-permute-start(bf16[2,144,256]{2,1,0:T(8,128)(2,1)S(1)} %get-tuple-element.58), channel_id=1, source_target_pairs={{0,4},{1,6},{2,5},{3,7},{4,0},{5,1},{6,2},{7,3},{8,12},{9,14},{10,... | collective-permute-start | bytes 442376 | tf_op jit(solution)/shard_map/ppermute | solution.py:356
  21.9 1.6 %collective-permute-start.8 = (bf16[2,128,256]{2,1,0:T(8,128)(2,1)S(1)}, bf16[2,128,256]{2,1,0:T(8,128)(2,1)S(1)}, u32[]{:S(2)}, u32[]{:S(2)}) collective-permute-start(bf16[2,128,256]{2,1,0:T(8,128)(2,1)S(1)} %get-tuple-element.56), channel_id=1, source_target_pairs={{0,4},{4,0},{8,12},{12,8},{16,20},{20,16},{24,28},{28,24},{1,5},{5... | collective-permute-start | bytes 393224 | tf_op jit(solution)/shard_map/ppermute | solution.py:395
  22.4 6.2 %collective-permute-start.15 = (bf16[2,128,256]{2,1,0:T(8,128)(2,1)S(1)}, bf16[2,128,256]{2,1,0:T(8,128)(2,1)S(1)}, u32[]{:S(2)}, u32[]{:S(2)}) collective-permute-start(bf16[2,128,256]{2,1,0:T(8,128)(2,1)S(1)} %get-tuple-element.65), channel_id=1, source_target_pairs={{0,4},{1,5},{2,6},{3,7},{4,9},{5,8},{6,11},{7,10},{8,12},{9,13},{1... | collective-permute-start | bytes 393224 | tf_op jit(solution)/shard_map/ppermute | solution.py:356
  23.5 5.6 %collective-permute-start.16 = (bf16[2,128,256]{2,1,0:T(8,128)(2,1)S(1)}, bf16[2,128,256]{2,1,0:T(8,128)(2,1)S(1)}, u32[]{:S(2)}, u32[]{:S(2)}) collective-permute-start(bf16[2,128,256]{2,1,0:T(8,128)(2,1)S(1)} %get-tuple-element.66), channel_id=1, source_target_pairs={{0,4},{1,5},{2,6},{3,7},{4,0},{5,10},{6,9},{7,3},{8,12},{9,13},{10... | collective-permute-start | bytes 393224 | tf_op jit(solution)/shard_map/ppermute | solution.py:356
  25.3 10.7 %collective-permute-start.11 = (bf16[4,128,256]{2,1,0:T(8,128)(2,1)S(1)}, bf16[4,128,256]{2,1,0:T(8,128)(2,1)S(1)}, u32[]{:S(2)}, u32[]{:S(2)}) collective-permute-start(bf16[4,128,256]{2,1,0:T(8,128)(2,1)S(1)} %get-tuple-element.59), channel_id=1, source_target_pairs={{0,4},{4,8},{8,12},{12,16},{16,20},{20,24},{24,28},{28,0},{1,5},{5... | collective-permute-start | bytes 786440 | tf_op jit(solution)/shard_map/ppermute | solution.py:391
  26.2 9.8 %collective-permute-start.12 = (bf16[2,144,256]{2,1,0:T(8,128)(2,1)S(1)}, bf16[2,144,256]{2,1,0:T(8,128)(2,1)S(1)}, u32[]{:S(2)}, u32[]{:S(2)}) collective-permute-start(bf16[2,144,256]{2,1,0:T(8,128)(2,1)S(1)} %get-tuple-element.60), channel_id=1, source_target_pairs={{0,4},{1,5},{2,6},{3,7},{4,9},{5,8},{6,11},{7,10},{8,12},{9,13},{1... | collective-permute-start | bytes 442376 | tf_op jit(solution)/shard_map/ppermute | solution.py:356
  28.6 7.4 %collective-permute-start.13 = (bf16[2,144,256]{2,1,0:T(8,128)(2,1)S(1)}, bf16[2,144,256]{2,1,0:T(8,128)(2,1)S(1)}, u32[]{:S(2)}, u32[]{:S(2)}) collective-permute-start(bf16[2,144,256]{2,1,0:T(8,128)(2,1)S(1)} %get-tuple-element.61), channel_id=1, source_target_pairs={{0,4},{1,5},{2,6},{3,7},{4,0},{5,10},{6,9},{7,3},{8,12},{9,13},{10... | collective-permute-start | bytes 442376 | tf_op jit(solution)/shard_map/ppermute | solution.py:356
  29.8 6.1 %collective-permute-start.17 = (bf16[2,128,256]{2,1,0:T(8,128)(2,1)S(1)}, bf16[2,128,256]{2,1,0:T(8,128)(2,1)S(1)}, u32[]{:S(2)}, u32[]{:S(2)}) collective-permute-start(bf16[2,128,256]{2,1,0:T(8,128)(2,1)S(1)} %get-tuple-element.70), channel_id=1, source_target_pairs={{0,5},{1,4},{2,7},{3,6},{4,0},{5,1},{6,2},{7,3},{8,13},{9,12},{10,... | collective-permute-start | bytes 393224 | tf_op jit(solution)/shard_map/ppermute | solution.py:356
  31.7 4.2 %collective-permute-start.18 = (bf16[2,128,256]{2,1,0:T(8,128)(2,1)S(1)}, bf16[2,128,256]{2,1,0:T(8,128)(2,1)S(1)}, u32[]{:S(2)}, u32[]{:S(2)}) collective-permute-start(bf16[2,128,256]{2,1,0:T(8,128)(2,1)S(1)} %get-tuple-element.71), channel_id=1, source_target_pairs={{0,4},{1,6},{2,5},{3,7},{4,0},{5,1},{6,2},{7,3},{8,12},{9,14},{10,... | collective-permute-start | bytes 393224 | tf_op jit(solution)/shard_map/ppermute | solution.py:356

commit v10 on v9

--- a/solution.py
+++ b/solution.py
@@ -24,8 +24,8 @@
 
 
 def write_lists(tile, plan_ref, blocks_ref, lists):
-    listed = lists[0].shape[0]
     points = blocks_ref.shape[1]
+    listed = lists[0].shape[0] // points
     parity = lax.rem(tile, 2)
     for list_ref, side in zip(lists, (UPPER - parity, parity)):
         count = plan_ref[2 * listed + side]
@@ -34,11 +34,15 @@
 
             @pl.when(live)
             def _():
-                list_ref[slot, :points] = blocks_ref[plan_ref[side * listed + slot]]
+                list_ref[slot * points : (slot + 1) * points] = blocks_ref[
+                    plan_ref[side * listed + slot]
+                ]
 
             @pl.when(jnp.logical_not(live))
             def _():
-                list_ref[slot, :points] = jnp.zeros(blocks_ref.shape[1:], list_ref.dtype)
+                list_ref[slot * points : (slot + 1) * points] = jnp.zeros(
+                    blocks_ref.shape[1:], list_ref.dtype
+                )
 
 
 def prepare_kernel(
@@ -102,14 +106,22 @@
 
 
 def fill_buffer(section, tick, source_ref, wave_refs, first_ref, second_ref, buffer):
-    blocks, listed = source_ref.shape[1], first_ref.shape[0]
+    blocks, points = source_ref.shape[1:3]
+    listed = (buffer.shape[0] - blocks) // 2
+
+    def fill(start, ref):
+        if len(ref.shape) == 2:
+            count = min(ref.shape[0] // points, blocks)
+            part = ref[: count * points].reshape(count, points, -1)
+        else:
+            part = ref[0] if len(ref.shape) == 4 else ref[...]
+        buffer[pl.ds(start, part.shape[0])] = part
+        return start + part.shape[0]
 
     def fill_wave():
         start = 0
         for wave_ref in wave_refs:
-            part = wave_ref[:, : buffer.shape[1]] if len(wave_ref.shape) == 3 else wave_ref[0]
-            buffer[start : start + part.shape[0]] = part
-            start += part.shape[0]
+            start = fill(start, wave_ref)
 
     if tick == 0:
         fill_wave()
@@ -121,9 +133,8 @@
             buffer[:blocks] = source_ref[tick - 1]
 
     parity = lax.rem(lax.axis_index("lat"), 2)
-    points = buffer.shape[1]
-    buffer[pl.ds(blocks + (1 - parity) * listed, listed)] = first_ref[:, :points]
-    buffer[pl.ds(blocks + parity * listed, listed)] = second_ref[:, :points]
+    fill(blocks + (1 - parity) * listed, first_ref)
+    fill(blocks + parity * listed, second_ref)
 
 
 def extrapolate_block(plan_ref, pattern_start, ops_ref, buffer, b):
@@ -142,6 +153,10 @@
     return real_part, imag_part
 
 
+def ids_of(plan_ref, ops_ref):
+    return (plan_ref.shape[0] - ops_ref.shape[1] * ops_ref.shape[2]) // 2 - 1
+
+
 def acts(section, parity):
     return lax.rem(section, 2) == parity
 
@@ -154,7 +169,7 @@
     echo_ref, first_ref, second_ref, *onward_refs = out_refs
     section = lax.axis_index("depth")
     tile = lax.axis_index("lat")
-    listed = first_ref.shape[0]
+    listed = ids_of(plan_ref, ops_ref)
 
     @pl.when(acts(section, parity))
     def _():
@@ -167,9 +182,13 @@
                 echo_ref[b, :, cols] = (reflect_ref[b] * part).astype(echo_ref.dtype)
         start = 0
         for onward_ref in onward_refs:
-            slot = onward_ref if len(onward_ref.shape) == 3 else onward_ref.at[1]
-            slot[:, : onward.shape[1]] = onward[start : start + slot.shape[0]]
-            start += slot.shape[0]
+            if len(onward_ref.shape) == 2:
+                rows = onward.shape[0] * onward.shape[1]
+                onward_ref[:rows] = onward[...].reshape(rows, onward.shape[2])
+            else:
+                slot = onward_ref if len(onward_ref.shape) == 3 else onward_ref.at[1]
+                slot[...] = onward[start : start + slot.shape[0]]
+                start += slot.shape[0]
 
         @pl.when(section != sections - 1)
         def _():
@@ -188,7 +207,7 @@
     del known_refs
     reflected_ref, transmitted_ref = out_refs
     section = lax.axis_index("depth")
-    listed = first_in_ref.shape[0]
+    listed = ids_of(plan_ref, ops_ref)
 
     @pl.when(acts(section, parity))
     def _():
@@ -275,7 +294,7 @@
     listed = send_ids.shape[-1]
     taken = operators.shape[2]
     wave_type = pltpu.VMEM((blocks, points, columns), WAVE)
-    list_type = pltpu.VMEM((listed, points, columns), WAVE)
+    list_type = pltpu.VMEM((listed * points, columns), WAVE)
     params = pltpu.CompilerParams(vmem_limit_bytes=VMEM_LIMIT)
     tick_cost = pl.CostEstimate(
         flops=0,
@@ -349,7 +368,7 @@
     half_types = [pltpu.VMEM((n, points, columns), WAVE) for n in (blocks // 2, blocks - blocks // 2)]
 
     def lists_of(extra):
-        return [pltpu.VMEM((listed, points + extra, columns), WAVE)] * 2
+        return [pltpu.VMEM((listed * points + extra, columns), WAVE)] * 2
 
     def exchange(lists, senders):
         routes = halo_routes(sections, tiles, senders)
@@ -370,7 +389,7 @@
                 extra = 0 if parity == ODD else 16
             if parity == ODD:
                 long = 0 if first_step or last_step else 16
-                to_next = [pltpu.VMEM((blocks, points + long, columns), WAVE)]
+                to_next = [pltpu.VMEM((blocks * points + long, columns), WAVE)]
             else:
                 to_next = [pair_type] if last_step else half_types if first_step else part_types
             outs = [wave_type, *lists_of(extra), *to_next]

time: 37.7 us -> 37.8 us (level)
  no operation moved by 1% of the time
where the time goes in v10:
time: 37.8 us; the launch traced here: 37.6 us
  starting transfers between devices  17 us (45%)
  waiting for transfers between devices  8.9 us (24%)
  Pallas kernels  6.83 us (18%)
  blocking collectives  4.15 us (11%)
  between operations  0.75 us (2%)
    ppermute x10, starting transfers between devices, exchange(): return [lax.ppermute(a, both, route) for a, route in zip(lists, routes)]  9.98 us
    ppermute x10, waiting for transfers between devices, exchange(): return [lax.ppermute(a, both, route) for a, route in zip(lists, routes)]  6.33 us
    all_to_all x1, blocking collectives, per_device(): lax.all_to_all(onward[0], 'depth', 0, 0, axis_index_groups=pairs)  4.15 us
    ppermute x1, starting transfers between devices, per_device(): first = lax.ppermute(first, both, routes[0])  4.15 us
    pallas_call x8, Pallas kernels, grouped_call(): pl.pallas_call(body, out_shape=tuple(outs), in_specs=[SMEM_SPEC] + [VMEM_...  3.94 us
    pallas_call x1, Pallas kernels, per_device(): pl.pallas_call(load_kernel, out_shape=(pltpu.VMEM(operators.shape, operat...  1.67 us
    ppermute x1, waiting for transfers between devices, per_device(): first = lax.ppermute(first, both, routes[0])  1.52 us
    ppermute x3, starting transfers between devices, per_device(): waves[EVEN] = [lax.ppermute(onward[0], 'depth', crossing)]  1.23 us
  transfers between devices with their start and end apart: 19, of which 4 were waited for; matrix products, arithmetic and copies ran while one was open for 0% of the time, Pallas kernels for 11%

profile of v10, /device:TPU:0, one launch (start us, length us, event | category | flops | bytes accessed | tf_op | source)
XLA Modules:
  0.0 37.6 jit_solution(10139235366322925048)
XLA Ops:
  0.6 1.2 %prepare.1 = (s32[30]{0:T(128)S(4)}, bf16[4,128,256]{2,1,0:T(8,128)(2,1)S(1)}, bf16[256,256]{1,0:T(8,128)(2,1)S(1)}, bf16[256,256]{1,0:T(8,128)(2,1)S(1)}) custom-call(s32[1,2,2]{2,1,0:T(2,128)} %ids_hbm.1, s32[1,2]{1,0:T(1,128)} %count_hbm.1, s32[4,6]{1,0:T(4,128)} %pattern_hbm.1, f32[1,4,128,256]{3,2,1,0:T(8,128)} %inflow_hbm.1), custom_call_target="tpu_custom_call" | custom-call | flops 131072 | bytes 1048576 | tf_op jit(solution)/shard_map/prepare/pallas_call | solution.py:307
  1.9 0.5 %collective-permute-start.1 = (bf16[256,256]{1,0:T(8,128)(2,1)S(1)}, bf16[256,256]{1,0:T(8,128)(2,1)S(1)}, u32[]{:S(2)}, u32[]{:S(2)}) collective-permute-start(bf16[256,256]{1,0:T(8,128)(2,1)S(1)} %get-tuple-element.45), channel_id=1, source_target_pairs={{0,4},{1,2},{2,1},{3,7},{4,0},{5,6},{6,5},{7,3},{8,12},{9,10},{10,... | collective-permute-start | bytes 393224 | tf_op jit(solution)/shard_map/ppermute | solution.py:334
  2.4 4.1 %collective-permute-start = (bf16[256,256]{1,0:T(8,128)(2,1)S(1)}, bf16[256,256]{1,0:T(8,128)(2,1)S(1)}, u32[]{:S(2)}, u32[]{:S(2)}) collective-permute-start(bf16[256,256]{1,0:T(8,128)(2,1)S(1)} %get-tuple-element.39.after_ref), channel_id=1, source_target_pairs={{0,1},{1,0},{2,3},{3,2},{4,5},{5,4},{6,7},{7,6},{8,9},{9,8},{10,11... | collective-permute-start | bytes 393224 | tf_op jit(solution)/shard_map/ppermute | solution.py:333
  6.5 1.7 %load.1 = (bf16[1,4,6,2,128,128]{5,4,3,2,1,0:T(8,128)(2,1)S(1)}, bf16[3,4,128,256]{3,2,1,0:T(8,128)(2,1)S(1)}, f32[4,128,128]{2,1,0:T(8,128)S(1)}, f32[4,128,128]{2,1,0:T(8,128)S(1)}) custom-call(bf16[1,4,6,2,128,128]{5,4,3,2,1,0:T(8,128)(2,1)} %ops_hbm.1, bf16[3,4,128,256]{3,2,1,0:T(8,128)(2,1)} %source_hbm.1, f32[1,4,128]{2,1,0:T(4,128)} %pass_hbm.1, ...), custom_call_target="tpu_custom_call" | custom-call | bytes 4718592 | tf_op jit(solution)/shard_map/load/pallas_call | solution.py:337
  8.2 0.0 collective-permute-done.1.refs_7_
  8.2 1.5 %collective-permute-done.refs_6_ = bf16[256,256]{1,0:T(8,128)(2,1)S(1)} collective-permute-done((bf16[256,256]{1,0:T(8,128)(2,1)S(1)}, bf16[256,256]{1,0:T(8,128)(2,1)S(1)}, u32[]{:S(2)}, u32[]{:S(2)}) %collective-permute-start) | collective-permute-done | bytes 131104 | tf_op jit(solution)/shard_map/ppermute | solution.py:333
  9.7 0.0 collective-permute-start.2
  9.7 0.8 %tick0_even.1 = (bf16[4,128,256]{2,1,0:T(8,128)(2,1)S(1)}, bf16[256,256]{1,0:T(8,128)(2,1)S(1)}, bf16[256,256]{1,0:T(8,128)(2,1)S(1)}, bf16[2,128,256]{2,1,0:T(8,128)(2,1)S(1)}, bf16[2,128,256]{2,1,0:T(8,128)(2,1)S(1)}) custom-call(s32[30]{0:T(128)S(4)} %get-tuple-element.38.refs_0_, ...), custom_call_target="tpu_custom_call", output_to_operand_aliasing={{0}: (8, {}), {1}: (9, {}), {2}: (10, {})} | custom-call | tf_op jit(solution)/shard_map/tick0_even/pallas_call | solution.py:246
  10.5 2.2 %collective-permute-start.3 = (bf16[256,256]{1,0:T(8,128)(2,1)S(1)}, bf16[256,256]{1,0:T(8,128)(2,1)S(1)}, u32[]{:S(2)}, u32[]{:S(2)}) collective-permute-start(bf16[256,256]{1,0:T(8,128)(2,1)S(1)} %get-tuple-element.50), channel_id=1, source_target_pairs={{0,5},{1,4},{2,7},{3,6},{4,9},{5,8},{6,11},{7,10},{8,13},{9,12},{1... | collective-permute-start | bytes 393224 | tf_op jit(solution)/shard_map/ppermute | solution.py:375
  12.7 0.7 %collective-permute-start.4 = (bf16[256,256]{1,0:T(8,128)(2,1)S(1)}, bf16[256,256]{1,0:T(8,128)(2,1)S(1)}, u32[]{:S(2)}, u32[]{:S(2)}) collective-permute-start(bf16[256,256]{1,0:T(8,128)(2,1)S(1)} %get-tuple-element.51), channel_id=1, source_target_pairs={{0,4},{1,6},{2,5},{3,7},{4,0},{5,10},{6,9},{7,3},{8,12},{9,14},{10... | collective-permute-start | bytes 393224 | tf_op jit(solution)/shard_map/ppermute | solution.py:375
  13.4 0.0 collective-permute-start.5
  13.4 0.5 %collective-permute-start.6 = (bf16[2,128,256]{2,1,0:T(8,128)(2,1)S(1)}, bf16[2,128,256]{2,1,0:T(8,128)(2,1)S(1)}, u32[]{:S(2)}, u32[]{:S(2)}) collective-permute-start(bf16[2,128,256]{2,1,0:T(8,128)(2,1)S(1)} %get-tuple-element.53), channel_id=1, source_target_pairs={{0,4},{4,0},{8,12},{12,8},{16,20},{20,16},{24,28},{28,24},{1,5},{5... | collective-permute-start | bytes 393224 | tf_op jit(solution)/shard_map/ppermute | solution.py:414
  13.9 4.0 %collective-permute-done.3.refs_7_.refs_6_ = bf16[256,256]{1,0:T(8,128)(2,1)S(1)} collective-permute-done((bf16[256,256]{1,0:T(8,128)(2,1)S(1)}, bf16[256,256]{1,0:T(8,128)(2,1)S(1)}, u32[]{:S(2)}, u32[]{:S(2)}) %collective-permute-start.3) | collective-permute-done | bytes 131104 | tf_op jit(solution)/shard_map/ppermute | solution.py:375
  17.9 0.0 collective-permute-done.4.refs_8_.refs_7_
  17.9 0.0 collective-permute-done.5.refs_5_
  17.9 0.0 collective-permute-done.6.refs_6_
  17.9 0.4 collective-permute-start.14
  18.3 0.0 collective-permute-done.2.refs_5_
  18.3 0.8 %tick1_even.1 = (bf16[4,128,256]{2,1,0:T(8,128)(2,1)S(1)}, bf16[272,256]{1,0:T(8,128)(2,1)S(1)}, bf16[272,256]{1,0:T(8,128)(2,1)S(1)}, bf16[2,128,256]{2,1,0:T(8,128)(2,1)S(1)}, bf16[2,128,256]{2,1,0:T(8,128)(2,1)S(1)}) custom-call(s32[30]{0:T(128)S(4)} %get-tuple-element.38.refs_0_, ...), custom_call_target="tpu_custom_call", output_to_operand_aliasing={{0}: (8, {})} | custom-call | tf_op jit(solution)/shard_map/tick1_even/pallas_call | solution.py:246
  19.0 0.1 collective-permute-start.7
  19.1 2.8 %collective-permute-start.9 = (bf16[272,256]{1,0:T(8,128)(2,1)S(1)}, bf16[272,256]{1,0:T(8,128)(2,1)S(1)}, u32[]{:S(2)}, u32[]{:S(2)}) collective-permute-start(bf16[272,256]{1,0:T(8,128)(2,1)S(1)} %get-tuple-element.57), channel_id=1, source_target_pairs={{0,5},{1,4},{2,7},{3,6},{4,0},{5,1},{6,2},{7,3},{8,13},{9,12},{10,... | collective-permute-start | bytes 417800 | tf_op jit(solution)/shard_map/ppermute | solution.py:375
  22.0 0.0 collective-permute-start.10
  22.0 0.5 %collective-permute-start.8 = (bf16[2,128,256]{2,1,0:T(8,128)(2,1)S(1)}, bf16[2,128,256]{2,1,0:T(8,128)(2,1)S(1)}, u32[]{:S(2)}, u32[]{:S(2)}) collective-permute-start(bf16[2,128,256]{2,1,0:T(8,128)(2,1)S(1)} %get-tuple-element.56), channel_id=1, source_target_pairs={{0,4},{4,0},{8,12},{12,8},{16,20},{20,16},{24,28},{28,24},{1,5},{5... | collective-permute-start | bytes 393224 | tf_op jit(solution)/shard_map/ppermute | solution.py:414
  22.5 0.0 collective-permute-done.7.refs_5_
  22.5 0.0 collective-permute-start.15
  22.5 1.0 %collective-permute-done.8.refs_6_ = bf16[2,128,256]{2,1,0:T(8,128)(2,1)S(1)} collective-permute-done((bf16[2,128,256]{2,1,0:T(8,128)(2,1)S(1)}, bf16[2,128,256]{2,1,0:T(8,128)(2,1)S(1)}, u32[]{:S(2)}, u32[]{:S(2)}) %collective-permute-start.8) | collective-permute-done | bytes 131104 | tf_op jit(solution)/shard_map/ppermute | solution.py:414
  23.5 1.9 %collective-permute-start.16 = (bf16[256,256]{1,0:T(8,128)(2,1)S(1)}, bf16[256,256]{1,0:T(8,128)(2,1)S(1)}, u32[]{:S(2)}, u32[]{:S(2)}) collective-permute-start(bf16[256,256]{1,0:T(8,128)(2,1)S(1)} %get-tuple-element.66), channel_id=1, source_target_pairs={{0,4},{1,5},{2,6},{3,7},{4,0},{5,10},{6,9},{7,3},{8,12},{9,13},{10... | collective-permute-start | bytes 393224 | tf_op jit(solution)/shard_map/ppermute | solution.py:375
  25.4 0.0 collective-permute-done.9.refs_7_
  25.4 0.0 collective-permute-done.10.refs_8_
  25.4 0.9 %collective-permute-start.11 = (bf16[512,256]{1,0:T(8,128)(2,1)S(1)}, bf16[512,256]{1,0:T(8,128)(2,1)S(1)}, u32[]{:S(2)}, u32[]{:S(2)}) collective-permute-start(bf16[512,256]{1,0:T(8,128)(2,1)S(1)} %get-tuple-element.59), channel_id=1, source_target_pairs={{0,4},{4,8},{8,12},{12,16},{16,20},{20,24},{24,28},{28,0},{1,5},{5... | collective-permute-start | bytes 786440 | tf_op jit(solution)/shard_map/ppermute | solution.py:410
  26.2 0.1 collective-permute-start.12
  26.3 2.3 %collective-permute-done.15.refs_6_ = bf16[256,256]{1,0:T(8,128)(2,1)S(1)} collective-permute-done((bf16[256,256]{1,0:T(8,128)(2,1)S(1)}, bf16[256,256]{1,0:T(8,128)(2,1)S(1)}, u32[]{:S(2)}, u32[]{:S(2)}) %collective-permute-start.15) | collective-permute-done | bytes 131104 | tf_op jit(solution)/shard_map/ppermute | solution.py:375
  28.7 0.4 collective-permute-start.13
  29.0 0.0 collective-permute-done.16.refs_7_
  29.0 0.0 collective-permute-done.14.refs_5_
  29.0 0.8 %tick2_even.1 = (bf16[4,128,256]{2,1,0:T(8,128)(2,1)S(1)}, bf16[256,256]{1,0:T(8,128)(2,1)S(1)}, bf16[256,256]{1,0:T(8,128)(2,1)S(1)}, bf16[2,4,128,256]{3,2,1,0:T(8,128)(2,1)S(1)}) custom-call(s32[30]{0:T(128)S(4)} %get-tuple-element.38.refs_0_, bf16[1,4,6,2,128,128]{5,4,3,2,1,0:T(8,128)(2,1)S(1)} %get-tuple-element.40.refs_1_, ...), custom_call_target="tpu_custom_call", output_to_operand_aliasing={{0}: (8, {})} | custom-call | tf_op jit(solution)/shard_map/tick2_even/pallas_call | solution.py:246
  29.8 2.0 %collective-permute-start.17 = (bf16[256,256]{1,0:T(8,128)(2,1)S(1)}, bf16[256,256]{1,0:T(8,128)(2,1)S(1)}, u32[]{:S(2)}, u32[]{:S(2)}) collective-permute-start(bf16[256,256]{1,0:T(8,128)(2,1)S(1)} %get-tuple-element.70), channel_id=1, source_target_pairs={{0,5},{1,4},{2,7},{3,6},{4,0},{5,1},{6,2},{7,3},{8,13},{9,12},{10,... | collective-permute-start | bytes 393224 | tf_op jit(solution)/shard_map/ppermute | solution.py:375
  31.8 0.0 collective-permute-start.18
  31.8 4.1 %all_to_all.5.refs_5_ = bf16[2,4,128,256]{3,2,1,0:T(8,128)(2,1)S(1)} all-to-all(bf16[2,4,128,256]{3,2,1,0:T(8,128)(2,1)S(1)} %get-tuple-element.69), channel_id=1, replica_groups={{0,4},{8,12},{16,20},{24,28},{1,5},{9,13},{17,21},{25,29},{2,6},{10,14}..., dimensions={0} | all-to-all | bytes 1048576 | tf_op jit(solution)/shard_map/all_to_all | solution.py:412
  35.9 0.0 collective-permute-done.17.refs_6_
  35.9 0.0 collective-permute-done.18.refs_7_
  35.9 0.1 last_tick_odd.1
  36.0 0.0 collective-permute-done.12.refs_6_
  36.1 0.0 collective-permute-done.13.refs_7_
  36.1 0.0 collective-permute-done.11.refs_5_
  36.1 1.5 %last_tick_even.1 = (bf16[4,1,4,128,256]{4,3,2,1,0:T(8,128)(2,1)}, f32[1,4,128,256]{3,2,1,0:T(8,128)}) custom-call(s32[30]{0:T(128)S(4)} %get-tuple-element.38.refs_0_, bf16[1,4,6,2,128,128]{5,4,3,2,1,0:T(8,128)(2,1)S(1)} %get-tuple-element.40.refs_1_, ...), custom_call_target="tpu_custom_call", output_to_operand_aliasing={{0}: (11, {}), {1}: (12, {})} | custom-call | tf_op jit(solution)/shard_map/last_tick_even/pallas_call | solution.py:246
  (3 shorter events, 0.0 us)
Async XLA Ops:
  1.9 6.3 %collective-permute-start.1 = (bf16[256,256]{1,0:T(8,128)(2,1)S(1)}, bf16[256,256]{1,0:T(8,128)(2,1)S(1)}, u32[]{:S(2)}, u32[]{:S(2)}) collective-permute-start(bf16[256,256]{1,0:T(8,128)(2,1)S(1)} %get-tuple-element.45), channel_id=1, source_target_pairs={{0,4},{1,2},{2,1},{3,7},{4,0},{5,6},{6,5},{7,3},{8,12},{9,10},{10,... | collective-permute-start | bytes 393224 | tf_op jit(solution)/shard_map/ppermute | solution.py:334
  2.4 7.4 %collective-permute-start = (bf16[256,256]{1,0:T(8,128)(2,1)S(1)}, bf16[256,256]{1,0:T(8,128)(2,1)S(1)}, u32[]{:S(2)}, u32[]{:S(2)}) collective-permute-start(bf16[256,256]{1,0:T(8,128)(2,1)S(1)} %get-tuple-element.39.after_ref), channel_id=1, source_target_pairs={{0,1},{1,0},{2,3},{3,2},{4,5},{5,4},{6,7},{7,6},{8,9},{9,8},{10,11... | collective-permute-start | bytes 393224 | tf_op jit(solution)/shard_map/ppermute | solution.py:333
  9.7 8.5 %collective-permute-start.2 = (bf16[512,256]{1,0:T(8,128)(2,1)S(1)}, bf16[512,256]{1,0:T(8,128)(2,1)S(1)}, u32[]{:S(2)}, u32[]{:S(2)}) collective-permute-start(bf16[512,256]{1,0:T(8,128)(2,1)S(1)} %get-tuple-element.46), channel_id=1, source_target_pairs={{0,4},{4,8},{8,12},{12,16},{16,20},{20,24},{24,28},{28,0},{1,5},{5... | collective-permute-start | bytes 786440 | tf_op jit(solution)/shard_map/ppermute | solution.py:410
  10.5 7.3 %collective-permute-start.3 = (bf16[256,256]{1,0:T(8,128)(2,1)S(1)}, bf16[256,256]{1,0:T(8,128)(2,1)S(1)}, u32[]{:S(2)}, u32[]{:S(2)}) collective-permute-start(bf16[256,256]{1,0:T(8,128)(2,1)S(1)} %get-tuple-element.50), channel_id=1, source_target_pairs={{0,5},{1,4},{2,7},{3,6},{4,9},{5,8},{6,11},{7,10},{8,13},{9,12},{1... | collective-permute-start | bytes 393224 | tf_op jit(solution)/shard_map/ppermute | solution.py:375
  12.7 5.2 %collective-permute-start.4 = (bf16[256,256]{1,0:T(8,128)(2,1)S(1)}, bf16[256,256]{1,0:T(8,128)(2,1)S(1)}, u32[]{:S(2)}, u32[]{:S(2)}) collective-permute-start(bf16[256,256]{1,0:T(8,128)(2,1)S(1)} %get-tuple-element.51), channel_id=1, source_target_pairs={{0,4},{1,6},{2,5},{3,7},{4,0},{5,10},{6,9},{7,3},{8,12},{9,14},{10... | collective-permute-start | bytes 393224 | tf_op jit(solution)/shard_map/ppermute | solution.py:375
  13.4 4.5 %collective-permute-start.5 = (bf16[2,128,256]{2,1,0:T(8,128)(2,1)S(1)}, bf16[2,128,256]{2,1,0:T(8,128)(2,1)S(1)}, u32[]{:S(2)}, u32[]{:S(2)}) collective-permute-start(bf16[2,128,256]{2,1,0:T(8,128)(2,1)S(1)} %get-tuple-element.52), channel_id=1, source_target_pairs={{0,4},{4,0},{8,12},{12,8},{16,20},{20,16},{24,28},{28,24},{1,5},{5... | collective-permute-start | bytes 393224 | tf_op jit(solution)/shard_map/ppermute | solution.py:414
  13.4 4.5 %collective-permute-start.6 = (bf16[2,128,256]{2,1,0:T(8,128)(2,1)S(1)}, bf16[2,128,256]{2,1,0:T(8,128)(2,1)S(1)}, u32[]{:S(2)}, u32[]{:S(2)}) collective-permute-start(bf16[2,128,256]{2,1,0:T(8,128)(2,1)S(1)} %get-tuple-element.53), channel_id=1, source_target_pairs={{0,4},{4,0},{8,12},{12,8},{16,20},{20,16},{24,28},{28,24},{1,5},{5... | collective-permute-start | bytes 393224 | tf_op jit(solution)/shard_map/ppermute | solution.py:414
  17.9 11.1 %collective-permute-start.14 = (bf16[528,256]{1,0:T(8,128)(2,1)S(1)}, bf16[528,256]{1,0:T(8,128)(2,1)S(1)}, u32[]{:S(2)}, u32[]{:S(2)}) collective-permute-start(bf16[528,256]{1,0:T(8,128)(2,1)S(1)} %get-tuple-element.64), channel_id=1, source_target_pairs={{0,4},{4,8},{8,12},{12,16},{16,20},{20,24},{24,28},{28,0},{1,5},{5... | collective-permute-start | bytes 811016 | tf_op jit(solution)/shard_map/ppermute | solution.py:410
  19.0 3.4 %collective-permute-start.7 = (bf16[2,128,256]{2,1,0:T(8,128)(2,1)S(1)}, bf16[2,128,256]{2,1,0:T(8,128)(2,1)S(1)}, u32[]{:S(2)}, u32[]{:S(2)}) collective-permute-start(bf16[2,128,256]{2,1,0:T(8,128)(2,1)S(1)} %get-tuple-element.55), channel_id=1, source_target_pairs={{0,4},{4,0},{8,12},{12,8},{16,20},{20,16},{24,28},{28,24},{1,5},{5... | collective-permute-start | bytes 393224 | tf_op jit(solution)/shard_map/ppermute | solution.py:414
  19.1 6.3 %collective-permute-start.9 = (bf16[272,256]{1,0:T(8,128)(2,1)S(1)}, bf16[272,256]{1,0:T(8,128)(2,1)S(1)}, u32[]{:S(2)}, u32[]{:S(2)}) collective-permute-start(bf16[272,256]{1,0:T(8,128)(2,1)S(1)} %get-tuple-element.57), channel_id=1, source_target_pairs={{0,5},{1,4},{2,7},{3,6},{4,0},{5,1},{6,2},{7,3},{8,13},{9,12},{10,... | collective-permute-start | bytes 417800 | tf_op jit(solution)/shard_map/ppermute | solution.py:375
  22.0 3.4 %collective-permute-start.10 = (bf16[272,256]{1,0:T(8,128)(2,1)S(1)}, bf16[272,256]{1,0:T(8,128)(2,1)S(1)}, u32[]{:S(2)}, u32[]{:S(2)}) collective-permute-start(bf16[272,256]{1,0:T(8,128)(2,1)S(1)} %get-tuple-element.58), channel_id=1, source_target_pairs={{0,4},{1,6},{2,5},{3,7},{4,0},{5,1},{6,2},{7,3},{8,12},{9,14},{10,... | collective-permute-start | bytes 417800 | tf_op jit(solution)/shard_map/ppermute | solution.py:375
  22.0 1.5 %collective-permute-start.8 = (bf16[2,128,256]{2,1,0:T(8,128)(2,1)S(1)}, bf16[2,128,256]{2,1,0:T(8,128)(2,1)S(1)}, u32[]{:S(2)}, u32[]{:S(2)}) collective-permute-start(bf16[2,128,256]{2,1,0:T(8,128)(2,1)S(1)} %get-tuple-element.56), channel_id=1, source_target_pairs={{0,4},{4,0},{8,12},{12,8},{16,20},{20,16},{24,28},{28,24},{1,5},{5... | collective-permute-start | bytes 393224 | tf_op jit(solution)/shard_map/ppermute | solution.py:414
  22.5 6.2 %collective-permute-start.15 = (bf16[256,256]{1,0:T(8,128)(2,1)S(1)}, bf16[256,256]{1,0:T(8,128)(2,1)S(1)}, u32[]{:S(2)}, u32[]{:S(2)}) collective-permute-start(bf16[256,256]{1,0:T(8,128)(2,1)S(1)} %get-tuple-element.65), channel_id=1, source_target_pairs={{0,4},{1,5},{2,6},{3,7},{4,9},{5,8},{6,11},{7,10},{8,12},{9,13},{1... | collective-permute-start | bytes 393224 | tf_op jit(solution)/shard_map/ppermute | solution.py:375
  23.5 5.5 %collective-permute-start.16 = (bf16[256,256]{1,0:T(8,128)(2,1)S(1)}, bf16[256,256]{1,0:T(8,128)(2,1)S(1)}, u32[]{:S(2)}, u32[]{:S(2)}) collective-permute-start(bf16[256,256]{1,0:T(8,128)(2,1)S(1)} %get-tuple-element.66), channel_id=1, source_target_pairs={{0,4},{1,5},{2,6},{3,7},{4,0},{5,10},{6,9},{7,3},{8,12},{9,13},{10... | collective-permute-start | bytes 393224 | tf_op jit(solution)/shard_map/ppermute | solution.py:375
  25.4 10.7 %collective-permute-start.11 = (bf16[512,256]{1,0:T(8,128)(2,1)S(1)}, bf16[512,256]{1,0:T(8,128)(2,1)S(1)}, u32[]{:S(2)}, u32[]{:S(2)}) collective-permute-start(bf16[512,256]{1,0:T(8,128)(2,1)S(1)} %get-tuple-element.59), channel_id=1, source_target_pairs={{0,4},{4,8},{8,12},{12,16},{16,20},{20,24},{24,28},{28,0},{1,5},{5... | collective-permute-start | bytes 786440 | tf_op jit(solution)/shard_map/ppermute | solution.py:410
  26.2 9.8 %collective-permute-start.12 = (bf16[272,256]{1,0:T(8,128)(2,1)S(1)}, bf16[272,256]{1,0:T(8,128)(2,1)S(1)}, u32[]{:S(2)}, u32[]{:S(2)}) collective-permute-start(bf16[272,256]{1,0:T(8,128)(2,1)S(1)} %get-tuple-element.60), channel_id=1, source_target_pairs={{0,4},{1,5},{2,6},{3,7},{4,9},{5,8},{6,11},{7,10},{8,12},{9,13},{1... | collective-permute-start | bytes 417800 | tf_op jit(solution)/shard_map/ppermute | solution.py:375
  28.7 7.4 %collective-permute-start.13 = (bf16[272,256]{1,0:T(8,128)(2,1)S(1)}, bf16[272,256]{1,0:T(8,128)(2,1)S(1)}, u32[]{:S(2)}, u32[]{:S(2)}) collective-permute-start(bf16[272,256]{1,0:T(8,128)(2,1)S(1)} %get-tuple-element.61), channel_id=1, source_target_pairs={{0,4},{1,5},{2,6},{3,7},{4,0},{5,10},{6,9},{7,3},{8,12},{9,13},{10... | collective-permute-start | bytes 417800 | tf_op jit(solution)/shard_map/ppermute | solution.py:375
  29.8 6.1 %collective-permute-start.17 = (bf16[256,256]{1,0:T(8,128)(2,1)S(1)}, bf16[256,256]{1,0:T(8,128)(2,1)S(1)}, u32[]{:S(2)}, u32[]{:S(2)}) collective-permute-start(bf16[256,256]{1,0:T(8,128)(2,1)S(1)} %get-tuple-element.70), channel_id=1, source_target_pairs={{0,5},{1,4},{2,7},{3,6},{4,0},{5,1},{6,2},{7,3},{8,13},{9,12},{10,... | collective-permute-start | bytes 393224 | tf_op jit(solution)/shard_map/ppermute | solution.py:375
  31.8 4.2 %collective-permute-start.18 = (bf16[256,256]{1,0:T(8,128)(2,1)S(1)}, bf16[256,256]{1,0:T(8,128)(2,1)S(1)}, u32[]{:S(2)}, u32[]{:S(2)}) collective-permute-start(bf16[256,256]{1,0:T(8,128)(2,1)S(1)} %get-tuple-element.71), channel_id=1, source_target_pairs={{0,4},{1,6},{2,5},{3,7},{4,0},{5,1},{6,2},{7,3},{8,12},{9,14},{10,... | collective-permute-start | bytes 393224 | tf_op jit(solution)/shard_map/ppermute | solution.py:375

commit v11 on v10

--- a/solution.py
+++ b/solution.py
@@ -45,9 +45,28 @@
                 )
 
 
+def start_rows(hbm_refs, rows_refs, sems):
+    copies = [
+        pltpu.make_async_copy(source, target, sems.at[i])
+        for i, (source, target) in enumerate(zip(hbm_refs, rows_refs))
+    ]
+    for copy in copies:
+        copy.start()
+    return copies
+
+
+def write_columns(copies, rows_refs, columns_refs):
+    for copy, rows, columns_ref in zip(copies, rows_refs, columns_refs):
+        copy.wait()
+        for b in range(columns_ref.shape[0]):
+            row = rows[0, pl.ds(b, 1), :]
+            columns_ref[b] = jnp.broadcast_to(row, columns_ref.shape[1:]).T
+
+
 def prepare_kernel(
-    ids_hbm, count_hbm, pattern_hbm, inflow_hbm, plan_ref, wave_ref, first_ref, second_ref,
-    ids, count, pattern, landed, small_sems, sems,
+    ids_hbm, count_hbm, pattern_hbm, inflow_hbm, pass_hbm, reflect_hbm,
+    plan_ref, wave_ref, first_ref, second_ref, pass_ref, reflect_ref,
+    ids, count, pattern, landed, small_sems, sems, pass_rows, reflect_rows, rows_sems,
 ):
     blocks = wave_ref.shape[0]
     small = [
@@ -77,31 +96,27 @@
         wave_ref[b] = landed[b].astype(wave_ref.dtype)
     write_lists(lax.axis_index("lat"), plan_ref, wave_ref, (first_ref, second_ref))
 
+    @pl.when(lax.rem(lax.axis_index("depth"), 2) == 1)
+    def _():
+        rows = (pass_rows, reflect_rows)
+        copies = start_rows((pass_hbm, reflect_hbm), rows, rows_sems)
+        write_columns(copies, rows, (pass_ref, reflect_ref))
+
 
 def load_kernel(
-    ops_hbm, source_hbm, pass_hbm, reflect_hbm, after_ref,
-    ops_ref, source_ref, pass_ref, reflect_ref, pass_rows, reflect_rows, sems,
+    ops_hbm, source_hbm, pass_hbm, reflect_hbm, known_pass_ref, known_reflect_ref,
+    ops_ref, source_ref, pass_ref, reflect_ref, pass_rows, reflect_rows, rows_sems, sems,
 ):
-    del after_ref
-    copies = [
-        pltpu.make_async_copy(source, target, sems.at[i])
-        for i, (source, target) in enumerate(
-            (
-                (pass_hbm, pass_rows),
-                (reflect_hbm, reflect_rows),
-                (ops_hbm, ops_ref),
-                (source_hbm, source_ref),
-            )
-        )
-    ]
+    del known_pass_ref, known_reflect_ref
+    copies = start_rows((ops_hbm, source_hbm), (ops_ref, source_ref), sems)
+
+    @pl.when(lax.rem(lax.axis_index("depth"), 2) == 0)
+    def _():
+        rows = (pass_rows, reflect_rows)
+        small = start_rows((pass_hbm, reflect_hbm), rows, rows_sems)
+        write_columns(small, rows, (pass_ref, reflect_ref))
+
     for copy in copies:
-        copy.start()
-    for copy, rows, columns_ref in zip(copies, (pass_rows, reflect_rows), (pass_ref, reflect_ref)):
-        copy.wait()
-        for b in range(columns_ref.shape[0]):
-            row = rows[0, pl.ds(b, 1), :]
-            columns_ref[b] = jnp.broadcast_to(row, columns_ref.shape[1:]).T
-    for copy in copies[2:]:
         copy.wait()
 
 
@@ -304,16 +319,25 @@
     both = ("depth", "lat")
     deeper = [(s, (s + 1) % sections) for s in range(sections)]
 
-    plan, wave, first, second = pl.pallas_call(
+    column_type = pltpu.VMEM((blocks, points, columns // 2), jnp.float32)
+    rows_scratch = [
+        pltpu.VMEM(transmission.shape, transmission.dtype),
+        pltpu.VMEM(reflectivity.shape, reflectivity.dtype),
+        pltpu.SemaphoreType.DMA((2,)),
+    ]
+    coefficients = [in_hbm(transmission), in_hbm(reflectivity)]
+    plan, wave, first, second, *coefficient_columns = pl.pallas_call(
         prepare_kernel,
         out_shape=(
             pltpu.SMEM((2 * (listed + 1) + blocks * taken,), jnp.int32),
             wave_type,
             list_type,
             list_type,
+            column_type,
+            column_type,
         ),
-        in_specs=[ANY_SPEC] * 4,
-        out_specs=(SMEM_SPEC,) + (VMEM_SPEC,) * 3,
+        in_specs=[ANY_SPEC] * 6,
+        out_specs=(SMEM_SPEC,) + (VMEM_SPEC,) * 5,
         scratch_shapes=[
             pltpu.SMEM(send_ids.shape, jnp.int32),
             pltpu.SMEM(send_count.shape, jnp.int32),
@@ -321,19 +345,18 @@
             pltpu.VMEM((blocks, points, columns), inflow.dtype),
             pltpu.SemaphoreType.DMA((3,)),
             pltpu.SemaphoreType.DMA((blocks,)),
+            *rows_scratch,
         ],
         compiler_params=params,
         cost_estimate=pl.CostEstimate(
             flops=inflow.size, bytes_accessed=8 * inflow.size, transcendentals=0
         ),
         name="prepare",
-    )(*map(in_hbm, (send_ids, send_count, pattern, inflow)))
-    loaded_first = first
+    )(*map(in_hbm, (send_ids, send_count, pattern, inflow)), *coefficients)
     routes = swap_routes(sections, tiles)
     first = lax.ppermute(first, both, routes[0])
     second = lax.ppermute(second, both, routes[1])
 
-    column_type = pltpu.VMEM((blocks, points, columns // 2), jnp.float32)
     fixed = pl.pallas_call(
         load_kernel,
         out_shape=(
@@ -342,19 +365,16 @@
             column_type,
             column_type,
         ),
-        in_specs=[ANY_SPEC] * 4 + [VMEM_SPEC],
+        in_specs=[ANY_SPEC] * 4 + [VMEM_SPEC] * 2,
         out_specs=(VMEM_SPEC,) * 4,
-        scratch_shapes=[
-            pltpu.VMEM(transmission.shape, transmission.dtype),
-            pltpu.VMEM(reflectivity.shape, reflectivity.dtype),
-            pltpu.SemaphoreType.DMA((4,)),
-        ],
+        input_output_aliases={4: 2, 5: 3},
+        scratch_shapes=[*rows_scratch, pltpu.SemaphoreType.DMA((2,))],
         compiler_params=params,
         cost_estimate=pl.CostEstimate(
             flops=0, bytes_accessed=4 * (operators.size + source.size), transcendentals=0
         ),
         name="load",
-    )(*map(in_hbm, (operators, source, transmission, reflectivity)), in_vmem(loaded_first))
+    )(in_hbm(operators), in_hbm(source), *coefficients, *map(in_vmem, coefficient_columns))
     fixed = [plan, *fixed]
 
     buffer_type = pltpu.VMEM((blocks + 2 * listed, points, columns), WAVE)

time: 37.8 us -> 38.3 us (1.013)
  starting transfers between devices: 17 us -> 18.7 us
  waiting for transfers between devices: 8.9 us -> 7.46 us
    ppermute x3, starting transfers between devices: 1.23 us -> 3.22 us  [per_device(): waves[EVEN] = [lax.ppermute(onward[0], 'depth', crossing)]]
    ppermute x10, waiting for transfers between devices: 6.33 us -> 4.35 us  [exchange(): return [lax.ppermute(a, both, route) for a, route in zip(lists, routes)]]
    ppermute x1, starting transfers between devices: 4.15 us -> 3.09 us  [per_device(): first = lax.ppermute(first, both, routes[0])]
    ppermute x10, starting transfers between devices: 9.98 us -> 10.8 us  [exchange(): return [lax.ppermute(a, both, route) for a, route in zip(lists, routes)]]
    ppermute x1, waiting for transfers between devices: 1.52 us -> 2.05 us  [per_device(): first = lax.ppermute(first, both, routes[0])]
where the time goes in v11:
time: 38.3 us; the launch traced here: 38 us
  starting transfers between devices  18.7 us (49%)
  waiting for transfers between devices  7.46 us (19%)
  Pallas kernels  6.88 us (18%)
  blocking collectives  4.15 us (11%)
  between operations  0.74 us (2%)
    ppermute x10, starting transfers between devices, exchange(): return [lax.ppermute(a, both, route) for a, route in zip(lists, routes)]  10.8 us
    ppermute x10, waiting for transfers between devices, exchange(): return [lax.ppermute(a, both, route) for a, route in zip(lists, routes)]  4.35 us
    all_to_all x1, blocking collectives, per_device(): lax.all_to_all(onward[0], 'depth', 0, 0, axis_index_groups=pairs)  4.15 us
    pallas_call x8, Pallas kernels, grouped_call(): pl.pallas_call(body, out_shape=tuple(outs), in_specs=[SMEM_SPEC] + [VMEM_...  3.94 us
    ppermute x3, starting transfers between devices, per_device(): waves[EVEN] = [lax.ppermute(onward[0], 'depth', crossing)]  3.22 us
    ppermute x1, starting transfers between devices, per_device(): first = lax.ppermute(first, both, routes[0])  3.09 us
    ppermute x1, waiting for transfers between devices, per_device(): first = lax.ppermute(first, both, routes[0])  2.05 us
    pallas_call x1, Pallas kernels, per_device(): pl.pallas_call(load_kernel, out_shape=(pltpu.VMEM(operators.shape, operat...  1.7 us
  transfers between devices with their start and end apart: 19, of which 4 were waited for; matrix products, arithmetic and copies ran while one was open for 0% of the time, Pallas kernels for 11%

profile of v11, /device:TPU:0, one launch (start us, length us, event | category | flops | bytes accessed | tf_op | source)
XLA Modules:
  0.0 38.0 jit_solution(4803217042696523846)
XLA Ops:
  0.6 1.2 %prepare.1 = (s32[30]{0:T(128)S(4)}, bf16[4,128,256]{2,1,0:T(8,128)(2,1)S(1)}, bf16[256,256]{1,0:T(8,128)(2,1)S(1)}, bf16[256,256]{1,0:T(8,128)(2,1)S(1)}, f32[4...) custom-call(s32[1,2,2]{2,1,0:T(2,128)} %ids_hbm.1, s32[1,2]{1,0:T(1,128)} %count_hbm.1, s32[4,6]{1,0:T(4,128)} %pattern_hbm.1, ...), custom_call_target="tpu_custom_call" | custom-call | flops 131072 | bytes 1048576 | tf_op jit(solution)/shard_map/prepare/pallas_call | solution.py:329
  1.9 3.1 %collective-permute-start = (bf16[256,256]{1,0:T(8,128)(2,1)S(1)}, bf16[256,256]{1,0:T(8,128)(2,1)S(1)}, u32[]{:S(2)}, u32[]{:S(2)}) collective-permute-start(bf16[256,256]{1,0:T(8,128)(2,1)S(1)} %get-tuple-element.48), channel_id=1, source_target_pairs={{0,1},{1,0},{2,3},{3,2},{4,5},{5,4},{6,7},{7,6},{8,9},{9,8},{10,11... | collective-permute-start | bytes 393224 | tf_op jit(solution)/shard_map/ppermute | solution.py:357
  5.0 0.5 %collective-permute-start.1 = (bf16[256,256]{1,0:T(8,128)(2,1)S(1)}, bf16[256,256]{1,0:T(8,128)(2,1)S(1)}, u32[]{:S(2)}, u32[]{:S(2)}) collective-permute-start(bf16[256,256]{1,0:T(8,128)(2,1)S(1)} %get-tuple-element.49), channel_id=1, source_target_pairs={{0,4},{1,2},{2,1},{3,7},{4,0},{5,6},{6,5},{7,3},{8,12},{9,10},{10,... | collective-permute-start | bytes 393224 | tf_op jit(solution)/shard_map/ppermute | solution.py:358
  5.5 1.7 %load.1 = (bf16[1,4,6,2,128,128]{5,4,3,2,1,0:T(8,128)(2,1)S(1)}, bf16[3,4,128,256]{3,2,1,0:T(8,128)(2,1)S(1)}, f32[4,128,128]{2,1,0:T(8,128)S(1)}, f32[4,128,128]{2,1,0:T(8,128)S(1)}) custom-call(bf16[1,4,6,2,128,128]{5,4,3,2,1,0:T(8,128)(2,1)} %ops_hbm.1, bf16[3,4,128,256]{3,2,1,0:T(8,128)(2,1)} %source_hbm.1, ...), custom_call_target="tpu_custom_call", output_to_operand_aliasing={{2}: (4, {}), {3}: (5, {})} | custom-call | bytes 4718592 | tf_op jit(solution)/shard_map/load/pallas_call | solution.py:360
  7.2 2.1 %collective-permute-done.refs_6_ = bf16[256,256]{1,0:T(8,128)(2,1)S(1)} collective-permute-done((bf16[256,256]{1,0:T(8,128)(2,1)S(1)}, bf16[256,256]{1,0:T(8,128)(2,1)S(1)}, u32[]{:S(2)}, u32[]{:S(2)}) %collective-permute-start) | collective-permute-done | bytes 131104 | tf_op jit(solution)/shard_map/ppermute | solution.py:357
  9.2 0.0 collective-permute-done.1.refs_7_
  9.2 0.9 %collective-permute-start.2 = (bf16[512,256]{1,0:T(8,128)(2,1)S(1)}, bf16[512,256]{1,0:T(8,128)(2,1)S(1)}, u32[]{:S(2)}, u32[]{:S(2)}) collective-permute-start(bf16[512,256]{1,0:T(8,128)(2,1)S(1)} %get-tuple-element.50), channel_id=1, source_target_pairs={{0,4},{4,8},{8,12},{12,16},{16,20},{20,24},{24,28},{28,0},{1,5},{5... | collective-permute-start | bytes 786440 | tf_op jit(solution)/shard_map/ppermute | solution.py:430
  10.2 0.8 %tick0_even.1 = (bf16[4,128,256]{2,1,0:T(8,128)(2,1)S(1)}, bf16[256,256]{1,0:T(8,128)(2,1)S(1)}, bf16[256,256]{1,0:T(8,128)(2,1)S(1)}, bf16[2,128,256]{2,1,0:T(8,128)(2,1)S(1)}, bf16[2,128,256]{2,1,0:T(8,128)(2,1)S(1)}) custom-call(s32[30]{0:T(128)S(4)} %get-tuple-element.40.refs_0_, ...), custom_call_target="tpu_custom_call", output_to_operand_aliasing={{0}: (8, {}), {1}: (9, {}), {2}: (10, {})} | custom-call | tf_op jit(solution)/shard_map/tick0_even/pallas_call | solution.py:261
  11.0 2.5 %collective-permute-start.3 = (bf16[256,256]{1,0:T(8,128)(2,1)S(1)}, bf16[256,256]{1,0:T(8,128)(2,1)S(1)}, u32[]{:S(2)}, u32[]{:S(2)}) collective-permute-start(bf16[256,256]{1,0:T(8,128)(2,1)S(1)} %get-tuple-element.54), channel_id=1, source_target_pairs={{0,5},{1,4},{2,7},{3,6},{4,9},{5,8},{6,11},{7,10},{8,13},{9,12},{1... | collective-permute-start | bytes 393224 | tf_op jit(solution)/shard_map/ppermute | solution.py:395
  13.5 1.4 %collective-permute-start.4 = (bf16[256,256]{1,0:T(8,128)(2,1)S(1)}, bf16[256,256]{1,0:T(8,128)(2,1)S(1)}, u32[]{:S(2)}, u32[]{:S(2)}) collective-permute-start(bf16[256,256]{1,0:T(8,128)(2,1)S(1)} %get-tuple-element.55), channel_id=1, source_target_pairs={{0,4},{1,6},{2,5},{3,7},{4,0},{5,10},{6,9},{7,3},{8,12},{9,14},{10... | collective-permute-start | bytes 393224 | tf_op jit(solution)/shard_map/ppermute | solution.py:395
  14.9 0.0 collective-permute-start.5
  14.9 0.5 %collective-permute-start.6 = (bf16[2,128,256]{2,1,0:T(8,128)(2,1)S(1)}, bf16[2,128,256]{2,1,0:T(8,128)(2,1)S(1)}, u32[]{:S(2)}, u32[]{:S(2)}) collective-permute-start(bf16[2,128,256]{2,1,0:T(8,128)(2,1)S(1)} %get-tuple-element.57), channel_id=1, source_target_pairs={{0,4},{4,0},{8,12},{12,8},{16,20},{20,16},{24,28},{28,24},{1,5},{5... | collective-permute-start | bytes 393224 | tf_op jit(solution)/shard_map/ppermute | solution.py:434
  15.4 2.0 %collective-permute-done.3.refs_7_.refs_6_ = bf16[256,256]{1,0:T(8,128)(2,1)S(1)} collective-permute-done((bf16[256,256]{1,0:T(8,128)(2,1)S(1)}, bf16[256,256]{1,0:T(8,128)(2,1)S(1)}, u32[]{:S(2)}, u32[]{:S(2)}) %collective-permute-start.3) | collective-permute-done | bytes 131104 | tf_op jit(solution)/shard_map/ppermute | solution.py:395
  17.4 0.0 collective-permute-done.4.refs_8_.refs_7_
  17.4 0.0 collective-permute-done.5.refs_5_
  17.4 0.0 collective-permute-done.6.refs_6_
  17.4 1.4 %collective-permute-start.14 = (bf16[528,256]{1,0:T(8,128)(2,1)S(1)}, bf16[528,256]{1,0:T(8,128)(2,1)S(1)}, u32[]{:S(2)}, u32[]{:S(2)}) collective-permute-start(bf16[528,256]{1,0:T(8,128)(2,1)S(1)} %get-tuple-element.68), channel_id=1, source_target_pairs={{0,4},{4,8},{8,12},{12,16},{16,20},{20,24},{24,28},{28,0},{1,5},{5... | collective-permute-start | bytes 811016 | tf_op jit(solution)/shard_map/ppermute | solution.py:430
  18.8 0.0 collective-permute-done.2.refs_5_
  18.8 0.8 %tick1_even.1 = (bf16[4,128,256]{2,1,0:T(8,128)(2,1)S(1)}, bf16[272,256]{1,0:T(8,128)(2,1)S(1)}, bf16[272,256]{1,0:T(8,128)(2,1)S(1)}, bf16[2,128,256]{2,1,0:T(8,128)(2,1)S(1)}, bf16[2,128,256]{2,1,0:T(8,128)(2,1)S(1)}) custom-call(s32[30]{0:T(128)S(4)} %get-tuple-element.40.refs_0_, ...), custom_call_target="tpu_custom_call", output_to_operand_aliasing={{0}: (8, {})} | custom-call | tf_op jit(solution)/shard_map/tick1_even/pallas_call | solution.py:261
  19.6 0.1 collective-permute-start.7
  19.7 3.2 %collective-permute-start.9 = (bf16[272,256]{1,0:T(8,128)(2,1)S(1)}, bf16[272,256]{1,0:T(8,128)(2,1)S(1)}, u32[]{:S(2)}, u32[]{:S(2)}) collective-permute-start(bf16[272,256]{1,0:T(8,128)(2,1)S(1)} %get-tuple-element.61), channel_id=1, source_target_pairs={{0,5},{1,4},{2,7},{3,6},{4,0},{5,1},{6,2},{7,3},{8,13},{9,12},{10,... | collective-permute-start | bytes 417800 | tf_op jit(solution)/shard_map/ppermute | solution.py:395
  22.9 0.0 collective-permute-start.10
  22.9 0.5 %collective-permute-start.8 = (bf16[2,128,256]{2,1,0:T(8,128)(2,1)S(1)}, bf16[2,128,256]{2,1,0:T(8,128)(2,1)S(1)}, u32[]{:S(2)}, u32[]{:S(2)}) collective-permute-start(bf16[2,128,256]{2,1,0:T(8,128)(2,1)S(1)} %get-tuple-element.60), channel_id=1, source_target_pairs={{0,4},{4,0},{8,12},{12,8},{16,20},{20,16},{24,28},{28,24},{1,5},{5... | collective-permute-start | bytes 393224 | tf_op jit(solution)/shard_map/ppermute | solution.py:434
  23.4 0.0 collective-permute-done.7.refs_5_
  23.4 0.0 collective-permute-start.15
  23.4 1.0 %collective-permute-done.8.refs_6_ = bf16[2,128,256]{2,1,0:T(8,128)(2,1)S(1)} collective-permute-done((bf16[2,128,256]{2,1,0:T(8,128)(2,1)S(1)}, bf16[2,128,256]{2,1,0:T(8,128)(2,1)S(1)}, u32[]{:S(2)}, u32[]{:S(2)}) %collective-permute-start.8) | collective-permute-done | bytes 131104 | tf_op jit(solution)/shard_map/ppermute | solution.py:434
  24.4 1.5 %collective-permute-start.16 = (bf16[256,256]{1,0:T(8,128)(2,1)S(1)}, bf16[256,256]{1,0:T(8,128)(2,1)S(1)}, u32[]{:S(2)}, u32[]{:S(2)}) collective-permute-start(bf16[256,256]{1,0:T(8,128)(2,1)S(1)} %get-tuple-element.70), channel_id=1, source_target_pairs={{0,4},{1,5},{2,6},{3,7},{4,0},{5,10},{6,9},{7,3},{8,12},{9,13},{10... | collective-permute-start | bytes 393224 | tf_op jit(solution)/shard_map/ppermute | solution.py:395
  25.9 0.0 collective-permute-done.9.refs_7_
  25.9 0.0 collective-permute-done.10.refs_8_
  26.0 0.9 %collective-permute-start.11 = (bf16[512,256]{1,0:T(8,128)(2,1)S(1)}, bf16[512,256]{1,0:T(8,128)(2,1)S(1)}, u32[]{:S(2)}, u32[]{:S(2)}) collective-permute-start(bf16[512,256]{1,0:T(8,128)(2,1)S(1)} %get-tuple-element.63), channel_id=1, source_target_pairs={{0,4},{4,8},{8,12},{12,16},{16,20},{20,24},{24,28},{28,0},{1,5},{5... | collective-permute-start | bytes 786440 | tf_op jit(solution)/shard_map/ppermute | solution.py:430
  26.8 0.4 %collective-permute-start.12 = (bf16[272,256]{1,0:T(8,128)(2,1)S(1)}, bf16[272,256]{1,0:T(8,128)(2,1)S(1)}, u32[]{:S(2)}, u32[]{:S(2)}) collective-permute-start(bf16[272,256]{1,0:T(8,128)(2,1)S(1)} %get-tuple-element.64), channel_id=1, source_target_pairs={{0,4},{1,5},{2,6},{3,7},{4,9},{5,8},{6,11},{7,10},{8,12},{9,13},{1... | collective-permute-start | bytes 417800 | tf_op jit(solution)/shard_map/ppermute | solution.py:395
  27.2 2.4 %collective-permute-done.15.refs_6_ = bf16[256,256]{1,0:T(8,128)(2,1)S(1)} collective-permute-done((bf16[256,256]{1,0:T(8,128)(2,1)S(1)}, bf16[256,256]{1,0:T(8,128)(2,1)S(1)}, u32[]{:S(2)}, u32[]{:S(2)}) %collective-permute-start.15) | collective-permute-done | bytes 131104 | tf_op jit(solution)/shard_map/ppermute | solution.py:395
  29.6 0.5 %collective-permute-start.13 = (bf16[272,256]{1,0:T(8,128)(2,1)S(1)}, bf16[272,256]{1,0:T(8,128)(2,1)S(1)}, u32[]{:S(2)}, u32[]{:S(2)}) collective-permute-start(bf16[272,256]{1,0:T(8,128)(2,1)S(1)} %get-tuple-element.65), channel_id=1, source_target_pairs={{0,4},{1,5},{2,6},{3,7},{4,0},{5,10},{6,9},{7,3},{8,12},{9,13},{10... | collective-permute-start | bytes 417800 | tf_op jit(solution)/shard_map/ppermute | solution.py:395
  30.1 0.0 collective-permute-done.16.refs_7_
  30.1 0.0 collective-permute-done.14.refs_5_
  30.1 0.8 %tick2_even.1 = (bf16[4,128,256]{2,1,0:T(8,128)(2,1)S(1)}, bf16[256,256]{1,0:T(8,128)(2,1)S(1)}, bf16[256,256]{1,0:T(8,128)(2,1)S(1)}, bf16[2,4,128,256]{3,2,1,0:T(8,128)(2,1)S(1)}) custom-call(s32[30]{0:T(128)S(4)} %get-tuple-element.40.refs_0_, bf16[1,4,6,2,128,128]{5,4,3,2,1,0:T(8,128)(2,1)S(1)} %get-tuple-element.43.refs_1_, ...), custom_call_target="tpu_custom_call", output_to_operand_aliasing={{0}: (8, {})} | custom-call | tf_op jit(solution)/shard_map/tick2_even/pallas_call | solution.py:261
  30.9 1.3 %collective-permute-start.17 = (bf16[256,256]{1,0:T(8,128)(2,1)S(1)}, bf16[256,256]{1,0:T(8,128)(2,1)S(1)}, u32[]{:S(2)}, u32[]{:S(2)}) collective-permute-start(bf16[256,256]{1,0:T(8,128)(2,1)S(1)} %get-tuple-element.74), channel_id=1, source_target_pairs={{0,5},{1,4},{2,7},{3,6},{4,0},{5,1},{6,2},{7,3},{8,13},{9,12},{10,... | collective-permute-start | bytes 393224 | tf_op jit(solution)/shard_map/ppermute | solution.py:395
  32.1 0.0 collective-permute-start.18
  32.2 4.1 %all_to_all.5.refs_5_ = bf16[2,4,128,256]{3,2,1,0:T(8,128)(2,1)S(1)} all-to-all(bf16[2,4,128,256]{3,2,1,0:T(8,128)(2,1)S(1)} %get-tuple-element.73), channel_id=1, replica_groups={{0,4},{8,12},{16,20},{24,28},{1,5},{9,13},{17,21},{25,29},{2,6},{10,14}..., dimensions={0} | all-to-all | bytes 1048576 | tf_op jit(solution)/shard_map/all_to_all | solution.py:432
  36.3 0.0 collective-permute-done.17.refs_6_
  36.3 0.0 collective-permute-done.18.refs_7_
  36.3 0.1 last_tick_odd.1
  36.4 0.0 collective-permute-done.12.refs_6_
  36.4 0.0 collective-permute-done.13.refs_7_
  36.4 0.0 collective-permute-done.11.refs_5_
  36.4 1.5 %last_tick_even.1 = (bf16[4,1,4,128,256]{4,3,2,1,0:T(8,128)(2,1)}, f32[1,4,128,256]{3,2,1,0:T(8,128)}) custom-call(s32[30]{0:T(128)S(4)} %get-tuple-element.40.refs_0_, bf16[1,4,6,2,128,128]{5,4,3,2,1,0:T(8,128)(2,1)S(1)} %get-tuple-element.43.refs_1_, ...), custom_call_target="tpu_custom_call", output_to_operand_aliasing={{0}: (11, {}), {1}: (12, {})} | custom-call | tf_op jit(solution)/shard_map/last_tick_even/pallas_call | solution.py:261
  (3 shorter events, 0.0 us)
Async XLA Ops:
  1.9 7.3 %collective-permute-start = (bf16[256,256]{1,0:T(8,128)(2,1)S(1)}, bf16[256,256]{1,0:T(8,128)(2,1)S(1)}, u32[]{:S(2)}, u32[]{:S(2)}) collective-permute-start(bf16[256,256]{1,0:T(8,128)(2,1)S(1)} %get-tuple-element.48), channel_id=1, source_target_pairs={{0,1},{1,0},{2,3},{3,2},{4,5},{5,4},{6,7},{7,6},{8,9},{9,8},{10,11... | collective-permute-start | bytes 393224 | tf_op jit(solution)/shard_map/ppermute | solution.py:357
  5.0 4.3 %collective-permute-start.1 = (bf16[256,256]{1,0:T(8,128)(2,1)S(1)}, bf16[256,256]{1,0:T(8,128)(2,1)S(1)}, u32[]{:S(2)}, u32[]{:S(2)}) collective-permute-start(bf16[256,256]{1,0:T(8,128)(2,1)S(1)} %get-tuple-element.49), channel_id=1, source_target_pairs={{0,4},{1,2},{2,1},{3,7},{4,0},{5,6},{6,5},{7,3},{8,12},{9,10},{10,... | collective-permute-start | bytes 393224 | tf_op jit(solution)/shard_map/ppermute | solution.py:358
  9.2 9.6 %collective-permute-start.2 = (bf16[512,256]{1,0:T(8,128)(2,1)S(1)}, bf16[512,256]{1,0:T(8,128)(2,1)S(1)}, u32[]{:S(2)}, u32[]{:S(2)}) collective-permute-start(bf16[512,256]{1,0:T(8,128)(2,1)S(1)} %get-tuple-element.50), channel_id=1, source_target_pairs={{0,4},{4,8},{8,12},{12,16},{16,20},{20,24},{24,28},{28,0},{1,5},{5... | collective-permute-start | bytes 786440 | tf_op jit(solution)/shard_map/ppermute | solution.py:430
  11.0 6.4 %collective-permute-start.3 = (bf16[256,256]{1,0:T(8,128)(2,1)S(1)}, bf16[256,256]{1,0:T(8,128)(2,1)S(1)}, u32[]{:S(2)}, u32[]{:S(2)}) collective-permute-start(bf16[256,256]{1,0:T(8,128)(2,1)S(1)} %get-tuple-element.54), channel_id=1, source_target_pairs={{0,5},{1,4},{2,7},{3,6},{4,9},{5,8},{6,11},{7,10},{8,13},{9,12},{1... | collective-permute-start | bytes 393224 | tf_op jit(solution)/shard_map/ppermute | solution.py:395
  13.5 3.9 %collective-permute-start.4 = (bf16[256,256]{1,0:T(8,128)(2,1)S(1)}, bf16[256,256]{1,0:T(8,128)(2,1)S(1)}, u32[]{:S(2)}, u32[]{:S(2)}) collective-permute-start(bf16[256,256]{1,0:T(8,128)(2,1)S(1)} %get-tuple-element.55), channel_id=1, source_target_pairs={{0,4},{1,6},{2,5},{3,7},{4,0},{5,10},{6,9},{7,3},{8,12},{9,14},{10... | collective-permute-start | bytes 393224 | tf_op jit(solution)/shard_map/ppermute | solution.py:395
  14.9 2.5 %collective-permute-start.5 = (bf16[2,128,256]{2,1,0:T(8,128)(2,1)S(1)}, bf16[2,128,256]{2,1,0:T(8,128)(2,1)S(1)}, u32[]{:S(2)}, u32[]{:S(2)}) collective-permute-start(bf16[2,128,256]{2,1,0:T(8,128)(2,1)S(1)} %get-tuple-element.56), channel_id=1, source_target_pairs={{0,4},{4,0},{8,12},{12,8},{16,20},{20,16},{24,28},{28,24},{1,5},{5... | collective-permute-start | bytes 393224 | tf_op jit(solution)/shard_map/ppermute | solution.py:434
  14.9 2.5 %collective-permute-start.6 = (bf16[2,128,256]{2,1,0:T(8,128)(2,1)S(1)}, bf16[2,128,256]{2,1,0:T(8,128)(2,1)S(1)}, u32[]{:S(2)}, u32[]{:S(2)}) collective-permute-start(bf16[2,128,256]{2,1,0:T(8,128)(2,1)S(1)} %get-tuple-element.57), channel_id=1, source_target_pairs={{0,4},{4,0},{8,12},{12,8},{16,20},{20,16},{24,28},{28,24},{1,5},{5... | collective-permute-start | bytes 393224 | tf_op jit(solution)/shard_map/ppermute | solution.py:434
  17.4 12.7 %collective-permute-start.14 = (bf16[528,256]{1,0:T(8,128)(2,1)S(1)}, bf16[528,256]{1,0:T(8,128)(2,1)S(1)}, u32[]{:S(2)}, u32[]{:S(2)}) collective-permute-start(bf16[528,256]{1,0:T(8,128)(2,1)S(1)} %get-tuple-element.68), channel_id=1, source_target_pairs={{0,4},{4,8},{8,12},{12,16},{16,20},{20,24},{24,28},{28,0},{1,5},{5... | collective-permute-start | bytes 811016 | tf_op jit(solution)/shard_map/ppermute | solution.py:430
  19.6 3.8 %collective-permute-start.7 = (bf16[2,128,256]{2,1,0:T(8,128)(2,1)S(1)}, bf16[2,128,256]{2,1,0:T(8,128)(2,1)S(1)}, u32[]{:S(2)}, u32[]{:S(2)}) collective-permute-start(bf16[2,128,256]{2,1,0:T(8,128)(2,1)S(1)} %get-tuple-element.59), channel_id=1, source_target_pairs={{0,4},{4,0},{8,12},{12,8},{16,20},{20,16},{24,28},{28,24},{1,5},{5... | collective-permute-start | bytes 393224 | tf_op jit(solution)/shard_map/ppermute | solution.py:434
  19.7 6.3 %collective-permute-start.9 = (bf16[272,256]{1,0:T(8,128)(2,1)S(1)}, bf16[272,256]{1,0:T(8,128)(2,1)S(1)}, u32[]{:S(2)}, u32[]{:S(2)}) collective-permute-start(bf16[272,256]{1,0:T(8,128)(2,1)S(1)} %get-tuple-element.61), channel_id=1, source_target_pairs={{0,5},{1,4},{2,7},{3,6},{4,0},{5,1},{6,2},{7,3},{8,13},{9,12},{10,... | collective-permute-start | bytes 417800 | tf_op jit(solution)/shard_map/ppermute | solution.py:395
  22.9 3.1 %collective-permute-start.10 = (bf16[272,256]{1,0:T(8,128)(2,1)S(1)}, bf16[272,256]{1,0:T(8,128)(2,1)S(1)}, u32[]{:S(2)}, u32[]{:S(2)}) collective-permute-start(bf16[272,256]{1,0:T(8,128)(2,1)S(1)} %get-tuple-element.62), channel_id=1, source_target_pairs={{0,4},{1,6},{2,5},{3,7},{4,0},{5,1},{6,2},{7,3},{8,12},{9,14},{10,... | collective-permute-start | bytes 417800 | tf_op jit(solution)/shard_map/ppermute | solution.py:395
  22.9 1.5 %collective-permute-start.8 = (bf16[2,128,256]{2,1,0:T(8,128)(2,1)S(1)}, bf16[2,128,256]{2,1,0:T(8,128)(2,1)S(1)}, u32[]{:S(2)}, u32[]{:S(2)}) collective-permute-start(bf16[2,128,256]{2,1,0:T(8,128)(2,1)S(1)} %get-tuple-element.60), channel_id=1, source_target_pairs={{0,4},{4,0},{8,12},{12,8},{16,20},{20,16},{24,28},{28,24},{1,5},{5... | collective-permute-start | bytes 393224 | tf_op jit(solution)/shard_map/ppermute | solution.py:434
  23.4 6.2 %collective-permute-start.15 = (bf16[256,256]{1,0:T(8,128)(2,1)S(1)}, bf16[256,256]{1,0:T(8,128)(2,1)S(1)}, u32[]{:S(2)}, u32[]{:S(2)}) collective-permute-start(bf16[256,256]{1,0:T(8,128)(2,1)S(1)} %get-tuple-element.69), channel_id=1, source_target_pairs={{0,4},{1,5},{2,6},{3,7},{4,9},{5,8},{6,11},{7,10},{8,12},{9,13},{1... | collective-permute-start | bytes 393224 | tf_op jit(solution)/shard_map/ppermute | solution.py:395
  24.4 5.7 %collective-permute-start.16 = (bf16[256,256]{1,0:T(8,128)(2,1)S(1)}, bf16[256,256]{1,0:T(8,128)(2,1)S(1)}, u32[]{:S(2)}, u32[]{:S(2)}) collective-permute-start(bf16[256,256]{1,0:T(8,128)(2,1)S(1)} %get-tuple-element.70), channel_id=1, source_target_pairs={{0,4},{1,5},{2,6},{3,7},{4,0},{5,10},{6,9},{7,3},{8,12},{9,13},{10... | collective-permute-start | bytes 393224 | tf_op jit(solution)/shard_map/ppermute | solution.py:395
  26.0 10.5 %collective-permute-start.11 = (bf16[512,256]{1,0:T(8,128)(2,1)S(1)}, bf16[512,256]{1,0:T(8,128)(2,1)S(1)}, u32[]{:S(2)}, u32[]{:S(2)}) collective-permute-start(bf16[512,256]{1,0:T(8,128)(2,1)S(1)} %get-tuple-element.63), channel_id=1, source_target_pairs={{0,4},{4,8},{8,12},{12,16},{16,20},{20,24},{24,28},{28,0},{1,5},{5... | collective-permute-start | bytes 786440 | tf_op jit(solution)/shard_map/ppermute | solution.py:430
  26.8 9.6 %collective-permute-start.12 = (bf16[272,256]{1,0:T(8,128)(2,1)S(1)}, bf16[272,256]{1,0:T(8,128)(2,1)S(1)}, u32[]{:S(2)}, u32[]{:S(2)}) collective-permute-start(bf16[272,256]{1,0:T(8,128)(2,1)S(1)} %get-tuple-element.64), channel_id=1, source_target_pairs={{0,4},{1,5},{2,6},{3,7},{4,9},{5,8},{6,11},{7,10},{8,12},{9,13},{1... | collective-permute-start | bytes 417800 | tf_op jit(solution)/shard_map/ppermute | solution.py:395
  29.6 6.8 %collective-permute-start.13 = (bf16[272,256]{1,0:T(8,128)(2,1)S(1)}, bf16[272,256]{1,0:T(8,128)(2,1)S(1)}, u32[]{:S(2)}, u32[]{:S(2)}) collective-permute-start(bf16[272,256]{1,0:T(8,128)(2,1)S(1)} %get-tuple-element.65), channel_id=1, source_target_pairs={{0,4},{1,5},{2,6},{3,7},{4,0},{5,10},{6,9},{7,3},{8,12},{9,13},{10... | collective-permute-start | bytes 417800 | tf_op jit(solution)/shard_map/ppermute | solution.py:395
  30.9 5.4 %collective-permute-start.17 = (bf16[256,256]{1,0:T(8,128)(2,1)S(1)}, bf16[256,256]{1,0:T(8,128)(2,1)S(1)}, u32[]{:S(2)}, u32[]{:S(2)}) collective-permute-start(bf16[256,256]{1,0:T(8,128)(2,1)S(1)} %get-tuple-element.74), channel_id=1, source_target_pairs={{0,5},{1,4},{2,7},{3,6},{4,0},{5,1},{6,2},{7,3},{8,13},{9,12},{10,... | collective-permute-start | bytes 393224 | tf_op jit(solution)/shard_map/ppermute | solution.py:395
  32.1 4.2 %collective-permute-start.18 = (bf16[256,256]{1,0:T(8,128)(2,1)S(1)}, bf16[256,256]{1,0:T(8,128)(2,1)S(1)}, u32[]{:S(2)}, u32[]{:S(2)}) collective-permute-start(bf16[256,256]{1,0:T(8,128)(2,1)S(1)} %get-tuple-element.75), channel_id=1, source_target_pairs={{0,4},{1,6},{2,5},{3,7},{4,0},{5,1},{6,2},{7,3},{8,12},{9,14},{10,... | collective-permute-start | bytes 393224 | tf_op jit(solution)/shard_map/ppermute | solution.py:395

commit v12 on v11

--- a/solution.py
+++ b/solution.py
@@ -55,9 +55,8 @@
     return copies
 
 
-def write_columns(copies, rows_refs, columns_refs):
-    for copy, rows, columns_ref in zip(copies, rows_refs, columns_refs):
-        copy.wait()
+def write_columns(rows_refs, columns_refs):
+    for rows, columns_ref in zip(rows_refs, columns_refs):
         for b in range(columns_ref.shape[0]):
             row = rows[0, pl.ds(b, 1), :]
             columns_ref[b] = jnp.broadcast_to(row, columns_ref.shape[1:]).T
@@ -78,8 +77,10 @@
     large = [
         pltpu.make_async_copy(inflow_hbm.at[0, b], landed.at[b], sems.at[b]) for b in range(blocks)
     ]
+    rows = (pass_rows, reflect_rows)
     for copy in small + large:
         copy.start()
+    rows_copies = start_rows((pass_hbm, reflect_hbm), rows, rows_sems)
     for copy in small:
         copy.wait()
     _, sides, listed = ids.shape
@@ -96,25 +97,27 @@
         wave_ref[b] = landed[b].astype(wave_ref.dtype)
     write_lists(lax.axis_index("lat"), plan_ref, wave_ref, (first_ref, second_ref))
 
+    for copy in rows_copies:
+        copy.wait()
+
     @pl.when(lax.rem(lax.axis_index("depth"), 2) == 1)
     def _():
-        rows = (pass_rows, reflect_rows)
-        copies = start_rows((pass_hbm, reflect_hbm), rows, rows_sems)
-        write_columns(copies, rows, (pass_ref, reflect_ref))
+        write_columns(rows, (pass_ref, reflect_ref))
 
 
 def load_kernel(
-    ops_hbm, source_hbm, pass_hbm, reflect_hbm, known_pass_ref, known_reflect_ref,
+    ops_hbm, source_hbm, pass_hbm, reflect_hbm, known_pass_ref, known_reflect_ref, after_ref,
     ops_ref, source_ref, pass_ref, reflect_ref, pass_rows, reflect_rows, rows_sems, sems,
 ):
-    del known_pass_ref, known_reflect_ref
+    del known_pass_ref, known_reflect_ref, after_ref
     copies = start_rows((ops_hbm, source_hbm), (ops_ref, source_ref), sems)
 
     @pl.when(lax.rem(lax.axis_index("depth"), 2) == 0)
     def _():
         rows = (pass_rows, reflect_rows)
-        small = start_rows((pass_hbm, reflect_hbm), rows, rows_sems)
-        write_columns(small, rows, (pass_ref, reflect_ref))
+        for copy in start_rows((pass_hbm, reflect_hbm), rows, rows_sems):
+            copy.wait()
+        write_columns(rows, (pass_ref, reflect_ref))
 
     for copy in copies:
         copy.wait()
@@ -353,6 +356,7 @@
         ),
         name="prepare",
     )(*map(in_hbm, (send_ids, send_count, pattern, inflow)), *coefficients)
+    listed_first = first
     routes = swap_routes(sections, tiles)
     first = lax.ppermute(first, both, routes[0])
     second = lax.ppermute(second, both, routes[1])
@@ -365,7 +369,7 @@
             column_type,
             column_type,
         ),
-        in_specs=[ANY_SPEC] * 4 + [VMEM_SPEC] * 2,
+        in_specs=[ANY_SPEC] * 4 + [VMEM_SPEC] * 3,
         out_specs=(VMEM_SPEC,) * 4,
         input_output_aliases={4: 2, 5: 3},
         scratch_shapes=[*rows_scratch, pltpu.SemaphoreType.DMA((2,))],
@@ -374,7 +378,7 @@
             flops=0, bytes_accessed=4 * (operators.size + source.size), transcendentals=0
         ),
         name="load",
-    )(in_hbm(operators), in_hbm(source), *coefficients, *map(in_vmem, coefficient_columns))
+    )(in_hbm(operators), in_hbm(source), *coefficients, *map(in_vmem, [*coefficient_columns, listed_first]))
     fixed = [plan, *fixed]
 
     buffer_type = pltpu.VMEM((blocks + 2 * listed, points, columns), WAVE)

time: 38.3 us -> 37.8 us (0.987)
  starting transfers between devices: 18.7 us -> 16.6 us
  waiting for transfers between devices: 7.46 us -> 9.2 us
    ppermute x10, waiting for transfers between devices: 4.35 us -> 6.51 us  [exchange(): return [lax.ppermute(a, both, route) for a, route in zip(lists, routes)]]
    ppermute x3, starting transfers between devices: 3.22 us -> 1.23 us  [per_device(): waves[EVEN] = [lax.ppermute(onward[0], 'depth', crossing)]]
    ppermute x10, starting transfers between devices: 10.8 us -> 9.62 us  [exchange(): return [lax.ppermute(a, both, route) for a, route in zip(lists, routes)]]
    ppermute x1, starting transfers between devices: 3.09 us -> 3.96 us  [per_device(): first = lax.ppermute(first, both, routes[0])]
    ppermute x1, waiting for transfers between devices: 2.05 us -> 1.64 us  [per_device(): first = lax.ppermute(first, both, routes[0])]
where the time goes in v12:
time: 37.8 us; the launch traced here: 37.6 us
  starting transfers between devices  16.6 us (44%)
  waiting for transfers between devices  9.2 us (24%)
  Pallas kernels  6.93 us (18%)
  blocking collectives  4.15 us (11%)
  between operations  0.75 us (2%)
    ppermute x10, starting transfers between devices, exchange(): return [lax.ppermute(a, both, route) for a, route in zip(lists, routes)]  9.62 us
    ppermute x10, waiting for transfers between devices, exchange(): return [lax.ppermute(a, both, route) for a, route in zip(lists, routes)]  6.51 us
    all_to_all x1, blocking collectives, per_device(): lax.all_to_all(onward[0], 'depth', 0, 0, axis_index_groups=pairs)  4.15 us
    ppermute x1, starting transfers between devices, per_device(): first = lax.ppermute(first, both, routes[0])  3.96 us
    pallas_call x8, Pallas kernels, grouped_call(): pl.pallas_call(body, out_shape=tuple(outs), in_specs=[SMEM_SPEC] + [VMEM_...  3.92 us
    pallas_call x1, Pallas kernels, per_device(): pl.pallas_call(load_kernel, out_shape=(pltpu.VMEM(operators.shape, operat...  1.75 us
    ppermute x1, waiting for transfers between devices, per_device(): first = lax.ppermute(first, both, routes[0])  1.64 us
    pallas_call x1, Pallas kernels, per_device(): pl.pallas_call(prepare_kernel, out_shape=(pltpu.SMEM((2 * (listed + 1) +...  1.26 us
  transfers between devices with their start and end apart: 19, of which 4 were waited for; matrix products, arithmetic and copies ran while one was open for 0% of the time, Pallas kernels for 11%

profile of v12, /device:TPU:0, one launch (start us, length us, event | category | flops | bytes accessed | tf_op | source)
XLA Modules:
  0.0 37.6 jit_solution(1617057057104048765)
XLA Ops:
  0.6 1.3 %prepare.1 = (s32[30]{0:T(128)S(4)}, bf16[4,128,256]{2,1,0:T(8,128)(2,1)S(1)}, bf16[256,256]{1,0:T(8,128)(2,1)S(1)}, bf16[256,256]{1,0:T(8,128)(2,1)S(1)}, f32[4...) custom-call(s32[1,2,2]{2,1,0:T(2,128)} %ids_hbm.1, s32[1,2]{1,0:T(1,128)} %count_hbm.1, s32[4,6]{1,0:T(4,128)} %pattern_hbm.1, ...), custom_call_target="tpu_custom_call" | custom-call | flops 131072 | bytes 1048576 | tf_op jit(solution)/shard_map/prepare/pallas_call | solution.py:332
  1.9 0.7 %collective-permute-start.1 = (bf16[256,256]{1,0:T(8,128)(2,1)S(1)}, bf16[256,256]{1,0:T(8,128)(2,1)S(1)}, u32[]{:S(2)}, u32[]{:S(2)}) collective-permute-start(bf16[256,256]{1,0:T(8,128)(2,1)S(1)} %get-tuple-element.49), channel_id=1, source_target_pairs={{0,4},{1,2},{2,1},{3,7},{4,0},{5,6},{6,5},{7,3},{8,12},{9,10},{10,... | collective-permute-start | bytes 393224 | tf_op jit(solution)/shard_map/ppermute | solution.py:362
  2.6 4.0 %collective-permute-start = (bf16[256,256]{1,0:T(8,128)(2,1)S(1)}, bf16[256,256]{1,0:T(8,128)(2,1)S(1)}, u32[]{:S(2)}, u32[]{:S(2)}) collective-permute-start(bf16[256,256]{1,0:T(8,128)(2,1)S(1)} %get-tuple-element.43.after_ref), channel_id=1, source_target_pairs={{0,1},{1,0},{2,3},{3,2},{4,5},{5,4},{6,7},{7,6},{8,9},{9,8},{10,11... | collective-permute-start | bytes 393224 | tf_op jit(solution)/shard_map/ppermute | solution.py:361
  6.6 1.8 %load.1 = (bf16[1,4,6,2,128,128]{5,4,3,2,1,0:T(8,128)(2,1)S(1)}, bf16[3,4,128,256]{3,2,1,0:T(8,128)(2,1)S(1)}, f32[4,128,128]{2,1,0:T(8,128)S(1)}, f32[4,128,128]{2,1,0:T(8,128)S(1)}) custom-call(bf16[1,4,6,2,128,128]{5,4,3,2,1,0:T(8,128)(2,1)} %ops_hbm.1, bf16[3,4,128,256]{3,2,1,0:T(8,128)(2,1)} %source_hbm.1, ...), custom_call_target="tpu_custom_call", output_to_operand_aliasing={{2}: (4, {}), {3}: (5, {})} | custom-call | bytes 4718592 | tf_op jit(solution)/shard_map/load/pallas_call | solution.py:364
  8.3 0.0 collective-permute-done.1.refs_7_
  8.3 1.6 %collective-permute-done.refs_6_ = bf16[256,256]{1,0:T(8,128)(2,1)S(1)} collective-permute-done((bf16[256,256]{1,0:T(8,128)(2,1)S(1)}, bf16[256,256]{1,0:T(8,128)(2,1)S(1)}, u32[]{:S(2)}, u32[]{:S(2)}) %collective-permute-start) | collective-permute-done | bytes 131104 | tf_op jit(solution)/shard_map/ppermute | solution.py:361
  10.0 0.0 collective-permute-start.2
  10.0 0.8 %tick0_even.1 = (bf16[4,128,256]{2,1,0:T(8,128)(2,1)S(1)}, bf16[256,256]{1,0:T(8,128)(2,1)S(1)}, bf16[256,256]{1,0:T(8,128)(2,1)S(1)}, bf16[2,128,256]{2,1,0:T(8,128)(2,1)S(1)}, bf16[2,128,256]{2,1,0:T(8,128)(2,1)S(1)}) custom-call(s32[30]{0:T(128)S(4)} %get-tuple-element.40.refs_0_, ...), custom_call_target="tpu_custom_call", output_to_operand_aliasing={{0}: (8, {}), {1}: (9, {}), {2}: (10, {})} | custom-call | tf_op jit(solution)/shard_map/tick0_even/pallas_call | solution.py:264
  10.7 2.2 %collective-permute-start.3 = (bf16[256,256]{1,0:T(8,128)(2,1)S(1)}, bf16[256,256]{1,0:T(8,128)(2,1)S(1)}, u32[]{:S(2)}, u32[]{:S(2)}) collective-permute-start(bf16[256,256]{1,0:T(8,128)(2,1)S(1)} %get-tuple-element.54), channel_id=1, source_target_pairs={{0,5},{1,4},{2,7},{3,6},{4,9},{5,8},{6,11},{7,10},{8,13},{9,12},{1... | collective-permute-start | bytes 393224 | tf_op jit(solution)/shard_map/ppermute | solution.py:399
  12.9 0.7 %collective-permute-start.4 = (bf16[256,256]{1,0:T(8,128)(2,1)S(1)}, bf16[256,256]{1,0:T(8,128)(2,1)S(1)}, u32[]{:S(2)}, u32[]{:S(2)}) collective-permute-start(bf16[256,256]{1,0:T(8,128)(2,1)S(1)} %get-tuple-element.55), channel_id=1, source_target_pairs={{0,4},{1,6},{2,5},{3,7},{4,0},{5,10},{6,9},{7,3},{8,12},{9,14},{10... | collective-permute-start | bytes 393224 | tf_op jit(solution)/shard_map/ppermute | solution.py:399
  13.6 0.0 collective-permute-start.5
  13.6 0.5 %collective-permute-start.6 = (bf16[2,128,256]{2,1,0:T(8,128)(2,1)S(1)}, bf16[2,128,256]{2,1,0:T(8,128)(2,1)S(1)}, u32[]{:S(2)}, u32[]{:S(2)}) collective-permute-start(bf16[2,128,256]{2,1,0:T(8,128)(2,1)S(1)} %get-tuple-element.57), channel_id=1, source_target_pairs={{0,4},{4,0},{8,12},{12,8},{16,20},{20,16},{24,28},{28,24},{1,5},{5... | collective-permute-start | bytes 393224 | tf_op jit(solution)/shard_map/ppermute | solution.py:438
  14.1 4.0 %collective-permute-done.3.refs_7_.refs_6_ = bf16[256,256]{1,0:T(8,128)(2,1)S(1)} collective-permute-done((bf16[256,256]{1,0:T(8,128)(2,1)S(1)}, bf16[256,256]{1,0:T(8,128)(2,1)S(1)}, u32[]{:S(2)}, u32[]{:S(2)}) %collective-permute-start.3) | collective-permute-done | bytes 131104 | tf_op jit(solution)/shard_map/ppermute | solution.py:399
  18.1 0.0 collective-permute-done.4.refs_8_.refs_7_
  18.1 0.0 collective-permute-done.5.refs_5_
  18.1 0.0 collective-permute-done.6.refs_6_
  18.1 0.4 collective-permute-start.14
  18.5 0.0 collective-permute-done.2.refs_5_
  18.5 0.8 %tick1_even.1 = (bf16[4,128,256]{2,1,0:T(8,128)(2,1)S(1)}, bf16[272,256]{1,0:T(8,128)(2,1)S(1)}, bf16[272,256]{1,0:T(8,128)(2,1)S(1)}, bf16[2,128,256]{2,1,0:T(8,128)(2,1)S(1)}, bf16[2,128,256]{2,1,0:T(8,128)(2,1)S(1)}) custom-call(s32[30]{0:T(128)S(4)} %get-tuple-element.40.refs_0_, ...), custom_call_target="tpu_custom_call", output_to_operand_aliasing={{0}: (8, {})} | custom-call | tf_op jit(solution)/shard_map/tick1_even/pallas_call | solution.py:264
  19.3 0.1 collective-permute-start.7
  19.4 2.8 %collective-permute-start.9 = (bf16[272,256]{1,0:T(8,128)(2,1)S(1)}, bf16[272,256]{1,0:T(8,128)(2,1)S(1)}, u32[]{:S(2)}, u32[]{:S(2)}) collective-permute-start(bf16[272,256]{1,0:T(8,128)(2,1)S(1)} %get-tuple-element.61), channel_id=1, source_target_pairs={{0,5},{1,4},{2,7},{3,6},{4,0},{5,1},{6,2},{7,3},{8,13},{9,12},{10,... | collective-permute-start | bytes 417800 | tf_op jit(solution)/shard_map/ppermute | solution.py:399
  22.2 0.0 collective-permute-start.10
  22.2 0.5 %collective-permute-start.8 = (bf16[2,128,256]{2,1,0:T(8,128)(2,1)S(1)}, bf16[2,128,256]{2,1,0:T(8,128)(2,1)S(1)}, u32[]{:S(2)}, u32[]{:S(2)}) collective-permute-start(bf16[2,128,256]{2,1,0:T(8,128)(2,1)S(1)} %get-tuple-element.60), channel_id=1, source_target_pairs={{0,4},{4,0},{8,12},{12,8},{16,20},{20,16},{24,28},{28,24},{1,5},{5... | collective-permute-start | bytes 393224 | tf_op jit(solution)/shard_map/ppermute | solution.py:438
  22.7 0.0 collective-permute-done.7.refs_5_
  22.7 0.0 collective-permute-start.15
  22.7 1.0 %collective-permute-done.8.refs_6_ = bf16[2,128,256]{2,1,0:T(8,128)(2,1)S(1)} collective-permute-done((bf16[2,128,256]{2,1,0:T(8,128)(2,1)S(1)}, bf16[2,128,256]{2,1,0:T(8,128)(2,1)S(1)}, u32[]{:S(2)}, u32[]{:S(2)}) %collective-permute-start.8) | collective-permute-done | bytes 131104 | tf_op jit(solution)/shard_map/ppermute | solution.py:438
  23.7 1.7 %collective-permute-start.16 = (bf16[256,256]{1,0:T(8,128)(2,1)S(1)}, bf16[256,256]{1,0:T(8,128)(2,1)S(1)}, u32[]{:S(2)}, u32[]{:S(2)}) collective-permute-start(bf16[256,256]{1,0:T(8,128)(2,1)S(1)} %get-tuple-element.70), channel_id=1, source_target_pairs={{0,4},{1,5},{2,6},{3,7},{4,0},{5,10},{6,9},{7,3},{8,12},{9,13},{10... | collective-permute-start | bytes 393224 | tf_op jit(solution)/shard_map/ppermute | solution.py:399
  25.4 0.0 collective-permute-done.9.refs_7_
  25.4 0.0 collective-permute-done.10.refs_8_
  25.4 0.9 %collective-permute-start.11 = (bf16[512,256]{1,0:T(8,128)(2,1)S(1)}, bf16[512,256]{1,0:T(8,128)(2,1)S(1)}, u32[]{:S(2)}, u32[]{:S(2)}) collective-permute-start(bf16[512,256]{1,0:T(8,128)(2,1)S(1)} %get-tuple-element.63), channel_id=1, source_target_pairs={{0,4},{4,8},{8,12},{12,16},{16,20},{20,24},{24,28},{28,0},{1,5},{5... | collective-permute-start | bytes 786440 | tf_op jit(solution)/shard_map/ppermute | solution.py:434
  26.3 0.1 collective-permute-start.12
  26.4 2.5 %collective-permute-done.15.refs_6_ = bf16[256,256]{1,0:T(8,128)(2,1)S(1)} collective-permute-done((bf16[256,256]{1,0:T(8,128)(2,1)S(1)}, bf16[256,256]{1,0:T(8,128)(2,1)S(1)}, u32[]{:S(2)}, u32[]{:S(2)}) %collective-permute-start.15) | collective-permute-done | bytes 131104 | tf_op jit(solution)/shard_map/ppermute | solution.py:399
  28.9 0.4 collective-permute-start.13
  29.3 0.0 collective-permute-done.16.refs_7_
  29.3 0.0 collective-permute-done.14.refs_5_
  29.3 0.8 %tick2_even.1 = (bf16[4,128,256]{2,1,0:T(8,128)(2,1)S(1)}, bf16[256,256]{1,0:T(8,128)(2,1)S(1)}, bf16[256,256]{1,0:T(8,128)(2,1)S(1)}, bf16[2,4,128,256]{3,2,1,0:T(8,128)(2,1)S(1)}) custom-call(s32[30]{0:T(128)S(4)} %get-tuple-element.40.refs_0_, bf16[1,4,6,2,128,128]{5,4,3,2,1,0:T(8,128)(2,1)S(1)} %get-tuple-element.44.refs_1_, ...), custom_call_target="tpu_custom_call", output_to_operand_aliasing={{0}: (8, {})} | custom-call | tf_op jit(solution)/shard_map/tick2_even/pallas_call | solution.py:264
  30.0 1.8 %collective-permute-start.17 = (bf16[256,256]{1,0:T(8,128)(2,1)S(1)}, bf16[256,256]{1,0:T(8,128)(2,1)S(1)}, u32[]{:S(2)}, u32[]{:S(2)}) collective-permute-start(bf16[256,256]{1,0:T(8,128)(2,1)S(1)} %get-tuple-element.74), channel_id=1, source_target_pairs={{0,5},{1,4},{2,7},{3,6},{4,0},{5,1},{6,2},{7,3},{8,13},{9,12},{10,... | collective-permute-start | bytes 393224 | tf_op jit(solution)/shard_map/ppermute | solution.py:399
  31.8 0.0 collective-permute-start.18
  31.8 4.1 %all_to_all.5.refs_5_ = bf16[2,4,128,256]{3,2,1,0:T(8,128)(2,1)S(1)} all-to-all(bf16[2,4,128,256]{3,2,1,0:T(8,128)(2,1)S(1)} %get-tuple-element.73), channel_id=1, replica_groups={{0,4},{8,12},{16,20},{24,28},{1,5},{9,13},{17,21},{25,29},{2,6},{10,14}..., dimensions={0} | all-to-all | bytes 1048576 | tf_op jit(solution)/shard_map/all_to_all | solution.py:436
  36.0 0.0 collective-permute-done.17.refs_6_
  36.0 0.0 collective-permute-done.18.refs_7_
  36.0 0.1 last_tick_odd.1
  36.1 0.0 collective-permute-done.12.refs_6_
  36.1 0.0 collective-permute-done.13.refs_7_
  36.1 0.0 collective-permute-done.11.refs_5_
  36.1 1.5 %last_tick_even.1 = (bf16[4,1,4,128,256]{4,3,2,1,0:T(8,128)(2,1)}, f32[1,4,128,256]{3,2,1,0:T(8,128)}) custom-call(s32[30]{0:T(128)S(4)} %get-tuple-element.40.refs_0_, bf16[1,4,6,2,128,128]{5,4,3,2,1,0:T(8,128)(2,1)S(1)} %get-tuple-element.44.refs_1_, ...), custom_call_target="tpu_custom_call", output_to_operand_aliasing={{0}: (11, {}), {1}: (12, {})} | custom-call | tf_op jit(solution)/shard_map/last_tick_even/pallas_call | solution.py:264
  (3 shorter events, 0.0 us)
Async XLA Ops:
  1.9 6.4 %collective-permute-start.1 = (bf16[256,256]{1,0:T(8,128)(2,1)S(1)}, bf16[256,256]{1,0:T(8,128)(2,1)S(1)}, u32[]{:S(2)}, u32[]{:S(2)}) collective-permute-start(bf16[256,256]{1,0:T(8,128)(2,1)S(1)} %get-tuple-element.49), channel_id=1, source_target_pairs={{0,4},{1,2},{2,1},{3,7},{4,0},{5,6},{6,5},{7,3},{8,12},{9,10},{10,... | collective-permute-start | bytes 393224 | tf_op jit(solution)/shard_map/ppermute | solution.py:362
  2.6 7.4 %collective-permute-start = (bf16[256,256]{1,0:T(8,128)(2,1)S(1)}, bf16[256,256]{1,0:T(8,128)(2,1)S(1)}, u32[]{:S(2)}, u32[]{:S(2)}) collective-permute-start(bf16[256,256]{1,0:T(8,128)(2,1)S(1)} %get-tuple-element.43.after_ref), channel_id=1, source_target_pairs={{0,1},{1,0},{2,3},{3,2},{4,5},{5,4},{6,7},{7,6},{8,9},{9,8},{10,11... | collective-permute-start | bytes 393224 | tf_op jit(solution)/shard_map/ppermute | solution.py:361
  10.0 8.5 %collective-permute-start.2 = (bf16[512,256]{1,0:T(8,128)(2,1)S(1)}, bf16[512,256]{1,0:T(8,128)(2,1)S(1)}, u32[]{:S(2)}, u32[]{:S(2)}) collective-permute-start(bf16[512,256]{1,0:T(8,128)(2,1)S(1)} %get-tuple-element.50), channel_id=1, source_target_pairs={{0,4},{4,8},{8,12},{12,16},{16,20},{20,24},{24,28},{28,0},{1,5},{5... | collective-permute-start | bytes 786440 | tf_op jit(solution)/shard_map/ppermute | solution.py:434
  10.7 7.3 %collective-permute-start.3 = (bf16[256,256]{1,0:T(8,128)(2,1)S(1)}, bf16[256,256]{1,0:T(8,128)(2,1)S(1)}, u32[]{:S(2)}, u32[]{:S(2)}) collective-permute-start(bf16[256,256]{1,0:T(8,128)(2,1)S(1)} %get-tuple-element.54), channel_id=1, source_target_pairs={{0,5},{1,4},{2,7},{3,6},{4,9},{5,8},{6,11},{7,10},{8,13},{9,12},{1... | collective-permute-start | bytes 393224 | tf_op jit(solution)/shard_map/ppermute | solution.py:399
  12.9 5.2 %collective-permute-start.4 = (bf16[256,256]{1,0:T(8,128)(2,1)S(1)}, bf16[256,256]{1,0:T(8,128)(2,1)S(1)}, u32[]{:S(2)}, u32[]{:S(2)}) collective-permute-start(bf16[256,256]{1,0:T(8,128)(2,1)S(1)} %get-tuple-element.55), channel_id=1, source_target_pairs={{0,4},{1,6},{2,5},{3,7},{4,0},{5,10},{6,9},{7,3},{8,12},{9,14},{10... | collective-permute-start | bytes 393224 | tf_op jit(solution)/shard_map/ppermute | solution.py:399
  13.6 4.5 %collective-permute-start.5 = (bf16[2,128,256]{2,1,0:T(8,128)(2,1)S(1)}, bf16[2,128,256]{2,1,0:T(8,128)(2,1)S(1)}, u32[]{:S(2)}, u32[]{:S(2)}) collective-permute-start(bf16[2,128,256]{2,1,0:T(8,128)(2,1)S(1)} %get-tuple-element.56), channel_id=1, source_target_pairs={{0,4},{4,0},{8,12},{12,8},{16,20},{20,16},{24,28},{28,24},{1,5},{5... | collective-permute-start | bytes 393224 | tf_op jit(solution)/shard_map/ppermute | solution.py:438
  13.6 4.5 %collective-permute-start.6 = (bf16[2,128,256]{2,1,0:T(8,128)(2,1)S(1)}, bf16[2,128,256]{2,1,0:T(8,128)(2,1)S(1)}, u32[]{:S(2)}, u32[]{:S(2)}) collective-permute-start(bf16[2,128,256]{2,1,0:T(8,128)(2,1)S(1)} %get-tuple-element.57), channel_id=1, source_target_pairs={{0,4},{4,0},{8,12},{12,8},{16,20},{20,16},{24,28},{28,24},{1,5},{5... | collective-permute-start | bytes 393224 | tf_op jit(solution)/shard_map/ppermute | solution.py:438
  18.1 11.1 %collective-permute-start.14 = (bf16[528,256]{1,0:T(8,128)(2,1)S(1)}, bf16[528,256]{1,0:T(8,128)(2,1)S(1)}, u32[]{:S(2)}, u32[]{:S(2)}) collective-permute-start(bf16[528,256]{1,0:T(8,128)(2,1)S(1)} %get-tuple-element.68), channel_id=1, source_target_pairs={{0,4},{4,8},{8,12},{12,16},{16,20},{20,24},{24,28},{28,0},{1,5},{5... | collective-permute-start | bytes 811016 | tf_op jit(solution)/shard_map/ppermute | solution.py:434
  19.3 3.4 %collective-permute-start.7 = (bf16[2,128,256]{2,1,0:T(8,128)(2,1)S(1)}, bf16[2,128,256]{2,1,0:T(8,128)(2,1)S(1)}, u32[]{:S(2)}, u32[]{:S(2)}) collective-permute-start(bf16[2,128,256]{2,1,0:T(8,128)(2,1)S(1)} %get-tuple-element.59), channel_id=1, source_target_pairs={{0,4},{4,0},{8,12},{12,8},{16,20},{20,16},{24,28},{28,24},{1,5},{5... | collective-permute-start | bytes 393224 | tf_op jit(solution)/shard_map/ppermute | solution.py:438
  19.4 6.1 %collective-permute-start.9 = (bf16[272,256]{1,0:T(8,128)(2,1)S(1)}, bf16[272,256]{1,0:T(8,128)(2,1)S(1)}, u32[]{:S(2)}, u32[]{:S(2)}) collective-permute-start(bf16[272,256]{1,0:T(8,128)(2,1)S(1)} %get-tuple-element.61), channel_id=1, source_target_pairs={{0,5},{1,4},{2,7},{3,6},{4,0},{5,1},{6,2},{7,3},{8,13},{9,12},{10,... | collective-permute-start | bytes 417800 | tf_op jit(solution)/shard_map/ppermute | solution.py:399
  22.2 3.2 %collective-permute-start.10 = (bf16[272,256]{1,0:T(8,128)(2,1)S(1)}, bf16[272,256]{1,0:T(8,128)(2,1)S(1)}, u32[]{:S(2)}, u32[]{:S(2)}) collective-permute-start(bf16[272,256]{1,0:T(8,128)(2,1)S(1)} %get-tuple-element.62), channel_id=1, source_target_pairs={{0,4},{1,6},{2,5},{3,7},{4,0},{5,1},{6,2},{7,3},{8,12},{9,14},{10,... | collective-permute-start | bytes 417800 | tf_op jit(solution)/shard_map/ppermute | solution.py:399
  22.2 1.5 %collective-permute-start.8 = (bf16[2,128,256]{2,1,0:T(8,128)(2,1)S(1)}, bf16[2,128,256]{2,1,0:T(8,128)(2,1)S(1)}, u32[]{:S(2)}, u32[]{:S(2)}) collective-permute-start(bf16[2,128,256]{2,1,0:T(8,128)(2,1)S(1)} %get-tuple-element.60), channel_id=1, source_target_pairs={{0,4},{4,0},{8,12},{12,8},{16,20},{20,16},{24,28},{28,24},{1,5},{5... | collective-permute-start | bytes 393224 | tf_op jit(solution)/shard_map/ppermute | solution.py:438
  22.7 6.2 %collective-permute-start.15 = (bf16[256,256]{1,0:T(8,128)(2,1)S(1)}, bf16[256,256]{1,0:T(8,128)(2,1)S(1)}, u32[]{:S(2)}, u32[]{:S(2)}) collective-permute-start(bf16[256,256]{1,0:T(8,128)(2,1)S(1)} %get-tuple-element.69), channel_id=1, source_target_pairs={{0,4},{1,5},{2,6},{3,7},{4,9},{5,8},{6,11},{7,10},{8,12},{9,13},{1... | collective-permute-start | bytes 393224 | tf_op jit(solution)/shard_map/ppermute | solution.py:399
  23.7 5.5 %collective-permute-start.16 = (bf16[256,256]{1,0:T(8,128)(2,1)S(1)}, bf16[256,256]{1,0:T(8,128)(2,1)S(1)}, u32[]{:S(2)}, u32[]{:S(2)}) collective-permute-start(bf16[256,256]{1,0:T(8,128)(2,1)S(1)} %get-tuple-element.70), channel_id=1, source_target_pairs={{0,4},{1,5},{2,6},{3,7},{4,0},{5,10},{6,9},{7,3},{8,12},{9,13},{10... | collective-permute-start | bytes 393224 | tf_op jit(solution)/shard_map/ppermute | solution.py:399
  25.4 10.7 %collective-permute-start.11 = (bf16[512,256]{1,0:T(8,128)(2,1)S(1)}, bf16[512,256]{1,0:T(8,128)(2,1)S(1)}, u32[]{:S(2)}, u32[]{:S(2)}) collective-permute-start(bf16[512,256]{1,0:T(8,128)(2,1)S(1)} %get-tuple-element.63), channel_id=1, source_target_pairs={{0,4},{4,8},{8,12},{12,16},{16,20},{20,24},{24,28},{28,0},{1,5},{5... | collective-permute-start | bytes 786440 | tf_op jit(solution)/shard_map/ppermute | solution.py:434
  26.3 9.8 %collective-permute-start.12 = (bf16[272,256]{1,0:T(8,128)(2,1)S(1)}, bf16[272,256]{1,0:T(8,128)(2,1)S(1)}, u32[]{:S(2)}, u32[]{:S(2)}) collective-permute-start(bf16[272,256]{1,0:T(8,128)(2,1)S(1)} %get-tuple-element.64), channel_id=1, source_target_pairs={{0,4},{1,5},{2,6},{3,7},{4,9},{5,8},{6,11},{7,10},{8,12},{9,13},{1... | collective-permute-start | bytes 417800 | tf_op jit(solution)/shard_map/ppermute | solution.py:399
  28.9 7.2 %collective-permute-start.13 = (bf16[272,256]{1,0:T(8,128)(2,1)S(1)}, bf16[272,256]{1,0:T(8,128)(2,1)S(1)}, u32[]{:S(2)}, u32[]{:S(2)}) collective-permute-start(bf16[272,256]{1,0:T(8,128)(2,1)S(1)} %get-tuple-element.65), channel_id=1, source_target_pairs={{0,4},{1,5},{2,6},{3,7},{4,0},{5,10},{6,9},{7,3},{8,12},{9,13},{10... | collective-permute-start | bytes 417800 | tf_op jit(solution)/shard_map/ppermute | solution.py:399
  30.0 5.9 %collective-permute-start.17 = (bf16[256,256]{1,0:T(8,128)(2,1)S(1)}, bf16[256,256]{1,0:T(8,128)(2,1)S(1)}, u32[]{:S(2)}, u32[]{:S(2)}) collective-permute-start(bf16[256,256]{1,0:T(8,128)(2,1)S(1)} %get-tuple-element.74), channel_id=1, source_target_pairs={{0,5},{1,4},{2,7},{3,6},{4,0},{5,1},{6,2},{7,3},{8,13},{9,12},{10,... | collective-permute-start | bytes 393224 | tf_op jit(solution)/shard_map/ppermute | solution.py:399
  31.8 4.2 %collective-permute-start.18 = (bf16[256,256]{1,0:T(8,128)(2,1)S(1)}, bf16[256,256]{1,0:T(8,128)(2,1)S(1)}, u32[]{:S(2)}, u32[]{:S(2)}) collective-permute-start(bf16[256,256]{1,0:T(8,128)(2,1)S(1)} %get-tuple-element.75), channel_id=1, source_target_pairs={{0,4},{1,6},{2,5},{3,7},{4,0},{5,1},{6,2},{7,3},{8,12},{9,14},{10,... | collective-permute-start | bytes 393224 | tf_op jit(solution)/shard_map/ppermute | solution.py:399

commit v13 on v12

--- a/solution.py
+++ b/solution.py
@@ -45,11 +45,15 @@
                 )
 
 
-def start_rows(hbm_refs, rows_refs, sems):
-    copies = [
+def copies_of(hbm_refs, refs, sems):
+    return [
         pltpu.make_async_copy(source, target, sems.at[i])
-        for i, (source, target) in enumerate(zip(hbm_refs, rows_refs))
+        for i, (source, target) in enumerate(zip(hbm_refs, refs))
     ]
+
+
+def start_copies(hbm_refs, refs, sems):
+    copies = copies_of(hbm_refs, refs, sems)
     for copy in copies:
         copy.start()
     return copies
@@ -63,10 +67,11 @@
 
 
 def prepare_kernel(
-    ids_hbm, count_hbm, pattern_hbm, inflow_hbm, pass_hbm, reflect_hbm,
-    plan_ref, wave_ref, first_ref, second_ref, pass_ref, reflect_ref,
-    ids, count, pattern, landed, small_sems, sems, pass_rows, reflect_rows, rows_sems,
+    ids_hbm, count_hbm, pattern_hbm, inflow_hbm, ops_hbm, source_hbm, pass_hbm, reflect_hbm,
+    plan_ref, wave_ref, first_ref, second_ref, ops_ref, source_ref, pass_ref, reflect_ref,
+    ids, count, pattern, landed, small_sems, sems, pass_rows, reflect_rows, rows_sems, load_sems,
 ):
+    odd = lax.rem(lax.axis_index("depth"), 2) == 1
     blocks = wave_ref.shape[0]
     small = [
         pltpu.make_async_copy(source, target, small_sems.at[i])
@@ -80,7 +85,12 @@
     rows = (pass_rows, reflect_rows)
     for copy in small + large:
         copy.start()
-    rows_copies = start_rows((pass_hbm, reflect_hbm), rows, rows_sems)
+    rows_copies = start_copies((pass_hbm, reflect_hbm), rows, rows_sems)
+
+    @pl.when(odd)
+    def _():
+        start_copies((ops_hbm, source_hbm), (ops_ref, source_ref), load_sems)
+
     for copy in small:
         copy.wait()
     _, sides, listed = ids.shape
@@ -100,27 +110,25 @@
     for copy in rows_copies:
         copy.wait()
 
-    @pl.when(lax.rem(lax.axis_index("depth"), 2) == 1)
+    @pl.when(odd)
     def _():
         write_columns(rows, (pass_ref, reflect_ref))
-
-
-def load_kernel(
-    ops_hbm, source_hbm, pass_hbm, reflect_hbm, known_pass_ref, known_reflect_ref, after_ref,
-    ops_ref, source_ref, pass_ref, reflect_ref, pass_rows, reflect_rows, rows_sems, sems,
-):
-    del known_pass_ref, known_reflect_ref, after_ref
-    copies = start_rows((ops_hbm, source_hbm), (ops_ref, source_ref), sems)
+        for copy in copies_of((ops_hbm, source_hbm), (ops_ref, source_ref), load_sems):
+            copy.wait()
+
+
+def load_kernel(ops_hbm, source_hbm, pass_hbm, reflect_hbm, *rest):
+    ops_ref, source_ref, pass_ref, reflect_ref, pass_rows, reflect_rows, rows_sems, sems = rest[-8:]
 
     @pl.when(lax.rem(lax.axis_index("depth"), 2) == 0)
     def _():
         rows = (pass_rows, reflect_rows)
-        for copy in start_rows((pass_hbm, reflect_hbm), rows, rows_sems):
+        copies = start_copies((ops_hbm, source_hbm), (ops_ref, source_ref), sems)
+        for copy in start_copies((pass_hbm, reflect_hbm), rows, rows_sems):
             copy.wait()
         write_columns(rows, (pass_ref, reflect_ref))
-
-    for copy in copies:
-        copy.wait()
+        for copy in copies:
+            copy.wait()
 
 
 def fill_buffer(section, tick, source_ref, wave_refs, first_ref, second_ref, buffer):
@@ -328,19 +336,24 @@
         pltpu.VMEM(reflectivity.shape, reflectivity.dtype),
         pltpu.SemaphoreType.DMA((2,)),
     ]
-    coefficients = [in_hbm(transmission), in_hbm(reflectivity)]
-    plan, wave, first, second, *coefficient_columns = pl.pallas_call(
+    fixed_types = (
+        pltpu.VMEM(operators.shape, operators.dtype),
+        pltpu.VMEM(source.shape, source.dtype),
+        column_type,
+        column_type,
+    )
+    stored = [in_hbm(a) for a in (operators, source, transmission, reflectivity)]
+    plan, wave, first, second, *loaded = pl.pallas_call(
         prepare_kernel,
         out_shape=(
             pltpu.SMEM((2 * (listed + 1) + blocks * taken,), jnp.int32),
             wave_type,
             list_type,
             list_type,
-            column_type,
-            column_type,
+            *fixed_types,
         ),
-        in_specs=[ANY_SPEC] * 6,
-        out_specs=(SMEM_SPEC,) + (VMEM_SPEC,) * 5,
+        in_specs=[ANY_SPEC] * 8,
+        out_specs=(SMEM_SPEC,) + (VMEM_SPEC,) * 7,
         scratch_shapes=[
             pltpu.SMEM(send_ids.shape, jnp.int32),
             pltpu.SMEM(send_count.shape, jnp.int32),
@@ -349,13 +362,14 @@
             pltpu.SemaphoreType.DMA((3,)),
             pltpu.SemaphoreType.DMA((blocks,)),
             *rows_scratch,
+            pltpu.SemaphoreType.DMA((2,)),
         ],
         compiler_params=params,
         cost_estimate=pl.CostEstimate(
             flops=inflow.size, bytes_accessed=8 * inflow.size, transcendentals=0
         ),
         name="prepare",
-    )(*map(in_hbm, (send_ids, send_count, pattern, inflow)), *coefficients)
+    )(*map(in_hbm, (send_ids, send_count, pattern, inflow)), *stored)
     listed_first = first
     routes = swap_routes(sections, tiles)
     first = lax.ppermute(first, both, routes[0])
@@ -363,22 +377,17 @@
 
     fixed = pl.pallas_call(
         load_kernel,
-        out_shape=(
-            pltpu.VMEM(operators.shape, operators.dtype),
-            pltpu.VMEM(source.shape, source.dtype),
-            column_type,
-            column_type,
-        ),
-        in_specs=[ANY_SPEC] * 4 + [VMEM_SPEC] * 3,
+        out_shape=fixed_types,
+        in_specs=[ANY_SPEC] * 4 + [VMEM_SPEC] * 5,
         out_specs=(VMEM_SPEC,) * 4,
-        input_output_aliases={4: 2, 5: 3},
+        input_output_aliases={4: 0, 5: 1, 6: 2, 7: 3},
         scratch_shapes=[*rows_scratch, pltpu.SemaphoreType.DMA((2,))],
         compiler_params=params,
         cost_estimate=pl.CostEstimate(
             flops=0, bytes_accessed=4 * (operators.size + source.size), transcendentals=0
         ),
         name="load",
-    )(in_hbm(operators), in_hbm(source), *coefficients, *map(in_vmem, [*coefficient_columns, listed_first]))
+    )(*stored, *map(in_vmem, [*loaded, listed_first]))
     fixed = [plan, *fixed]
 
     buffer_type = pltpu.VMEM((blocks + 2 * listed, points, columns), WAVE)

time: 37.8 us -> 38.2 us (1.011)
  waiting for transfers between devices: 9.2 us -> 10.5 us
  starting transfers between devices: 16.6 us -> 15.6 us
    ppermute x10, starting transfers between devices: 9.62 us -> 8.35 us  [exchange(): return [lax.ppermute(a, both, route) for a, route in zip(lists, routes)]]
    ppermute x10, waiting for transfers between devices: 6.51 us -> 7.24 us  [exchange(): return [lax.ppermute(a, both, route) for a, route in zip(lists, routes)]]
    ppermute x1, starting transfers between devices: 3.96 us -> 3.41 us  [per_device(): first = lax.ppermute(first, both, routes[0])]
    ppermute x1, waiting for transfers between devices: 1.64 us -> 2.18 us  [per_device(): first = lax.ppermute(first, both, routes[0])]
    ppermute x1, starting transfers between devices: 0.72 us -> 1.25 us  [per_device(): second = lax.ppermute(second, both, routes[1])]
where the time goes in v13:
time: 38.2 us; the launch traced here: 38 us
  starting transfers between devices  15.6 us (41%)
  waiting for transfers between devices  10.5 us (27%)
  Pallas kernels  6.99 us (18%)
  blocking collectives  4.15 us (11%)
  between operations  0.76 us (2%)
    ppermute x10, starting transfers between devices, exchange(): return [lax.ppermute(a, both, route) for a, route in zip(lists, routes)]  8.35 us
    ppermute x10, waiting for transfers between devices, exchange(): return [lax.ppermute(a, both, route) for a, route in zip(lists, routes)]  7.24 us
    all_to_all x1, blocking collectives, per_device(): lax.all_to_all(onward[0], 'depth', 0, 0, axis_index_groups=pairs)  4.15 us
    pallas_call x8, Pallas kernels, grouped_call(): pl.pallas_call(body, out_shape=tuple(outs), in_specs=[SMEM_SPEC] + [VMEM_...  3.96 us
    ppermute x1, starting transfers between devices, per_device(): first = lax.ppermute(first, both, routes[0])  3.41 us
    ppermute x1, waiting for transfers between devices, per_device(): first = lax.ppermute(first, both, routes[0])  2.18 us
    pallas_call x1, Pallas kernels, per_device(): pl.pallas_call(load_kernel, out_shape=fixed_types, in_specs=[ANY_SPEC] *...  1.75 us
    ppermute x3, starting transfers between devices, per_device(): waves[EVEN] = [lax.ppermute(onward[0], 'depth', crossing)]  1.55 us
  transfers between devices with their start and end apart: 19, of which 4 were waited for; matrix products, arithmetic and copies ran while one was open for 0% of the time, Pallas kernels for 11%

profile of v13, /device:TPU:0, one launch (start us, length us, event | category | flops | bytes accessed | tf_op | source)
XLA Modules:
  0.0 38.0 jit_solution(14983266645761276177)
XLA Ops:
  0.6 1.3 %prepare.1 = (s32[30]{0:T(128)S(4)}, bf16[4,128,256]{2,1,0:T(8,128)(2,1)S(1)}, bf16[256,256]{1,0:T(8,128)(2,1)S(1)}, bf16[256,256]{1,0:T(8,128)(2,1)S(1)}, bf16[...) custom-call(s32[1,2,2]{2,1,0:T(2,128)} %ids_hbm.1, ...), custom_call_target="tpu_custom_call" | custom-call | flops 131072 | bytes 1048576 | tf_op jit(solution)/shard_map/prepare/pallas_call | solution.py:346
  1.9 1.3 %collective-permute-start.1 = (bf16[256,256]{1,0:T(8,128)(2,1)S(1)}, bf16[256,256]{1,0:T(8,128)(2,1)S(1)}, u32[]{:S(2)}, u32[]{:S(2)}) collective-permute-start(bf16[256,256]{1,0:T(8,128)(2,1)S(1)} %get-tuple-element.53), channel_id=1, source_target_pairs={{0,4},{1,2},{2,1},{3,7},{4,0},{5,6},{6,5},{7,3},{8,12},{9,10},{10,... | collective-permute-start | bytes 393224 | tf_op jit(solution)/shard_map/ppermute | solution.py:376
  3.2 3.4 %collective-permute-start = (bf16[256,256]{1,0:T(8,128)(2,1)S(1)}, bf16[256,256]{1,0:T(8,128)(2,1)S(1)}, u32[]{:S(2)}, u32[]{:S(2)}) collective-permute-start(bf16[256,256]{1,0:T(8,128)(2,1)S(1)} %get-tuple-element.47.rest_4_), channel_id=1, source_target_pairs={{0,1},{1,0},{2,3},{3,2},{4,5},{5,4},{6,7},{7,6},{8,9},{9,8},{10,11... | collective-permute-start | bytes 393224 | tf_op jit(solution)/shard_map/ppermute | solution.py:375
  6.6 1.8 %load.1 = (bf16[1,4,6,2,128,128]{5,4,3,2,1,0:T(8,128)(2,1)S(1)}, bf16[3,4,128,256]{3,2,1,0:T(8,128)(2,1)S(1)}, f32[4,128,128]{2,1,0:T(8,128)S(1)}, f32[4,128,128]{2,1,0:T(8,128)S(1)}) custom-call(bf16[1,4,6,2,128,128]{5,4,3,2,1,0:T(8,128)(2,1)} %ops_hbm.3, ...), custom_call_target="tpu_custom_call", output_to_operand_aliasing={{0}: (4, {}), {1}: (5, {}), {2}: (6, {}), {3}: (7, {})} | custom-call | bytes 4718592 | tf_op jit(solution)/shard_map/load/pallas_call | solution.py:378
  8.3 0.0 collective-permute-done.1.refs_7_
  8.3 2.2 %collective-permute-done.refs_6_ = bf16[256,256]{1,0:T(8,128)(2,1)S(1)} collective-permute-done((bf16[256,256]{1,0:T(8,128)(2,1)S(1)}, bf16[256,256]{1,0:T(8,128)(2,1)S(1)}, u32[]{:S(2)}, u32[]{:S(2)}) %collective-permute-start) | collective-permute-done | bytes 131104 | tf_op jit(solution)/shard_map/ppermute | solution.py:375
  10.5 0.6 %collective-permute-start.2 = (bf16[512,256]{1,0:T(8,128)(2,1)S(1)}, bf16[512,256]{1,0:T(8,128)(2,1)S(1)}, u32[]{:S(2)}, u32[]{:S(2)}) collective-permute-start(bf16[512,256]{1,0:T(8,128)(2,1)S(1)} %get-tuple-element.54), channel_id=1, source_target_pairs={{0,4},{4,8},{8,12},{12,16},{16,20},{20,24},{24,28},{28,0},{1,5},{5... | collective-permute-start | bytes 786440 | tf_op jit(solution)/shard_map/ppermute | solution.py:443
  11.2 0.8 %tick0_even.1 = (bf16[4,128,256]{2,1,0:T(8,128)(2,1)S(1)}, bf16[256,256]{1,0:T(8,128)(2,1)S(1)}, bf16[256,256]{1,0:T(8,128)(2,1)S(1)}, bf16[2,128,256]{2,1,0:T(8,128)(2,1)S(1)}, bf16[2,128,256]{2,1,0:T(8,128)(2,1)S(1)}) custom-call(s32[30]{0:T(128)S(4)} %get-tuple-element.42.refs_0_, ...), custom_call_target="tpu_custom_call", output_to_operand_aliasing={{0}: (8, {}), {1}: (9, {}), {2}: (10, {})} | custom-call | tf_op jit(solution)/shard_map/tick0_even/pallas_call | solution.py:272
  11.9 1.6 %collective-permute-start.3 = (bf16[256,256]{1,0:T(8,128)(2,1)S(1)}, bf16[256,256]{1,0:T(8,128)(2,1)S(1)}, u32[]{:S(2)}, u32[]{:S(2)}) collective-permute-start(bf16[256,256]{1,0:T(8,128)(2,1)S(1)} %get-tuple-element.58), channel_id=1, source_target_pairs={{0,5},{1,4},{2,7},{3,6},{4,9},{5,8},{6,11},{7,10},{8,13},{9,12},{1... | collective-permute-start | bytes 393224 | tf_op jit(solution)/shard_map/ppermute | solution.py:408
  13.5 1.0 %collective-permute-start.4 = (bf16[256,256]{1,0:T(8,128)(2,1)S(1)}, bf16[256,256]{1,0:T(8,128)(2,1)S(1)}, u32[]{:S(2)}, u32[]{:S(2)}) collective-permute-start(bf16[256,256]{1,0:T(8,128)(2,1)S(1)} %get-tuple-element.59), channel_id=1, source_target_pairs={{0,4},{1,6},{2,5},{3,7},{4,0},{5,10},{6,9},{7,3},{8,12},{9,14},{10... | collective-permute-start | bytes 393224 | tf_op jit(solution)/shard_map/ppermute | solution.py:408
  14.4 0.0 collective-permute-start.5
  14.4 0.5 %collective-permute-start.6 = (bf16[2,128,256]{2,1,0:T(8,128)(2,1)S(1)}, bf16[2,128,256]{2,1,0:T(8,128)(2,1)S(1)}, u32[]{:S(2)}, u32[]{:S(2)}) collective-permute-start(bf16[2,128,256]{2,1,0:T(8,128)(2,1)S(1)} %get-tuple-element.61), channel_id=1, source_target_pairs={{0,4},{4,0},{8,12},{12,8},{16,20},{20,16},{24,28},{28,24},{1,5},{5... | collective-permute-start | bytes 393224 | tf_op jit(solution)/shard_map/ppermute | solution.py:447
  15.0 4.6 %collective-permute-done.3.refs_7_.refs_6_ = bf16[256,256]{1,0:T(8,128)(2,1)S(1)} collective-permute-done((bf16[256,256]{1,0:T(8,128)(2,1)S(1)}, bf16[256,256]{1,0:T(8,128)(2,1)S(1)}, u32[]{:S(2)}, u32[]{:S(2)}) %collective-permute-start.3) | collective-permute-done | bytes 131104 | tf_op jit(solution)/shard_map/ppermute | solution.py:408
  19.5 0.0 collective-permute-done.4.refs_8_.refs_7_
  19.5 0.0 collective-permute-done.5.refs_5_
  19.5 0.0 collective-permute-done.6.refs_6_
  19.6 0.1 collective-permute-start.14
  19.6 0.0 collective-permute-done.2.refs_5_
  19.6 0.8 %tick1_even.1 = (bf16[4,128,256]{2,1,0:T(8,128)(2,1)S(1)}, bf16[272,256]{1,0:T(8,128)(2,1)S(1)}, bf16[272,256]{1,0:T(8,128)(2,1)S(1)}, bf16[2,128,256]{2,1,0:T(8,128)(2,1)S(1)}, bf16[2,128,256]{2,1,0:T(8,128)(2,1)S(1)}) custom-call(s32[30]{0:T(128)S(4)} %get-tuple-element.42.refs_0_, ...), custom_call_target="tpu_custom_call", output_to_operand_aliasing={{0}: (8, {})} | custom-call | tf_op jit(solution)/shard_map/tick1_even/pallas_call | solution.py:272
  20.4 0.1 collective-permute-start.7
  20.5 2.2 %collective-permute-start.9 = (bf16[272,256]{1,0:T(8,128)(2,1)S(1)}, bf16[272,256]{1,0:T(8,128)(2,1)S(1)}, u32[]{:S(2)}, u32[]{:S(2)}) collective-permute-start(bf16[272,256]{1,0:T(8,128)(2,1)S(1)} %get-tuple-element.65), channel_id=1, source_target_pairs={{0,5},{1,4},{2,7},{3,6},{4,0},{5,1},{6,2},{7,3},{8,13},{9,12},{10,... | collective-permute-start | bytes 417800 | tf_op jit(solution)/shard_map/ppermute | solution.py:408
  22.7 0.0 collective-permute-start.10
  22.7 0.5 %collective-permute-start.8 = (bf16[2,128,256]{2,1,0:T(8,128)(2,1)S(1)}, bf16[2,128,256]{2,1,0:T(8,128)(2,1)S(1)}, u32[]{:S(2)}, u32[]{:S(2)}) collective-permute-start(bf16[2,128,256]{2,1,0:T(8,128)(2,1)S(1)} %get-tuple-element.64), channel_id=1, source_target_pairs={{0,4},{4,0},{8,12},{12,8},{16,20},{20,16},{24,28},{28,24},{1,5},{5... | collective-permute-start | bytes 393224 | tf_op jit(solution)/shard_map/ppermute | solution.py:447
  23.2 0.0 collective-permute-done.7.refs_5_
  23.2 0.0 collective-permute-start.15
  23.2 1.0 %collective-permute-done.8.refs_6_ = bf16[2,128,256]{2,1,0:T(8,128)(2,1)S(1)} collective-permute-done((bf16[2,128,256]{2,1,0:T(8,128)(2,1)S(1)}, bf16[2,128,256]{2,1,0:T(8,128)(2,1)S(1)}, u32[]{:S(2)}, u32[]{:S(2)}) %collective-permute-start.8) | collective-permute-done | bytes 131104 | tf_op jit(solution)/shard_map/ppermute | solution.py:447
  24.3 1.6 %collective-permute-start.16 = (bf16[256,256]{1,0:T(8,128)(2,1)S(1)}, bf16[256,256]{1,0:T(8,128)(2,1)S(1)}, u32[]{:S(2)}, u32[]{:S(2)}) collective-permute-start(bf16[256,256]{1,0:T(8,128)(2,1)S(1)} %get-tuple-element.74), channel_id=1, source_target_pairs={{0,4},{1,5},{2,6},{3,7},{4,0},{5,10},{6,9},{7,3},{8,12},{9,13},{10... | collective-permute-start | bytes 393224 | tf_op jit(solution)/shard_map/ppermute | solution.py:408
  25.8 0.0 collective-permute-done.9.refs_7_
  25.8 0.0 collective-permute-done.10.refs_8_
  25.8 0.9 %collective-permute-start.11 = (bf16[512,256]{1,0:T(8,128)(2,1)S(1)}, bf16[512,256]{1,0:T(8,128)(2,1)S(1)}, u32[]{:S(2)}, u32[]{:S(2)}) collective-permute-start(bf16[512,256]{1,0:T(8,128)(2,1)S(1)} %get-tuple-element.67), channel_id=1, source_target_pairs={{0,4},{4,8},{8,12},{12,16},{16,20},{20,24},{24,28},{28,0},{1,5},{5... | collective-permute-start | bytes 786440 | tf_op jit(solution)/shard_map/ppermute | solution.py:443
  26.7 0.1 collective-permute-start.12
  26.8 2.6 %collective-permute-done.15.refs_6_ = bf16[256,256]{1,0:T(8,128)(2,1)S(1)} collective-permute-done((bf16[256,256]{1,0:T(8,128)(2,1)S(1)}, bf16[256,256]{1,0:T(8,128)(2,1)S(1)}, u32[]{:S(2)}, u32[]{:S(2)}) %collective-permute-start.15) | collective-permute-done | bytes 131104 | tf_op jit(solution)/shard_map/ppermute | solution.py:408
  29.4 0.4 collective-permute-start.13
  29.8 0.0 collective-permute-done.16.refs_7_
  29.8 0.0 collective-permute-done.14.refs_5_
  29.8 0.8 %tick2_even.1 = (bf16[4,128,256]{2,1,0:T(8,128)(2,1)S(1)}, bf16[256,256]{1,0:T(8,128)(2,1)S(1)}, bf16[256,256]{1,0:T(8,128)(2,1)S(1)}, bf16[2,4,128,256]{3,2,1,0:T(8,128)(2,1)S(1)}) custom-call(s32[30]{0:T(128)S(4)} %get-tuple-element.42.refs_0_, bf16[1,4,6,2,128,128]{5,4,3,2,1,0:T(8,128)(2,1)S(1)} %get-tuple-element.48.refs_1_, ...), custom_call_target="tpu_custom_call", output_to_operand_aliasing={{0}: (8, {})} | custom-call | tf_op jit(solution)/shard_map/tick2_even/pallas_call | solution.py:272
  30.6 1.6 %collective-permute-start.17 = (bf16[256,256]{1,0:T(8,128)(2,1)S(1)}, bf16[256,256]{1,0:T(8,128)(2,1)S(1)}, u32[]{:S(2)}, u32[]{:S(2)}) collective-permute-start(bf16[256,256]{1,0:T(8,128)(2,1)S(1)} %get-tuple-element.78), channel_id=1, source_target_pairs={{0,5},{1,4},{2,7},{3,6},{4,0},{5,1},{6,2},{7,3},{8,13},{9,12},{10,... | collective-permute-start | bytes 393224 | tf_op jit(solution)/shard_map/ppermute | solution.py:408
  32.2 0.0 collective-permute-start.18
  32.2 4.1 %all_to_all.5.refs_5_ = bf16[2,4,128,256]{3,2,1,0:T(8,128)(2,1)S(1)} all-to-all(bf16[2,4,128,256]{3,2,1,0:T(8,128)(2,1)S(1)} %get-tuple-element.77), channel_id=1, replica_groups={{0,4},{8,12},{16,20},{24,28},{1,5},{9,13},{17,21},{25,29},{2,6},{10,14}..., dimensions={0} | all-to-all | bytes 1048576 | tf_op jit(solution)/shard_map/all_to_all | solution.py:445
  36.4 0.0 collective-permute-done.17.refs_6_
  36.4 0.0 collective-permute-done.18.refs_7_
  36.4 0.1 last_tick_odd.1
  36.5 0.0 collective-permute-done.12.refs_6_
  36.5 0.0 collective-permute-done.13.refs_7_
  36.5 0.0 collective-permute-done.11.refs_5_
  36.5 1.5 %last_tick_even.1 = (bf16[4,1,4,128,256]{4,3,2,1,0:T(8,128)(2,1)}, f32[1,4,128,256]{3,2,1,0:T(8,128)}) custom-call(s32[30]{0:T(128)S(4)} %get-tuple-element.42.refs_0_, bf16[1,4,6,2,128,128]{5,4,3,2,1,0:T(8,128)(2,1)S(1)} %get-tuple-element.48.refs_1_, ...), custom_call_target="tpu_custom_call", output_to_operand_aliasing={{0}: (11, {}), {1}: (12, {})} | custom-call | tf_op jit(solution)/shard_map/last_tick_even/pallas_call | solution.py:272
  (3 shorter events, 0.0 us)
Async XLA Ops:
  1.9 6.4 %collective-permute-start.1 = (bf16[256,256]{1,0:T(8,128)(2,1)S(1)}, bf16[256,256]{1,0:T(8,128)(2,1)S(1)}, u32[]{:S(2)}, u32[]{:S(2)}) collective-permute-start(bf16[256,256]{1,0:T(8,128)(2,1)S(1)} %get-tuple-element.53), channel_id=1, source_target_pairs={{0,4},{1,2},{2,1},{3,7},{4,0},{5,6},{6,5},{7,3},{8,12},{9,10},{10,... | collective-permute-start | bytes 393224 | tf_op jit(solution)/shard_map/ppermute | solution.py:376
  3.2 7.4 %collective-permute-start = (bf16[256,256]{1,0:T(8,128)(2,1)S(1)}, bf16[256,256]{1,0:T(8,128)(2,1)S(1)}, u32[]{:S(2)}, u32[]{:S(2)}) collective-permute-start(bf16[256,256]{1,0:T(8,128)(2,1)S(1)} %get-tuple-element.47.rest_4_), channel_id=1, source_target_pairs={{0,1},{1,0},{2,3},{3,2},{4,5},{5,4},{6,7},{7,6},{8,9},{9,8},{10,11... | collective-permute-start | bytes 393224 | tf_op jit(solution)/shard_map/ppermute | solution.py:375
  10.5 9.1 %collective-permute-start.2 = (bf16[512,256]{1,0:T(8,128)(2,1)S(1)}, bf16[512,256]{1,0:T(8,128)(2,1)S(1)}, u32[]{:S(2)}, u32[]{:S(2)}) collective-permute-start(bf16[512,256]{1,0:T(8,128)(2,1)S(1)} %get-tuple-element.54), channel_id=1, source_target_pairs={{0,4},{4,8},{8,12},{12,16},{16,20},{20,24},{24,28},{28,0},{1,5},{5... | collective-permute-start | bytes 786440 | tf_op jit(solution)/shard_map/ppermute | solution.py:443
  11.9 7.6 %collective-permute-start.3 = (bf16[256,256]{1,0:T(8,128)(2,1)S(1)}, bf16[256,256]{1,0:T(8,128)(2,1)S(1)}, u32[]{:S(2)}, u32[]{:S(2)}) collective-permute-start(bf16[256,256]{1,0:T(8,128)(2,1)S(1)} %get-tuple-element.58), channel_id=1, source_target_pairs={{0,5},{1,4},{2,7},{3,6},{4,9},{5,8},{6,11},{7,10},{8,13},{9,12},{1... | collective-permute-start | bytes 393224 | tf_op jit(solution)/shard_map/ppermute | solution.py:408
  13.5 6.0 %collective-permute-start.4 = (bf16[256,256]{1,0:T(8,128)(2,1)S(1)}, bf16[256,256]{1,0:T(8,128)(2,1)S(1)}, u32[]{:S(2)}, u32[]{:S(2)}) collective-permute-start(bf16[256,256]{1,0:T(8,128)(2,1)S(1)} %get-tuple-element.59), channel_id=1, source_target_pairs={{0,4},{1,6},{2,5},{3,7},{4,0},{5,10},{6,9},{7,3},{8,12},{9,14},{10... | collective-permute-start | bytes 393224 | tf_op jit(solution)/shard_map/ppermute | solution.py:408
  14.4 5.1 %collective-permute-start.5 = (bf16[2,128,256]{2,1,0:T(8,128)(2,1)S(1)}, bf16[2,128,256]{2,1,0:T(8,128)(2,1)S(1)}, u32[]{:S(2)}, u32[]{:S(2)}) collective-permute-start(bf16[2,128,256]{2,1,0:T(8,128)(2,1)S(1)} %get-tuple-element.60), channel_id=1, source_target_pairs={{0,4},{4,0},{8,12},{12,8},{16,20},{20,16},{24,28},{28,24},{1,5},{5... | collective-permute-start | bytes 393224 | tf_op jit(solution)/shard_map/ppermute | solution.py:447
  14.4 5.1 %collective-permute-start.6 = (bf16[2,128,256]{2,1,0:T(8,128)(2,1)S(1)}, bf16[2,128,256]{2,1,0:T(8,128)(2,1)S(1)}, u32[]{:S(2)}, u32[]{:S(2)}) collective-permute-start(bf16[2,128,256]{2,1,0:T(8,128)(2,1)S(1)} %get-tuple-element.61), channel_id=1, source_target_pairs={{0,4},{4,0},{8,12},{12,8},{16,20},{20,16},{24,28},{28,24},{1,5},{5... | collective-permute-start | bytes 393224 | tf_op jit(solution)/shard_map/ppermute | solution.py:447
  19.6 10.3 %collective-permute-start.14 = (bf16[528,256]{1,0:T(8,128)(2,1)S(1)}, bf16[528,256]{1,0:T(8,128)(2,1)S(1)}, u32[]{:S(2)}, u32[]{:S(2)}) collective-permute-start(bf16[528,256]{1,0:T(8,128)(2,1)S(1)} %get-tuple-element.72), channel_id=1, source_target_pairs={{0,4},{4,8},{8,12},{12,16},{16,20},{20,24},{24,28},{28,0},{1,5},{5... | collective-permute-start | bytes 811016 | tf_op jit(solution)/shard_map/ppermute | solution.py:443
  20.4 2.8 %collective-permute-start.7 = (bf16[2,128,256]{2,1,0:T(8,128)(2,1)S(1)}, bf16[2,128,256]{2,1,0:T(8,128)(2,1)S(1)}, u32[]{:S(2)}, u32[]{:S(2)}) collective-permute-start(bf16[2,128,256]{2,1,0:T(8,128)(2,1)S(1)} %get-tuple-element.63), channel_id=1, source_target_pairs={{0,4},{4,0},{8,12},{12,8},{16,20},{20,16},{24,28},{28,24},{1,5},{5... | collective-permute-start | bytes 393224 | tf_op jit(solution)/shard_map/ppermute | solution.py:447
  20.5 5.3 %collective-permute-start.9 = (bf16[272,256]{1,0:T(8,128)(2,1)S(1)}, bf16[272,256]{1,0:T(8,128)(2,1)S(1)}, u32[]{:S(2)}, u32[]{:S(2)}) collective-permute-start(bf16[272,256]{1,0:T(8,128)(2,1)S(1)} %get-tuple-element.65), channel_id=1, source_target_pairs={{0,5},{1,4},{2,7},{3,6},{4,0},{5,1},{6,2},{7,3},{8,13},{9,12},{10,... | collective-permute-start | bytes 417800 | tf_op jit(solution)/shard_map/ppermute | solution.py:408
  22.7 3.1 %collective-permute-start.10 = (bf16[272,256]{1,0:T(8,128)(2,1)S(1)}, bf16[272,256]{1,0:T(8,128)(2,1)S(1)}, u32[]{:S(2)}, u32[]{:S(2)}) collective-permute-start(bf16[272,256]{1,0:T(8,128)(2,1)S(1)} %get-tuple-element.66), channel_id=1, source_target_pairs={{0,4},{1,6},{2,5},{3,7},{4,0},{5,1},{6,2},{7,3},{8,12},{9,14},{10,... | collective-permute-start | bytes 417800 | tf_op jit(solution)/shard_map/ppermute | solution.py:408
  22.7 1.5 %collective-permute-start.8 = (bf16[2,128,256]{2,1,0:T(8,128)(2,1)S(1)}, bf16[2,128,256]{2,1,0:T(8,128)(2,1)S(1)}, u32[]{:S(2)}, u32[]{:S(2)}) collective-permute-start(bf16[2,128,256]{2,1,0:T(8,128)(2,1)S(1)} %get-tuple-element.64), channel_id=1, source_target_pairs={{0,4},{4,0},{8,12},{12,8},{16,20},{20,16},{24,28},{28,24},{1,5},{5... | collective-permute-start | bytes 393224 | tf_op jit(solution)/shard_map/ppermute | solution.py:447
  23.2 6.2 %collective-permute-start.15 = (bf16[256,256]{1,0:T(8,128)(2,1)S(1)}, bf16[256,256]{1,0:T(8,128)(2,1)S(1)}, u32[]{:S(2)}, u32[]{:S(2)}) collective-permute-start(bf16[256,256]{1,0:T(8,128)(2,1)S(1)} %get-tuple-element.73), channel_id=1, source_target_pairs={{0,4},{1,5},{2,6},{3,7},{4,9},{5,8},{6,11},{7,10},{8,12},{9,13},{1... | collective-permute-start | bytes 393224 | tf_op jit(solution)/shard_map/ppermute | solution.py:408
  24.3 5.5 %collective-permute-start.16 = (bf16[256,256]{1,0:T(8,128)(2,1)S(1)}, bf16[256,256]{1,0:T(8,128)(2,1)S(1)}, u32[]{:S(2)}, u32[]{:S(2)}) collective-permute-start(bf16[256,256]{1,0:T(8,128)(2,1)S(1)} %get-tuple-element.74), channel_id=1, source_target_pairs={{0,4},{1,5},{2,6},{3,7},{4,0},{5,10},{6,9},{7,3},{8,12},{9,13},{10... | collective-permute-start | bytes 393224 | tf_op jit(solution)/shard_map/ppermute | solution.py:408
  25.8 10.7 %collective-permute-start.11 = (bf16[512,256]{1,0:T(8,128)(2,1)S(1)}, bf16[512,256]{1,0:T(8,128)(2,1)S(1)}, u32[]{:S(2)}, u32[]{:S(2)}) collective-permute-start(bf16[512,256]{1,0:T(8,128)(2,1)S(1)} %get-tuple-element.67), channel_id=1, source_target_pairs={{0,4},{4,8},{8,12},{12,16},{16,20},{20,24},{24,28},{28,0},{1,5},{5... | collective-permute-start | bytes 786440 | tf_op jit(solution)/shard_map/ppermute | solution.py:443
  26.7 9.8 %collective-permute-start.12 = (bf16[272,256]{1,0:T(8,128)(2,1)S(1)}, bf16[272,256]{1,0:T(8,128)(2,1)S(1)}, u32[]{:S(2)}, u32[]{:S(2)}) collective-permute-start(bf16[272,256]{1,0:T(8,128)(2,1)S(1)} %get-tuple-element.68), channel_id=1, source_target_pairs={{0,4},{1,5},{2,6},{3,7},{4,9},{5,8},{6,11},{7,10},{8,12},{9,13},{1... | collective-permute-start | bytes 417800 | tf_op jit(solution)/shard_map/ppermute | solution.py:408
  29.4 7.1 %collective-permute-start.13 = (bf16[272,256]{1,0:T(8,128)(2,1)S(1)}, bf16[272,256]{1,0:T(8,128)(2,1)S(1)}, u32[]{:S(2)}, u32[]{:S(2)}) collective-permute-start(bf16[272,256]{1,0:T(8,128)(2,1)S(1)} %get-tuple-element.69), channel_id=1, source_target_pairs={{0,4},{1,5},{2,6},{3,7},{4,0},{5,10},{6,9},{7,3},{8,12},{9,13},{10... | collective-permute-start | bytes 417800 | tf_op jit(solution)/shard_map/ppermute | solution.py:408
  30.6 5.8 %collective-permute-start.17 = (bf16[256,256]{1,0:T(8,128)(2,1)S(1)}, bf16[256,256]{1,0:T(8,128)(2,1)S(1)}, u32[]{:S(2)}, u32[]{:S(2)}) collective-permute-start(bf16[256,256]{1,0:T(8,128)(2,1)S(1)} %get-tuple-element.78), channel_id=1, source_target_pairs={{0,5},{1,4},{2,7},{3,6},{4,0},{5,1},{6,2},{7,3},{8,13},{9,12},{10,... | collective-permute-start | bytes 393224 | tf_op jit(solution)/shard_map/ppermute | solution.py:408
  32.2 4.2 %collective-permute-start.18 = (bf16[256,256]{1,0:T(8,128)(2,1)S(1)}, bf16[256,256]{1,0:T(8,128)(2,1)S(1)}, u32[]{:S(2)}, u32[]{:S(2)}) collective-permute-start(bf16[256,256]{1,0:T(8,128)(2,1)S(1)} %get-tuple-element.79), channel_id=1, source_target_pairs={{0,4},{1,6},{2,5},{3,7},{4,0},{5,1},{6,2},{7,3},{8,12},{9,14},{10,... | collective-permute-start | bytes 393224 | tf_op jit(solution)/shard_map/ppermute | solution.py:408

commit v14 on v10

--- a/solution.py
+++ b/solution.py
@@ -163,9 +163,9 @@
 
 def tick_kernel(
     parity, tick, sections, plan_ref, ops_ref, source_ref, pass_ref, reflect_ref,
-    wave_refs, first_in_ref, second_in_ref, known_refs, out_refs, buffer, onward,
+    wave_refs, first_in_ref, second_in_ref, settled_refs, known_refs, out_refs, buffer, onward,
 ):
-    del known_refs
+    del known_refs, settled_refs
     echo_ref, first_ref, second_ref, *onward_refs = out_refs
     section = lax.axis_index("depth")
     tile = lax.axis_index("lat")
@@ -388,14 +388,15 @@
             else:
                 extra = 0 if parity == ODD else 16
             if parity == ODD:
-                long = 0 if first_step or last_step else 16
+                long = 0 if last_step else 16
                 to_next = [pltpu.VMEM((blocks * points + long, columns), WAVE)]
             else:
                 to_next = [pair_type] if last_step else half_types if first_step else part_types
             outs = [wave_type, *lists_of(extra), *to_next]
+            settled = arrived[EVEN][0] if last_step and parity == ODD else []
             echo, *lists = grouped_call(
                 functools.partial(tick_kernel, parity, tick, sections),
-                [*fixed, *arrived[parity]],
+                [*fixed, *arrived[parity], settled],
                 outs,
                 [VMEM_SPEC] * len(outs),
                 [in_vmem(a) for a in known],

time: 37.8 us -> 37.9 us (level)
  waiting for transfers between devices: 8.9 us -> 6.68 us
  starting transfers between devices: 17 us -> 19.1 us
    ppermute x10, starting transfers between devices: 9.98 us -> 12.2 us  [exchange(): return [lax.ppermute(a, both, route) for a, route in zip(lists, routes)]]
    ppermute x10, waiting for transfers between devices: 6.33 us -> 4.1 us  [exchange(): return [lax.ppermute(a, both, route) for a, route in zip(lists, routes)]]
where the time goes in v14:
time: 37.9 us; the launch traced here: 37.5 us
  starting transfers between devices  19.1 us (50%)
  Pallas kernels  6.83 us (18%)
  waiting for transfers between devices  6.68 us (18%)
  blocking collectives  4.15 us (11%)
  between operations  0.75 us (2%)
    ppermute x10, starting transfers between devices, exchange(): return [lax.ppermute(a, both, route) for a, route in zip(lists, routes)]  12.2 us
    ppermute x1, starting transfers between devices, per_device(): first = lax.ppermute(first, both, routes[0])  4.15 us
    all_to_all x1, blocking collectives, per_device(): lax.all_to_all(onward[0], 'depth', 0, 0, axis_index_groups=pairs)  4.15 us
    ppermute x10, waiting for transfers between devices, exchange(): return [lax.ppermute(a, both, route) for a, route in zip(lists, routes)]  4.1 us
    pallas_call x8, Pallas kernels, grouped_call(): pl.pallas_call(body, out_shape=tuple(outs), in_specs=[SMEM_SPEC] + [VMEM_...  3.95 us
    pallas_call x1, Pallas kernels, per_device(): pl.pallas_call(load_kernel, out_shape=(pltpu.VMEM(operators.shape, operat...  1.67 us
    ppermute x1, waiting for transfers between devices, per_device(): first = lax.ppermute(first, both, routes[0])  1.52 us
    pallas_call x1, Pallas kernels, per_device(): pl.pallas_call(prepare_kernel, out_shape=(pltpu.SMEM((2 * (listed + 1) +...  1.21 us
  transfers between devices with their start and end apart: 19, of which 4 were waited for; matrix products, arithmetic and copies ran while one was open for 0% of the time, Pallas kernels for 11%

profile of v14, /device:TPU:0, one launch (start us, length us, event | category | flops | bytes accessed | tf_op | source)
XLA Modules:
  0.0 37.5 jit_solution(62785567337357841)
XLA Ops:
  0.6 1.2 %prepare.1 = (s32[30]{0:T(128)S(4)}, bf16[4,128,256]{2,1,0:T(8,128)(2,1)S(1)}, bf16[256,256]{1,0:T(8,128)(2,1)S(1)}, bf16[256,256]{1,0:T(8,128)(2,1)S(1)}) custom-call(s32[1,2,2]{2,1,0:T(2,128)} %ids_hbm.1, s32[1,2]{1,0:T(1,128)} %count_hbm.1, s32[4,6]{1,0:T(4,128)} %pattern_hbm.1, f32[1,4,128,256]{3,2,1,0:T(8,128)} %inflow_hbm.1), custom_call_target="tpu_custom_call" | custom-call | flops 131072 | bytes 1048576 | tf_op jit(solution)/shard_map/prepare/pallas_call | solution.py:307
  1.8 0.5 %collective-permute-start.1 = (bf16[256,256]{1,0:T(8,128)(2,1)S(1)}, bf16[256,256]{1,0:T(8,128)(2,1)S(1)}, u32[]{:S(2)}, u32[]{:S(2)}) collective-permute-start(bf16[256,256]{1,0:T(8,128)(2,1)S(1)} %get-tuple-element.45), channel_id=1, source_target_pairs={{0,4},{1,2},{2,1},{3,7},{4,0},{5,6},{6,5},{7,3},{8,12},{9,10},{10,... | collective-permute-start | bytes 393224 | tf_op jit(solution)/shard_map/ppermute | solution.py:334
  2.4 4.2 %collective-permute-start = (bf16[256,256]{1,0:T(8,128)(2,1)S(1)}, bf16[256,256]{1,0:T(8,128)(2,1)S(1)}, u32[]{:S(2)}, u32[]{:S(2)}) collective-permute-start(bf16[256,256]{1,0:T(8,128)(2,1)S(1)} %get-tuple-element.39.after_ref), channel_id=1, source_target_pairs={{0,1},{1,0},{2,3},{3,2},{4,5},{5,4},{6,7},{7,6},{8,9},{9,8},{10,11... | collective-permute-start | bytes 393224 | tf_op jit(solution)/shard_map/ppermute | solution.py:333
  6.5 1.7 %load.1 = (bf16[1,4,6,2,128,128]{5,4,3,2,1,0:T(8,128)(2,1)S(1)}, bf16[3,4,128,256]{3,2,1,0:T(8,128)(2,1)S(1)}, f32[4,128,128]{2,1,0:T(8,128)S(1)}, f32[4,128,128]{2,1,0:T(8,128)S(1)}) custom-call(bf16[1,4,6,2,128,128]{5,4,3,2,1,0:T(8,128)(2,1)} %ops_hbm.1, bf16[3,4,128,256]{3,2,1,0:T(8,128)(2,1)} %source_hbm.1, f32[1,4,128]{2,1,0:T(4,128)} %pass_hbm.1, ...), custom_call_target="tpu_custom_call" | custom-call | bytes 4718592 | tf_op jit(solution)/shard_map/load/pallas_call | solution.py:337
  8.2 0.0 collective-permute-done.1.refs_7_
  8.2 1.5 %collective-permute-done.refs_6_ = bf16[256,256]{1,0:T(8,128)(2,1)S(1)} collective-permute-done((bf16[256,256]{1,0:T(8,128)(2,1)S(1)}, bf16[256,256]{1,0:T(8,128)(2,1)S(1)}, u32[]{:S(2)}, u32[]{:S(2)}) %collective-permute-start) | collective-permute-done | bytes 131104 | tf_op jit(solution)/shard_map/ppermute | solution.py:333
  9.7 0.0 collective-permute-start.2
  9.7 0.8 %tick0_even.1 = (bf16[4,128,256]{2,1,0:T(8,128)(2,1)S(1)}, bf16[256,256]{1,0:T(8,128)(2,1)S(1)}, bf16[256,256]{1,0:T(8,128)(2,1)S(1)}, bf16[2,128,256]{2,1,0:T(8,128)(2,1)S(1)}, bf16[2,128,256]{2,1,0:T(8,128)(2,1)S(1)}) custom-call(s32[30]{0:T(128)S(4)} %get-tuple-element.38.refs_0_, ...), custom_call_target="tpu_custom_call", output_to_operand_aliasing={{0}: (8, {}), {1}: (9, {}), {2}: (10, {})} | custom-call | tf_op jit(solution)/shard_map/tick0_even/pallas_call | solution.py:246
  10.5 2.2 %collective-permute-start.3 = (bf16[256,256]{1,0:T(8,128)(2,1)S(1)}, bf16[256,256]{1,0:T(8,128)(2,1)S(1)}, u32[]{:S(2)}, u32[]{:S(2)}) collective-permute-start(bf16[256,256]{1,0:T(8,128)(2,1)S(1)} %get-tuple-element.50), channel_id=1, source_target_pairs={{0,5},{1,4},{2,7},{3,6},{4,9},{5,8},{6,11},{7,10},{8,13},{9,12},{1... | collective-permute-start | bytes 393224 | tf_op jit(solution)/shard_map/ppermute | solution.py:375
  12.7 0.7 %collective-permute-start.4 = (bf16[256,256]{1,0:T(8,128)(2,1)S(1)}, bf16[256,256]{1,0:T(8,128)(2,1)S(1)}, u32[]{:S(2)}, u32[]{:S(2)}) collective-permute-start(bf16[256,256]{1,0:T(8,128)(2,1)S(1)} %get-tuple-element.51), channel_id=1, source_target_pairs={{0,4},{1,6},{2,5},{3,7},{4,0},{5,10},{6,9},{7,3},{8,12},{9,14},{10... | collective-permute-start | bytes 393224 | tf_op jit(solution)/shard_map/ppermute | solution.py:375
  13.4 0.0 collective-permute-start.5
  13.4 0.5 %collective-permute-start.6 = (bf16[2,128,256]{2,1,0:T(8,128)(2,1)S(1)}, bf16[2,128,256]{2,1,0:T(8,128)(2,1)S(1)}, u32[]{:S(2)}, u32[]{:S(2)}) collective-permute-start(bf16[2,128,256]{2,1,0:T(8,128)(2,1)S(1)} %get-tuple-element.53), channel_id=1, source_target_pairs={{0,4},{4,0},{8,12},{12,8},{16,20},{20,16},{24,28},{28,24},{1,5},{5... | collective-permute-start | bytes 393224 | tf_op jit(solution)/shard_map/ppermute | solution.py:415
  13.9 4.0 %collective-permute-done.3.refs_7_.refs_6_ = bf16[256,256]{1,0:T(8,128)(2,1)S(1)} collective-permute-done((bf16[256,256]{1,0:T(8,128)(2,1)S(1)}, bf16[256,256]{1,0:T(8,128)(2,1)S(1)}, u32[]{:S(2)}, u32[]{:S(2)}) %collective-permute-start.3) | collective-permute-done | bytes 131104 | tf_op jit(solution)/shard_map/ppermute | solution.py:375
  17.9 0.0 collective-permute-done.4.refs_8_.refs_7_
  17.9 0.0 collective-permute-done.5.refs_5_
  17.9 0.0 collective-permute-done.6.refs_6_
  17.9 0.4 collective-permute-start.11
  18.3 0.0 collective-permute-done.2.refs_5_
  18.3 0.8 %tick1_even.1 = (bf16[4,128,256]{2,1,0:T(8,128)(2,1)S(1)}, bf16[272,256]{1,0:T(8,128)(2,1)S(1)}, bf16[272,256]{1,0:T(8,128)(2,1)S(1)}, bf16[2,128,256]{2,1,0:T(8,128)(2,1)S(1)}, bf16[2,128,256]{2,1,0:T(8,128)(2,1)S(1)}) custom-call(s32[30]{0:T(128)S(4)} %get-tuple-element.38.refs_0_, ...), custom_call_target="tpu_custom_call", output_to_operand_aliasing={{0}: (8, {})} | custom-call | tf_op jit(solution)/shard_map/tick1_even/pallas_call | solution.py:246
  19.0 1.9 %collective-permute-start.9 = (bf16[272,256]{1,0:T(8,128)(2,1)S(1)}, bf16[272,256]{1,0:T(8,128)(2,1)S(1)}, u32[]{:S(2)}, u32[]{:S(2)}) collective-permute-start(bf16[272,256]{1,0:T(8,128)(2,1)S(1)} %get-tuple-element.57), channel_id=1, source_target_pairs={{0,5},{1,4},{2,7},{3,6},{4,0},{5,1},{6,2},{7,3},{8,13},{9,12},{10,... | collective-permute-start | bytes 417800 | tf_op jit(solution)/shard_map/ppermute | solution.py:375
  20.9 0.0 collective-permute-start.10
  20.9 0.5 %collective-permute-start.7 = (bf16[2,128,256]{2,1,0:T(8,128)(2,1)S(1)}, bf16[2,128,256]{2,1,0:T(8,128)(2,1)S(1)}, u32[]{:S(2)}, u32[]{:S(2)}) collective-permute-start(bf16[2,128,256]{2,1,0:T(8,128)(2,1)S(1)} %get-tuple-element.55), channel_id=1, source_target_pairs={{0,4},{4,0},{8,12},{12,8},{16,20},{20,16},{24,28},{28,24},{1,5},{5... | collective-permute-start | bytes 393224 | tf_op jit(solution)/shard_map/ppermute | solution.py:415
  21.4 0.0 collective-permute-start.8
  21.4 1.0 %collective-permute-done.7.refs_5_ = bf16[2,128,256]{2,1,0:T(8,128)(2,1)S(1)} collective-permute-done((bf16[2,128,256]{2,1,0:T(8,128)(2,1)S(1)}, bf16[2,128,256]{2,1,0:T(8,128)(2,1)S(1)}, u32[]{:S(2)}, u32[]{:S(2)}) %collective-permute-start.7) | collective-permute-done | bytes 131104 | tf_op jit(solution)/shard_map/ppermute | solution.py:415
  22.4 0.3 collective-permute-start.15
  22.7 0.0 collective-permute-done.8.refs_6_
  22.7 3.5 %collective-permute-start.16 = (bf16[256,256]{1,0:T(8,128)(2,1)S(1)}, bf16[256,256]{1,0:T(8,128)(2,1)S(1)}, u32[]{:S(2)}, u32[]{:S(2)}) collective-permute-start(bf16[256,256]{1,0:T(8,128)(2,1)S(1)} %get-tuple-element.66), channel_id=1, source_target_pairs={{0,4},{1,5},{2,6},{3,7},{4,0},{5,10},{6,9},{7,3},{8,12},{9,13},{10... | collective-permute-start | bytes 393224 | tf_op jit(solution)/shard_map/ppermute | solution.py:375
  26.2 0.0 collective-permute-done.11.refs_9_.refs_5_
  26.2 0.0 collective-permute-done.9.refs_7_
  26.2 0.0 collective-permute-done.10.refs_8_
  26.2 0.8 %collective-permute-start.12 = (bf16[512,256]{1,0:T(8,128)(2,1)S(1)}, bf16[512,256]{1,0:T(8,128)(2,1)S(1)}, u32[]{:S(2)}, u32[]{:S(2)}) collective-permute-start(bf16[512,256]{1,0:T(8,128)(2,1)S(1)} %get-tuple-element.60), channel_id=1, source_target_pairs={{0,4},{4,8},{8,12},{12,16},{16,20},{20,24},{24,28},{28,0},{1,5},{5... | collective-permute-start | bytes 786440 | tf_op jit(solution)/shard_map/ppermute | solution.py:411
  27.1 0.6 %collective-permute-start.13 = (bf16[272,256]{1,0:T(8,128)(2,1)S(1)}, bf16[272,256]{1,0:T(8,128)(2,1)S(1)}, u32[]{:S(2)}, u32[]{:S(2)}) collective-permute-start(bf16[272,256]{1,0:T(8,128)(2,1)S(1)} %get-tuple-element.61), channel_id=1, source_target_pairs={{0,4},{1,5},{2,6},{3,7},{4,9},{5,8},{6,11},{7,10},{8,12},{9,13},{1... | collective-permute-start | bytes 417800 | tf_op jit(solution)/shard_map/ppermute | solution.py:375
  27.7 0.8 %collective-permute-start.14 = (bf16[272,256]{1,0:T(8,128)(2,1)S(1)}, bf16[272,256]{1,0:T(8,128)(2,1)S(1)}, u32[]{:S(2)}, u32[]{:S(2)}) collective-permute-start(bf16[272,256]{1,0:T(8,128)(2,1)S(1)} %get-tuple-element.62), channel_id=1, source_target_pairs={{0,4},{1,5},{2,6},{3,7},{4,0},{5,10},{6,9},{7,3},{8,12},{9,13},{10... | collective-permute-start | bytes 417800 | tf_op jit(solution)/shard_map/ppermute | solution.py:375
  28.5 0.1 collective-permute-done.15.refs_6_
  28.6 0.0 collective-permute-done.16.refs_7_
  28.6 0.8 %tick2_even.1 = (bf16[4,128,256]{2,1,0:T(8,128)(2,1)S(1)}, bf16[256,256]{1,0:T(8,128)(2,1)S(1)}, bf16[256,256]{1,0:T(8,128)(2,1)S(1)}, bf16[2,4,128,256]{3,2,1,0:T(8,128)(2,1)S(1)}) custom-call(s32[30]{0:T(128)S(4)} %get-tuple-element.38.refs_0_, bf16[1,4,6,2,128,128]{5,4,3,2,1,0:T(8,128)(2,1)S(1)} %get-tuple-element.40.refs_1_, ...), custom_call_target="tpu_custom_call", output_to_operand_aliasing={{0}: (8, {})} | custom-call | tf_op jit(solution)/shard_map/tick2_even/pallas_call | solution.py:246
  29.4 2.3 %collective-permute-start.17 = (bf16[256,256]{1,0:T(8,128)(2,1)S(1)}, bf16[256,256]{1,0:T(8,128)(2,1)S(1)}, u32[]{:S(2)}, u32[]{:S(2)}) collective-permute-start(bf16[256,256]{1,0:T(8,128)(2,1)S(1)} %get-tuple-element.70), channel_id=1, source_target_pairs={{0,5},{1,4},{2,7},{3,6},{4,0},{5,1},{6,2},{7,3},{8,13},{9,12},{10,... | collective-permute-start | bytes 393224 | tf_op jit(solution)/shard_map/ppermute | solution.py:375
  31.7 0.0 collective-permute-start.18
  31.7 4.1 %all_to_all.5.refs_5_ = bf16[2,4,128,256]{3,2,1,0:T(8,128)(2,1)S(1)} all-to-all(bf16[2,4,128,256]{3,2,1,0:T(8,128)(2,1)S(1)} %get-tuple-element.69), channel_id=1, replica_groups={{0,4},{8,12},{16,20},{24,28},{1,5},{9,13},{17,21},{25,29},{2,6},{10,14}..., dimensions={0} | all-to-all | bytes 1048576 | tf_op jit(solution)/shard_map/all_to_all | solution.py:413
  35.8 0.0 collective-permute-done.17.refs_6_
  35.9 0.0 collective-permute-done.18.refs_7_
  35.9 0.1 last_tick_odd.1
  36.0 0.0 collective-permute-done.13.refs_6_
  36.0 0.0 collective-permute-done.14.refs_7_
  36.0 0.0 collective-permute-done.12.refs_5_
  36.0 1.5 %last_tick_even.1 = (bf16[4,1,4,128,256]{4,3,2,1,0:T(8,128)(2,1)}, f32[1,4,128,256]{3,2,1,0:T(8,128)}) custom-call(s32[30]{0:T(128)S(4)} %get-tuple-element.38.refs_0_, bf16[1,4,6,2,128,128]{5,4,3,2,1,0:T(8,128)(2,1)S(1)} %get-tuple-element.40.refs_1_, ...), custom_call_target="tpu_custom_call", output_to_operand_aliasing={{0}: (11, {}), {1}: (12, {})} | custom-call | tf_op jit(solution)/shard_map/last_tick_even/pallas_call | solution.py:246
  (3 shorter events, 0.0 us)
Async XLA Ops:
  1.8 6.4 %collective-permute-start.1 = (bf16[256,256]{1,0:T(8,128)(2,1)S(1)}, bf16[256,256]{1,0:T(8,128)(2,1)S(1)}, u32[]{:S(2)}, u32[]{:S(2)}) collective-permute-start(bf16[256,256]{1,0:T(8,128)(2,1)S(1)} %get-tuple-element.45), channel_id=1, source_target_pairs={{0,4},{1,2},{2,1},{3,7},{4,0},{5,6},{6,5},{7,3},{8,12},{9,10},{10,... | collective-permute-start | bytes 393224 | tf_op jit(solution)/shard_map/ppermute | solution.py:334
  2.4 7.4 %collective-permute-start = (bf16[256,256]{1,0:T(8,128)(2,1)S(1)}, bf16[256,256]{1,0:T(8,128)(2,1)S(1)}, u32[]{:S(2)}, u32[]{:S(2)}) collective-permute-start(bf16[256,256]{1,0:T(8,128)(2,1)S(1)} %get-tuple-element.39.after_ref), channel_id=1, source_target_pairs={{0,1},{1,0},{2,3},{3,2},{4,5},{5,4},{6,7},{7,6},{8,9},{9,8},{10,11... | collective-permute-start | bytes 393224 | tf_op jit(solution)/shard_map/ppermute | solution.py:333
  9.7 8.5 %collective-permute-start.2 = (bf16[528,256]{1,0:T(8,128)(2,1)S(1)}, bf16[528,256]{1,0:T(8,128)(2,1)S(1)}, u32[]{:S(2)}, u32[]{:S(2)}) collective-permute-start(bf16[528,256]{1,0:T(8,128)(2,1)S(1)} %get-tuple-element.46), channel_id=1, source_target_pairs={{0,4},{4,8},{8,12},{12,16},{16,20},{20,24},{24,28},{28,0},{1,5},{5... | collective-permute-start | bytes 811016 | tf_op jit(solution)/shard_map/ppermute | solution.py:411
  10.5 7.3 %collective-permute-start.3 = (bf16[256,256]{1,0:T(8,128)(2,1)S(1)}, bf16[256,256]{1,0:T(8,128)(2,1)S(1)}, u32[]{:S(2)}, u32[]{:S(2)}) collective-permute-start(bf16[256,256]{1,0:T(8,128)(2,1)S(1)} %get-tuple-element.50), channel_id=1, source_target_pairs={{0,5},{1,4},{2,7},{3,6},{4,9},{5,8},{6,11},{7,10},{8,13},{9,12},{1... | collective-permute-start | bytes 393224 | tf_op jit(solution)/shard_map/ppermute | solution.py:375
  12.7 5.2 %collective-permute-start.4 = (bf16[256,256]{1,0:T(8,128)(2,1)S(1)}, bf16[256,256]{1,0:T(8,128)(2,1)S(1)}, u32[]{:S(2)}, u32[]{:S(2)}) collective-permute-start(bf16[256,256]{1,0:T(8,128)(2,1)S(1)} %get-tuple-element.51), channel_id=1, source_target_pairs={{0,4},{1,6},{2,5},{3,7},{4,0},{5,10},{6,9},{7,3},{8,12},{9,14},{10... | collective-permute-start | bytes 393224 | tf_op jit(solution)/shard_map/ppermute | solution.py:375
  13.4 4.5 %collective-permute-start.5 = (bf16[2,128,256]{2,1,0:T(8,128)(2,1)S(1)}, bf16[2,128,256]{2,1,0:T(8,128)(2,1)S(1)}, u32[]{:S(2)}, u32[]{:S(2)}) collective-permute-start(bf16[2,128,256]{2,1,0:T(8,128)(2,1)S(1)} %get-tuple-element.52), channel_id=1, source_target_pairs={{0,4},{4,0},{8,12},{12,8},{16,20},{20,16},{24,28},{28,24},{1,5},{5... | collective-permute-start | bytes 393224 | tf_op jit(solution)/shard_map/ppermute | solution.py:415
  13.4 4.5 %collective-permute-start.6 = (bf16[2,128,256]{2,1,0:T(8,128)(2,1)S(1)}, bf16[2,128,256]{2,1,0:T(8,128)(2,1)S(1)}, u32[]{:S(2)}, u32[]{:S(2)}) collective-permute-start(bf16[2,128,256]{2,1,0:T(8,128)(2,1)S(1)} %get-tuple-element.53), channel_id=1, source_target_pairs={{0,4},{4,0},{8,12},{12,8},{16,20},{20,16},{24,28},{28,24},{1,5},{5... | collective-permute-start | bytes 393224 | tf_op jit(solution)/shard_map/ppermute | solution.py:415
  17.9 8.3 %collective-permute-start.11 = (bf16[528,256]{1,0:T(8,128)(2,1)S(1)}, bf16[528,256]{1,0:T(8,128)(2,1)S(1)}, u32[]{:S(2)}, u32[]{:S(2)}) collective-permute-start(bf16[528,256]{1,0:T(8,128)(2,1)S(1)} %get-tuple-element.59), channel_id=1, source_target_pairs={{0,4},{4,8},{8,12},{12,16},{16,20},{20,24},{24,28},{28,0},{1,5},{5... | collective-permute-start | bytes 811016 | tf_op jit(solution)/shard_map/ppermute | solution.py:411
  19.0 7.2 %collective-permute-start.9 = (bf16[272,256]{1,0:T(8,128)(2,1)S(1)}, bf16[272,256]{1,0:T(8,128)(2,1)S(1)}, u32[]{:S(2)}, u32[]{:S(2)}) collective-permute-start(bf16[272,256]{1,0:T(8,128)(2,1)S(1)} %get-tuple-element.57), channel_id=1, source_target_pairs={{0,5},{1,4},{2,7},{3,6},{4,0},{5,1},{6,2},{7,3},{8,13},{9,12},{10,... | collective-permute-start | bytes 417800 | tf_op jit(solution)/shard_map/ppermute | solution.py:375
  20.9 5.3 %collective-permute-start.10 = (bf16[272,256]{1,0:T(8,128)(2,1)S(1)}, bf16[272,256]{1,0:T(8,128)(2,1)S(1)}, u32[]{:S(2)}, u32[]{:S(2)}) collective-permute-start(bf16[272,256]{1,0:T(8,128)(2,1)S(1)} %get-tuple-element.58), channel_id=1, source_target_pairs={{0,4},{1,6},{2,5},{3,7},{4,0},{5,1},{6,2},{7,3},{8,12},{9,14},{10,... | collective-permute-start | bytes 417800 | tf_op jit(solution)/shard_map/ppermute | solution.py:375
  20.9 1.5 %collective-permute-start.7 = (bf16[2,128,256]{2,1,0:T(8,128)(2,1)S(1)}, bf16[2,128,256]{2,1,0:T(8,128)(2,1)S(1)}, u32[]{:S(2)}, u32[]{:S(2)}) collective-permute-start(bf16[2,128,256]{2,1,0:T(8,128)(2,1)S(1)} %get-tuple-element.55), channel_id=1, source_target_pairs={{0,4},{4,0},{8,12},{12,8},{16,20},{20,16},{24,28},{28,24},{1,5},{5... | collective-permute-start | bytes 393224 | tf_op jit(solution)/shard_map/ppermute | solution.py:415
  21.4 1.4 %collective-permute-start.8 = (bf16[2,128,256]{2,1,0:T(8,128)(2,1)S(1)}, bf16[2,128,256]{2,1,0:T(8,128)(2,1)S(1)}, u32[]{:S(2)}, u32[]{:S(2)}) collective-permute-start(bf16[2,128,256]{2,1,0:T(8,128)(2,1)S(1)} %get-tuple-element.56), channel_id=1, source_target_pairs={{0,4},{4,0},{8,12},{12,8},{16,20},{20,16},{24,28},{28,24},{1,5},{5... | collective-permute-start | bytes 393224 | tf_op jit(solution)/shard_map/ppermute | solution.py:415
  22.4 6.2 %collective-permute-start.15 = (bf16[256,256]{1,0:T(8,128)(2,1)S(1)}, bf16[256,256]{1,0:T(8,128)(2,1)S(1)}, u32[]{:S(2)}, u32[]{:S(2)}) collective-permute-start(bf16[256,256]{1,0:T(8,128)(2,1)S(1)} %get-tuple-element.65), channel_id=1, source_target_pairs={{0,4},{1,5},{2,6},{3,7},{4,9},{5,8},{6,11},{7,10},{8,12},{9,13},{1... | collective-permute-start | bytes 393224 | tf_op jit(solution)/shard_map/ppermute | solution.py:375
  22.7 5.9 %collective-permute-start.16 = (bf16[256,256]{1,0:T(8,128)(2,1)S(1)}, bf16[256,256]{1,0:T(8,128)(2,1)S(1)}, u32[]{:S(2)}, u32[]{:S(2)}) collective-permute-start(bf16[256,256]{1,0:T(8,128)(2,1)S(1)} %get-tuple-element.66), channel_id=1, source_target_pairs={{0,4},{1,5},{2,6},{3,7},{4,0},{5,10},{6,9},{7,3},{8,12},{9,13},{10... | collective-permute-start | bytes 393224 | tf_op jit(solution)/shard_map/ppermute | solution.py:375
  26.2 9.7 %collective-permute-start.12 = (bf16[512,256]{1,0:T(8,128)(2,1)S(1)}, bf16[512,256]{1,0:T(8,128)(2,1)S(1)}, u32[]{:S(2)}, u32[]{:S(2)}) collective-permute-start(bf16[512,256]{1,0:T(8,128)(2,1)S(1)} %get-tuple-element.60), channel_id=1, source_target_pairs={{0,4},{4,8},{8,12},{12,16},{16,20},{20,24},{24,28},{28,0},{1,5},{5... | collective-permute-start | bytes 786440 | tf_op jit(solution)/shard_map/ppermute | solution.py:411
  27.1 8.9 %collective-permute-start.13 = (bf16[272,256]{1,0:T(8,128)(2,1)S(1)}, bf16[272,256]{1,0:T(8,128)(2,1)S(1)}, u32[]{:S(2)}, u32[]{:S(2)}) collective-permute-start(bf16[272,256]{1,0:T(8,128)(2,1)S(1)} %get-tuple-element.61), channel_id=1, source_target_pairs={{0,4},{1,5},{2,6},{3,7},{4,9},{5,8},{6,11},{7,10},{8,12},{9,13},{1... | collective-permute-start | bytes 417800 | tf_op jit(solution)/shard_map/ppermute | solution.py:375
  27.7 8.3 %collective-permute-start.14 = (bf16[272,256]{1,0:T(8,128)(2,1)S(1)}, bf16[272,256]{1,0:T(8,128)(2,1)S(1)}, u32[]{:S(2)}, u32[]{:S(2)}) collective-permute-start(bf16[272,256]{1,0:T(8,128)(2,1)S(1)} %get-tuple-element.62), channel_id=1, source_target_pairs={{0,4},{1,5},{2,6},{3,7},{4,0},{5,10},{6,9},{7,3},{8,12},{9,13},{10... | collective-permute-start | bytes 417800 | tf_op jit(solution)/shard_map/ppermute | solution.py:375
  29.4 6.5 %collective-permute-start.17 = (bf16[256,256]{1,0:T(8,128)(2,1)S(1)}, bf16[256,256]{1,0:T(8,128)(2,1)S(1)}, u32[]{:S(2)}, u32[]{:S(2)}) collective-permute-start(bf16[256,256]{1,0:T(8,128)(2,1)S(1)} %get-tuple-element.70), channel_id=1, source_target_pairs={{0,5},{1,4},{2,7},{3,6},{4,0},{5,1},{6,2},{7,3},{8,13},{9,12},{10,... | collective-permute-start | bytes 393224 | tf_op jit(solution)/shard_map/ppermute | solution.py:375
  31.7 4.2 %collective-permute-start.18 = (bf16[256,256]{1,0:T(8,128)(2,1)S(1)}, bf16[256,256]{1,0:T(8,128)(2,1)S(1)}, u32[]{:S(2)}, u32[]{:S(2)}) collective-permute-start(bf16[256,256]{1,0:T(8,128)(2,1)S(1)} %get-tuple-element.71), channel_id=1, source_target_pairs={{0,4},{1,6},{2,5},{3,7},{4,0},{5,1},{6,2},{7,3},{8,12},{9,14},{10,... | collective-permute-start | bytes 393224 | tf_op jit(solution)/shard_map/ppermute | solution.py:375

commit v15 on v10

--- a/solution.py
+++ b/solution.py
@@ -162,12 +162,31 @@
 
 
 def tick_kernel(
-    parity, tick, sections, plan_ref, ops_ref, source_ref, pass_ref, reflect_ref,
-    wave_refs, first_in_ref, second_in_ref, known_refs, out_refs, buffer, onward,
+    parity, tick, sections, writes, plan_ref, ops_ref, source_ref, pass_ref, reflect_ref,
+    wave_refs, first_in_ref, second_in_ref, earlier, known_refs, out_refs,
+    buffer, onward, write_sems,
 ):
     del known_refs
     echo_ref, first_ref, second_ref, *onward_refs = out_refs
     section = lax.axis_index("depth")
+    if writes:
+        reflected_ref = onward_refs.pop()
+
+        @pl.when(jnp.logical_not(acts(section, parity)))
+        def _():
+            copies = [
+                pltpu.make_async_copy(
+                    (earlier[i] if i < len(earlier) else echo_ref).at[...],
+                    reflected_ref.at[t, 0],
+                    write_sems.at[i],
+                )
+                for i, t in enumerate(writes)
+            ]
+            for copy in copies:
+                copy.start()
+            for copy in copies:
+                copy.wait()
+
     tile = lax.axis_index("lat")
     listed = ids_of(plan_ref, ops_ref)
 
@@ -212,8 +231,10 @@
     @pl.when(acts(section, parity))
     def _():
         copies = [
-            pltpu.make_async_copy(earlier[t], reflected_ref.at[t, 0], early_sems.at[t])
-            for t in range(tick)
+            pltpu.make_async_copy(
+                ref, reflected_ref.at[tick - len(earlier) + i, 0], early_sems.at[i]
+            )
+            for i, ref in enumerate(earlier)
         ]
         for copy in copies:
             copy.start()
@@ -236,21 +257,26 @@
 
 def grouped_call(kernel, groups, outs, out_specs, known, **options):
     flat = [array for group in groups for array in (group if isinstance(group, list) else [group])]
+    kept = [(i, array) for i, array in enumerate(known) if array is not None]
 
     def body(*refs):
         refs = list(refs)
         take = lambda count: [refs.pop(0) for _ in range(count)]
         inputs = [take(len(g)) if isinstance(g, list) else refs.pop(0) for g in groups]
-        kernel(*inputs, take(len(known)), take(len(outs)), *refs)
+        kernel(*inputs, take(len(kept)), take(len(outs)), *refs)
 
     return pl.pallas_call(
         body,
         out_shape=tuple(outs),
-        in_specs=[SMEM_SPEC] + [VMEM_SPEC] * (len(flat) - 1) + list(out_specs[: len(known)]),
+        in_specs=[SMEM_SPEC] + [VMEM_SPEC] * (len(flat) - 1) + [out_specs[i] for i, _ in kept],
         out_specs=tuple(out_specs),
-        input_output_aliases={len(flat) + i: i for i in range(len(known))},
+        input_output_aliases={len(flat) + n: i for n, (i, _) in enumerate(kept)},
         **options,
-    )(flat[0], *map(in_vmem, flat[1:]), *known)
+    )(
+        flat[0],
+        *map(in_vmem, flat[1:]),
+        *[a if out_specs[i] is ANY_SPEC else in_vmem(a) for i, a in kept],
+    )
 
 
 def neighbour(j, turn, tiles):
@@ -374,8 +400,13 @@
         routes = halo_routes(sections, tiles, senders)
         return [lax.ppermute(a, both, route) for a, route in zip(lists, routes)]
 
+    result_types = (
+        jax.ShapeDtypeStruct((ticks, 1, blocks, points, columns), WAVE),
+        jax.ShapeDtypeStruct((1, blocks, points, columns), jnp.float32),
+    )
     arrived = {parity: ([wave], first, second) for parity in (ODD, EVEN)}
     echoes = []
+    reflected = None
     for tick in range(ticks - 1):
         first_step, last_step = tick == 0, tick == ticks - 2
         known = []
@@ -393,17 +424,32 @@
             else:
                 to_next = [pair_type] if last_step else half_types if first_step else part_types
             outs = [wave_type, *lists_of(extra), *to_next]
+            specs = [VMEM_SPEC] * len(outs)
+            writes = range(0)
+            if parity == EVEN and tick >= 1:
+                writes = range(0 if tick == 1 else tick, tick + 1)
+            if parity == ODD and tick >= 2:
+                writes = range(0 if tick == 2 else tick - 1, tick)
+            known = known + [None] * (len(outs) - len(known))
+            if writes:
+                outs, specs, known = outs + [result_types[0]], specs + [ANY_SPEC], known + [reflected]
             echo, *lists = grouped_call(
-                functools.partial(tick_kernel, parity, tick, sections),
-                [*fixed, *arrived[parity]],
+                functools.partial(tick_kernel, parity, tick, sections, tuple(writes)),
+                [*fixed, *arrived[parity], [echoes[t] for t in writes if t < tick]],
                 outs,
-                [VMEM_SPEC] * len(outs),
-                [in_vmem(a) for a in known],
-                scratch_shapes=[buffer_type, pltpu.VMEM(wave_type.shape, WAVE)],
+                specs,
+                known,
+                scratch_shapes=[
+                    buffer_type,
+                    pltpu.VMEM(wave_type.shape, WAVE),
+                    pltpu.SemaphoreType.DMA((2,)),
+                ],
                 compiler_params=params,
                 cost_estimate=tick_cost,
                 name=f"tick{tick}" + ("_odd" if parity else "_even"),
             )
+            if writes:
+                reflected = lists.pop()
             lists, onward = lists[:2], lists[2:]
             known = [echo, *lists] if first_step else [echo]
             if parity == ODD:
@@ -420,15 +466,12 @@
         echoes.append(echo)
 
     tick = ticks - 1
-    results = []
-    result_types = (
-        jax.ShapeDtypeStruct((ticks, 1, blocks, points, columns), WAVE),
-        jax.ShapeDtypeStruct((1, blocks, points, columns), jnp.float32),
-    )
+    unwritten = {ODD: [], EVEN: echoes[-1:] if ticks > 3 else echoes}
+    results = [reflected, None]
     for parity in (ODD, EVEN):
         results = grouped_call(
             functools.partial(last_kernel, parity, tick),
-            [*fixed, *arrived[parity], echoes],
+            [*fixed, *arrived[parity], unwritten[parity]],
             result_types,
             [ANY_SPEC] * 2,
             list(results),

time: 37.8 us -> 39.7 us (1.050)
  starting transfers between devices: 17 us -> 19.2 us
  waiting for transfers between devices: 8.9 us -> 7.73 us
  Pallas kernels: 6.83 us -> 7.65 us
    ppermute x10, starting transfers between devices: 9.98 us -> 12.3 us  [exchange(): return [lax.ppermute(a, both, route) for a, route in zip(lists, routes)]]
    ppermute x10, waiting for transfers between devices: 6.33 us -> 5.16 us  [exchange(): return [lax.ppermute(a, both, route) for a, route in zip(lists, routes)]]
    pallas_call x8, Pallas kernels: 3.94 us -> 4.76 us  [grouped_call(): pl.pallas_call(body, out_shape=tuple(outs), in_specs=[SMEM_SPEC] + [VMEM_...]
    ppermute x3, starting transfers between devices: 1.23 us -> 0.48 us  [per_device(): waves[EVEN] = [lax.ppermute(onward[0], 'depth', crossing)]]
    ppermute x4, starting transfers between devices: 1.09 us -> 1.75 us  [per_device(): waves[ODD] = [lax.ppermute(a, 'depth', inside) for a in onward]]
  transfers between devices with their start and end apart: 19 -> 19, of which waited for: 4 -> 4; matrix products, arithmetic and copies ran while one was open for 0% -> 0% of each run, Pallas kernels for 11% -> 12%
where the time goes in v15:
time: 39.7 us; the launch traced here: 39.5 us
  starting transfers between devices  19.2 us (48%)
  waiting for transfers between devices  7.73 us (19%)
  Pallas kernels  7.65 us (19%)
  blocking collectives  4.15 us (10%)
  between operations  0.76 us (2%)
    ppermute x10, starting transfers between devices, exchange(): return [lax.ppermute(a, both, route) for a, route in zip(lists, routes)]  12.3 us
    ppermute x10, waiting for transfers between devices, exchange(): return [lax.ppermute(a, both, route) for a, route in zip(lists, routes)]  5.16 us
    pallas_call x8, Pallas kernels, grouped_call(): pl.pallas_call(body, out_shape=tuple(outs), in_specs=[SMEM_SPEC] + [VMEM_...  4.76 us
    all_to_all x1, blocking collectives, per_device(): lax.all_to_all(onward[0], 'depth', 0, 0, axis_index_groups=pairs)  4.15 us
    ppermute x1, starting transfers between devices, per_device(): first = lax.ppermute(first, both, routes[0])  4.14 us
    ppermute x4, starting transfers between devices, per_device(): waves[ODD] = [lax.ppermute(a, 'depth', inside) for a in onward]  1.75 us
    pallas_call x1, Pallas kernels, per_device(): pl.pallas_call(load_kernel, out_shape=(pltpu.VMEM(operators.shape, operat...  1.67 us
    ppermute x1, waiting for transfers between devices, per_device(): first = lax.ppermute(first, both, routes[0])  1.52 us
  transfers between devices with their start and end apart: 19, of which 4 were waited for; matrix products, arithmetic and copies ran while one was open for 0% of the time, Pallas kernels for 12%

profile of v15, /device:TPU:0, one launch (start us, length us, event | category | flops | bytes accessed | tf_op | source)
XLA Modules:
  0.0 39.5 jit_solution(1732798269875839680)
XLA Ops:
  0.6 1.2 %prepare.1 = (s32[30]{0:T(128)S(4)}, bf16[4,128,256]{2,1,0:T(8,128)(2,1)S(1)}, bf16[256,256]{1,0:T(8,128)(2,1)S(1)}, bf16[256,256]{1,0:T(8,128)(2,1)S(1)}) custom-call(s32[1,2,2]{2,1,0:T(2,128)} %ids_hbm.1, s32[1,2]{1,0:T(1,128)} %count_hbm.1, s32[4,6]{1,0:T(4,128)} %pattern_hbm.1, f32[1,4,128,256]{3,2,1,0:T(8,128)} %inflow_hbm.1), custom_call_target="tpu_custom_call" | custom-call | flops 131072 | bytes 1048576 | tf_op jit(solution)/shard_map/prepare/pallas_call | solution.py:333
  1.9 0.5 %collective-permute-start.1 = (bf16[256,256]{1,0:T(8,128)(2,1)S(1)}, bf16[256,256]{1,0:T(8,128)(2,1)S(1)}, u32[]{:S(2)}, u32[]{:S(2)}) collective-permute-start(bf16[256,256]{1,0:T(8,128)(2,1)S(1)} %get-tuple-element.48), channel_id=1, source_target_pairs={{0,4},{1,2},{2,1},{3,7},{4,0},{5,6},{6,5},{7,3},{8,12},{9,10},{10,... | collective-permute-start | bytes 393224 | tf_op jit(solution)/shard_map/ppermute | solution.py:360
  2.4 4.1 %collective-permute-start = (bf16[256,256]{1,0:T(8,128)(2,1)S(1)}, bf16[256,256]{1,0:T(8,128)(2,1)S(1)}, u32[]{:S(2)}, u32[]{:S(2)}) collective-permute-start(bf16[256,256]{1,0:T(8,128)(2,1)S(1)} %get-tuple-element.42.after_ref), channel_id=1, source_target_pairs={{0,1},{1,0},{2,3},{3,2},{4,5},{5,4},{6,7},{7,6},{8,9},{9,8},{10,11... | collective-permute-start | bytes 393224 | tf_op jit(solution)/shard_map/ppermute | solution.py:359
  6.5 1.7 %load.1 = (bf16[1,4,6,2,128,128]{5,4,3,2,1,0:T(8,128)(2,1)S(1)}, bf16[3,4,128,256]{3,2,1,0:T(8,128)(2,1)S(1)}, f32[4,128,128]{2,1,0:T(8,128)S(1)}, f32[4,128,128]{2,1,0:T(8,128)S(1)}) custom-call(bf16[1,4,6,2,128,128]{5,4,3,2,1,0:T(8,128)(2,1)} %ops_hbm.1, bf16[3,4,128,256]{3,2,1,0:T(8,128)(2,1)} %source_hbm.1, f32[1,4,128]{2,1,0:T(4,128)} %pass_hbm.1, ...), custom_call_target="tpu_custom_call" | custom-call | bytes 4718592 | tf_op jit(solution)/shard_map/load/pallas_call | solution.py:363
  8.2 0.0 collective-permute-done.1.refs_7_
  8.2 1.5 %collective-permute-done.refs_6_ = bf16[256,256]{1,0:T(8,128)(2,1)S(1)} collective-permute-done((bf16[256,256]{1,0:T(8,128)(2,1)S(1)}, bf16[256,256]{1,0:T(8,128)(2,1)S(1)}, u32[]{:S(2)}, u32[]{:S(2)}) %collective-permute-start) | collective-permute-done | bytes 131104 | tf_op jit(solution)/shard_map/ppermute | solution.py:359
  9.8 0.1 collective-permute-start.2
  9.8 0.8 %tick0_even.1 = (bf16[4,128,256]{2,1,0:T(8,128)(2,1)S(1)}, bf16[256,256]{1,0:T(8,128)(2,1)S(1)}, bf16[256,256]{1,0:T(8,128)(2,1)S(1)}, bf16[2,128,256]{2,1,0:T(8,128)(2,1)S(1)}, bf16[2,128,256]{2,1,0:T(8,128)(2,1)S(1)}) custom-call(s32[30]{0:T(128)S(4)} %get-tuple-element.41.refs_0_, ...), custom_call_target="tpu_custom_call", output_to_operand_aliasing={{0}: (8, {}), {1}: (9, {}), {2}: (10, {})} | custom-call | tf_op jit(solution)/shard_map/tick0_even/pallas_call | solution.py:268
  10.6 2.2 %collective-permute-start.3 = (bf16[256,256]{1,0:T(8,128)(2,1)S(1)}, bf16[256,256]{1,0:T(8,128)(2,1)S(1)}, u32[]{:S(2)}, u32[]{:S(2)}) collective-permute-start(bf16[256,256]{1,0:T(8,128)(2,1)S(1)} %get-tuple-element.53), channel_id=1, source_target_pairs={{0,5},{1,4},{2,7},{3,6},{4,9},{5,8},{6,11},{7,10},{8,13},{9,12},{1... | collective-permute-start | bytes 393224 | tf_op jit(solution)/shard_map/ppermute | solution.py:401
  12.9 0.6 %collective-permute-start.4 = (bf16[256,256]{1,0:T(8,128)(2,1)S(1)}, bf16[256,256]{1,0:T(8,128)(2,1)S(1)}, u32[]{:S(2)}, u32[]{:S(2)}) collective-permute-start(bf16[256,256]{1,0:T(8,128)(2,1)S(1)} %get-tuple-element.54), channel_id=1, source_target_pairs={{0,4},{1,6},{2,5},{3,7},{4,0},{5,10},{6,9},{7,3},{8,12},{9,14},{10... | collective-permute-start | bytes 393224 | tf_op jit(solution)/shard_map/ppermute | solution.py:401
  13.5 0.0 collective-permute-start.5
  13.5 0.5 %collective-permute-start.6 = (bf16[2,128,256]{2,1,0:T(8,128)(2,1)S(1)}, bf16[2,128,256]{2,1,0:T(8,128)(2,1)S(1)}, u32[]{:S(2)}, u32[]{:S(2)}) collective-permute-start(bf16[2,128,256]{2,1,0:T(8,128)(2,1)S(1)} %get-tuple-element.57), channel_id=1, source_target_pairs={{0,4},{4,0},{8,12},{12,8},{16,20},{20,16},{24,28},{28,24},{1,5},{5... | collective-permute-start | bytes 393224 | tf_op jit(solution)/shard_map/ppermute | solution.py:460
  14.0 4.0 %collective-permute-done.3.refs_7_.refs_6_ = bf16[256,256]{1,0:T(8,128)(2,1)S(1)} collective-permute-done((bf16[256,256]{1,0:T(8,128)(2,1)S(1)}, bf16[256,256]{1,0:T(8,128)(2,1)S(1)}, u32[]{:S(2)}, u32[]{:S(2)}) %collective-permute-start.3) | collective-permute-done | bytes 131104 | tf_op jit(solution)/shard_map/ppermute | solution.py:401
  17.9 0.0 collective-permute-done.4.refs_8_.refs_7_
  18.0 0.0 collective-permute-done.5.refs_5_
  18.0 0.0 collective-permute-done.6.refs_6_
  18.0 0.4 collective-permute-start.14
  18.4 0.0 collective-permute-done.2.refs_5_
  18.4 0.8 %tick1_even.1 = (bf16[4,128,256]{2,1,0:T(8,128)(2,1)S(1)}, bf16[272,256]{1,0:T(8,128)(2,1)S(1)}, bf16[272,256]{1,0:T(8,128)(2,1)S(1)}, bf16[2,128,256]{2,1,0:T(8...) custom-call(s32[30]{0:T(128)S(4)} %get-tuple-element.41.refs_0_, ...), custom_call_target="tpu_custom_call", output_to_operand_aliasing={{0}: (9, {})} | custom-call | tf_op jit(solution)/shard_map/tick1_even/pallas_call | solution.py:268
  19.1 0.7 %collective-permute-start.7 = (bf16[2,128,256]{2,1,0:T(8,128)(2,1)S(1)}, bf16[2,128,256]{2,1,0:T(8,128)(2,1)S(1)}, u32[]{:S(2)}, u32[]{:S(2)}) collective-permute-start(bf16[2,128,256]{2,1,0:T(8,128)(2,1)S(1)} %get-tuple-element.59), channel_id=1, source_target_pairs={{0,4},{4,0},{8,12},{12,8},{16,20},{20,16},{24,28},{28,24},{1,5},{5... | collective-permute-start | bytes 393224 | tf_op jit(solution)/shard_map/ppermute | solution.py:460
  19.9 2.1 %collective-permute-start.9 = (bf16[272,256]{1,0:T(8,128)(2,1)S(1)}, bf16[272,256]{1,0:T(8,128)(2,1)S(1)}, u32[]{:S(2)}, u32[]{:S(2)}) collective-permute-start(bf16[272,256]{1,0:T(8,128)(2,1)S(1)} %get-tuple-element.61), channel_id=1, source_target_pairs={{0,5},{1,4},{2,7},{3,6},{4,0},{5,1},{6,2},{7,3},{8,13},{9,12},{10,... | collective-permute-start | bytes 417800 | tf_op jit(solution)/shard_map/ppermute | solution.py:401
  22.0 0.0 collective-permute-start.10
  22.0 0.5 %collective-permute-start.8 = (bf16[2,128,256]{2,1,0:T(8,128)(2,1)S(1)}, bf16[2,128,256]{2,1,0:T(8,128)(2,1)S(1)}, u32[]{:S(2)}, u32[]{:S(2)}) collective-permute-start(bf16[2,128,256]{2,1,0:T(8,128)(2,1)S(1)} %get-tuple-element.60), channel_id=1, source_target_pairs={{0,4},{4,0},{8,12},{12,8},{16,20},{20,16},{24,28},{28,24},{1,5},{5... | collective-permute-start | bytes 393224 | tf_op jit(solution)/shard_map/ppermute | solution.py:460
  22.5 0.0 collective-permute-done.7.refs_5_
  22.5 0.0 collective-permute-start.15
  22.5 1.0 %collective-permute-done.8.refs_6_ = bf16[2,128,256]{2,1,0:T(8,128)(2,1)S(1)} collective-permute-done((bf16[2,128,256]{2,1,0:T(8,128)(2,1)S(1)}, bf16[2,128,256]{2,1,0:T(8,128)(2,1)S(1)}, u32[]{:S(2)}, u32[]{:S(2)}) %collective-permute-start.8) | collective-permute-done | bytes 131104 | tf_op jit(solution)/shard_map/ppermute | solution.py:460
  23.6 2.9 %collective-permute-start.16 = (bf16[256,256]{1,0:T(8,128)(2,1)S(1)}, bf16[256,256]{1,0:T(8,128)(2,1)S(1)}, u32[]{:S(2)}, u32[]{:S(2)}) collective-permute-start(bf16[256,256]{1,0:T(8,128)(2,1)S(1)} %get-tuple-element.70), channel_id=1, source_target_pairs={{0,4},{1,5},{2,6},{3,7},{4,0},{5,10},{6,9},{7,3},{8,12},{9,13},{10... | collective-permute-start | bytes 393224 | tf_op jit(solution)/shard_map/ppermute | solution.py:401
  26.5 0.0 collective-permute-done.9.refs_7_
  26.5 0.0 collective-permute-done.10.refs_8_
  26.5 0.8 %tick2_odd.1 = (bf16[4,128,256]{2,1,0:T(8,128)(2,1)S(1)}, bf16[272,256]{1,0:T(8,128)(2,1)S(1)}, bf16[272,256]{1,0:T(8,128)(2,1)S(1)}, bf16[512,256]{1,0:T(8,128)(2,1)S(1)}, bf16[4,1,4,128,256]{4,3,2,1,0:T(8,128)(2,1)}) custom-call(s32[30]{0:T(128)S(4)} %get-tuple-element.41.refs_0_, ...), custom_call_target="tpu_custom_call", output_to_operand_aliasing={{4}: (11, {})} | custom-call | tf_op jit(solution)/shard_map/tick2_odd/pallas_call | solution.py:268
  27.3 0.1 collective-permute-start.11
  27.4 0.5 %collective-permute-start.12 = (bf16[272,256]{1,0:T(8,128)(2,1)S(1)}, bf16[272,256]{1,0:T(8,128)(2,1)S(1)}, u32[]{:S(2)}, u32[]{:S(2)}) collective-permute-start(bf16[272,256]{1,0:T(8,128)(2,1)S(1)} %get-tuple-element.66), channel_id=1, source_target_pairs={{0,4},{1,5},{2,6},{3,7},{4,9},{5,8},{6,11},{7,10},{8,12},{9,13},{1... | collective-permute-start | bytes 417800 | tf_op jit(solution)/shard_map/ppermute | solution.py:401
  27.9 1.2 %collective-permute-done.15.refs_6_ = bf16[256,256]{1,0:T(8,128)(2,1)S(1)} collective-permute-done((bf16[256,256]{1,0:T(8,128)(2,1)S(1)}, bf16[256,256]{1,0:T(8,128)(2,1)S(1)}, u32[]{:S(2)}, u32[]{:S(2)}) %collective-permute-start.15) | collective-permute-done | bytes 131104 | tf_op jit(solution)/shard_map/ppermute | solution.py:401
  29.1 1.6 %collective-permute-start.13 = (bf16[272,256]{1,0:T(8,128)(2,1)S(1)}, bf16[272,256]{1,0:T(8,128)(2,1)S(1)}, u32[]{:S(2)}, u32[]{:S(2)}) collective-permute-start(bf16[272,256]{1,0:T(8,128)(2,1)S(1)} %get-tuple-element.67), channel_id=1, source_target_pairs={{0,4},{1,5},{2,6},{3,7},{4,0},{5,10},{6,9},{7,3},{8,12},{9,13},{10... | collective-permute-start | bytes 417800 | tf_op jit(solution)/shard_map/ppermute | solution.py:401
  30.7 0.0 collective-permute-done.16.refs_7_
  30.7 0.0 collective-permute-done.14.refs_5_
  30.7 0.8 %tick2_even.1 = (bf16[4,128,256]{2,1,0:T(8,128)(2,1)S(1)}, bf16[256,256]{1,0:T(8,128)(2,1)S(1)}, bf16[256,256]{1,0:T(8,128)(2,1)S(1)}, bf16[2,4,128,256]{3,2,1,0:T(8,128)(2,1)S(1)}, bf16[4,1,4,128,256]{4,3,2,1,0:T(8,128)(2,1)}) custom-call(s32[30]{0:T(128)S(4)} %get-tuple-element.41.refs_0_, ...), custom_call_target="tpu_custom_call", output_to_operand_aliasing={{0}: (8, {}), {4}: (9, {})} | custom-call | tf_op jit(solution)/shard_map/tick2_even/pallas_call | solution.py:268
  31.5 2.2 %collective-permute-start.17 = (bf16[256,256]{1,0:T(8,128)(2,1)S(1)}, bf16[256,256]{1,0:T(8,128)(2,1)S(1)}, u32[]{:S(2)}, u32[]{:S(2)}) collective-permute-start(bf16[256,256]{1,0:T(8,128)(2,1)S(1)} %get-tuple-element.75), channel_id=1, source_target_pairs={{0,5},{1,4},{2,7},{3,6},{4,0},{5,1},{6,2},{7,3},{8,13},{9,12},{10,... | collective-permute-start | bytes 393224 | tf_op jit(solution)/shard_map/ppermute | solution.py:401
  33.7 0.0 collective-permute-start.18
  33.7 4.1 %all_to_all.5.refs_5_ = bf16[2,4,128,256]{3,2,1,0:T(8,128)(2,1)S(1)} all-to-all(bf16[2,4,128,256]{3,2,1,0:T(8,128)(2,1)S(1)} %get-tuple-element.74), channel_id=1, replica_groups={{0,4},{8,12},{16,20},{24,28},{1,5},{9,13},{17,21},{25,29},{2,6},{10,14}..., dimensions={0} | all-to-all | bytes 1048576 | tf_op jit(solution)/shard_map/all_to_all | solution.py:458
  37.9 0.0 collective-permute-done.17.refs_6_
  37.9 0.0 collective-permute-done.18.refs_7_
  37.9 0.1 last_tick_odd.1
  38.0 0.0 collective-permute-done.12.refs_6_
  38.0 0.0 collective-permute-done.13.refs_7_
  38.0 0.0 collective-permute-done.11.refs_5_
  38.0 1.5 %last_tick_even.1 = (bf16[4,1,4,128,256]{4,3,2,1,0:T(8,128)(2,1)}, f32[1,4,128,256]{3,2,1,0:T(8,128)}) custom-call(s32[30]{0:T(128)S(4)} %get-tuple-element.41.refs_0_, bf16[1,4,6,2,128,128]{5,4,3,2,1,0:T(8,128)(2,1)S(1)} %get-tuple-element.43.refs_1_, ...), custom_call_target="tpu_custom_call", output_to_operand_aliasing={{0}: (9, {}), {1}: (10, {})} | custom-call | tf_op jit(solution)/shard_map/last_tick_even/pallas_call | solution.py:268
  (2 shorter events, 0.1 us)
Async XLA Ops:
  1.9 6.3 %collective-permute-start.1 = (bf16[256,256]{1,0:T(8,128)(2,1)S(1)}, bf16[256,256]{1,0:T(8,128)(2,1)S(1)}, u32[]{:S(2)}, u32[]{:S(2)}) collective-permute-start(bf16[256,256]{1,0:T(8,128)(2,1)S(1)} %get-tuple-element.48), channel_id=1, source_target_pairs={{0,4},{1,2},{2,1},{3,7},{4,0},{5,6},{6,5},{7,3},{8,12},{9,10},{10,... | collective-permute-start | bytes 393224 | tf_op jit(solution)/shard_map/ppermute | solution.py:360
  2.4 7.4 %collective-permute-start = (bf16[256,256]{1,0:T(8,128)(2,1)S(1)}, bf16[256,256]{1,0:T(8,128)(2,1)S(1)}, u32[]{:S(2)}, u32[]{:S(2)}) collective-permute-start(bf16[256,256]{1,0:T(8,128)(2,1)S(1)} %get-tuple-element.42.after_ref), channel_id=1, source_target_pairs={{0,1},{1,0},{2,3},{3,2},{4,5},{5,4},{6,7},{7,6},{8,9},{9,8},{10,11... | collective-permute-start | bytes 393224 | tf_op jit(solution)/shard_map/ppermute | solution.py:359
  9.8 8.6 %collective-permute-start.2 = (bf16[512,256]{1,0:T(8,128)(2,1)S(1)}, bf16[512,256]{1,0:T(8,128)(2,1)S(1)}, u32[]{:S(2)}, u32[]{:S(2)}) collective-permute-start(bf16[512,256]{1,0:T(8,128)(2,1)S(1)} %get-tuple-element.49), channel_id=1, source_target_pairs={{0,4},{4,8},{8,12},{12,16},{16,20},{20,24},{24,28},{28,0},{1,5},{5... | collective-permute-start | bytes 786440 | tf_op jit(solution)/shard_map/ppermute | solution.py:456
  10.6 7.3 %collective-permute-start.3 = (bf16[256,256]{1,0:T(8,128)(2,1)S(1)}, bf16[256,256]{1,0:T(8,128)(2,1)S(1)}, u32[]{:S(2)}, u32[]{:S(2)}) collective-permute-start(bf16[256,256]{1,0:T(8,128)(2,1)S(1)} %get-tuple-element.53), channel_id=1, source_target_pairs={{0,5},{1,4},{2,7},{3,6},{4,9},{5,8},{6,11},{7,10},{8,13},{9,12},{1... | collective-permute-start | bytes 393224 | tf_op jit(solution)/shard_map/ppermute | solution.py:401
  12.9 5.1 %collective-permute-start.4 = (bf16[256,256]{1,0:T(8,128)(2,1)S(1)}, bf16[256,256]{1,0:T(8,128)(2,1)S(1)}, u32[]{:S(2)}, u32[]{:S(2)}) collective-permute-start(bf16[256,256]{1,0:T(8,128)(2,1)S(1)} %get-tuple-element.54), channel_id=1, source_target_pairs={{0,4},{1,6},{2,5},{3,7},{4,0},{5,10},{6,9},{7,3},{8,12},{9,14},{10... | collective-permute-start | bytes 393224 | tf_op jit(solution)/shard_map/ppermute | solution.py:401
  13.5 4.5 %collective-permute-start.5 = (bf16[2,128,256]{2,1,0:T(8,128)(2,1)S(1)}, bf16[2,128,256]{2,1,0:T(8,128)(2,1)S(1)}, u32[]{:S(2)}, u32[]{:S(2)}) collective-permute-start(bf16[2,128,256]{2,1,0:T(8,128)(2,1)S(1)} %get-tuple-element.56), channel_id=1, source_target_pairs={{0,4},{4,0},{8,12},{12,8},{16,20},{20,16},{24,28},{28,24},{1,5},{5... | collective-permute-start | bytes 393224 | tf_op jit(solution)/shard_map/ppermute | solution.py:460
  13.5 4.5 %collective-permute-start.6 = (bf16[2,128,256]{2,1,0:T(8,128)(2,1)S(1)}, bf16[2,128,256]{2,1,0:T(8,128)(2,1)S(1)}, u32[]{:S(2)}, u32[]{:S(2)}) collective-permute-start(bf16[2,128,256]{2,1,0:T(8,128)(2,1)S(1)} %get-tuple-element.57), channel_id=1, source_target_pairs={{0,4},{4,0},{8,12},{12,8},{16,20},{20,16},{24,28},{28,24},{1,5},{5... | collective-permute-start | bytes 393224 | tf_op jit(solution)/shard_map/ppermute | solution.py:460
  18.0 12.7 %collective-permute-start.14 = (bf16[528,256]{1,0:T(8,128)(2,1)S(1)}, bf16[528,256]{1,0:T(8,128)(2,1)S(1)}, u32[]{:S(2)}, u32[]{:S(2)}) collective-permute-start(bf16[528,256]{1,0:T(8,128)(2,1)S(1)} %get-tuple-element.68), channel_id=1, source_target_pairs={{0,4},{4,8},{8,12},{12,16},{16,20},{20,24},{24,28},{28,0},{1,5},{5... | collective-permute-start | bytes 811016 | tf_op jit(solution)/shard_map/ppermute | solution.py:456
  19.1 3.4 %collective-permute-start.7 = (bf16[2,128,256]{2,1,0:T(8,128)(2,1)S(1)}, bf16[2,128,256]{2,1,0:T(8,128)(2,1)S(1)}, u32[]{:S(2)}, u32[]{:S(2)}) collective-permute-start(bf16[2,128,256]{2,1,0:T(8,128)(2,1)S(1)} %get-tuple-element.59), channel_id=1, source_target_pairs={{0,4},{4,0},{8,12},{12,8},{16,20},{20,16},{24,28},{28,24},{1,5},{5... | collective-permute-start | bytes 393224 | tf_op jit(solution)/shard_map/ppermute | solution.py:460
  19.9 6.6 %collective-permute-start.9 = (bf16[272,256]{1,0:T(8,128)(2,1)S(1)}, bf16[272,256]{1,0:T(8,128)(2,1)S(1)}, u32[]{:S(2)}, u32[]{:S(2)}) collective-permute-start(bf16[272,256]{1,0:T(8,128)(2,1)S(1)} %get-tuple-element.61), channel_id=1, source_target_pairs={{0,5},{1,4},{2,7},{3,6},{4,0},{5,1},{6,2},{7,3},{8,13},{9,12},{10,... | collective-permute-start | bytes 417800 | tf_op jit(solution)/shard_map/ppermute | solution.py:401
  22.0 4.5 %collective-permute-start.10 = (bf16[272,256]{1,0:T(8,128)(2,1)S(1)}, bf16[272,256]{1,0:T(8,128)(2,1)S(1)}, u32[]{:S(2)}, u32[]{:S(2)}) collective-permute-start(bf16[272,256]{1,0:T(8,128)(2,1)S(1)} %get-tuple-element.62), channel_id=1, source_target_pairs={{0,4},{1,6},{2,5},{3,7},{4,0},{5,1},{6,2},{7,3},{8,12},{9,14},{10,... | collective-permute-start | bytes 417800 | tf_op jit(solution)/shard_map/ppermute | solution.py:401
  22.0 1.5 %collective-permute-start.8 = (bf16[2,128,256]{2,1,0:T(8,128)(2,1)S(1)}, bf16[2,128,256]{2,1,0:T(8,128)(2,1)S(1)}, u32[]{:S(2)}, u32[]{:S(2)}) collective-permute-start(bf16[2,128,256]{2,1,0:T(8,128)(2,1)S(1)} %get-tuple-element.60), channel_id=1, source_target_pairs={{0,4},{4,0},{8,12},{12,8},{16,20},{20,16},{24,28},{28,24},{1,5},{5... | collective-permute-start | bytes 393224 | tf_op jit(solution)/shard_map/ppermute | solution.py:460
  22.5 6.6 %collective-permute-start.15 = (bf16[256,256]{1,0:T(8,128)(2,1)S(1)}, bf16[256,256]{1,0:T(8,128)(2,1)S(1)}, u32[]{:S(2)}, u32[]{:S(2)}) collective-permute-start(bf16[256,256]{1,0:T(8,128)(2,1)S(1)} %get-tuple-element.69), channel_id=1, source_target_pairs={{0,4},{1,5},{2,6},{3,7},{4,9},{5,8},{6,11},{7,10},{8,12},{9,13},{1... | collective-permute-start | bytes 393224 | tf_op jit(solution)/shard_map/ppermute | solution.py:401
  23.6 7.1 %collective-permute-start.16 = (bf16[256,256]{1,0:T(8,128)(2,1)S(1)}, bf16[256,256]{1,0:T(8,128)(2,1)S(1)}, u32[]{:S(2)}, u32[]{:S(2)}) collective-permute-start(bf16[256,256]{1,0:T(8,128)(2,1)S(1)} %get-tuple-element.70), channel_id=1, source_target_pairs={{0,4},{1,5},{2,6},{3,7},{4,0},{5,10},{6,9},{7,3},{8,12},{9,13},{10... | collective-permute-start | bytes 393224 | tf_op jit(solution)/shard_map/ppermute | solution.py:401
  27.3 10.7 %collective-permute-start.11 = (bf16[512,256]{1,0:T(8,128)(2,1)S(1)}, bf16[512,256]{1,0:T(8,128)(2,1)S(1)}, u32[]{:S(2)}, u32[]{:S(2)}) collective-permute-start(bf16[512,256]{1,0:T(8,128)(2,1)S(1)} %get-tuple-element.65), channel_id=1, source_target_pairs={{0,4},{4,8},{8,12},{12,16},{16,20},{20,24},{24,28},{28,0},{1,5},{5... | collective-permute-start | bytes 786440 | tf_op jit(solution)/shard_map/ppermute | solution.py:456
  27.4 10.6 %collective-permute-start.12 = (bf16[272,256]{1,0:T(8,128)(2,1)S(1)}, bf16[272,256]{1,0:T(8,128)(2,1)S(1)}, u32[]{:S(2)}, u32[]{:S(2)}) collective-permute-start(bf16[272,256]{1,0:T(8,128)(2,1)S(1)} %get-tuple-element.66), channel_id=1, source_target_pairs={{0,4},{1,5},{2,6},{3,7},{4,9},{5,8},{6,11},{7,10},{8,12},{9,13},{1... | collective-permute-start | bytes 417800 | tf_op jit(solution)/shard_map/ppermute | solution.py:401
  29.1 8.9 %collective-permute-start.13 = (bf16[272,256]{1,0:T(8,128)(2,1)S(1)}, bf16[272,256]{1,0:T(8,128)(2,1)S(1)}, u32[]{:S(2)}, u32[]{:S(2)}) collective-permute-start(bf16[272,256]{1,0:T(8,128)(2,1)S(1)} %get-tuple-element.67), channel_id=1, source_target_pairs={{0,4},{1,5},{2,6},{3,7},{4,0},{5,10},{6,9},{7,3},{8,12},{9,13},{10... | collective-permute-start | bytes 417800 | tf_op jit(solution)/shard_map/ppermute | solution.py:401
  31.5 6.4 %collective-permute-start.17 = (bf16[256,256]{1,0:T(8,128)(2,1)S(1)}, bf16[256,256]{1,0:T(8,128)(2,1)S(1)}, u32[]{:S(2)}, u32[]{:S(2)}) collective-permute-start(bf16[256,256]{1,0:T(8,128)(2,1)S(1)} %get-tuple-element.75), channel_id=1, source_target_pairs={{0,5},{1,4},{2,7},{3,6},{4,0},{5,1},{6,2},{7,3},{8,13},{9,12},{10,... | collective-permute-start | bytes 393224 | tf_op jit(solution)/shard_map/ppermute | solution.py:401
  33.7 4.2 %collective-permute-start.18 = (bf16[256,256]{1,0:T(8,128)(2,1)S(1)}, bf16[256,256]{1,0:T(8,128)(2,1)S(1)}, u32[]{:S(2)}, u32[]{:S(2)}) collective-permute-start(bf16[256,256]{1,0:T(8,128)(2,1)S(1)} %get-tuple-element.76), channel_id=1, source_target_pairs={{0,4},{1,6},{2,5},{3,7},{4,0},{5,1},{6,2},{7,3},{8,12},{9,14},{10,... | collective-permute-start | bytes 393224 | tf_op jit(solution)/shard_map/ppermute | solution.py:401

commit v16 on v10

--- a/solution.py
+++ b/solution.py
@@ -386,9 +386,9 @@
             elif last_step:
                 extra = 16 if parity == ODD else 0
             else:
-                extra = 0 if parity == ODD else 16
+                extra = 0 if parity == ODD else 32
             if parity == ODD:
-                long = 0 if first_step or last_step else 16
+                long = 0 if first_step or last_step else 32
                 to_next = [pltpu.VMEM((blocks * points + long, columns), WAVE)]
             else:
                 to_next = [pair_type] if last_step else half_types if first_step else part_types

time: 37.8 us -> 38.7 us (1.024)
  starting transfers between devices: 17 us -> 19.1 us
  waiting for transfers between devices: 8.9 us -> 7.68 us
    ppermute x10, starting transfers between devices: 9.98 us -> 12.2 us  [exchange(): return [lax.ppermute(a, both, route) for a, route in zip(lists, routes)]]
    ppermute x10, waiting for transfers between devices: 6.33 us -> 5.09 us  [exchange(): return [lax.ppermute(a, both, route) for a, route in zip(lists, routes)]]
where the time goes in v16:
time: 38.7 us; the launch traced here: 38.4 us
  starting transfers between devices  19.1 us (49%)
  waiting for transfers between devices  7.68 us (20%)
  Pallas kernels  6.74 us (17%)
  blocking collectives  4.15 us (11%)
  between operations  0.74 us (2%)
    ppermute x10, starting transfers between devices, exchange(): return [lax.ppermute(a, both, route) for a, route in zip(lists, routes)]  12.2 us
    ppermute x10, waiting for transfers between devices, exchange(): return [lax.ppermute(a, both, route) for a, route in zip(lists, routes)]  5.09 us
    ppermute x1, starting transfers between devices, per_device(): first = lax.ppermute(first, both, routes[0])  4.15 us
    all_to_all x1, blocking collectives, per_device(): lax.all_to_all(onward[0], 'depth', 0, 0, axis_index_groups=pairs)  4.15 us
    pallas_call x8, Pallas kernels, grouped_call(): pl.pallas_call(body, out_shape=tuple(outs), in_specs=[SMEM_SPEC] + [VMEM_...  3.86 us
    pallas_call x1, Pallas kernels, per_device(): pl.pallas_call(load_kernel, out_shape=(pltpu.VMEM(operators.shape, operat...  1.67 us
    ppermute x1, waiting for transfers between devices, per_device(): first = lax.ppermute(first, both, routes[0])  1.52 us
    pallas_call x1, Pallas kernels, per_device(): pl.pallas_call(prepare_kernel, out_shape=(pltpu.SMEM((2 * (listed + 1) +...  1.21 us
  transfers between devices with their start and end apart: 19, of which 4 were waited for; matrix products, arithmetic and copies ran while one was open for 0% of the time, Pallas kernels for 11%

profile of v16, /device:TPU:0, one launch (start us, length us, event | category | flops | bytes accessed | tf_op | source)
XLA Modules:
  0.0 38.4 jit_solution(9430044149151938828)
XLA Ops:
  0.6 1.2 %prepare.1 = (s32[30]{0:T(128)S(4)}, bf16[4,128,256]{2,1,0:T(8,128)(2,1)S(1)}, bf16[256,256]{1,0:T(8,128)(2,1)S(1)}, bf16[256,256]{1,0:T(8,128)(2,1)S(1)}) custom-call(s32[1,2,2]{2,1,0:T(2,128)} %ids_hbm.1, s32[1,2]{1,0:T(1,128)} %count_hbm.1, s32[4,6]{1,0:T(4,128)} %pattern_hbm.1, f32[1,4,128,256]{3,2,1,0:T(8,128)} %inflow_hbm.1), custom_call_target="tpu_custom_call" | custom-call | flops 131072 | bytes 1048576 | tf_op jit(solution)/shard_map/prepare/pallas_call | solution.py:307
  1.8 0.5 %collective-permute-start.1 = (bf16[256,256]{1,0:T(8,128)(2,1)S(1)}, bf16[256,256]{1,0:T(8,128)(2,1)S(1)}, u32[]{:S(2)}, u32[]{:S(2)}) collective-permute-start(bf16[256,256]{1,0:T(8,128)(2,1)S(1)} %get-tuple-element.45), channel_id=1, source_target_pairs={{0,4},{1,2},{2,1},{3,7},{4,0},{5,6},{6,5},{7,3},{8,12},{9,10},{10,... | collective-permute-start | bytes 393224 | tf_op jit(solution)/shard_map/ppermute | solution.py:334
  2.4 4.2 %collective-permute-start = (bf16[256,256]{1,0:T(8,128)(2,1)S(1)}, bf16[256,256]{1,0:T(8,128)(2,1)S(1)}, u32[]{:S(2)}, u32[]{:S(2)}) collective-permute-start(bf16[256,256]{1,0:T(8,128)(2,1)S(1)} %get-tuple-element.39.after_ref), channel_id=1, source_target_pairs={{0,1},{1,0},{2,3},{3,2},{4,5},{5,4},{6,7},{7,6},{8,9},{9,8},{10,11... | collective-permute-start | bytes 393224 | tf_op jit(solution)/shard_map/ppermute | solution.py:333
  6.5 1.7 %load.1 = (bf16[1,4,6,2,128,128]{5,4,3,2,1,0:T(8,128)(2,1)S(1)}, bf16[3,4,128,256]{3,2,1,0:T(8,128)(2,1)S(1)}, f32[4,128,128]{2,1,0:T(8,128)S(1)}, f32[4,128,128]{2,1,0:T(8,128)S(1)}) custom-call(bf16[1,4,6,2,128,128]{5,4,3,2,1,0:T(8,128)(2,1)} %ops_hbm.1, bf16[3,4,128,256]{3,2,1,0:T(8,128)(2,1)} %source_hbm.1, f32[1,4,128]{2,1,0:T(4,128)} %pass_hbm.1, ...), custom_call_target="tpu_custom_call" | custom-call | bytes 4718592 | tf_op jit(solution)/shard_map/load/pallas_call | solution.py:337
  8.2 0.0 collective-permute-done.1.refs_7_
  8.2 1.5 %collective-permute-done.refs_6_ = bf16[256,256]{1,0:T(8,128)(2,1)S(1)} collective-permute-done((bf16[256,256]{1,0:T(8,128)(2,1)S(1)}, bf16[256,256]{1,0:T(8,128)(2,1)S(1)}, u32[]{:S(2)}, u32[]{:S(2)}) %collective-permute-start) | collective-permute-done | bytes 131104 | tf_op jit(solution)/shard_map/ppermute | solution.py:333
  9.7 0.0 collective-permute-start.2
  9.7 0.7 %tick0_even.1 = (bf16[4,128,256]{2,1,0:T(8,128)(2,1)S(1)}, bf16[256,256]{1,0:T(8,128)(2,1)S(1)}, bf16[256,256]{1,0:T(8,128)(2,1)S(1)}, bf16[2,128,256]{2,1,0:T(8,128)(2,1)S(1)}, bf16[2,128,256]{2,1,0:T(8,128)(2,1)S(1)}) custom-call(s32[30]{0:T(128)S(4)} %get-tuple-element.38.refs_0_, ...), custom_call_target="tpu_custom_call", output_to_operand_aliasing={{0}: (8, {}), {1}: (9, {}), {2}: (10, {})} | custom-call | tf_op jit(solution)/shard_map/tick0_even/pallas_call | solution.py:246
  10.5 2.2 %collective-permute-start.3 = (bf16[256,256]{1,0:T(8,128)(2,1)S(1)}, bf16[256,256]{1,0:T(8,128)(2,1)S(1)}, u32[]{:S(2)}, u32[]{:S(2)}) collective-permute-start(bf16[256,256]{1,0:T(8,128)(2,1)S(1)} %get-tuple-element.50), channel_id=1, source_target_pairs={{0,5},{1,4},{2,7},{3,6},{4,9},{5,8},{6,11},{7,10},{8,13},{9,12},{1... | collective-permute-start | bytes 393224 | tf_op jit(solution)/shard_map/ppermute | solution.py:375
  12.7 0.6 %collective-permute-start.4 = (bf16[256,256]{1,0:T(8,128)(2,1)S(1)}, bf16[256,256]{1,0:T(8,128)(2,1)S(1)}, u32[]{:S(2)}, u32[]{:S(2)}) collective-permute-start(bf16[256,256]{1,0:T(8,128)(2,1)S(1)} %get-tuple-element.51), channel_id=1, source_target_pairs={{0,4},{1,6},{2,5},{3,7},{4,0},{5,10},{6,9},{7,3},{8,12},{9,14},{10... | collective-permute-start | bytes 393224 | tf_op jit(solution)/shard_map/ppermute | solution.py:375
  13.3 0.0 collective-permute-start.5
  13.3 0.5 %collective-permute-start.6 = (bf16[2,128,256]{2,1,0:T(8,128)(2,1)S(1)}, bf16[2,128,256]{2,1,0:T(8,128)(2,1)S(1)}, u32[]{:S(2)}, u32[]{:S(2)}) collective-permute-start(bf16[2,128,256]{2,1,0:T(8,128)(2,1)S(1)} %get-tuple-element.53), channel_id=1, source_target_pairs={{0,4},{4,0},{8,12},{12,8},{16,20},{20,16},{24,28},{28,24},{1,5},{5... | collective-permute-start | bytes 393224 | tf_op jit(solution)/shard_map/ppermute | solution.py:414
  13.8 4.0 %collective-permute-done.3.refs_7_.refs_6_ = bf16[256,256]{1,0:T(8,128)(2,1)S(1)} collective-permute-done((bf16[256,256]{1,0:T(8,128)(2,1)S(1)}, bf16[256,256]{1,0:T(8,128)(2,1)S(1)}, u32[]{:S(2)}, u32[]{:S(2)}) %collective-permute-start.3) | collective-permute-done | bytes 131104 | tf_op jit(solution)/shard_map/ppermute | solution.py:375
  17.8 0.0 collective-permute-done.4.refs_8_.refs_7_
  17.8 0.0 collective-permute-done.5.refs_5_
  17.8 0.0 collective-permute-done.6.refs_6_
  17.9 0.3 collective-permute-start.14
  18.2 0.0 collective-permute-done.2.refs_5_
  18.2 0.7 %tick1_even.1 = (bf16[4,128,256]{2,1,0:T(8,128)(2,1)S(1)}, bf16[288,256]{1,0:T(8,128)(2,1)S(1)}, bf16[288,256]{1,0:T(8,128)(2,1)S(1)}, bf16[2,128,256]{2,1,0:T(8,128)(2,1)S(1)}, bf16[2,128,256]{2,1,0:T(8,128)(2,1)S(1)}) custom-call(s32[30]{0:T(128)S(4)} %get-tuple-element.38.refs_0_, ...), custom_call_target="tpu_custom_call", output_to_operand_aliasing={{0}: (8, {})} | custom-call | tf_op jit(solution)/shard_map/tick1_even/pallas_call | solution.py:246
  19.0 1.9 %collective-permute-start.9 = (bf16[288,256]{1,0:T(8,128)(2,1)S(1)}, bf16[288,256]{1,0:T(8,128)(2,1)S(1)}, u32[]{:S(2)}, u32[]{:S(2)}) collective-permute-start(bf16[288,256]{1,0:T(8,128)(2,1)S(1)} %get-tuple-element.57), channel_id=1, source_target_pairs={{0,5},{1,4},{2,7},{3,6},{4,0},{5,1},{6,2},{7,3},{8,13},{9,12},{10,... | collective-permute-start | bytes 442376 | tf_op jit(solution)/shard_map/ppermute | solution.py:375
  20.9 0.0 collective-permute-start.10
  20.9 0.5 %collective-permute-start.7 = (bf16[2,128,256]{2,1,0:T(8,128)(2,1)S(1)}, bf16[2,128,256]{2,1,0:T(8,128)(2,1)S(1)}, u32[]{:S(2)}, u32[]{:S(2)}) collective-permute-start(bf16[2,128,256]{2,1,0:T(8,128)(2,1)S(1)} %get-tuple-element.55), channel_id=1, source_target_pairs={{0,4},{4,0},{8,12},{12,8},{16,20},{20,16},{24,28},{28,24},{1,5},{5... | collective-permute-start | bytes 393224 | tf_op jit(solution)/shard_map/ppermute | solution.py:414
  21.4 0.0 collective-permute-start.8
  21.4 1.0 %collective-permute-done.7.refs_5_ = bf16[2,128,256]{2,1,0:T(8,128)(2,1)S(1)} collective-permute-done((bf16[2,128,256]{2,1,0:T(8,128)(2,1)S(1)}, bf16[2,128,256]{2,1,0:T(8,128)(2,1)S(1)}, u32[]{:S(2)}, u32[]{:S(2)}) %collective-permute-start.7) | collective-permute-done | bytes 131104 | tf_op jit(solution)/shard_map/ppermute | solution.py:414
  22.4 0.3 collective-permute-start.15
  22.7 0.0 collective-permute-done.8.refs_6_
  22.7 3.4 %collective-permute-start.16 = (bf16[256,256]{1,0:T(8,128)(2,1)S(1)}, bf16[256,256]{1,0:T(8,128)(2,1)S(1)}, u32[]{:S(2)}, u32[]{:S(2)}) collective-permute-start(bf16[256,256]{1,0:T(8,128)(2,1)S(1)} %get-tuple-element.66), channel_id=1, source_target_pairs={{0,4},{1,5},{2,6},{3,7},{4,0},{5,10},{6,9},{7,3},{8,12},{9,13},{10... | collective-permute-start | bytes 393224 | tf_op jit(solution)/shard_map/ppermute | solution.py:375
  26.2 0.0 collective-permute-done.9.refs_7_
  26.2 0.0 collective-permute-done.10.refs_8_
  26.2 0.8 %collective-permute-start.11 = (bf16[512,256]{1,0:T(8,128)(2,1)S(1)}, bf16[512,256]{1,0:T(8,128)(2,1)S(1)}, u32[]{:S(2)}, u32[]{:S(2)}) collective-permute-start(bf16[512,256]{1,0:T(8,128)(2,1)S(1)} %get-tuple-element.59), channel_id=1, source_target_pairs={{0,4},{4,8},{8,12},{12,16},{16,20},{20,24},{24,28},{28,0},{1,5},{5... | collective-permute-start | bytes 786440 | tf_op jit(solution)/shard_map/ppermute | solution.py:410
  27.0 0.5 %collective-permute-start.12 = (bf16[272,256]{1,0:T(8,128)(2,1)S(1)}, bf16[272,256]{1,0:T(8,128)(2,1)S(1)}, u32[]{:S(2)}, u32[]{:S(2)}) collective-permute-start(bf16[272,256]{1,0:T(8,128)(2,1)S(1)} %get-tuple-element.60), channel_id=1, source_target_pairs={{0,4},{1,5},{2,6},{3,7},{4,9},{5,8},{6,11},{7,10},{8,12},{9,13},{1... | collective-permute-start | bytes 417800 | tf_op jit(solution)/shard_map/ppermute | solution.py:375
  27.5 1.1 %collective-permute-done.15.refs_6_ = bf16[256,256]{1,0:T(8,128)(2,1)S(1)} collective-permute-done((bf16[256,256]{1,0:T(8,128)(2,1)S(1)}, bf16[256,256]{1,0:T(8,128)(2,1)S(1)}, u32[]{:S(2)}, u32[]{:S(2)}) %collective-permute-start.15) | collective-permute-done | bytes 131104 | tf_op jit(solution)/shard_map/ppermute | solution.py:375
  28.6 0.0 collective-permute-start.13
  28.6 0.0 collective-permute-done.16.refs_7_
  28.6 0.0 collective-permute-done.14.refs_5_
  28.6 0.8 %tick2_even.1 = (bf16[4,128,256]{2,1,0:T(8,128)(2,1)S(1)}, bf16[256,256]{1,0:T(8,128)(2,1)S(1)}, bf16[256,256]{1,0:T(8,128)(2,1)S(1)}, bf16[2,4,128,256]{3,2,1,0:T(8,128)(2,1)S(1)}) custom-call(s32[30]{0:T(128)S(4)} %get-tuple-element.38.refs_0_, bf16[1,4,6,2,128,128]{5,4,3,2,1,0:T(8,128)(2,1)S(1)} %get-tuple-element.40.refs_1_, ...), custom_call_target="tpu_custom_call", output_to_operand_aliasing={{0}: (8, {})} | custom-call | tf_op jit(solution)/shard_map/tick2_even/pallas_call | solution.py:246
  29.4 3.2 %collective-permute-start.17 = (bf16[256,256]{1,0:T(8,128)(2,1)S(1)}, bf16[256,256]{1,0:T(8,128)(2,1)S(1)}, u32[]{:S(2)}, u32[]{:S(2)}) collective-permute-start(bf16[256,256]{1,0:T(8,128)(2,1)S(1)} %get-tuple-element.70), channel_id=1, source_target_pairs={{0,5},{1,4},{2,7},{3,6},{4,0},{5,1},{6,2},{7,3},{8,13},{9,12},{10,... | collective-permute-start | bytes 393224 | tf_op jit(solution)/shard_map/ppermute | solution.py:375
  32.6 0.0 collective-permute-start.18
  32.6 4.1 %all_to_all.5.refs_5_ = bf16[2,4,128,256]{3,2,1,0:T(8,128)(2,1)S(1)} all-to-all(bf16[2,4,128,256]{3,2,1,0:T(8,128)(2,1)S(1)} %get-tuple-element.69), channel_id=1, replica_groups={{0,4},{8,12},{16,20},{24,28},{1,5},{9,13},{17,21},{25,29},{2,6},{10,14}..., dimensions={0} | all-to-all | bytes 1048576 | tf_op jit(solution)/shard_map/all_to_all | solution.py:412
  36.8 0.0 collective-permute-done.17.refs_6_
  36.8 0.0 collective-permute-done.18.refs_7_
  36.8 0.1 last_tick_odd.1
  36.9 0.0 collective-permute-done.12.refs_6_
  36.9 0.0 collective-permute-done.13.refs_7_
  36.9 0.0 collective-permute-done.11.refs_5_
  36.9 1.5 %last_tick_even.1 = (bf16[4,1,4,128,256]{4,3,2,1,0:T(8,128)(2,1)}, f32[1,4,128,256]{3,2,1,0:T(8,128)}) custom-call(s32[30]{0:T(128)S(4)} %get-tuple-element.38.refs_0_, bf16[1,4,6,2,128,128]{5,4,3,2,1,0:T(8,128)(2,1)S(1)} %get-tuple-element.40.refs_1_, ...), custom_call_target="tpu_custom_call", output_to_operand_aliasing={{0}: (11, {}), {1}: (12, {})} | custom-call | tf_op jit(solution)/shard_map/last_tick_even/pallas_call | solution.py:246
  (3 shorter events, 0.0 us)
Async XLA Ops:
  1.8 6.4 %collective-permute-start.1 = (bf16[256,256]{1,0:T(8,128)(2,1)S(1)}, bf16[256,256]{1,0:T(8,128)(2,1)S(1)}, u32[]{:S(2)}, u32[]{:S(2)}) collective-permute-start(bf16[256,256]{1,0:T(8,128)(2,1)S(1)} %get-tuple-element.45), channel_id=1, source_target_pairs={{0,4},{1,2},{2,1},{3,7},{4,0},{5,6},{6,5},{7,3},{8,12},{9,10},{10,... | collective-permute-start | bytes 393224 | tf_op jit(solution)/shard_map/ppermute | solution.py:334
  2.4 7.4 %collective-permute-start = (bf16[256,256]{1,0:T(8,128)(2,1)S(1)}, bf16[256,256]{1,0:T(8,128)(2,1)S(1)}, u32[]{:S(2)}, u32[]{:S(2)}) collective-permute-start(bf16[256,256]{1,0:T(8,128)(2,1)S(1)} %get-tuple-element.39.after_ref), channel_id=1, source_target_pairs={{0,1},{1,0},{2,3},{3,2},{4,5},{5,4},{6,7},{7,6},{8,9},{9,8},{10,11... | collective-permute-start | bytes 393224 | tf_op jit(solution)/shard_map/ppermute | solution.py:333
  9.7 8.5 %collective-permute-start.2 = (bf16[512,256]{1,0:T(8,128)(2,1)S(1)}, bf16[512,256]{1,0:T(8,128)(2,1)S(1)}, u32[]{:S(2)}, u32[]{:S(2)}) collective-permute-start(bf16[512,256]{1,0:T(8,128)(2,1)S(1)} %get-tuple-element.46), channel_id=1, source_target_pairs={{0,4},{4,8},{8,12},{12,16},{16,20},{20,24},{24,28},{28,0},{1,5},{5... | collective-permute-start | bytes 786440 | tf_op jit(solution)/shard_map/ppermute | solution.py:410
  10.5 7.3 %collective-permute-start.3 = (bf16[256,256]{1,0:T(8,128)(2,1)S(1)}, bf16[256,256]{1,0:T(8,128)(2,1)S(1)}, u32[]{:S(2)}, u32[]{:S(2)}) collective-permute-start(bf16[256,256]{1,0:T(8,128)(2,1)S(1)} %get-tuple-element.50), channel_id=1, source_target_pairs={{0,5},{1,4},{2,7},{3,6},{4,9},{5,8},{6,11},{7,10},{8,13},{9,12},{1... | collective-permute-start | bytes 393224 | tf_op jit(solution)/shard_map/ppermute | solution.py:375
  12.7 5.1 %collective-permute-start.4 = (bf16[256,256]{1,0:T(8,128)(2,1)S(1)}, bf16[256,256]{1,0:T(8,128)(2,1)S(1)}, u32[]{:S(2)}, u32[]{:S(2)}) collective-permute-start(bf16[256,256]{1,0:T(8,128)(2,1)S(1)} %get-tuple-element.51), channel_id=1, source_target_pairs={{0,4},{1,6},{2,5},{3,7},{4,0},{5,10},{6,9},{7,3},{8,12},{9,14},{10... | collective-permute-start | bytes 393224 | tf_op jit(solution)/shard_map/ppermute | solution.py:375
  13.3 4.5 %collective-permute-start.5 = (bf16[2,128,256]{2,1,0:T(8,128)(2,1)S(1)}, bf16[2,128,256]{2,1,0:T(8,128)(2,1)S(1)}, u32[]{:S(2)}, u32[]{:S(2)}) collective-permute-start(bf16[2,128,256]{2,1,0:T(8,128)(2,1)S(1)} %get-tuple-element.52), channel_id=1, source_target_pairs={{0,4},{4,0},{8,12},{12,8},{16,20},{20,16},{24,28},{28,24},{1,5},{5... | collective-permute-start | bytes 393224 | tf_op jit(solution)/shard_map/ppermute | solution.py:414
  13.3 4.5 %collective-permute-start.6 = (bf16[2,128,256]{2,1,0:T(8,128)(2,1)S(1)}, bf16[2,128,256]{2,1,0:T(8,128)(2,1)S(1)}, u32[]{:S(2)}, u32[]{:S(2)}) collective-permute-start(bf16[2,128,256]{2,1,0:T(8,128)(2,1)S(1)} %get-tuple-element.53), channel_id=1, source_target_pairs={{0,4},{4,0},{8,12},{12,8},{16,20},{20,16},{24,28},{28,24},{1,5},{5... | collective-permute-start | bytes 393224 | tf_op jit(solution)/shard_map/ppermute | solution.py:414
  17.9 10.8 %collective-permute-start.14 = (bf16[544,256]{1,0:T(8,128)(2,1)S(1)}, bf16[544,256]{1,0:T(8,128)(2,1)S(1)}, u32[]{:S(2)}, u32[]{:S(2)}) collective-permute-start(bf16[544,256]{1,0:T(8,128)(2,1)S(1)} %get-tuple-element.64), channel_id=1, source_target_pairs={{0,4},{4,8},{8,12},{12,16},{16,20},{20,24},{24,28},{28,0},{1,5},{5... | collective-permute-start | bytes 835592 | tf_op jit(solution)/shard_map/ppermute | solution.py:410
  19.0 7.2 %collective-permute-start.9 = (bf16[288,256]{1,0:T(8,128)(2,1)S(1)}, bf16[288,256]{1,0:T(8,128)(2,1)S(1)}, u32[]{:S(2)}, u32[]{:S(2)}) collective-permute-start(bf16[288,256]{1,0:T(8,128)(2,1)S(1)} %get-tuple-element.57), channel_id=1, source_target_pairs={{0,5},{1,4},{2,7},{3,6},{4,0},{5,1},{6,2},{7,3},{8,13},{9,12},{10,... | collective-permute-start | bytes 442376 | tf_op jit(solution)/shard_map/ppermute | solution.py:375
  20.9 5.3 %collective-permute-start.10 = (bf16[288,256]{1,0:T(8,128)(2,1)S(1)}, bf16[288,256]{1,0:T(8,128)(2,1)S(1)}, u32[]{:S(2)}, u32[]{:S(2)}) collective-permute-start(bf16[288,256]{1,0:T(8,128)(2,1)S(1)} %get-tuple-element.58), channel_id=1, source_target_pairs={{0,4},{1,6},{2,5},{3,7},{4,0},{5,1},{6,2},{7,3},{8,12},{9,14},{10,... | collective-permute-start | bytes 442376 | tf_op jit(solution)/shard_map/ppermute | solution.py:375
  20.9 1.6 %collective-permute-start.7 = (bf16[2,128,256]{2,1,0:T(8,128)(2,1)S(1)}, bf16[2,128,256]{2,1,0:T(8,128)(2,1)S(1)}, u32[]{:S(2)}, u32[]{:S(2)}) collective-permute-start(bf16[2,128,256]{2,1,0:T(8,128)(2,1)S(1)} %get-tuple-element.55), channel_id=1, source_target_pairs={{0,4},{4,0},{8,12},{12,8},{16,20},{20,16},{24,28},{28,24},{1,5},{5... | collective-permute-start | bytes 393224 | tf_op jit(solution)/shard_map/ppermute | solution.py:414
  21.4 1.4 %collective-permute-start.8 = (bf16[2,128,256]{2,1,0:T(8,128)(2,1)S(1)}, bf16[2,128,256]{2,1,0:T(8,128)(2,1)S(1)}, u32[]{:S(2)}, u32[]{:S(2)}) collective-permute-start(bf16[2,128,256]{2,1,0:T(8,128)(2,1)S(1)} %get-tuple-element.56), channel_id=1, source_target_pairs={{0,4},{4,0},{8,12},{12,8},{16,20},{20,16},{24,28},{28,24},{1,5},{5... | collective-permute-start | bytes 393224 | tf_op jit(solution)/shard_map/ppermute | solution.py:414
  22.4 6.2 %collective-permute-start.15 = (bf16[256,256]{1,0:T(8,128)(2,1)S(1)}, bf16[256,256]{1,0:T(8,128)(2,1)S(1)}, u32[]{:S(2)}, u32[]{:S(2)}) collective-permute-start(bf16[256,256]{1,0:T(8,128)(2,1)S(1)} %get-tuple-element.65), channel_id=1, source_target_pairs={{0,4},{1,5},{2,6},{3,7},{4,9},{5,8},{6,11},{7,10},{8,12},{9,13},{1... | collective-permute-start | bytes 393224 | tf_op jit(solution)/shard_map/ppermute | solution.py:375
  22.7 5.9 %collective-permute-start.16 = (bf16[256,256]{1,0:T(8,128)(2,1)S(1)}, bf16[256,256]{1,0:T(8,128)(2,1)S(1)}, u32[]{:S(2)}, u32[]{:S(2)}) collective-permute-start(bf16[256,256]{1,0:T(8,128)(2,1)S(1)} %get-tuple-element.66), channel_id=1, source_target_pairs={{0,4},{1,5},{2,6},{3,7},{4,0},{5,10},{6,9},{7,3},{8,12},{9,13},{10... | collective-permute-start | bytes 393224 | tf_op jit(solution)/shard_map/ppermute | solution.py:375
  26.2 10.7 %collective-permute-start.11 = (bf16[512,256]{1,0:T(8,128)(2,1)S(1)}, bf16[512,256]{1,0:T(8,128)(2,1)S(1)}, u32[]{:S(2)}, u32[]{:S(2)}) collective-permute-start(bf16[512,256]{1,0:T(8,128)(2,1)S(1)} %get-tuple-element.59), channel_id=1, source_target_pairs={{0,4},{4,8},{8,12},{12,16},{16,20},{20,24},{24,28},{28,0},{1,5},{5... | collective-permute-start | bytes 786440 | tf_op jit(solution)/shard_map/ppermute | solution.py:410
  27.0 9.9 %collective-permute-start.12 = (bf16[272,256]{1,0:T(8,128)(2,1)S(1)}, bf16[272,256]{1,0:T(8,128)(2,1)S(1)}, u32[]{:S(2)}, u32[]{:S(2)}) collective-permute-start(bf16[272,256]{1,0:T(8,128)(2,1)S(1)} %get-tuple-element.60), channel_id=1, source_target_pairs={{0,4},{1,5},{2,6},{3,7},{4,9},{5,8},{6,11},{7,10},{8,12},{9,13},{1... | collective-permute-start | bytes 417800 | tf_op jit(solution)/shard_map/ppermute | solution.py:375
  28.6 8.3 %collective-permute-start.13 = (bf16[272,256]{1,0:T(8,128)(2,1)S(1)}, bf16[272,256]{1,0:T(8,128)(2,1)S(1)}, u32[]{:S(2)}, u32[]{:S(2)}) collective-permute-start(bf16[272,256]{1,0:T(8,128)(2,1)S(1)} %get-tuple-element.61), channel_id=1, source_target_pairs={{0,4},{1,5},{2,6},{3,7},{4,0},{5,10},{6,9},{7,3},{8,12},{9,13},{10... | collective-permute-start | bytes 417800 | tf_op jit(solution)/shard_map/ppermute | solution.py:375
  29.4 7.4 %collective-permute-start.17 = (bf16[256,256]{1,0:T(8,128)(2,1)S(1)}, bf16[256,256]{1,0:T(8,128)(2,1)S(1)}, u32[]{:S(2)}, u32[]{:S(2)}) collective-permute-start(bf16[256,256]{1,0:T(8,128)(2,1)S(1)} %get-tuple-element.70), channel_id=1, source_target_pairs={{0,5},{1,4},{2,7},{3,6},{4,0},{5,1},{6,2},{7,3},{8,13},{9,12},{10,... | collective-permute-start | bytes 393224 | tf_op jit(solution)/shard_map/ppermute | solution.py:375
  32.6 4.2 %collective-permute-start.18 = (bf16[256,256]{1,0:T(8,128)(2,1)S(1)}, bf16[256,256]{1,0:T(8,128)(2,1)S(1)}, u32[]{:S(2)}, u32[]{:S(2)}) collective-permute-start(bf16[256,256]{1,0:T(8,128)(2,1)S(1)} %get-tuple-element.71), channel_id=1, source_target_pairs={{0,4},{1,6},{2,5},{3,7},{4,0},{5,1},{6,2},{7,3},{8,12},{9,14},{10,... | collective-permute-start | bytes 393224 | tf_op jit(solution)/shard_map/ppermute | solution.py:375

commit v17 on v10

--- a/solution.py
+++ b/solution.py
@@ -377,7 +377,7 @@
     arrived = {parity: ([wave], first, second) for parity in (ODD, EVEN)}
     echoes = []
     for tick in range(ticks - 1):
-        first_step, last_step = tick == 0, tick == ticks - 2
+        first_step, last_step = tick in (0, ticks - 2), False
         known = []
         waves, halos = {}, {}
         for parity in (ODD, EVEN):

time: 37.8 us -> 40 us (1.058)
  the two profiles are of different devices: /device:TPU:0 before, /device:TPU:8 now
where the time goes in v17:
time: 40 us; the launch traced here: 39.9 us
  waiting for transfers between devices  20.1 us (50%)
  starting transfers between devices  12.3 us (31%)
  Pallas kernels  6.72 us (17%)
  between operations  0.73 us (2%)
    ppermute x8, waiting for transfers between devices, exchange(): return [lax.ppermute(a, both, route) for a, route in zip(lists, routes)]  15.5 us
    ppermute x8, starting transfers between devices, exchange(): return [lax.ppermute(a, both, route) for a, route in zip(lists, routes)]  7.57 us
    pallas_call x8, Pallas kernels, grouped_call(): pl.pallas_call(body, out_shape=tuple(outs), in_specs=[SMEM_SPEC] + [VMEM_...  3.83 us
    ppermute x1, waiting for transfers between devices, per_device(): second = lax.ppermute(second, both, routes[1])  1.98 us
    pallas_call x1, Pallas kernels, per_device(): pl.pallas_call(load_kernel, out_shape=(pltpu.VMEM(operators.shape, operat...  1.67 us
    ppermute x1, starting transfers between devices, per_device(): second = lax.ppermute(second, both, routes[1])  1.64 us
    ppermute x3, starting transfers between devices, per_device(): waves[EVEN] = [lax.ppermute(onward[0], 'depth', crossing)]  1.54 us
    ppermute x6, starting transfers between devices, per_device(): waves[ODD] = [lax.ppermute(a, 'depth', inside) for a in onward]  1.53 us
  transfers between devices with their start and end apart: 19, of which 11 were waited for; matrix products, arithmetic and copies ran while one was open for 0% of the time, Pallas kernels for 10%

profile of v17, /device:TPU:8, one launch (start us, length us, event | category | flops | bytes accessed | tf_op | source)
XLA Modules:
  0.0 39.9 jit_solution(3719317753955009800)
XLA Ops:
  0.6 1.2 %prepare.1 = (s32[30]{0:T(128)S(4)}, bf16[4,128,256]{2,1,0:T(8,128)(2,1)S(1)}, bf16[256,256]{1,0:T(8,128)(2,1)S(1)}, bf16[256,256]{1,0:T(8,128)(2,1)S(1)}) custom-call(s32[1,2,2]{2,1,0:T(2,128)} %ids_hbm.1, s32[1,2]{1,0:T(1,128)} %count_hbm.1, s32[4,6]{1,0:T(4,128)} %pattern_hbm.1, f32[1,4,128,256]{3,2,1,0:T(8,128)} %inflow_hbm.1), custom_call_target="tpu_custom_call" | custom-call | flops 131072 | bytes 1048576 | tf_op jit(solution)/shard_map/prepare/pallas_call | solution.py:307
  1.9 1.6 %collective-permute-start.1 = (bf16[256,256]{1,0:T(8,128)(2,1)S(1)}, bf16[256,256]{1,0:T(8,128)(2,1)S(1)}, u32[]{:S(2)}, u32[]{:S(2)}) collective-permute-start(bf16[256,256]{1,0:T(8,128)(2,1)S(1)} %get-tuple-element.46), channel_id=1, source_target_pairs={{0,4},{1,2},{2,1},{3,7},{4,0},{5,6},{6,5},{7,3},{8,12},{9,10},{10,... | collective-permute-start | bytes 393224 | tf_op jit(solution)/shard_map/ppermute | solution.py:334
  3.5 0.0 collective-permute-start
  3.5 1.7 %load.1 = (bf16[1,4,6,2,128,128]{5,4,3,2,1,0:T(8,128)(2,1)S(1)}, bf16[3,4,128,256]{3,2,1,0:T(8,128)(2,1)S(1)}, f32[4,128,128]{2,1,0:T(8,128)S(1)}, f32[4,128,128]{2,1,0:T(8,128)S(1)}) custom-call(bf16[1,4,6,2,128,128]{5,4,3,2,1,0:T(8,128)(2,1)} %ops_hbm.1, bf16[3,4,128,256]{3,2,1,0:T(8,128)(2,1)} %source_hbm.1, f32[1,4,128]{2,1,0:T(4,128)} %pass_hbm.1, ...), custom_call_target="tpu_custom_call" | custom-call | bytes 4718592 | tf_op jit(solution)/shard_map/load/pallas_call | solution.py:337
  5.2 2.0 %collective-permute-done.1.refs_7_ = bf16[256,256]{1,0:T(8,128)(2,1)S(1)} collective-permute-done((bf16[256,256]{1,0:T(8,128)(2,1)S(1)}, bf16[256,256]{1,0:T(8,128)(2,1)S(1)}, u32[]{:S(2)}, u32[]{:S(2)}) %collective-permute-start.1) | collective-permute-done | bytes 131104 | tf_op jit(solution)/shard_map/ppermute | solution.py:334
  7.2 1.3 %collective-permute-done.refs_6_ = bf16[256,256]{1,0:T(8,128)(2,1)S(1)} collective-permute-done((bf16[256,256]{1,0:T(8,128)(2,1)S(1)}, bf16[256,256]{1,0:T(8,128)(2,1)S(1)}, u32[]{:S(2)}, u32[]{:S(2)}) %collective-permute-start) | collective-permute-done | bytes 131104 | tf_op jit(solution)/shard_map/ppermute | solution.py:333
  8.5 0.0 collective-permute-start.2
  8.5 0.7 %tick0_even.1 = (bf16[4,128,256]{2,1,0:T(8,128)(2,1)S(1)}, bf16[256,256]{1,0:T(8,128)(2,1)S(1)}, bf16[256,256]{1,0:T(8,128)(2,1)S(1)}, bf16[2,128,256]{2,1,0:T(8,128)(2,1)S(1)}, bf16[2,128,256]{2,1,0:T(8,128)(2,1)S(1)}) custom-call(s32[30]{0:T(128)S(4)} %get-tuple-element.39.refs_0_, ...), custom_call_target="tpu_custom_call", output_to_operand_aliasing={{0}: (8, {}), {1}: (9, {}), {2}: (10, {})} | custom-call | tf_op jit(solution)/shard_map/tick0_even/pallas_call | solution.py:246
  9.2 0.7 %collective-permute-start.3 = (bf16[256,256]{1,0:T(8,128)(2,1)S(1)}, bf16[256,256]{1,0:T(8,128)(2,1)S(1)}, u32[]{:S(2)}, u32[]{:S(2)}) collective-permute-start(bf16[256,256]{1,0:T(8,128)(2,1)S(1)} %get-tuple-element.51), channel_id=1, source_target_pairs={{0,5},{1,4},{2,7},{3,6},{4,9},{5,8},{6,11},{7,10},{8,13},{9,12},{1... | collective-permute-start | bytes 393224 | tf_op jit(solution)/shard_map/ppermute | solution.py:375
  9.9 3.0 %collective-permute-start.4 = (bf16[256,256]{1,0:T(8,128)(2,1)S(1)}, bf16[256,256]{1,0:T(8,128)(2,1)S(1)}, u32[]{:S(2)}, u32[]{:S(2)}) collective-permute-start(bf16[256,256]{1,0:T(8,128)(2,1)S(1)} %get-tuple-element.52), channel_id=1, source_target_pairs={{0,4},{1,6},{2,5},{3,7},{4,0},{5,10},{6,9},{7,3},{8,12},{9,14},{10... | collective-permute-start | bytes 393224 | tf_op jit(solution)/shard_map/ppermute | solution.py:375
  12.9 0.3 collective-permute-start.5
  13.3 0.2 collective-permute-start.6
  13.4 3.4 %collective-permute-done.3.refs_7_.refs_6_ = bf16[256,256]{1,0:T(8,128)(2,1)S(1)} collective-permute-done((bf16[256,256]{1,0:T(8,128)(2,1)S(1)}, bf16[256,256]{1,0:T(8,128)(2,1)S(1)}, u32[]{:S(2)}, u32[]{:S(2)}) %collective-permute-start.3) | collective-permute-done | bytes 131104 | tf_op jit(solution)/shard_map/ppermute | solution.py:375
  16.9 0.6 %collective-permute-done.4.refs_8_.refs_7_ = bf16[256,256]{1,0:T(8,128)(2,1)S(1)} collective-permute-done((bf16[256,256]{1,0:T(8,128)(2,1)S(1)}, bf16[256,256]{1,0:T(8,128)(2,1)S(1)}, u32[]{:S(2)}, u32[]{:S(2)}) %collective-permute-start.4) | collective-permute-done | bytes 131104 | tf_op jit(solution)/shard_map/ppermute | solution.py:375
  17.4 0.0 collective-permute-done.5.refs_5_
  17.4 0.0 collective-permute-done.6.refs_6_
  17.4 0.1 collective-permute-start.12
  17.5 0.5 %collective-permute-done.2.refs_5_ = bf16[512,256]{1,0:T(8,128)(2,1)S(1)} collective-permute-done((bf16[512,256]{1,0:T(8,128)(2,1)S(1)}, bf16[512,256]{1,0:T(8,128)(2,1)S(1)}, u32[]{:S(2)}, u32[]{:S(2)}) %collective-permute-start.2) | collective-permute-done | bytes 262176 | tf_op jit(solution)/shard_map/ppermute | solution.py:410
  18.0 0.7 %tick1_even.1 = (bf16[4,128,256]{2,1,0:T(8,128)(2,1)S(1)}, bf16[272,256]{1,0:T(8,128)(2,1)S(1)}, bf16[272,256]{1,0:T(8,128)(2,1)S(1)}, bf16[2,128,256]{2,1,0:T(8,128)(2,1)S(1)}, bf16[2,128,256]{2,1,0:T(8,128)(2,1)S(1)}) custom-call(s32[30]{0:T(128)S(4)} %get-tuple-element.39.refs_0_, ...), custom_call_target="tpu_custom_call", output_to_operand_aliasing={{0}: (8, {})} | custom-call | tf_op jit(solution)/shard_map/tick1_even/pallas_call | solution.py:246
  18.7 0.1 collective-permute-start.9
  18.8 2.0 %collective-permute-start.10 = (bf16[272,256]{1,0:T(8,128)(2,1)S(1)}, bf16[272,256]{1,0:T(8,128)(2,1)S(1)}, u32[]{:S(2)}, u32[]{:S(2)}) collective-permute-start(bf16[272,256]{1,0:T(8,128)(2,1)S(1)} %get-tuple-element.59), channel_id=1, source_target_pairs={{0,4},{1,6},{2,5},{3,7},{4,0},{5,1},{6,2},{7,3},{8,12},{9,14},{10,... | collective-permute-start | bytes 417800 | tf_op jit(solution)/shard_map/ppermute | solution.py:375
  20.8 0.0 collective-permute-start.7
  20.8 0.5 %collective-permute-start.8 = (bf16[2,128,256]{2,1,0:T(8,128)(2,1)S(1)}, bf16[2,128,256]{2,1,0:T(8,128)(2,1)S(1)}, u32[]{:S(2)}, u32[]{:S(2)}) collective-permute-start(bf16[2,128,256]{2,1,0:T(8,128)(2,1)S(1)} %get-tuple-element.57), channel_id=1, source_target_pairs={{0,4},{4,0},{8,12},{12,8},{16,20},{20,16},{24,28},{28,24},{1,5},{5... | collective-permute-start | bytes 393224 | tf_op jit(solution)/shard_map/ppermute | solution.py:414
  21.3 0.8 %collective-permute-done.7.refs_5_ = bf16[2,128,256]{2,1,0:T(8,128)(2,1)S(1)} collective-permute-done((bf16[2,128,256]{2,1,0:T(8,128)(2,1)S(1)}, bf16[2,128,256]{2,1,0:T(8,128)(2,1)S(1)}, u32[]{:S(2)}, u32[]{:S(2)}) %collective-permute-start.7) | collective-permute-done | bytes 131104 | tf_op jit(solution)/shard_map/ppermute | solution.py:414
  22.1 0.1 collective-permute-start.13
  22.3 0.0 collective-permute-done.8.refs_6_
  22.3 1.0 %collective-permute-start.14 = (bf16[256,256]{1,0:T(8,128)(2,1)S(1)}, bf16[256,256]{1,0:T(8,128)(2,1)S(1)}, u32[]{:S(2)}, u32[]{:S(2)}) collective-permute-start(bf16[256,256]{1,0:T(8,128)(2,1)S(1)} %get-tuple-element.63), channel_id=1, source_target_pairs={{0,4},{1,5},{2,6},{3,7},{4,0},{5,10},{6,9},{7,3},{8,12},{9,13},{10... | collective-permute-start | bytes 393224 | tf_op jit(solution)/shard_map/ppermute | solution.py:375
  23.3 0.0 collective-permute-done.9.refs_7_
  23.3 0.1 collective-permute-done.10.refs_8_
  23.4 1.5 %collective-permute-start.11 = (bf16[512,256]{1,0:T(8,128)(2,1)S(1)}, bf16[512,256]{1,0:T(8,128)(2,1)S(1)}, u32[]{:S(2)}, u32[]{:S(2)}) collective-permute-start(bf16[512,256]{1,0:T(8,128)(2,1)S(1)} %get-tuple-element.60), channel_id=1, source_target_pairs={{0,4},{4,8},{8,12},{12,16},{16,20},{20,24},{24,28},{28,0},{1,5},{5... | collective-permute-start | bytes 786440 | tf_op jit(solution)/shard_map/ppermute | solution.py:410
  24.9 4.8 %collective-permute-done.13.refs_6_ = bf16[256,256]{1,0:T(8,128)(2,1)S(1)} collective-permute-done((bf16[256,256]{1,0:T(8,128)(2,1)S(1)}, bf16[256,256]{1,0:T(8,128)(2,1)S(1)}, u32[]{:S(2)}, u32[]{:S(2)}) %collective-permute-start.13) | collective-permute-done | bytes 131104 | tf_op jit(solution)/shard_map/ppermute | solution.py:375
  29.6 0.2 collective-permute-done.14.refs_7_
  29.8 0.0 collective-permute-done.12.refs_5_
  29.8 0.7 %tick2_even.1 = (bf16[4,128,256]{2,1,0:T(8,128)(2,1)S(1)}, bf16[256,256]{1,0:T(8,128)(2,1)S(1)}, bf16[256,256]{1,0:T(8,128)(2,1)S(1)}, bf16[2,128,256]{2,1,0:T(8,128)(2,1)S(1)}, bf16[2,128,256]{2,1,0:T(8,128)(2,1)S(1)}) custom-call(s32[30]{0:T(128)S(4)} %get-tuple-element.39.refs_0_, ...), custom_call_target="tpu_custom_call", output_to_operand_aliasing={{0}: (8, {}), {1}: (9, {}), {2}: (10, {})} | custom-call | tf_op jit(solution)/shard_map/tick2_even/pallas_call | solution.py:246
  30.6 0.1 collective-permute-start.15
  30.7 0.6 %collective-permute-start.16 = (bf16[256,256]{1,0:T(8,128)(2,1)S(1)}, bf16[256,256]{1,0:T(8,128)(2,1)S(1)}, u32[]{:S(2)}, u32[]{:S(2)}) collective-permute-start(bf16[256,256]{1,0:T(8,128)(2,1)S(1)} %get-tuple-element.68), channel_id=1, source_target_pairs={{0,4},{1,6},{2,5},{3,7},{4,0},{5,10},{6,9},{7,3},{8,12},{9,14},{10... | collective-permute-start | bytes 393224 | tf_op jit(solution)/shard_map/ppermute | solution.py:375
  31.3 0.0 collective-permute-start.17
  31.3 0.5 %collective-permute-start.18 = (bf16[2,128,256]{2,1,0:T(8,128)(2,1)S(1)}, bf16[2,128,256]{2,1,0:T(8,128)(2,1)S(1)}, u32[]{:S(2)}, u32[]{:S(2)}) collective-permute-start(bf16[2,128,256]{2,1,0:T(8,128)(2,1)S(1)} %get-tuple-element.73), channel_id=1, source_target_pairs={{0,4},{4,0},{8,12},{12,8},{16,20},{20,16},{24,28},{28,24},{1,5},{5... | collective-permute-start | bytes 393224 | tf_op jit(solution)/shard_map/ppermute | solution.py:414
  31.8 6.4 %collective-permute-done.15.refs_7_.refs_6_ = bf16[256,256]{1,0:T(8,128)(2,1)S(1)} collective-permute-done((bf16[256,256]{1,0:T(8,128)(2,1)S(1)}, bf16[256,256]{1,0:T(8,128)(2,1)S(1)}, u32[]{:S(2)}, u32[]{:S(2)}) %collective-permute-start.15) | collective-permute-done | bytes 131104 | tf_op jit(solution)/shard_map/ppermute | solution.py:375
  38.2 0.1 collective-permute-done.16.refs_8_.refs_7_
  38.2 0.0 collective-permute-done.17.refs_5_
  38.2 0.0 collective-permute-done.18.refs_6_
  38.2 0.1 last_tick_odd.1
  38.4 0.0 collective-permute-done.11.refs_5_
  38.4 1.5 %last_tick_even.1 = (bf16[4,1,4,128,256]{4,3,2,1,0:T(8,128)(2,1)}, f32[1,4,128,256]{3,2,1,0:T(8,128)}) custom-call(s32[30]{0:T(128)S(4)} %get-tuple-element.39.refs_0_, bf16[1,4,6,2,128,128]{5,4,3,2,1,0:T(8,128)(2,1)S(1)} %get-tuple-element.41.refs_1_, ...), custom_call_target="tpu_custom_call", output_to_operand_aliasing={{0}: (11, {}), {1}: (12, {})} | custom-call | tf_op jit(solution)/shard_map/last_tick_even/pallas_call | solution.py:246
  (3 shorter events, 0.0 us)
Async XLA Ops:
  1.9 5.3 %collective-permute-start.1 = (bf16[256,256]{1,0:T(8,128)(2,1)S(1)}, bf16[256,256]{1,0:T(8,128)(2,1)S(1)}, u32[]{:S(2)}, u32[]{:S(2)}) collective-permute-start(bf16[256,256]{1,0:T(8,128)(2,1)S(1)} %get-tuple-element.46), channel_id=1, source_target_pairs={{0,4},{1,2},{2,1},{3,7},{4,0},{5,6},{6,5},{7,3},{8,12},{9,10},{10,... | collective-permute-start | bytes 393224 | tf_op jit(solution)/shard_map/ppermute | solution.py:334
  3.5 5.0 %collective-permute-start = (bf16[256,256]{1,0:T(8,128)(2,1)S(1)}, bf16[256,256]{1,0:T(8,128)(2,1)S(1)}, u32[]{:S(2)}, u32[]{:S(2)}) collective-permute-start(bf16[256,256]{1,0:T(8,128)(2,1)S(1)} %get-tuple-element.40.after_ref), channel_id=1, source_target_pairs={{0,1},{1,0},{2,3},{3,2},{4,5},{5,4},{6,7},{7,6},{8,9},{9,8},{10,11... | collective-permute-start | bytes 393224 | tf_op jit(solution)/shard_map/ppermute | solution.py:333
  8.5 9.5 %collective-permute-start.2 = (bf16[512,256]{1,0:T(8,128)(2,1)S(1)}, bf16[512,256]{1,0:T(8,128)(2,1)S(1)}, u32[]{:S(2)}, u32[]{:S(2)}) collective-permute-start(bf16[512,256]{1,0:T(8,128)(2,1)S(1)} %get-tuple-element.47), channel_id=1, source_target_pairs={{0,4},{4,8},{8,12},{12,16},{16,20},{20,24},{24,28},{28,0},{1,5},{5... | collective-permute-start | bytes 786440 | tf_op jit(solution)/shard_map/ppermute | solution.py:410
  9.2 7.6 %collective-permute-start.3 = (bf16[256,256]{1,0:T(8,128)(2,1)S(1)}, bf16[256,256]{1,0:T(8,128)(2,1)S(1)}, u32[]{:S(2)}, u32[]{:S(2)}) collective-permute-start(bf16[256,256]{1,0:T(8,128)(2,1)S(1)} %get-tuple-element.51), channel_id=1, source_target_pairs={{0,5},{1,4},{2,7},{3,6},{4,9},{5,8},{6,11},{7,10},{8,13},{9,12},{1... | collective-permute-start | bytes 393224 | tf_op jit(solution)/shard_map/ppermute | solution.py:375
  9.9 7.5 %collective-permute-start.4 = (bf16[256,256]{1,0:T(8,128)(2,1)S(1)}, bf16[256,256]{1,0:T(8,128)(2,1)S(1)}, u32[]{:S(2)}, u32[]{:S(2)}) collective-permute-start(bf16[256,256]{1,0:T(8,128)(2,1)S(1)} %get-tuple-element.52), channel_id=1, source_target_pairs={{0,4},{1,6},{2,5},{3,7},{4,0},{5,10},{6,9},{7,3},{8,12},{9,14},{10... | collective-permute-start | bytes 393224 | tf_op jit(solution)/shard_map/ppermute | solution.py:375
  12.9 4.5 %collective-permute-start.5 = (bf16[2,128,256]{2,1,0:T(8,128)(2,1)S(1)}, bf16[2,128,256]{2,1,0:T(8,128)(2,1)S(1)}, u32[]{:S(2)}, u32[]{:S(2)}) collective-permute-start(bf16[2,128,256]{2,1,0:T(8,128)(2,1)S(1)} %get-tuple-element.53), channel_id=1, source_target_pairs={{0,4},{4,0},{8,12},{12,8},{16,20},{20,16},{24,28},{28,24},{1,5},{5... | collective-permute-start | bytes 393224 | tf_op jit(solution)/shard_map/ppermute | solution.py:414
  13.3 4.2 %collective-permute-start.6 = (bf16[2,128,256]{2,1,0:T(8,128)(2,1)S(1)}, bf16[2,128,256]{2,1,0:T(8,128)(2,1)S(1)}, u32[]{:S(2)}, u32[]{:S(2)}) collective-permute-start(bf16[2,128,256]{2,1,0:T(8,128)(2,1)S(1)} %get-tuple-element.54), channel_id=1, source_target_pairs={{0,4},{4,0},{8,12},{12,8},{16,20},{20,16},{24,28},{28,24},{1,5},{5... | collective-permute-start | bytes 393224 | tf_op jit(solution)/shard_map/ppermute | solution.py:414
  17.4 12.4 %collective-permute-start.12 = (bf16[528,256]{1,0:T(8,128)(2,1)S(1)}, bf16[528,256]{1,0:T(8,128)(2,1)S(1)}, u32[]{:S(2)}, u32[]{:S(2)}) collective-permute-start(bf16[528,256]{1,0:T(8,128)(2,1)S(1)} %get-tuple-element.61), channel_id=1, source_target_pairs={{0,4},{4,8},{8,12},{12,16},{16,20},{20,24},{24,28},{28,0},{1,5},{5... | collective-permute-start | bytes 811016 | tf_op jit(solution)/shard_map/ppermute | solution.py:410
  18.7 4.6 %collective-permute-start.9 = (bf16[272,256]{1,0:T(8,128)(2,1)S(1)}, bf16[272,256]{1,0:T(8,128)(2,1)S(1)}, u32[]{:S(2)}, u32[]{:S(2)}) collective-permute-start(bf16[272,256]{1,0:T(8,128)(2,1)S(1)} %get-tuple-element.58), channel_id=1, source_target_pairs={{0,5},{1,4},{2,7},{3,6},{4,0},{5,1},{6,2},{7,3},{8,13},{9,12},{10,... | collective-permute-start | bytes 417800 | tf_op jit(solution)/shard_map/ppermute | solution.py:375
  18.8 4.6 %collective-permute-start.10 = (bf16[272,256]{1,0:T(8,128)(2,1)S(1)}, bf16[272,256]{1,0:T(8,128)(2,1)S(1)}, u32[]{:S(2)}, u32[]{:S(2)}) collective-permute-start(bf16[272,256]{1,0:T(8,128)(2,1)S(1)} %get-tuple-element.59), channel_id=1, source_target_pairs={{0,4},{1,6},{2,5},{3,7},{4,0},{5,1},{6,2},{7,3},{8,12},{9,14},{10,... | collective-permute-start | bytes 417800 | tf_op jit(solution)/shard_map/ppermute | solution.py:375
  20.8 1.3 %collective-permute-start.7 = (bf16[2,128,256]{2,1,0:T(8,128)(2,1)S(1)}, bf16[2,128,256]{2,1,0:T(8,128)(2,1)S(1)}, u32[]{:S(2)}, u32[]{:S(2)}) collective-permute-start(bf16[2,128,256]{2,1,0:T(8,128)(2,1)S(1)} %get-tuple-element.56), channel_id=1, source_target_pairs={{0,4},{4,0},{8,12},{12,8},{16,20},{20,16},{24,28},{28,24},{1,5},{5... | collective-permute-start | bytes 393224 | tf_op jit(solution)/shard_map/ppermute | solution.py:414
  20.8 1.5 %collective-permute-start.8 = (bf16[2,128,256]{2,1,0:T(8,128)(2,1)S(1)}, bf16[2,128,256]{2,1,0:T(8,128)(2,1)S(1)}, u32[]{:S(2)}, u32[]{:S(2)}) collective-permute-start(bf16[2,128,256]{2,1,0:T(8,128)(2,1)S(1)} %get-tuple-element.57), channel_id=1, source_target_pairs={{0,4},{4,0},{8,12},{12,8},{16,20},{20,16},{24,28},{28,24},{1,5},{5... | collective-permute-start | bytes 393224 | tf_op jit(solution)/shard_map/ppermute | solution.py:414
  22.1 7.5 %collective-permute-start.13 = (bf16[256,256]{1,0:T(8,128)(2,1)S(1)}, bf16[256,256]{1,0:T(8,128)(2,1)S(1)}, u32[]{:S(2)}, u32[]{:S(2)}) collective-permute-start(bf16[256,256]{1,0:T(8,128)(2,1)S(1)} %get-tuple-element.62), channel_id=1, source_target_pairs={{0,4},{1,5},{2,6},{3,7},{4,9},{5,8},{6,11},{7,10},{8,12},{9,13},{1... | collective-permute-start | bytes 393224 | tf_op jit(solution)/shard_map/ppermute | solution.py:375
  22.3 7.5 %collective-permute-start.14 = (bf16[256,256]{1,0:T(8,128)(2,1)S(1)}, bf16[256,256]{1,0:T(8,128)(2,1)S(1)}, u32[]{:S(2)}, u32[]{:S(2)}) collective-permute-start(bf16[256,256]{1,0:T(8,128)(2,1)S(1)} %get-tuple-element.63), channel_id=1, source_target_pairs={{0,4},{1,5},{2,6},{3,7},{4,0},{5,10},{6,9},{7,3},{8,12},{9,13},{10... | collective-permute-start | bytes 393224 | tf_op jit(solution)/shard_map/ppermute | solution.py:375
  23.4 15.0 %collective-permute-start.11 = (bf16[512,256]{1,0:T(8,128)(2,1)S(1)}, bf16[512,256]{1,0:T(8,128)(2,1)S(1)}, u32[]{:S(2)}, u32[]{:S(2)}) collective-permute-start(bf16[512,256]{1,0:T(8,128)(2,1)S(1)} %get-tuple-element.60), channel_id=1, source_target_pairs={{0,4},{4,8},{8,12},{12,16},{16,20},{20,24},{24,28},{28,0},{1,5},{5... | collective-permute-start | bytes 786440 | tf_op jit(solution)/shard_map/ppermute | solution.py:410
  30.6 7.6 %collective-permute-start.15 = (bf16[256,256]{1,0:T(8,128)(2,1)S(1)}, bf16[256,256]{1,0:T(8,128)(2,1)S(1)}, u32[]{:S(2)}, u32[]{:S(2)}) collective-permute-start(bf16[256,256]{1,0:T(8,128)(2,1)S(1)} %get-tuple-element.67), channel_id=1, source_target_pairs={{0,5},{1,4},{2,7},{3,6},{4,9},{5,8},{6,11},{7,10},{8,13},{9,12},{1... | collective-permute-start | bytes 393224 | tf_op jit(solution)/shard_map/ppermute | solution.py:375
  30.7 7.6 %collective-permute-start.16 = (bf16[256,256]{1,0:T(8,128)(2,1)S(1)}, bf16[256,256]{1,0:T(8,128)(2,1)S(1)}, u32[]{:S(2)}, u32[]{:S(2)}) collective-permute-start(bf16[256,256]{1,0:T(8,128)(2,1)S(1)} %get-tuple-element.68), channel_id=1, source_target_pairs={{0,4},{1,6},{2,5},{3,7},{4,0},{5,10},{6,9},{7,3},{8,12},{9,14},{10... | collective-permute-start | bytes 393224 | tf_op jit(solution)/shard_map/ppermute | solution.py:375
  31.3 7.0 %collective-permute-start.17 = (bf16[2,128,256]{2,1,0:T(8,128)(2,1)S(1)}, bf16[2,128,256]{2,1,0:T(8,128)(2,1)S(1)}, u32[]{:S(2)}, u32[]{:S(2)}) collective-permute-start(bf16[2,128,256]{2,1,0:T(8,128)(2,1)S(1)} %get-tuple-element.72), channel_id=1, source_target_pairs={{0,4},{4,0},{8,12},{12,8},{16,20},{20,16},{24,28},{28,24},{1,5},{5... | collective-permute-start | bytes 393224 | tf_op jit(solution)/shard_map/ppermute | solution.py:414
  31.3 7.0 %collective-permute-start.18 = (bf16[2,128,256]{2,1,0:T(8,128)(2,1)S(1)}, bf16[2,128,256]{2,1,0:T(8,128)(2,1)S(1)}, u32[]{:S(2)}, u32[]{:S(2)}) collective-permute-start(bf16[2,128,256]{2,1,0:T(8,128)(2,1)S(1)} %get-tuple-element.73), channel_id=1, source_target_pairs={{0,4},{4,0},{8,12},{12,8},{16,20},{20,16},{24,28},{28,24},{1,5},{5... | collective-permute-start | bytes 393224 | tf_op jit(solution)/shard_map/ppermute | solution.py:414

commit v18 on v17

--- a/solution.py
+++ b/solution.py
@@ -377,7 +377,7 @@
     arrived = {parity: ([wave], first, second) for parity in (ODD, EVEN)}
     echoes = []
     for tick in range(ticks - 1):
-        first_step, last_step = tick in (0, ticks - 2), False
+        first_step, last_step = False, tick == ticks - 2
         known = []
         waves, halos = {}, {}
         for parity in (ODD, EVEN):

time: 40 us -> 38.4 us (0.960)
  the two profiles are of different devices: /device:TPU:8 before, /device:TPU:0 now
where the time goes in v18:
time: 38.4 us; the launch traced here: 38.2 us
  starting transfers between devices  17.4 us (45%)
  waiting for transfers between devices  9.09 us (24%)
  Pallas kernels  6.82 us (18%)
  blocking collectives  4.15 us (11%)
  between operations  0.74 us (2%)
    ppermute x12, starting transfers between devices, exchange(): return [lax.ppermute(a, both, route) for a, route in zip(lists, routes)]  9.26 us
    ppermute x12, waiting for transfers between devices, exchange(): return [lax.ppermute(a, both, route) for a, route in zip(lists, routes)]  6.52 us
    ppermute x1, starting transfers between devices, per_device(): first = lax.ppermute(first, both, routes[0])  4.15 us
    all_to_all x1, blocking collectives, per_device(): lax.all_to_all(onward[0], 'depth', 0, 0, axis_index_groups=pairs)  4.15 us
    pallas_call x8, Pallas kernels, grouped_call(): pl.pallas_call(body, out_shape=tuple(outs), in_specs=[SMEM_SPEC] + [VMEM_...  3.94 us
    ppermute x3, starting transfers between devices, per_device(): waves[EVEN] = [lax.ppermute(onward[0], 'depth', crossing)]  2.02 us
    pallas_call x1, Pallas kernels, per_device(): pl.pallas_call(load_kernel, out_shape=(pltpu.VMEM(operators.shape, operat...  1.67 us
    ppermute x1, waiting for transfers between devices, per_device(): first = lax.ppermute(first, both, routes[0])  1.52 us
  transfers between devices with their start and end apart: 21, of which 6 were waited for; matrix products, arithmetic and copies ran while one was open for 0% of the time, Pallas kernels for 11%

profile of v18, /device:TPU:0, one launch (start us, length us, event | category | flops | bytes accessed | tf_op | source)
XLA Modules:
  0.0 38.2 jit_solution(10585411945238575904)
XLA Ops:
  0.6 1.2 %prepare.1 = (s32[30]{0:T(128)S(4)}, bf16[4,128,256]{2,1,0:T(8,128)(2,1)S(1)}, bf16[256,256]{1,0:T(8,128)(2,1)S(1)}, bf16[256,256]{1,0:T(8,128)(2,1)S(1)}) custom-call(s32[1,2,2]{2,1,0:T(2,128)} %ids_hbm.1, s32[1,2]{1,0:T(1,128)} %count_hbm.1, s32[4,6]{1,0:T(4,128)} %pattern_hbm.1, f32[1,4,128,256]{3,2,1,0:T(8,128)} %inflow_hbm.1), custom_call_target="tpu_custom_call" | custom-call | flops 131072 | bytes 1048576 | tf_op jit(solution)/shard_map/prepare/pallas_call | solution.py:307
  1.8 0.5 %collective-permute-start.1 = (bf16[256,256]{1,0:T(8,128)(2,1)S(1)}, bf16[256,256]{1,0:T(8,128)(2,1)S(1)}, u32[]{:S(2)}, u32[]{:S(2)}) collective-permute-start(bf16[256,256]{1,0:T(8,128)(2,1)S(1)} %get-tuple-element.45), channel_id=1, source_target_pairs={{0,4},{1,2},{2,1},{3,7},{4,0},{5,6},{6,5},{7,3},{8,12},{9,10},{10,... | collective-permute-start | bytes 393224 | tf_op jit(solution)/shard_map/ppermute | solution.py:334
  2.4 4.2 %collective-permute-start = (bf16[256,256]{1,0:T(8,128)(2,1)S(1)}, bf16[256,256]{1,0:T(8,128)(2,1)S(1)}, u32[]{:S(2)}, u32[]{:S(2)}) collective-permute-start(bf16[256,256]{1,0:T(8,128)(2,1)S(1)} %get-tuple-element.39.after_ref), channel_id=1, source_target_pairs={{0,1},{1,0},{2,3},{3,2},{4,5},{5,4},{6,7},{7,6},{8,9},{9,8},{10,11... | collective-permute-start | bytes 393224 | tf_op jit(solution)/shard_map/ppermute | solution.py:333
  6.5 1.7 %load.1 = (bf16[1,4,6,2,128,128]{5,4,3,2,1,0:T(8,128)(2,1)S(1)}, bf16[3,4,128,256]{3,2,1,0:T(8,128)(2,1)S(1)}, f32[4,128,128]{2,1,0:T(8,128)S(1)}, f32[4,128,128]{2,1,0:T(8,128)S(1)}) custom-call(bf16[1,4,6,2,128,128]{5,4,3,2,1,0:T(8,128)(2,1)} %ops_hbm.1, bf16[3,4,128,256]{3,2,1,0:T(8,128)(2,1)} %source_hbm.1, f32[1,4,128]{2,1,0:T(4,128)} %pass_hbm.1, ...), custom_call_target="tpu_custom_call" | custom-call | bytes 4718592 | tf_op jit(solution)/shard_map/load/pallas_call | solution.py:337
  8.2 0.0 collective-permute-done.1.refs_7_
  8.2 1.5 %collective-permute-done.refs_6_ = bf16[256,256]{1,0:T(8,128)(2,1)S(1)} collective-permute-done((bf16[256,256]{1,0:T(8,128)(2,1)S(1)}, bf16[256,256]{1,0:T(8,128)(2,1)S(1)}, u32[]{:S(2)}, u32[]{:S(2)}) %collective-permute-start) | collective-permute-done | bytes 131104 | tf_op jit(solution)/shard_map/ppermute | solution.py:333
  9.7 0.0 collective-permute-start.2
  9.7 0.8 %tick0_even.1 = (bf16[4,128,256]{2,1,0:T(8,128)(2,1)S(1)}, bf16[272,256]{1,0:T(8,128)(2,1)S(1)}, bf16[272,256]{1,0:T(8,128)(2,1)S(1)}, bf16[2,128,256]{2,1,0:T(8,128)(2,1)S(1)}, bf16[2,128,256]{2,1,0:T(8,128)(2,1)S(1)}) custom-call(s32[30]{0:T(128)S(4)} %get-tuple-element.38.refs_0_, ...), custom_call_target="tpu_custom_call", output_to_operand_aliasing={{0}: (8, {})} | custom-call | tf_op jit(solution)/shard_map/tick0_even/pallas_call | solution.py:246
  10.5 0.8 %collective-permute-start.5 = (bf16[2,128,256]{2,1,0:T(8,128)(2,1)S(1)}, bf16[2,128,256]{2,1,0:T(8,128)(2,1)S(1)}, u32[]{:S(2)}, u32[]{:S(2)}) collective-permute-start(bf16[2,128,256]{2,1,0:T(8,128)(2,1)S(1)} %get-tuple-element.50), channel_id=1, source_target_pairs={{0,4},{4,0},{8,12},{12,8},{16,20},{20,16},{24,28},{28,24},{1,5},{5... | collective-permute-start | bytes 393224 | tf_op jit(solution)/shard_map/ppermute | solution.py:414
  11.3 0.0 collective-permute-start.6
  11.3 1.9 %collective-permute-start.7 = (bf16[272,256]{1,0:T(8,128)(2,1)S(1)}, bf16[272,256]{1,0:T(8,128)(2,1)S(1)}, u32[]{:S(2)}, u32[]{:S(2)}) collective-permute-start(bf16[272,256]{1,0:T(8,128)(2,1)S(1)} %get-tuple-element.52), channel_id=1, source_target_pairs={{0,5},{1,4},{2,7},{3,6},{4,0},{5,1},{6,2},{7,3},{8,13},{9,12},{10,... | collective-permute-start | bytes 417800 | tf_op jit(solution)/shard_map/ppermute | solution.py:375
  13.2 0.0 collective-permute-start.8
  13.2 0.0 collective-permute-done.5.refs_5_
  13.2 0.5 %collective-permute-start.3 = (bf16[256,256]{1,0:T(8,128)(2,1)S(1)}, bf16[256,256]{1,0:T(8,128)(2,1)S(1)}, u32[]{:S(2)}, u32[]{:S(2)}) collective-permute-start(bf16[256,256]{1,0:T(8,128)(2,1)S(1)} %get-tuple-element.47), channel_id=1, source_target_pairs={{0,4},{1,5},{2,6},{3,7},{4,9},{5,8},{6,11},{7,10},{8,12},{9,13},{1... | collective-permute-start | bytes 393224 | tf_op jit(solution)/shard_map/ppermute | solution.py:375
  13.7 0.0 collective-permute-done.6.refs_6_
  13.7 1.4 %collective-permute-start.4 = (bf16[256,256]{1,0:T(8,128)(2,1)S(1)}, bf16[256,256]{1,0:T(8,128)(2,1)S(1)}, u32[]{:S(2)}, u32[]{:S(2)}) collective-permute-start(bf16[256,256]{1,0:T(8,128)(2,1)S(1)} %get-tuple-element.48), channel_id=1, source_target_pairs={{0,4},{1,5},{2,6},{3,7},{4,0},{5,10},{6,9},{7,3},{8,12},{9,13},{10... | collective-permute-start | bytes 393224 | tf_op jit(solution)/shard_map/ppermute | solution.py:375
  15.1 0.9 %collective-permute-done.7.refs_7_ = bf16[272,256]{1,0:T(8,128)(2,1)S(1)} collective-permute-done((bf16[272,256]{1,0:T(8,128)(2,1)S(1)}, bf16[272,256]{1,0:T(8,128)(2,1)S(1)}, u32[]{:S(2)}, u32[]{:S(2)}) %collective-permute-start.7) | collective-permute-done | bytes 139296 | tf_op jit(solution)/shard_map/ppermute | solution.py:375
  16.0 0.0 collective-permute-done.8.refs_8_
  16.0 1.4 %collective-permute-start.16 = (bf16[528,256]{1,0:T(8,128)(2,1)S(1)}, bf16[528,256]{1,0:T(8,128)(2,1)S(1)}, u32[]{:S(2)}, u32[]{:S(2)}) collective-permute-start(bf16[528,256]{1,0:T(8,128)(2,1)S(1)} %get-tuple-element.64), channel_id=1, source_target_pairs={{0,4},{4,8},{8,12},{12,16},{16,20},{20,24},{24,28},{28,0},{1,5},{5... | collective-permute-start | bytes 811016 | tf_op jit(solution)/shard_map/ppermute | solution.py:410
  17.5 2.0 %collective-permute-done.3.refs_6_ = bf16[256,256]{1,0:T(8,128)(2,1)S(1)} collective-permute-done((bf16[256,256]{1,0:T(8,128)(2,1)S(1)}, bf16[256,256]{1,0:T(8,128)(2,1)S(1)}, u32[]{:S(2)}, u32[]{:S(2)}) %collective-permute-start.3) | collective-permute-done | bytes 131104 | tf_op jit(solution)/shard_map/ppermute | solution.py:375
  19.4 0.0 collective-permute-done.4.refs_7_
  19.4 0.0 collective-permute-done.2.refs_5_
  19.4 0.8 %tick1_even.1 = (bf16[4,128,256]{2,1,0:T(8,128)(2,1)S(1)}, bf16[272,256]{1,0:T(8,128)(2,1)S(1)}, bf16[272,256]{1,0:T(8,128)(2,1)S(1)}, bf16[2,128,256]{2,1,0:T(8,128)(2,1)S(1)}, bf16[2,128,256]{2,1,0:T(8,128)(2,1)S(1)}) custom-call(s32[30]{0:T(128)S(4)} %get-tuple-element.38.refs_0_, ...), custom_call_target="tpu_custom_call", output_to_operand_aliasing={{0}: (8, {})} | custom-call | tf_op jit(solution)/shard_map/tick1_even/pallas_call | solution.py:246
  20.2 0.1 collective-permute-start.9
  20.3 2.6 %collective-permute-start.11 = (bf16[272,256]{1,0:T(8,128)(2,1)S(1)}, bf16[272,256]{1,0:T(8,128)(2,1)S(1)}, u32[]{:S(2)}, u32[]{:S(2)}) collective-permute-start(bf16[272,256]{1,0:T(8,128)(2,1)S(1)} %get-tuple-element.57), channel_id=1, source_target_pairs={{0,5},{1,4},{2,7},{3,6},{4,0},{5,1},{6,2},{7,3},{8,13},{9,12},{10,... | collective-permute-start | bytes 417800 | tf_op jit(solution)/shard_map/ppermute | solution.py:375
  22.9 0.0 collective-permute-start.12
  22.9 0.5 %collective-permute-start.10 = (bf16[2,128,256]{2,1,0:T(8,128)(2,1)S(1)}, bf16[2,128,256]{2,1,0:T(8,128)(2,1)S(1)}, u32[]{:S(2)}, u32[]{:S(2)}) collective-permute-start(bf16[2,128,256]{2,1,0:T(8,128)(2,1)S(1)} %get-tuple-element.56), channel_id=1, source_target_pairs={{0,4},{4,0},{8,12},{12,8},{16,20},{20,16},{24,28},{28,24},{1,5},{5... | collective-permute-start | bytes 393224 | tf_op jit(solution)/shard_map/ppermute | solution.py:414
  23.4 0.0 collective-permute-done.9.refs_5_
  23.4 0.0 collective-permute-start.17
  23.4 1.0 %collective-permute-done.10.refs_6_ = bf16[2,128,256]{2,1,0:T(8,128)(2,1)S(1)} collective-permute-done((bf16[2,128,256]{2,1,0:T(8,128)(2,1)S(1)}, bf16[2,128,256]{2,1,0:T(8,128)(2,1)S(1)}, u32[]{:S(2)}, u32[]{:S(2)}) %collective-permute-start.10) | collective-permute-done | bytes 131104 | tf_op jit(solution)/shard_map/ppermute | solution.py:414
  24.5 0.3 collective-permute-start.18
  24.8 1.2 %collective-permute-done.11.refs_7_ = bf16[272,256]{1,0:T(8,128)(2,1)S(1)} collective-permute-done((bf16[272,256]{1,0:T(8,128)(2,1)S(1)}, bf16[272,256]{1,0:T(8,128)(2,1)S(1)}, u32[]{:S(2)}, u32[]{:S(2)}) %collective-permute-start.11) | collective-permute-done | bytes 139296 | tf_op jit(solution)/shard_map/ppermute | solution.py:375
  26.0 0.0 collective-permute-done.12.refs_8_
  26.0 0.6 %collective-permute-start.13 = (bf16[512,256]{1,0:T(8,128)(2,1)S(1)}, bf16[512,256]{1,0:T(8,128)(2,1)S(1)}, u32[]{:S(2)}, u32[]{:S(2)}) collective-permute-start(bf16[512,256]{1,0:T(8,128)(2,1)S(1)} %get-tuple-element.59), channel_id=1, source_target_pairs={{0,4},{4,8},{8,12},{12,16},{16,20},{20,24},{24,28},{28,0},{1,5},{5... | collective-permute-start | bytes 786440 | tf_op jit(solution)/shard_map/ppermute | solution.py:410
  26.6 0.6 %collective-permute-start.14 = (bf16[272,256]{1,0:T(8,128)(2,1)S(1)}, bf16[272,256]{1,0:T(8,128)(2,1)S(1)}, u32[]{:S(2)}, u32[]{:S(2)}) collective-permute-start(bf16[272,256]{1,0:T(8,128)(2,1)S(1)} %get-tuple-element.60), channel_id=1, source_target_pairs={{0,4},{1,5},{2,6},{3,7},{4,9},{5,8},{6,11},{7,10},{8,12},{9,13},{1... | collective-permute-start | bytes 417800 | tf_op jit(solution)/shard_map/ppermute | solution.py:375
  27.1 2.5 %collective-permute-done.17.refs_6_ = bf16[256,256]{1,0:T(8,128)(2,1)S(1)} collective-permute-done((bf16[256,256]{1,0:T(8,128)(2,1)S(1)}, bf16[256,256]{1,0:T(8,128)(2,1)S(1)}, u32[]{:S(2)}, u32[]{:S(2)}) %collective-permute-start.17) | collective-permute-done | bytes 131104 | tf_op jit(solution)/shard_map/ppermute | solution.py:375
  29.6 0.0 collective-permute-start.15
  29.6 0.0 collective-permute-done.18.refs_7_
  29.6 0.0 collective-permute-done.16.refs_5_
  29.6 0.8 %tick2_even.1 = (bf16[4,128,256]{2,1,0:T(8,128)(2,1)S(1)}, bf16[256,256]{1,0:T(8,128)(2,1)S(1)}, bf16[256,256]{1,0:T(8,128)(2,1)S(1)}, bf16[2,4,128,256]{3,2,1,0:T(8,128)(2,1)S(1)}) custom-call(s32[30]{0:T(128)S(4)} %get-tuple-element.38.refs_0_, bf16[1,4,6,2,128,128]{5,4,3,2,1,0:T(8,128)(2,1)S(1)} %get-tuple-element.40.refs_1_, ...), custom_call_target="tpu_custom_call", output_to_operand_aliasing={{0}: (8, {})} | custom-call | tf_op jit(solution)/shard_map/tick2_even/pallas_call | solution.py:246
  30.4 1.9 %collective-permute-start.19 = (bf16[256,256]{1,0:T(8,128)(2,1)S(1)}, bf16[256,256]{1,0:T(8,128)(2,1)S(1)}, u32[]{:S(2)}, u32[]{:S(2)}) collective-permute-start(bf16[256,256]{1,0:T(8,128)(2,1)S(1)} %get-tuple-element.70), channel_id=1, source_target_pairs={{0,5},{1,4},{2,7},{3,6},{4,0},{5,1},{6,2},{7,3},{8,13},{9,12},{10,... | collective-permute-start | bytes 393224 | tf_op jit(solution)/shard_map/ppermute | solution.py:375
  32.4 0.0 collective-permute-start.20
  32.4 4.1 %all_to_all.5.refs_5_ = bf16[2,4,128,256]{3,2,1,0:T(8,128)(2,1)S(1)} all-to-all(bf16[2,4,128,256]{3,2,1,0:T(8,128)(2,1)S(1)} %get-tuple-element.69), channel_id=1, replica_groups={{0,4},{8,12},{16,20},{24,28},{1,5},{9,13},{17,21},{25,29},{2,6},{10,14}..., dimensions={0} | all-to-all | bytes 1048576 | tf_op jit(solution)/shard_map/all_to_all | solution.py:412
  36.5 0.0 collective-permute-done.19.refs_6_
  36.5 0.0 collective-permute-done.20.refs_7_
  36.5 0.1 last_tick_odd.1
  36.6 0.0 collective-permute-done.14.refs_6_
  36.6 0.0 collective-permute-done.15.refs_7_
  36.6 0.0 collective-permute-done.13.refs_5_
  36.7 1.5 %last_tick_even.1 = (bf16[4,1,4,128,256]{4,3,2,1,0:T(8,128)(2,1)}, f32[1,4,128,256]{3,2,1,0:T(8,128)}) custom-call(s32[30]{0:T(128)S(4)} %get-tuple-element.38.refs_0_, bf16[1,4,6,2,128,128]{5,4,3,2,1,0:T(8,128)(2,1)S(1)} %get-tuple-element.40.refs_1_, ...), custom_call_target="tpu_custom_call", output_to_operand_aliasing={{0}: (11, {}), {1}: (12, {})} | custom-call | tf_op jit(solution)/shard_map/last_tick_even/pallas_call | solution.py:246
  (3 shorter events, 0.0 us)
Async XLA Ops:
  1.8 6.4 %collective-permute-start.1 = (bf16[256,256]{1,0:T(8,128)(2,1)S(1)}, bf16[256,256]{1,0:T(8,128)(2,1)S(1)}, u32[]{:S(2)}, u32[]{:S(2)}) collective-permute-start(bf16[256,256]{1,0:T(8,128)(2,1)S(1)} %get-tuple-element.45), channel_id=1, source_target_pairs={{0,4},{1,2},{2,1},{3,7},{4,0},{5,6},{6,5},{7,3},{8,12},{9,10},{10,... | collective-permute-start | bytes 393224 | tf_op jit(solution)/shard_map/ppermute | solution.py:334
  2.4 7.4 %collective-permute-start = (bf16[256,256]{1,0:T(8,128)(2,1)S(1)}, bf16[256,256]{1,0:T(8,128)(2,1)S(1)}, u32[]{:S(2)}, u32[]{:S(2)}) collective-permute-start(bf16[256,256]{1,0:T(8,128)(2,1)S(1)} %get-tuple-element.39.after_ref), channel_id=1, source_target_pairs={{0,1},{1,0},{2,3},{3,2},{4,5},{5,4},{6,7},{7,6},{8,9},{9,8},{10,11... | collective-permute-start | bytes 393224 | tf_op jit(solution)/shard_map/ppermute | solution.py:333
  9.7 9.7 %collective-permute-start.2 = (bf16[528,256]{1,0:T(8,128)(2,1)S(1)}, bf16[528,256]{1,0:T(8,128)(2,1)S(1)}, u32[]{:S(2)}, u32[]{:S(2)}) collective-permute-start(bf16[528,256]{1,0:T(8,128)(2,1)S(1)} %get-tuple-element.46), channel_id=1, source_target_pairs={{0,4},{4,8},{8,12},{12,16},{16,20},{20,24},{24,28},{28,0},{1,5},{5... | collective-permute-start | bytes 811016 | tf_op jit(solution)/shard_map/ppermute | solution.py:410
  10.5 2.7 %collective-permute-start.5 = (bf16[2,128,256]{2,1,0:T(8,128)(2,1)S(1)}, bf16[2,128,256]{2,1,0:T(8,128)(2,1)S(1)}, u32[]{:S(2)}, u32[]{:S(2)}) collective-permute-start(bf16[2,128,256]{2,1,0:T(8,128)(2,1)S(1)} %get-tuple-element.50), channel_id=1, source_target_pairs={{0,4},{4,0},{8,12},{12,8},{16,20},{20,16},{24,28},{28,24},{1,5},{5... | collective-permute-start | bytes 393224 | tf_op jit(solution)/shard_map/ppermute | solution.py:414
  11.3 2.4 %collective-permute-start.6 = (bf16[2,128,256]{2,1,0:T(8,128)(2,1)S(1)}, bf16[2,128,256]{2,1,0:T(8,128)(2,1)S(1)}, u32[]{:S(2)}, u32[]{:S(2)}) collective-permute-start(bf16[2,128,256]{2,1,0:T(8,128)(2,1)S(1)} %get-tuple-element.51), channel_id=1, source_target_pairs={{0,4},{4,0},{8,12},{12,8},{16,20},{20,16},{24,28},{28,24},{1,5},{5... | collective-permute-start | bytes 393224 | tf_op jit(solution)/shard_map/ppermute | solution.py:414
  11.3 4.7 %collective-permute-start.7 = (bf16[272,256]{1,0:T(8,128)(2,1)S(1)}, bf16[272,256]{1,0:T(8,128)(2,1)S(1)}, u32[]{:S(2)}, u32[]{:S(2)}) collective-permute-start(bf16[272,256]{1,0:T(8,128)(2,1)S(1)} %get-tuple-element.52), channel_id=1, source_target_pairs={{0,5},{1,4},{2,7},{3,6},{4,0},{5,1},{6,2},{7,3},{8,13},{9,12},{10,... | collective-permute-start | bytes 417800 | tf_op jit(solution)/shard_map/ppermute | solution.py:375
  13.2 2.8 %collective-permute-start.8 = (bf16[272,256]{1,0:T(8,128)(2,1)S(1)}, bf16[272,256]{1,0:T(8,128)(2,1)S(1)}, u32[]{:S(2)}, u32[]{:S(2)}) collective-permute-start(bf16[272,256]{1,0:T(8,128)(2,1)S(1)} %get-tuple-element.53), channel_id=1, source_target_pairs={{0,4},{1,6},{2,5},{3,7},{4,0},{5,1},{6,2},{7,3},{8,12},{9,14},{10,... | collective-permute-start | bytes 417800 | tf_op jit(solution)/shard_map/ppermute | solution.py:375
  13.2 6.2 %collective-permute-start.3 = (bf16[256,256]{1,0:T(8,128)(2,1)S(1)}, bf16[256,256]{1,0:T(8,128)(2,1)S(1)}, u32[]{:S(2)}, u32[]{:S(2)}) collective-permute-start(bf16[256,256]{1,0:T(8,128)(2,1)S(1)} %get-tuple-element.47), channel_id=1, source_target_pairs={{0,4},{1,5},{2,6},{3,7},{4,9},{5,8},{6,11},{7,10},{8,12},{9,13},{1... | collective-permute-start | bytes 393224 | tf_op jit(solution)/shard_map/ppermute | solution.py:375
  13.7 5.7 %collective-permute-start.4 = (bf16[256,256]{1,0:T(8,128)(2,1)S(1)}, bf16[256,256]{1,0:T(8,128)(2,1)S(1)}, u32[]{:S(2)}, u32[]{:S(2)}) collective-permute-start(bf16[256,256]{1,0:T(8,128)(2,1)S(1)} %get-tuple-element.48), channel_id=1, source_target_pairs={{0,4},{1,5},{2,6},{3,7},{4,0},{5,10},{6,9},{7,3},{8,12},{9,13},{10... | collective-permute-start | bytes 393224 | tf_op jit(solution)/shard_map/ppermute | solution.py:375
  16.0 13.6 %collective-permute-start.16 = (bf16[528,256]{1,0:T(8,128)(2,1)S(1)}, bf16[528,256]{1,0:T(8,128)(2,1)S(1)}, u32[]{:S(2)}, u32[]{:S(2)}) collective-permute-start(bf16[528,256]{1,0:T(8,128)(2,1)S(1)} %get-tuple-element.64), channel_id=1, source_target_pairs={{0,4},{4,8},{8,12},{12,16},{16,20},{20,24},{24,28},{28,0},{1,5},{5... | collective-permute-start | bytes 811016 | tf_op jit(solution)/shard_map/ppermute | solution.py:410
  20.2 3.2 %collective-permute-start.9 = (bf16[2,128,256]{2,1,0:T(8,128)(2,1)S(1)}, bf16[2,128,256]{2,1,0:T(8,128)(2,1)S(1)}, u32[]{:S(2)}, u32[]{:S(2)}) collective-permute-start(bf16[2,128,256]{2,1,0:T(8,128)(2,1)S(1)} %get-tuple-element.55), channel_id=1, source_target_pairs={{0,4},{4,0},{8,12},{12,8},{16,20},{20,16},{24,28},{28,24},{1,5},{5... | collective-permute-start | bytes 393224 | tf_op jit(solution)/shard_map/ppermute | solution.py:414
  20.3 5.7 %collective-permute-start.11 = (bf16[272,256]{1,0:T(8,128)(2,1)S(1)}, bf16[272,256]{1,0:T(8,128)(2,1)S(1)}, u32[]{:S(2)}, u32[]{:S(2)}) collective-permute-start(bf16[272,256]{1,0:T(8,128)(2,1)S(1)} %get-tuple-element.57), channel_id=1, source_target_pairs={{0,5},{1,4},{2,7},{3,6},{4,0},{5,1},{6,2},{7,3},{8,13},{9,12},{10,... | collective-permute-start | bytes 417800 | tf_op jit(solution)/shard_map/ppermute | solution.py:375
  22.9 3.0 %collective-permute-start.12 = (bf16[272,256]{1,0:T(8,128)(2,1)S(1)}, bf16[272,256]{1,0:T(8,128)(2,1)S(1)}, u32[]{:S(2)}, u32[]{:S(2)}) collective-permute-start(bf16[272,256]{1,0:T(8,128)(2,1)S(1)} %get-tuple-element.58), channel_id=1, source_target_pairs={{0,4},{1,6},{2,5},{3,7},{4,0},{5,1},{6,2},{7,3},{8,12},{9,14},{10,... | collective-permute-start | bytes 417800 | tf_op jit(solution)/shard_map/ppermute | solution.py:375
  22.9 1.5 %collective-permute-start.10 = (bf16[2,128,256]{2,1,0:T(8,128)(2,1)S(1)}, bf16[2,128,256]{2,1,0:T(8,128)(2,1)S(1)}, u32[]{:S(2)}, u32[]{:S(2)}) collective-permute-start(bf16[2,128,256]{2,1,0:T(8,128)(2,1)S(1)} %get-tuple-element.56), channel_id=1, source_target_pairs={{0,4},{4,0},{8,12},{12,8},{16,20},{20,16},{24,28},{28,24},{1,5},{5... | collective-permute-start | bytes 393224 | tf_op jit(solution)/shard_map/ppermute | solution.py:414
  23.4 6.2 %collective-permute-start.17 = (bf16[256,256]{1,0:T(8,128)(2,1)S(1)}, bf16[256,256]{1,0:T(8,128)(2,1)S(1)}, u32[]{:S(2)}, u32[]{:S(2)}) collective-permute-start(bf16[256,256]{1,0:T(8,128)(2,1)S(1)} %get-tuple-element.65), channel_id=1, source_target_pairs={{0,4},{1,5},{2,6},{3,7},{4,9},{5,8},{6,11},{7,10},{8,12},{9,13},{1... | collective-permute-start | bytes 393224 | tf_op jit(solution)/shard_map/ppermute | solution.py:375
  24.5 5.2 %collective-permute-start.18 = (bf16[256,256]{1,0:T(8,128)(2,1)S(1)}, bf16[256,256]{1,0:T(8,128)(2,1)S(1)}, u32[]{:S(2)}, u32[]{:S(2)}) collective-permute-start(bf16[256,256]{1,0:T(8,128)(2,1)S(1)} %get-tuple-element.66), channel_id=1, source_target_pairs={{0,4},{1,5},{2,6},{3,7},{4,0},{5,10},{6,9},{7,3},{8,12},{9,13},{10... | collective-permute-start | bytes 393224 | tf_op jit(solution)/shard_map/ppermute | solution.py:375
  26.0 10.7 %collective-permute-start.13 = (bf16[512,256]{1,0:T(8,128)(2,1)S(1)}, bf16[512,256]{1,0:T(8,128)(2,1)S(1)}, u32[]{:S(2)}, u32[]{:S(2)}) collective-permute-start(bf16[512,256]{1,0:T(8,128)(2,1)S(1)} %get-tuple-element.59), channel_id=1, source_target_pairs={{0,4},{4,8},{8,12},{12,16},{16,20},{20,24},{24,28},{28,0},{1,5},{5... | collective-permute-start | bytes 786440 | tf_op jit(solution)/shard_map/ppermute | solution.py:410
  26.6 10.1 %collective-permute-start.14 = (bf16[272,256]{1,0:T(8,128)(2,1)S(1)}, bf16[272,256]{1,0:T(8,128)(2,1)S(1)}, u32[]{:S(2)}, u32[]{:S(2)}) collective-permute-start(bf16[272,256]{1,0:T(8,128)(2,1)S(1)} %get-tuple-element.60), channel_id=1, source_target_pairs={{0,4},{1,5},{2,6},{3,7},{4,9},{5,8},{6,11},{7,10},{8,12},{9,13},{1... | collective-permute-start | bytes 417800 | tf_op jit(solution)/shard_map/ppermute | solution.py:375
  29.6 7.0 %collective-permute-start.15 = (bf16[272,256]{1,0:T(8,128)(2,1)S(1)}, bf16[272,256]{1,0:T(8,128)(2,1)S(1)}, u32[]{:S(2)}, u32[]{:S(2)}) collective-permute-start(bf16[272,256]{1,0:T(8,128)(2,1)S(1)} %get-tuple-element.61), channel_id=1, source_target_pairs={{0,4},{1,5},{2,6},{3,7},{4,0},{5,10},{6,9},{7,3},{8,12},{9,13},{10... | collective-permute-start | bytes 417800 | tf_op jit(solution)/shard_map/ppermute | solution.py:375
  30.4 6.1 %collective-permute-start.19 = (bf16[256,256]{1,0:T(8,128)(2,1)S(1)}, bf16[256,256]{1,0:T(8,128)(2,1)S(1)}, u32[]{:S(2)}, u32[]{:S(2)}) collective-permute-start(bf16[256,256]{1,0:T(8,128)(2,1)S(1)} %get-tuple-element.70), channel_id=1, source_target_pairs={{0,5},{1,4},{2,7},{3,6},{4,0},{5,1},{6,2},{7,3},{8,13},{9,12},{10,... | collective-permute-start | bytes 393224 | tf_op jit(solution)/shard_map/ppermute | solution.py:375
  32.4 4.2 %collective-permute-start.20 = (bf16[256,256]{1,0:T(8,128)(2,1)S(1)}, bf16[256,256]{1,0:T(8,128)(2,1)S(1)}, u32[]{:S(2)}, u32[]{:S(2)}) collective-permute-start(bf16[256,256]{1,0:T(8,128)(2,1)S(1)} %get-tuple-element.71), channel_id=1, source_target_pairs={{0,4},{1,6},{2,5},{3,7},{4,0},{5,1},{6,2},{7,3},{8,12},{9,14},{10,... | collective-permute-start | bytes 393224 | tf_op jit(solution)/shard_map/ppermute | solution.py:375

commit v19 on v10

--- a/solution.py
+++ b/solution.py
@@ -140,13 +140,17 @@
 def extrapolate_block(plan_ref, pattern_start, ops_ref, buffer, b):
     taken = ops_ref.shape[2]
     points = ops_ref.shape[5]
-    left = jnp.concatenate(
-        [ops_ref[0, b, k].reshape(2 * points, points) for k in range(taken)], axis=1
-    )
-    right = jnp.concatenate(
-        [buffer[plan_ref[pattern_start + b * taken + k]] for k in range(taken)], axis=0
-    )
-    products = jnp.dot(left, right, preferred_element_type=jnp.float32)
+    products = None
+    for start in range(0, taken, 2):
+        pair = range(start, min(start + 2, taken))
+        left = jnp.concatenate(
+            [ops_ref[0, b, k].reshape(2 * points, points) for k in pair], axis=1
+        )
+        right = jnp.concatenate(
+            [buffer[plan_ref[pattern_start + b * taken + k]] for k in pair], axis=0
+        )
+        part = jnp.dot(left, right, preferred_element_type=jnp.float32)
+        products = part if products is None else products + part
     half = products.shape[1] // 2
     real_part = products[:points, :half] - products[points:, half:]
     imag_part = products[:points, half:] + products[points:, :half]

time: 37.8 us -> 37.8 us (level)
  no operation moved by 1% of the time
where the time goes in v19:
time: 37.8 us; the launch traced here: 37.6 us
  starting transfers between devices  16.9 us (45%)
  waiting for transfers between devices  8.92 us (24%)
  Pallas kernels  6.83 us (18%)
  blocking collectives  4.15 us (11%)
  between operations  0.75 us (2%)
    ppermute x10, starting transfers between devices, exchange(): return [lax.ppermute(a, both, route) for a, route in zip(lists, routes)]  9.95 us
    ppermute x10, waiting for transfers between devices, exchange(): return [lax.ppermute(a, both, route) for a, route in zip(lists, routes)]  6.35 us
    all_to_all x1, blocking collectives, per_device(): lax.all_to_all(onward[0], 'depth', 0, 0, axis_index_groups=pairs)  4.15 us
    ppermute x1, starting transfers between devices, per_device(): first = lax.ppermute(first, both, routes[0])  4.15 us
    pallas_call x8, Pallas kernels, grouped_call(): pl.pallas_call(body, out_shape=tuple(outs), in_specs=[SMEM_SPEC] + [VMEM_...  3.94 us
    pallas_call x1, Pallas kernels, per_device(): pl.pallas_call(load_kernel, out_shape=(pltpu.VMEM(operators.shape, operat...  1.67 us
    ppermute x1, waiting for transfers between devices, per_device(): first = lax.ppermute(first, both, routes[0])  1.52 us
    ppermute x3, starting transfers between devices, per_device(): waves[EVEN] = [lax.ppermute(onward[0], 'depth', crossing)]  1.23 us
  transfers between devices with their start and end apart: 19, of which 4 were waited for; matrix products, arithmetic and copies ran while one was open for 0% of the time, Pallas kernels for 11%

profile of v19, /device:TPU:0, one launch (start us, length us, event | category | flops | bytes accessed | tf_op | source)
XLA Modules:
  0.0 37.6 jit_solution(2900229016392521281)
XLA Ops:
  0.6 1.2 %prepare.1 = (s32[30]{0:T(128)S(4)}, bf16[4,128,256]{2,1,0:T(8,128)(2,1)S(1)}, bf16[256,256]{1,0:T(8,128)(2,1)S(1)}, bf16[256,256]{1,0:T(8,128)(2,1)S(1)}) custom-call(s32[1,2,2]{2,1,0:T(2,128)} %ids_hbm.1, s32[1,2]{1,0:T(1,128)} %count_hbm.1, s32[4,6]{1,0:T(4,128)} %pattern_hbm.1, f32[1,4,128,256]{3,2,1,0:T(8,128)} %inflow_hbm.1), custom_call_target="tpu_custom_call" | custom-call | flops 131072 | bytes 1048576 | tf_op jit(solution)/shard_map/prepare/pallas_call | solution.py:311
  1.9 0.5 %collective-permute-start.1 = (bf16[256,256]{1,0:T(8,128)(2,1)S(1)}, bf16[256,256]{1,0:T(8,128)(2,1)S(1)}, u32[]{:S(2)}, u32[]{:S(2)}) collective-permute-start(bf16[256,256]{1,0:T(8,128)(2,1)S(1)} %get-tuple-element.45), channel_id=1, source_target_pairs={{0,4},{1,2},{2,1},{3,7},{4,0},{5,6},{6,5},{7,3},{8,12},{9,10},{10,... | collective-permute-start | bytes 393224 | tf_op jit(solution)/shard_map/ppermute | solution.py:338
  2.4 4.1 %collective-permute-start = (bf16[256,256]{1,0:T(8,128)(2,1)S(1)}, bf16[256,256]{1,0:T(8,128)(2,1)S(1)}, u32[]{:S(2)}, u32[]{:S(2)}) collective-permute-start(bf16[256,256]{1,0:T(8,128)(2,1)S(1)} %get-tuple-element.39.after_ref), channel_id=1, source_target_pairs={{0,1},{1,0},{2,3},{3,2},{4,5},{5,4},{6,7},{7,6},{8,9},{9,8},{10,11... | collective-permute-start | bytes 393224 | tf_op jit(solution)/shard_map/ppermute | solution.py:337
  6.5 1.7 %load.1 = (bf16[1,4,6,2,128,128]{5,4,3,2,1,0:T(8,128)(2,1)S(1)}, bf16[3,4,128,256]{3,2,1,0:T(8,128)(2,1)S(1)}, f32[4,128,128]{2,1,0:T(8,128)S(1)}, f32[4,128,128]{2,1,0:T(8,128)S(1)}) custom-call(bf16[1,4,6,2,128,128]{5,4,3,2,1,0:T(8,128)(2,1)} %ops_hbm.1, bf16[3,4,128,256]{3,2,1,0:T(8,128)(2,1)} %source_hbm.1, f32[1,4,128]{2,1,0:T(4,128)} %pass_hbm.1, ...), custom_call_target="tpu_custom_call" | custom-call | bytes 4718592 | tf_op jit(solution)/shard_map/load/pallas_call | solution.py:341
  8.2 0.0 collective-permute-done.1.refs_7_
  8.2 1.5 %collective-permute-done.refs_6_ = bf16[256,256]{1,0:T(8,128)(2,1)S(1)} collective-permute-done((bf16[256,256]{1,0:T(8,128)(2,1)S(1)}, bf16[256,256]{1,0:T(8,128)(2,1)S(1)}, u32[]{:S(2)}, u32[]{:S(2)}) %collective-permute-start) | collective-permute-done | bytes 131104 | tf_op jit(solution)/shard_map/ppermute | solution.py:337
  9.7 0.0 collective-permute-start.2
  9.7 0.8 %tick0_even.1 = (bf16[4,128,256]{2,1,0:T(8,128)(2,1)S(1)}, bf16[256,256]{1,0:T(8,128)(2,1)S(1)}, bf16[256,256]{1,0:T(8,128)(2,1)S(1)}, bf16[2,128,256]{2,1,0:T(8,128)(2,1)S(1)}, bf16[2,128,256]{2,1,0:T(8,128)(2,1)S(1)}) custom-call(s32[30]{0:T(128)S(4)} %get-tuple-element.38.refs_0_, ...), custom_call_target="tpu_custom_call", output_to_operand_aliasing={{0}: (8, {}), {1}: (9, {}), {2}: (10, {})} | custom-call | tf_op jit(solution)/shard_map/tick0_even/pallas_call | solution.py:250
  10.5 2.2 %collective-permute-start.3 = (bf16[256,256]{1,0:T(8,128)(2,1)S(1)}, bf16[256,256]{1,0:T(8,128)(2,1)S(1)}, u32[]{:S(2)}, u32[]{:S(2)}) collective-permute-start(bf16[256,256]{1,0:T(8,128)(2,1)S(1)} %get-tuple-element.50), channel_id=1, source_target_pairs={{0,5},{1,4},{2,7},{3,6},{4,9},{5,8},{6,11},{7,10},{8,13},{9,12},{1... | collective-permute-start | bytes 393224 | tf_op jit(solution)/shard_map/ppermute | solution.py:379
  12.7 0.7 %collective-permute-start.4 = (bf16[256,256]{1,0:T(8,128)(2,1)S(1)}, bf16[256,256]{1,0:T(8,128)(2,1)S(1)}, u32[]{:S(2)}, u32[]{:S(2)}) collective-permute-start(bf16[256,256]{1,0:T(8,128)(2,1)S(1)} %get-tuple-element.51), channel_id=1, source_target_pairs={{0,4},{1,6},{2,5},{3,7},{4,0},{5,10},{6,9},{7,3},{8,12},{9,14},{10... | collective-permute-start | bytes 393224 | tf_op jit(solution)/shard_map/ppermute | solution.py:379
  13.4 0.0 collective-permute-start.5
  13.4 0.5 %collective-permute-start.6 = (bf16[2,128,256]{2,1,0:T(8,128)(2,1)S(1)}, bf16[2,128,256]{2,1,0:T(8,128)(2,1)S(1)}, u32[]{:S(2)}, u32[]{:S(2)}) collective-permute-start(bf16[2,128,256]{2,1,0:T(8,128)(2,1)S(1)} %get-tuple-element.53), channel_id=1, source_target_pairs={{0,4},{4,0},{8,12},{12,8},{16,20},{20,16},{24,28},{28,24},{1,5},{5... | collective-permute-start | bytes 393224 | tf_op jit(solution)/shard_map/ppermute | solution.py:418
  13.9 4.0 %collective-permute-done.3.refs_7_.refs_6_ = bf16[256,256]{1,0:T(8,128)(2,1)S(1)} collective-permute-done((bf16[256,256]{1,0:T(8,128)(2,1)S(1)}, bf16[256,256]{1,0:T(8,128)(2,1)S(1)}, u32[]{:S(2)}, u32[]{:S(2)}) %collective-permute-start.3) | collective-permute-done | bytes 131104 | tf_op jit(solution)/shard_map/ppermute | solution.py:379
  17.9 0.0 collective-permute-done.4.refs_8_.refs_7_
  17.9 0.0 collective-permute-done.5.refs_5_
  17.9 0.0 collective-permute-done.6.refs_6_
  17.9 0.4 collective-permute-start.14
  18.3 0.0 collective-permute-done.2.refs_5_
  18.3 0.8 %tick1_even.1 = (bf16[4,128,256]{2,1,0:T(8,128)(2,1)S(1)}, bf16[272,256]{1,0:T(8,128)(2,1)S(1)}, bf16[272,256]{1,0:T(8,128)(2,1)S(1)}, bf16[2,128,256]{2,1,0:T(8,128)(2,1)S(1)}, bf16[2,128,256]{2,1,0:T(8,128)(2,1)S(1)}) custom-call(s32[30]{0:T(128)S(4)} %get-tuple-element.38.refs_0_, ...), custom_call_target="tpu_custom_call", output_to_operand_aliasing={{0}: (8, {})} | custom-call | tf_op jit(solution)/shard_map/tick1_even/pallas_call | solution.py:250
  19.0 0.1 collective-permute-start.7
  19.1 2.8 %collective-permute-start.9 = (bf16[272,256]{1,0:T(8,128)(2,1)S(1)}, bf16[272,256]{1,0:T(8,128)(2,1)S(1)}, u32[]{:S(2)}, u32[]{:S(2)}) collective-permute-start(bf16[272,256]{1,0:T(8,128)(2,1)S(1)} %get-tuple-element.57), channel_id=1, source_target_pairs={{0,5},{1,4},{2,7},{3,6},{4,0},{5,1},{6,2},{7,3},{8,13},{9,12},{10,... | collective-permute-start | bytes 417800 | tf_op jit(solution)/shard_map/ppermute | solution.py:379
  22.0 0.0 collective-permute-start.10
  22.0 0.5 %collective-permute-start.8 = (bf16[2,128,256]{2,1,0:T(8,128)(2,1)S(1)}, bf16[2,128,256]{2,1,0:T(8,128)(2,1)S(1)}, u32[]{:S(2)}, u32[]{:S(2)}) collective-permute-start(bf16[2,128,256]{2,1,0:T(8,128)(2,1)S(1)} %get-tuple-element.56), channel_id=1, source_target_pairs={{0,4},{4,0},{8,12},{12,8},{16,20},{20,16},{24,28},{28,24},{1,5},{5... | collective-permute-start | bytes 393224 | tf_op jit(solution)/shard_map/ppermute | solution.py:418
  22.5 0.0 collective-permute-done.7.refs_5_
  22.5 0.0 collective-permute-start.15
  22.5 1.0 %collective-permute-done.8.refs_6_ = bf16[2,128,256]{2,1,0:T(8,128)(2,1)S(1)} collective-permute-done((bf16[2,128,256]{2,1,0:T(8,128)(2,1)S(1)}, bf16[2,128,256]{2,1,0:T(8,128)(2,1)S(1)}, u32[]{:S(2)}, u32[]{:S(2)}) %collective-permute-start.8) | collective-permute-done | bytes 131104 | tf_op jit(solution)/shard_map/ppermute | solution.py:418
  23.5 1.9 %collective-permute-start.16 = (bf16[256,256]{1,0:T(8,128)(2,1)S(1)}, bf16[256,256]{1,0:T(8,128)(2,1)S(1)}, u32[]{:S(2)}, u32[]{:S(2)}) collective-permute-start(bf16[256,256]{1,0:T(8,128)(2,1)S(1)} %get-tuple-element.66), channel_id=1, source_target_pairs={{0,4},{1,5},{2,6},{3,7},{4,0},{5,10},{6,9},{7,3},{8,12},{9,13},{10... | collective-permute-start | bytes 393224 | tf_op jit(solution)/shard_map/ppermute | solution.py:379
  25.4 0.0 collective-permute-done.9.refs_7_
  25.4 0.0 collective-permute-done.10.refs_8_
  25.4 0.9 %collective-permute-start.11 = (bf16[512,256]{1,0:T(8,128)(2,1)S(1)}, bf16[512,256]{1,0:T(8,128)(2,1)S(1)}, u32[]{:S(2)}, u32[]{:S(2)}) collective-permute-start(bf16[512,256]{1,0:T(8,128)(2,1)S(1)} %get-tuple-element.59), channel_id=1, source_target_pairs={{0,4},{4,8},{8,12},{12,16},{16,20},{20,24},{24,28},{28,0},{1,5},{5... | collective-permute-start | bytes 786440 | tf_op jit(solution)/shard_map/ppermute | solution.py:414
  26.2 0.1 collective-permute-start.12
  26.3 2.3 %collective-permute-done.15.refs_6_ = bf16[256,256]{1,0:T(8,128)(2,1)S(1)} collective-permute-done((bf16[256,256]{1,0:T(8,128)(2,1)S(1)}, bf16[256,256]{1,0:T(8,128)(2,1)S(1)}, u32[]{:S(2)}, u32[]{:S(2)}) %collective-permute-start.15) | collective-permute-done | bytes 131104 | tf_op jit(solution)/shard_map/ppermute | solution.py:379
  28.7 0.4 collective-permute-start.13
  29.0 0.0 collective-permute-done.16.refs_7_
  29.0 0.0 collective-permute-done.14.refs_5_
  29.0 0.8 %tick2_even.1 = (bf16[4,128,256]{2,1,0:T(8,128)(2,1)S(1)}, bf16[256,256]{1,0:T(8,128)(2,1)S(1)}, bf16[256,256]{1,0:T(8,128)(2,1)S(1)}, bf16[2,4,128,256]{3,2,1,0:T(8,128)(2,1)S(1)}) custom-call(s32[30]{0:T(128)S(4)} %get-tuple-element.38.refs_0_, bf16[1,4,6,2,128,128]{5,4,3,2,1,0:T(8,128)(2,1)S(1)} %get-tuple-element.40.refs_1_, ...), custom_call_target="tpu_custom_call", output_to_operand_aliasing={{0}: (8, {})} | custom-call | tf_op jit(solution)/shard_map/tick2_even/pallas_call | solution.py:250
  29.8 2.0 %collective-permute-start.17 = (bf16[256,256]{1,0:T(8,128)(2,1)S(1)}, bf16[256,256]{1,0:T(8,128)(2,1)S(1)}, u32[]{:S(2)}, u32[]{:S(2)}) collective-permute-start(bf16[256,256]{1,0:T(8,128)(2,1)S(1)} %get-tuple-element.70), channel_id=1, source_target_pairs={{0,5},{1,4},{2,7},{3,6},{4,0},{5,1},{6,2},{7,3},{8,13},{9,12},{10,... | collective-permute-start | bytes 393224 | tf_op jit(solution)/shard_map/ppermute | solution.py:379
  31.8 0.0 collective-permute-start.18
  31.8 4.1 %all_to_all.5.refs_5_ = bf16[2,4,128,256]{3,2,1,0:T(8,128)(2,1)S(1)} all-to-all(bf16[2,4,128,256]{3,2,1,0:T(8,128)(2,1)S(1)} %get-tuple-element.69), channel_id=1, replica_groups={{0,4},{8,12},{16,20},{24,28},{1,5},{9,13},{17,21},{25,29},{2,6},{10,14}..., dimensions={0} | all-to-all | bytes 1048576 | tf_op jit(solution)/shard_map/all_to_all | solution.py:416
  35.9 0.0 collective-permute-done.17.refs_6_
  35.9 0.0 collective-permute-done.18.refs_7_
  35.9 0.1 last_tick_odd.1
  36.0 0.0 collective-permute-done.12.refs_6_
  36.0 0.0 collective-permute-done.13.refs_7_
  36.1 0.0 collective-permute-done.11.refs_5_
  36.1 1.5 %last_tick_even.1 = (bf16[4,1,4,128,256]{4,3,2,1,0:T(8,128)(2,1)}, f32[1,4,128,256]{3,2,1,0:T(8,128)}) custom-call(s32[30]{0:T(128)S(4)} %get-tuple-element.38.refs_0_, bf16[1,4,6,2,128,128]{5,4,3,2,1,0:T(8,128)(2,1)S(1)} %get-tuple-element.40.refs_1_, ...), custom_call_target="tpu_custom_call", output_to_operand_aliasing={{0}: (11, {}), {1}: (12, {})} | custom-call | tf_op jit(solution)/shard_map/last_tick_even/pallas_call | solution.py:250
  (3 shorter events, 0.0 us)
Async XLA Ops:
  1.9 6.3 %collective-permute-start.1 = (bf16[256,256]{1,0:T(8,128)(2,1)S(1)}, bf16[256,256]{1,0:T(8,128)(2,1)S(1)}, u32[]{:S(2)}, u32[]{:S(2)}) collective-permute-start(bf16[256,256]{1,0:T(8,128)(2,1)S(1)} %get-tuple-element.45), channel_id=1, source_target_pairs={{0,4},{1,2},{2,1},{3,7},{4,0},{5,6},{6,5},{7,3},{8,12},{9,10},{10,... | collective-permute-start | bytes 393224 | tf_op jit(solution)/shard_map/ppermute | solution.py:338
  2.4 7.4 %collective-permute-start = (bf16[256,256]{1,0:T(8,128)(2,1)S(1)}, bf16[256,256]{1,0:T(8,128)(2,1)S(1)}, u32[]{:S(2)}, u32[]{:S(2)}) collective-permute-start(bf16[256,256]{1,0:T(8,128)(2,1)S(1)} %get-tuple-element.39.after_ref), channel_id=1, source_target_pairs={{0,1},{1,0},{2,3},{3,2},{4,5},{5,4},{6,7},{7,6},{8,9},{9,8},{10,11... | collective-permute-start | bytes 393224 | tf_op jit(solution)/shard_map/ppermute | solution.py:337
  9.7 8.5 %collective-permute-start.2 = (bf16[512,256]{1,0:T(8,128)(2,1)S(1)}, bf16[512,256]{1,0:T(8,128)(2,1)S(1)}, u32[]{:S(2)}, u32[]{:S(2)}) collective-permute-start(bf16[512,256]{1,0:T(8,128)(2,1)S(1)} %get-tuple-element.46), channel_id=1, source_target_pairs={{0,4},{4,8},{8,12},{12,16},{16,20},{20,24},{24,28},{28,0},{1,5},{5... | collective-permute-start | bytes 786440 | tf_op jit(solution)/shard_map/ppermute | solution.py:414
  10.5 7.3 %collective-permute-start.3 = (bf16[256,256]{1,0:T(8,128)(2,1)S(1)}, bf16[256,256]{1,0:T(8,128)(2,1)S(1)}, u32[]{:S(2)}, u32[]{:S(2)}) collective-permute-start(bf16[256,256]{1,0:T(8,128)(2,1)S(1)} %get-tuple-element.50), channel_id=1, source_target_pairs={{0,5},{1,4},{2,7},{3,6},{4,9},{5,8},{6,11},{7,10},{8,13},{9,12},{1... | collective-permute-start | bytes 393224 | tf_op jit(solution)/shard_map/ppermute | solution.py:379
  12.7 5.2 %collective-permute-start.4 = (bf16[256,256]{1,0:T(8,128)(2,1)S(1)}, bf16[256,256]{1,0:T(8,128)(2,1)S(1)}, u32[]{:S(2)}, u32[]{:S(2)}) collective-permute-start(bf16[256,256]{1,0:T(8,128)(2,1)S(1)} %get-tuple-element.51), channel_id=1, source_target_pairs={{0,4},{1,6},{2,5},{3,7},{4,0},{5,10},{6,9},{7,3},{8,12},{9,14},{10... | collective-permute-start | bytes 393224 | tf_op jit(solution)/shard_map/ppermute | solution.py:379
  13.4 4.5 %collective-permute-start.5 = (bf16[2,128,256]{2,1,0:T(8,128)(2,1)S(1)}, bf16[2,128,256]{2,1,0:T(8,128)(2,1)S(1)}, u32[]{:S(2)}, u32[]{:S(2)}) collective-permute-start(bf16[2,128,256]{2,1,0:T(8,128)(2,1)S(1)} %get-tuple-element.52), channel_id=1, source_target_pairs={{0,4},{4,0},{8,12},{12,8},{16,20},{20,16},{24,28},{28,24},{1,5},{5... | collective-permute-start | bytes 393224 | tf_op jit(solution)/shard_map/ppermute | solution.py:418
  13.4 4.5 %collective-permute-start.6 = (bf16[2,128,256]{2,1,0:T(8,128)(2,1)S(1)}, bf16[2,128,256]{2,1,0:T(8,128)(2,1)S(1)}, u32[]{:S(2)}, u32[]{:S(2)}) collective-permute-start(bf16[2,128,256]{2,1,0:T(8,128)(2,1)S(1)} %get-tuple-element.53), channel_id=1, source_target_pairs={{0,4},{4,0},{8,12},{12,8},{16,20},{20,16},{24,28},{28,24},{1,5},{5... | collective-permute-start | bytes 393224 | tf_op jit(solution)/shard_map/ppermute | solution.py:418
  17.9 11.1 %collective-permute-start.14 = (bf16[528,256]{1,0:T(8,128)(2,1)S(1)}, bf16[528,256]{1,0:T(8,128)(2,1)S(1)}, u32[]{:S(2)}, u32[]{:S(2)}) collective-permute-start(bf16[528,256]{1,0:T(8,128)(2,1)S(1)} %get-tuple-element.64), channel_id=1, source_target_pairs={{0,4},{4,8},{8,12},{12,16},{16,20},{20,24},{24,28},{28,0},{1,5},{5... | collective-permute-start | bytes 811016 | tf_op jit(solution)/shard_map/ppermute | solution.py:414
  19.0 3.4 %collective-permute-start.7 = (bf16[2,128,256]{2,1,0:T(8,128)(2,1)S(1)}, bf16[2,128,256]{2,1,0:T(8,128)(2,1)S(1)}, u32[]{:S(2)}, u32[]{:S(2)}) collective-permute-start(bf16[2,128,256]{2,1,0:T(8,128)(2,1)S(1)} %get-tuple-element.55), channel_id=1, source_target_pairs={{0,4},{4,0},{8,12},{12,8},{16,20},{20,16},{24,28},{28,24},{1,5},{5... | collective-permute-start | bytes 393224 | tf_op jit(solution)/shard_map/ppermute | solution.py:418
  19.1 6.2 %collective-permute-start.9 = (bf16[272,256]{1,0:T(8,128)(2,1)S(1)}, bf16[272,256]{1,0:T(8,128)(2,1)S(1)}, u32[]{:S(2)}, u32[]{:S(2)}) collective-permute-start(bf16[272,256]{1,0:T(8,128)(2,1)S(1)} %get-tuple-element.57), channel_id=1, source_target_pairs={{0,5},{1,4},{2,7},{3,6},{4,0},{5,1},{6,2},{7,3},{8,13},{9,12},{10,... | collective-permute-start | bytes 417800 | tf_op jit(solution)/shard_map/ppermute | solution.py:379
  22.0 3.4 %collective-permute-start.10 = (bf16[272,256]{1,0:T(8,128)(2,1)S(1)}, bf16[272,256]{1,0:T(8,128)(2,1)S(1)}, u32[]{:S(2)}, u32[]{:S(2)}) collective-permute-start(bf16[272,256]{1,0:T(8,128)(2,1)S(1)} %get-tuple-element.58), channel_id=1, source_target_pairs={{0,4},{1,6},{2,5},{3,7},{4,0},{5,1},{6,2},{7,3},{8,12},{9,14},{10,... | collective-permute-start | bytes 417800 | tf_op jit(solution)/shard_map/ppermute | solution.py:379
  22.0 1.5 %collective-permute-start.8 = (bf16[2,128,256]{2,1,0:T(8,128)(2,1)S(1)}, bf16[2,128,256]{2,1,0:T(8,128)(2,1)S(1)}, u32[]{:S(2)}, u32[]{:S(2)}) collective-permute-start(bf16[2,128,256]{2,1,0:T(8,128)(2,1)S(1)} %get-tuple-element.56), channel_id=1, source_target_pairs={{0,4},{4,0},{8,12},{12,8},{16,20},{20,16},{24,28},{28,24},{1,5},{5... | collective-permute-start | bytes 393224 | tf_op jit(solution)/shard_map/ppermute | solution.py:418
  22.5 6.2 %collective-permute-start.15 = (bf16[256,256]{1,0:T(8,128)(2,1)S(1)}, bf16[256,256]{1,0:T(8,128)(2,1)S(1)}, u32[]{:S(2)}, u32[]{:S(2)}) collective-permute-start(bf16[256,256]{1,0:T(8,128)(2,1)S(1)} %get-tuple-element.65), channel_id=1, source_target_pairs={{0,4},{1,5},{2,6},{3,7},{4,9},{5,8},{6,11},{7,10},{8,12},{9,13},{1... | collective-permute-start | bytes 393224 | tf_op jit(solution)/shard_map/ppermute | solution.py:379
  23.5 5.5 %collective-permute-start.16 = (bf16[256,256]{1,0:T(8,128)(2,1)S(1)}, bf16[256,256]{1,0:T(8,128)(2,1)S(1)}, u32[]{:S(2)}, u32[]{:S(2)}) collective-permute-start(bf16[256,256]{1,0:T(8,128)(2,1)S(1)} %get-tuple-element.66), channel_id=1, source_target_pairs={{0,4},{1,5},{2,6},{3,7},{4,0},{5,10},{6,9},{7,3},{8,12},{9,13},{10... | collective-permute-start | bytes 393224 | tf_op jit(solution)/shard_map/ppermute | solution.py:379
  25.4 10.7 %collective-permute-start.11 = (bf16[512,256]{1,0:T(8,128)(2,1)S(1)}, bf16[512,256]{1,0:T(8,128)(2,1)S(1)}, u32[]{:S(2)}, u32[]{:S(2)}) collective-permute-start(bf16[512,256]{1,0:T(8,128)(2,1)S(1)} %get-tuple-element.59), channel_id=1, source_target_pairs={{0,4},{4,8},{8,12},{12,16},{16,20},{20,24},{24,28},{28,0},{1,5},{5... | collective-permute-start | bytes 786440 | tf_op jit(solution)/shard_map/ppermute | solution.py:414
  26.2 9.8 %collective-permute-start.12 = (bf16[272,256]{1,0:T(8,128)(2,1)S(1)}, bf16[272,256]{1,0:T(8,128)(2,1)S(1)}, u32[]{:S(2)}, u32[]{:S(2)}) collective-permute-start(bf16[272,256]{1,0:T(8,128)(2,1)S(1)} %get-tuple-element.60), channel_id=1, source_target_pairs={{0,4},{1,5},{2,6},{3,7},{4,9},{5,8},{6,11},{7,10},{8,12},{9,13},{1... | collective-permute-start | bytes 417800 | tf_op jit(solution)/shard_map/ppermute | solution.py:379
  28.7 7.4 %collective-permute-start.13 = (bf16[272,256]{1,0:T(8,128)(2,1)S(1)}, bf16[272,256]{1,0:T(8,128)(2,1)S(1)}, u32[]{:S(2)}, u32[]{:S(2)}) collective-permute-start(bf16[272,256]{1,0:T(8,128)(2,1)S(1)} %get-tuple-element.61), channel_id=1, source_target_pairs={{0,4},{1,5},{2,6},{3,7},{4,0},{5,10},{6,9},{7,3},{8,12},{9,13},{10... | collective-permute-start | bytes 417800 | tf_op jit(solution)/shard_map/ppermute | solution.py:379
  29.8 6.1 %collective-permute-start.17 = (bf16[256,256]{1,0:T(8,128)(2,1)S(1)}, bf16[256,256]{1,0:T(8,128)(2,1)S(1)}, u32[]{:S(2)}, u32[]{:S(2)}) collective-permute-start(bf16[256,256]{1,0:T(8,128)(2,1)S(1)} %get-tuple-element.70), channel_id=1, source_target_pairs={{0,5},{1,4},{2,7},{3,6},{4,0},{5,1},{6,2},{7,3},{8,13},{9,12},{10,... | collective-permute-start | bytes 393224 | tf_op jit(solution)/shard_map/ppermute | solution.py:379
  31.8 4.2 %collective-permute-start.18 = (bf16[256,256]{1,0:T(8,128)(2,1)S(1)}, bf16[256,256]{1,0:T(8,128)(2,1)S(1)}, u32[]{:S(2)}, u32[]{:S(2)}) collective-permute-start(bf16[256,256]{1,0:T(8,128)(2,1)S(1)} %get-tuple-element.71), channel_id=1, source_target_pairs={{0,4},{1,6},{2,5},{3,7},{4,0},{5,1},{6,2},{7,3},{8,12},{9,14},{10,... | collective-permute-start | bytes 393224 | tf_op jit(solution)/shard_map/ppermute | solution.py:379

commit v20 on v10

--- a/solution.py
+++ b/solution.py
@@ -23,8 +23,13 @@
     return pltpu.with_memory_space_constraint(array, pltpu.HBM)
 
 
-def write_lists(tile, plan_ref, blocks_ref, lists):
-    points = blocks_ref.shape[1]
+def block_of(ref, index, points):
+    if len(ref.shape) == 2:
+        return ref[pl.ds(pl.multiple_of(index * points, points), points)]
+    return ref[index]
+
+
+def write_lists(tile, plan_ref, blocks_ref, lists, points):
     listed = lists[0].shape[0] // points
     parity = lax.rem(tile, 2)
     for list_ref, side in zip(lists, (UPPER - parity, parity)):
@@ -34,14 +39,14 @@
 
             @pl.when(live)
             def _():
-                list_ref[slot * points : (slot + 1) * points] = blocks_ref[
-                    plan_ref[side * listed + slot]
-                ]
+                list_ref[slot * points : (slot + 1) * points] = block_of(
+                    blocks_ref, plan_ref[side * listed + slot], points
+                )
 
             @pl.when(jnp.logical_not(live))
             def _():
                 list_ref[slot * points : (slot + 1) * points] = jnp.zeros(
-                    blocks_ref.shape[1:], list_ref.dtype
+                    (points, list_ref.shape[1]), list_ref.dtype
                 )
 
 
@@ -49,7 +54,7 @@
     ids_hbm, count_hbm, pattern_hbm, inflow_hbm, plan_ref, wave_ref, first_ref, second_ref,
     ids, count, pattern, landed, small_sems, sems,
 ):
-    blocks = wave_ref.shape[0]
+    blocks, points = wave_ref.shape[:2]
     small = [
         pltpu.make_async_copy(source, target, small_sems.at[i])
         for i, (source, target) in enumerate(
@@ -75,7 +80,7 @@
     for b, copy in enumerate(large):
         copy.wait()
         wave_ref[b] = landed[b].astype(wave_ref.dtype)
-    write_lists(lax.axis_index("lat"), plan_ref, wave_ref, (first_ref, second_ref))
+    write_lists(lax.axis_index("lat"), plan_ref, wave_ref, (first_ref, second_ref), points)
 
 
 def load_kernel(
@@ -161,6 +166,27 @@
     return lax.rem(section, 2) == parity
 
 
+def wave_of(onward_refs, onward):
+    if len(onward_refs) > 1:
+        return onward
+    ref = onward_refs[0]
+    return ref.at[1] if len(ref.shape) == 4 else ref
+
+
+def targets_of(onward_refs, onward, b):
+    whole = wave_of(onward_refs, onward)
+    points = onward.shape[1]
+    if len(whole.shape) == 2:
+        return [whole.at[pl.ds(b * points, points)]]
+    targets = [whole.at[b]]
+    start = 0
+    for ref in onward_refs if len(onward_refs) > 1 else []:
+        if start <= b < start + ref.shape[0]:
+            targets.append(ref.at[b - start])
+        start += ref.shape[0]
+    return targets
+
+
 def tick_kernel(
     parity, tick, sections, plan_ref, ops_ref, source_ref, pass_ref, reflect_ref,
     wave_refs, first_in_ref, second_in_ref, known_refs, out_refs, buffer, onward,
@@ -169,6 +195,7 @@
     echo_ref, first_ref, second_ref, *onward_refs = out_refs
     section = lax.axis_index("depth")
     tile = lax.axis_index("lat")
+    points = onward.shape[1]
     listed = ids_of(plan_ref, ops_ref)
 
     @pl.when(acts(section, parity))
@@ -178,25 +205,17 @@
             parts = extrapolate_block(plan_ref, 2 * (listed + 1), ops_ref, buffer, b)
             for i, part in enumerate(parts):
                 cols = pl.ds(i * part.shape[1], part.shape[1])
-                onward[b, :, cols] = (pass_ref[b] * part).astype(onward.dtype)
+                leaving = (pass_ref[b] * part).astype(onward.dtype)
+                for target in targets_of(onward_refs, onward, b):
+                    target[:, cols] = leaving
                 echo_ref[b, :, cols] = (reflect_ref[b] * part).astype(echo_ref.dtype)
-        start = 0
-        for onward_ref in onward_refs:
-            if len(onward_ref.shape) == 2:
-                rows = onward.shape[0] * onward.shape[1]
-                onward_ref[:rows] = onward[...].reshape(rows, onward.shape[2])
-            else:
-                slot = onward_ref if len(onward_ref.shape) == 3 else onward_ref.at[1]
-                slot[...] = onward[start : start + slot.shape[0]]
-                start += slot.shape[0]
-
         @pl.when(section != sections - 1)
         def _():
-            write_lists(tile, plan_ref, onward, (first_ref, second_ref))
+            write_lists(tile, plan_ref, wave_of(onward_refs, onward), (first_ref, second_ref), points)
 
         @pl.when(section == sections - 1)
         def _():
-            write_lists(tile, plan_ref, source_ref.at[tick], (first_ref, second_ref))
+            write_lists(tile, plan_ref, source_ref.at[tick], (first_ref, second_ref), points)
 
 
 def last_kernel(

time: 37.8 us -> 37.8 us (level)
  no operation moved by 1% of the time
where the time goes in v20:
time: 37.8 us; the launch traced here: 37.6 us
  starting transfers between devices  17 us (45%)
  waiting for transfers between devices  8.92 us (24%)
  Pallas kernels  6.72 us (18%)
  blocking collectives  4.15 us (11%)
  between operations  0.75 us (2%)
    ppermute x10, starting transfers between devices, exchange(): return [lax.ppermute(a, both, route) for a, route in zip(lists, routes)]  10.1 us
    ppermute x10, waiting for transfers between devices, exchange(): return [lax.ppermute(a, both, route) for a, route in zip(lists, routes)]  6.35 us
    ppermute x1, starting transfers between devices, per_device(): first = lax.ppermute(first, both, routes[0])  4.15 us
    all_to_all x1, blocking collectives, per_device(): lax.all_to_all(onward[0], 'depth', 0, 0, axis_index_groups=pairs)  4.15 us
    pallas_call x8, Pallas kernels, grouped_call(): pl.pallas_call(body, out_shape=tuple(outs), in_specs=[SMEM_SPEC] + [VMEM_...  3.84 us
    pallas_call x1, Pallas kernels, per_device(): pl.pallas_call(load_kernel, out_shape=(pltpu.VMEM(operators.shape, operat...  1.67 us
    ppermute x1, waiting for transfers between devices, per_device(): first = lax.ppermute(first, both, routes[0])  1.52 us
    pallas_call x1, Pallas kernels, per_device(): pl.pallas_call(prepare_kernel, out_shape=(pltpu.SMEM((2 * (listed + 1) +...  1.21 us
  transfers between devices with their start and end apart: 19, of which 4 were waited for; matrix products, arithmetic and copies ran while one was open for 0% of the time, Pallas kernels for 11%

profile of v20, /device:TPU:0, one launch (start us, length us, event | category | flops | bytes accessed | tf_op | source)
XLA Modules:
  0.0 37.6 jit_solution(5682964520993255346)
XLA Ops:
  0.6 1.2 %prepare.1 = (s32[30]{0:T(128)S(4)}, bf16[4,128,256]{2,1,0:T(8,128)(2,1)S(1)}, bf16[256,256]{1,0:T(8,128)(2,1)S(1)}, bf16[256,256]{1,0:T(8,128)(2,1)S(1)}) custom-call(s32[1,2,2]{2,1,0:T(2,128)} %ids_hbm.1, s32[1,2]{1,0:T(1,128)} %count_hbm.1, s32[4,6]{1,0:T(4,128)} %pattern_hbm.1, f32[1,4,128,256]{3,2,1,0:T(8,128)} %inflow_hbm.1), custom_call_target="tpu_custom_call" | custom-call | flops 131072 | bytes 1048576 | tf_op jit(solution)/shard_map/prepare/pallas_call | solution.py:326
  1.8 0.5 %collective-permute-start.1 = (bf16[256,256]{1,0:T(8,128)(2,1)S(1)}, bf16[256,256]{1,0:T(8,128)(2,1)S(1)}, u32[]{:S(2)}, u32[]{:S(2)}) collective-permute-start(bf16[256,256]{1,0:T(8,128)(2,1)S(1)} %get-tuple-element.45), channel_id=1, source_target_pairs={{0,4},{1,2},{2,1},{3,7},{4,0},{5,6},{6,5},{7,3},{8,12},{9,10},{10,... | collective-permute-start | bytes 393224 | tf_op jit(solution)/shard_map/ppermute | solution.py:353
  2.4 4.2 %collective-permute-start = (bf16[256,256]{1,0:T(8,128)(2,1)S(1)}, bf16[256,256]{1,0:T(8,128)(2,1)S(1)}, u32[]{:S(2)}, u32[]{:S(2)}) collective-permute-start(bf16[256,256]{1,0:T(8,128)(2,1)S(1)} %get-tuple-element.39.after_ref), channel_id=1, source_target_pairs={{0,1},{1,0},{2,3},{3,2},{4,5},{5,4},{6,7},{7,6},{8,9},{9,8},{10,11... | collective-permute-start | bytes 393224 | tf_op jit(solution)/shard_map/ppermute | solution.py:352
  6.5 1.7 %load.1 = (bf16[1,4,6,2,128,128]{5,4,3,2,1,0:T(8,128)(2,1)S(1)}, bf16[3,4,128,256]{3,2,1,0:T(8,128)(2,1)S(1)}, f32[4,128,128]{2,1,0:T(8,128)S(1)}, f32[4,128,128]{2,1,0:T(8,128)S(1)}) custom-call(bf16[1,4,6,2,128,128]{5,4,3,2,1,0:T(8,128)(2,1)} %ops_hbm.1, bf16[3,4,128,256]{3,2,1,0:T(8,128)(2,1)} %source_hbm.1, f32[1,4,128]{2,1,0:T(4,128)} %pass_hbm.1, ...), custom_call_target="tpu_custom_call" | custom-call | bytes 4718592 | tf_op jit(solution)/shard_map/load/pallas_call | solution.py:356
  8.2 0.0 collective-permute-done.1.refs_7_
  8.2 1.5 %collective-permute-done.refs_6_ = bf16[256,256]{1,0:T(8,128)(2,1)S(1)} collective-permute-done((bf16[256,256]{1,0:T(8,128)(2,1)S(1)}, bf16[256,256]{1,0:T(8,128)(2,1)S(1)}, u32[]{:S(2)}, u32[]{:S(2)}) %collective-permute-start) | collective-permute-done | bytes 131104 | tf_op jit(solution)/shard_map/ppermute | solution.py:352
  9.7 0.0 collective-permute-start.2
  9.7 0.7 %tick0_even.1 = (bf16[4,128,256]{2,1,0:T(8,128)(2,1)S(1)}, bf16[256,256]{1,0:T(8,128)(2,1)S(1)}, bf16[256,256]{1,0:T(8,128)(2,1)S(1)}, bf16[2,128,256]{2,1,0:T(8,128)(2,1)S(1)}, bf16[2,128,256]{2,1,0:T(8,128)(2,1)S(1)}) custom-call(s32[30]{0:T(128)S(4)} %get-tuple-element.38.refs_0_, ...), custom_call_target="tpu_custom_call", output_to_operand_aliasing={{0}: (8, {}), {1}: (9, {}), {2}: (10, {})} | custom-call | tf_op jit(solution)/shard_map/tick0_even/pallas_call | solution.py:265
  10.5 2.2 %collective-permute-start.3 = (bf16[256,256]{1,0:T(8,128)(2,1)S(1)}, bf16[256,256]{1,0:T(8,128)(2,1)S(1)}, u32[]{:S(2)}, u32[]{:S(2)}) collective-permute-start(bf16[256,256]{1,0:T(8,128)(2,1)S(1)} %get-tuple-element.50), channel_id=1, source_target_pairs={{0,5},{1,4},{2,7},{3,6},{4,9},{5,8},{6,11},{7,10},{8,13},{9,12},{1... | collective-permute-start | bytes 393224 | tf_op jit(solution)/shard_map/ppermute | solution.py:394
  12.7 0.6 %collective-permute-start.4 = (bf16[256,256]{1,0:T(8,128)(2,1)S(1)}, bf16[256,256]{1,0:T(8,128)(2,1)S(1)}, u32[]{:S(2)}, u32[]{:S(2)}) collective-permute-start(bf16[256,256]{1,0:T(8,128)(2,1)S(1)} %get-tuple-element.51), channel_id=1, source_target_pairs={{0,4},{1,6},{2,5},{3,7},{4,0},{5,10},{6,9},{7,3},{8,12},{9,14},{10... | collective-permute-start | bytes 393224 | tf_op jit(solution)/shard_map/ppermute | solution.py:394
  13.3 0.0 collective-permute-start.5
  13.3 0.5 %collective-permute-start.6 = (bf16[2,128,256]{2,1,0:T(8,128)(2,1)S(1)}, bf16[2,128,256]{2,1,0:T(8,128)(2,1)S(1)}, u32[]{:S(2)}, u32[]{:S(2)}) collective-permute-start(bf16[2,128,256]{2,1,0:T(8,128)(2,1)S(1)} %get-tuple-element.53), channel_id=1, source_target_pairs={{0,4},{4,0},{8,12},{12,8},{16,20},{20,16},{24,28},{28,24},{1,5},{5... | collective-permute-start | bytes 393224 | tf_op jit(solution)/shard_map/ppermute | solution.py:433
  13.8 4.0 %collective-permute-done.3.refs_7_.refs_6_ = bf16[256,256]{1,0:T(8,128)(2,1)S(1)} collective-permute-done((bf16[256,256]{1,0:T(8,128)(2,1)S(1)}, bf16[256,256]{1,0:T(8,128)(2,1)S(1)}, u32[]{:S(2)}, u32[]{:S(2)}) %collective-permute-start.3) | collective-permute-done | bytes 131104 | tf_op jit(solution)/shard_map/ppermute | solution.py:394
  17.8 0.0 collective-permute-done.4.refs_8_.refs_7_
  17.8 0.0 collective-permute-done.5.refs_5_
  17.8 0.0 collective-permute-done.6.refs_6_
  17.9 0.3 collective-permute-start.14
  18.2 0.0 collective-permute-done.2.refs_5_
  18.2 0.7 %tick1_even.1 = (bf16[4,128,256]{2,1,0:T(8,128)(2,1)S(1)}, bf16[272,256]{1,0:T(8,128)(2,1)S(1)}, bf16[272,256]{1,0:T(8,128)(2,1)S(1)}, bf16[2,128,256]{2,1,0:T(8,128)(2,1)S(1)}, bf16[2,128,256]{2,1,0:T(8,128)(2,1)S(1)}) custom-call(s32[30]{0:T(128)S(4)} %get-tuple-element.38.refs_0_, ...), custom_call_target="tpu_custom_call", output_to_operand_aliasing={{0}: (8, {})} | custom-call | tf_op jit(solution)/shard_map/tick1_even/pallas_call | solution.py:265
  18.9 0.1 collective-permute-start.7
  19.0 2.9 %collective-permute-start.9 = (bf16[272,256]{1,0:T(8,128)(2,1)S(1)}, bf16[272,256]{1,0:T(8,128)(2,1)S(1)}, u32[]{:S(2)}, u32[]{:S(2)}) collective-permute-start(bf16[272,256]{1,0:T(8,128)(2,1)S(1)} %get-tuple-element.57), channel_id=1, source_target_pairs={{0,5},{1,4},{2,7},{3,6},{4,0},{5,1},{6,2},{7,3},{8,13},{9,12},{10,... | collective-permute-start | bytes 417800 | tf_op jit(solution)/shard_map/ppermute | solution.py:394
  21.9 0.0 collective-permute-start.10
  21.9 0.5 %collective-permute-start.8 = (bf16[2,128,256]{2,1,0:T(8,128)(2,1)S(1)}, bf16[2,128,256]{2,1,0:T(8,128)(2,1)S(1)}, u32[]{:S(2)}, u32[]{:S(2)}) collective-permute-start(bf16[2,128,256]{2,1,0:T(8,128)(2,1)S(1)} %get-tuple-element.56), channel_id=1, source_target_pairs={{0,4},{4,0},{8,12},{12,8},{16,20},{20,16},{24,28},{28,24},{1,5},{5... | collective-permute-start | bytes 393224 | tf_op jit(solution)/shard_map/ppermute | solution.py:433
  22.4 0.0 collective-permute-done.7.refs_5_
  22.4 0.0 collective-permute-start.15
  22.4 1.0 %collective-permute-done.8.refs_6_ = bf16[2,128,256]{2,1,0:T(8,128)(2,1)S(1)} collective-permute-done((bf16[2,128,256]{2,1,0:T(8,128)(2,1)S(1)}, bf16[2,128,256]{2,1,0:T(8,128)(2,1)S(1)}, u32[]{:S(2)}, u32[]{:S(2)}) %collective-permute-start.8) | collective-permute-done | bytes 131104 | tf_op jit(solution)/shard_map/ppermute | solution.py:433
  23.5 1.9 %collective-permute-start.16 = (bf16[256,256]{1,0:T(8,128)(2,1)S(1)}, bf16[256,256]{1,0:T(8,128)(2,1)S(1)}, u32[]{:S(2)}, u32[]{:S(2)}) collective-permute-start(bf16[256,256]{1,0:T(8,128)(2,1)S(1)} %get-tuple-element.66), channel_id=1, source_target_pairs={{0,4},{1,5},{2,6},{3,7},{4,0},{5,10},{6,9},{7,3},{8,12},{9,13},{10... | collective-permute-start | bytes 393224 | tf_op jit(solution)/shard_map/ppermute | solution.py:394
  25.4 0.0 collective-permute-done.9.refs_7_
  25.4 0.0 collective-permute-done.10.refs_8_
  25.4 0.8 %collective-permute-start.11 = (bf16[512,256]{1,0:T(8,128)(2,1)S(1)}, bf16[512,256]{1,0:T(8,128)(2,1)S(1)}, u32[]{:S(2)}, u32[]{:S(2)}) collective-permute-start(bf16[512,256]{1,0:T(8,128)(2,1)S(1)} %get-tuple-element.59), channel_id=1, source_target_pairs={{0,4},{4,8},{8,12},{12,16},{16,20},{20,24},{24,28},{28,0},{1,5},{5... | collective-permute-start | bytes 786440 | tf_op jit(solution)/shard_map/ppermute | solution.py:429
  26.2 0.1 collective-permute-start.12
  26.3 2.4 %collective-permute-done.15.refs_6_ = bf16[256,256]{1,0:T(8,128)(2,1)S(1)} collective-permute-done((bf16[256,256]{1,0:T(8,128)(2,1)S(1)}, bf16[256,256]{1,0:T(8,128)(2,1)S(1)}, u32[]{:S(2)}, u32[]{:S(2)}) %collective-permute-start.15) | collective-permute-done | bytes 131104 | tf_op jit(solution)/shard_map/ppermute | solution.py:394
  28.6 0.3 collective-permute-start.13
  29.0 0.0 collective-permute-done.16.refs_7_
  29.0 0.0 collective-permute-done.14.refs_5_
  29.0 0.7 %tick2_even.1 = (bf16[4,128,256]{2,1,0:T(8,128)(2,1)S(1)}, bf16[256,256]{1,0:T(8,128)(2,1)S(1)}, bf16[256,256]{1,0:T(8,128)(2,1)S(1)}, bf16[2,4,128,256]{3,2,1,0:T(8,128)(2,1)S(1)}) custom-call(s32[30]{0:T(128)S(4)} %get-tuple-element.38.refs_0_, bf16[1,4,6,2,128,128]{5,4,3,2,1,0:T(8,128)(2,1)S(1)} %get-tuple-element.40.refs_1_, ...), custom_call_target="tpu_custom_call", output_to_operand_aliasing={{0}: (8, {})} | custom-call | tf_op jit(solution)/shard_map/tick2_even/pallas_call | solution.py:265
  29.7 2.1 %collective-permute-start.17 = (bf16[256,256]{1,0:T(8,128)(2,1)S(1)}, bf16[256,256]{1,0:T(8,128)(2,1)S(1)}, u32[]{:S(2)}, u32[]{:S(2)}) collective-permute-start(bf16[256,256]{1,0:T(8,128)(2,1)S(1)} %get-tuple-element.70), channel_id=1, source_target_pairs={{0,5},{1,4},{2,7},{3,6},{4,0},{5,1},{6,2},{7,3},{8,13},{9,12},{10,... | collective-permute-start | bytes 393224 | tf_op jit(solution)/shard_map/ppermute | solution.py:394
  31.8 0.0 collective-permute-start.18
  31.8 4.1 %all_to_all.5.refs_5_ = bf16[2,4,128,256]{3,2,1,0:T(8,128)(2,1)S(1)} all-to-all(bf16[2,4,128,256]{3,2,1,0:T(8,128)(2,1)S(1)} %get-tuple-element.69), channel_id=1, replica_groups={{0,4},{8,12},{16,20},{24,28},{1,5},{9,13},{17,21},{25,29},{2,6},{10,14}..., dimensions={0} | all-to-all | bytes 1048576 | tf_op jit(solution)/shard_map/all_to_all | solution.py:431
  35.9 0.0 collective-permute-done.17.refs_6_
  35.9 0.0 collective-permute-done.18.refs_7_
  35.9 0.1 last_tick_odd.1
  36.0 0.0 collective-permute-done.12.refs_6_
  36.0 0.0 collective-permute-done.13.refs_7_
  36.0 0.0 collective-permute-done.11.refs_5_
  36.1 1.5 %last_tick_even.1 = (bf16[4,1,4,128,256]{4,3,2,1,0:T(8,128)(2,1)}, f32[1,4,128,256]{3,2,1,0:T(8,128)}) custom-call(s32[30]{0:T(128)S(4)} %get-tuple-element.38.refs_0_, bf16[1,4,6,2,128,128]{5,4,3,2,1,0:T(8,128)(2,1)S(1)} %get-tuple-element.40.refs_1_, ...), custom_call_target="tpu_custom_call", output_to_operand_aliasing={{0}: (11, {}), {1}: (12, {})} | custom-call | tf_op jit(solution)/shard_map/last_tick_even/pallas_call | solution.py:265
  (3 shorter events, 0.0 us)
Async XLA Ops:
  1.8 6.4 %collective-permute-start.1 = (bf16[256,256]{1,0:T(8,128)(2,1)S(1)}, bf16[256,256]{1,0:T(8,128)(2,1)S(1)}, u32[]{:S(2)}, u32[]{:S(2)}) collective-permute-start(bf16[256,256]{1,0:T(8,128)(2,1)S(1)} %get-tuple-element.45), channel_id=1, source_target_pairs={{0,4},{1,2},{2,1},{3,7},{4,0},{5,6},{6,5},{7,3},{8,12},{9,10},{10,... | collective-permute-start | bytes 393224 | tf_op jit(solution)/shard_map/ppermute | solution.py:353
  2.4 7.4 %collective-permute-start = (bf16[256,256]{1,0:T(8,128)(2,1)S(1)}, bf16[256,256]{1,0:T(8,128)(2,1)S(1)}, u32[]{:S(2)}, u32[]{:S(2)}) collective-permute-start(bf16[256,256]{1,0:T(8,128)(2,1)S(1)} %get-tuple-element.39.after_ref), channel_id=1, source_target_pairs={{0,1},{1,0},{2,3},{3,2},{4,5},{5,4},{6,7},{7,6},{8,9},{9,8},{10,11... | collective-permute-start | bytes 393224 | tf_op jit(solution)/shard_map/ppermute | solution.py:352
  9.7 8.5 %collective-permute-start.2 = (bf16[512,256]{1,0:T(8,128)(2,1)S(1)}, bf16[512,256]{1,0:T(8,128)(2,1)S(1)}, u32[]{:S(2)}, u32[]{:S(2)}) collective-permute-start(bf16[512,256]{1,0:T(8,128)(2,1)S(1)} %get-tuple-element.46), channel_id=1, source_target_pairs={{0,4},{4,8},{8,12},{12,16},{16,20},{20,24},{24,28},{28,0},{1,5},{5... | collective-permute-start | bytes 786440 | tf_op jit(solution)/shard_map/ppermute | solution.py:429
  10.5 7.3 %collective-permute-start.3 = (bf16[256,256]{1,0:T(8,128)(2,1)S(1)}, bf16[256,256]{1,0:T(8,128)(2,1)S(1)}, u32[]{:S(2)}, u32[]{:S(2)}) collective-permute-start(bf16[256,256]{1,0:T(8,128)(2,1)S(1)} %get-tuple-element.50), channel_id=1, source_target_pairs={{0,5},{1,4},{2,7},{3,6},{4,9},{5,8},{6,11},{7,10},{8,13},{9,12},{1... | collective-permute-start | bytes 393224 | tf_op jit(solution)/shard_map/ppermute | solution.py:394
  12.7 5.1 %collective-permute-start.4 = (bf16[256,256]{1,0:T(8,128)(2,1)S(1)}, bf16[256,256]{1,0:T(8,128)(2,1)S(1)}, u32[]{:S(2)}, u32[]{:S(2)}) collective-permute-start(bf16[256,256]{1,0:T(8,128)(2,1)S(1)} %get-tuple-element.51), channel_id=1, source_target_pairs={{0,4},{1,6},{2,5},{3,7},{4,0},{5,10},{6,9},{7,3},{8,12},{9,14},{10... | collective-permute-start | bytes 393224 | tf_op jit(solution)/shard_map/ppermute | solution.py:394
  13.3 4.5 %collective-permute-start.5 = (bf16[2,128,256]{2,1,0:T(8,128)(2,1)S(1)}, bf16[2,128,256]{2,1,0:T(8,128)(2,1)S(1)}, u32[]{:S(2)}, u32[]{:S(2)}) collective-permute-start(bf16[2,128,256]{2,1,0:T(8,128)(2,1)S(1)} %get-tuple-element.52), channel_id=1, source_target_pairs={{0,4},{4,0},{8,12},{12,8},{16,20},{20,16},{24,28},{28,24},{1,5},{5... | collective-permute-start | bytes 393224 | tf_op jit(solution)/shard_map/ppermute | solution.py:433
  13.3 4.5 %collective-permute-start.6 = (bf16[2,128,256]{2,1,0:T(8,128)(2,1)S(1)}, bf16[2,128,256]{2,1,0:T(8,128)(2,1)S(1)}, u32[]{:S(2)}, u32[]{:S(2)}) collective-permute-start(bf16[2,128,256]{2,1,0:T(8,128)(2,1)S(1)} %get-tuple-element.53), channel_id=1, source_target_pairs={{0,4},{4,0},{8,12},{12,8},{16,20},{20,16},{24,28},{28,24},{1,5},{5... | collective-permute-start | bytes 393224 | tf_op jit(solution)/shard_map/ppermute | solution.py:433
  17.9 11.1 %collective-permute-start.14 = (bf16[528,256]{1,0:T(8,128)(2,1)S(1)}, bf16[528,256]{1,0:T(8,128)(2,1)S(1)}, u32[]{:S(2)}, u32[]{:S(2)}) collective-permute-start(bf16[528,256]{1,0:T(8,128)(2,1)S(1)} %get-tuple-element.64), channel_id=1, source_target_pairs={{0,4},{4,8},{8,12},{12,16},{16,20},{20,24},{24,28},{28,0},{1,5},{5... | collective-permute-start | bytes 811016 | tf_op jit(solution)/shard_map/ppermute | solution.py:429
  18.9 3.5 %collective-permute-start.7 = (bf16[2,128,256]{2,1,0:T(8,128)(2,1)S(1)}, bf16[2,128,256]{2,1,0:T(8,128)(2,1)S(1)}, u32[]{:S(2)}, u32[]{:S(2)}) collective-permute-start(bf16[2,128,256]{2,1,0:T(8,128)(2,1)S(1)} %get-tuple-element.55), channel_id=1, source_target_pairs={{0,4},{4,0},{8,12},{12,8},{16,20},{20,16},{24,28},{28,24},{1,5},{5... | collective-permute-start | bytes 393224 | tf_op jit(solution)/shard_map/ppermute | solution.py:433
  19.0 6.3 %collective-permute-start.9 = (bf16[272,256]{1,0:T(8,128)(2,1)S(1)}, bf16[272,256]{1,0:T(8,128)(2,1)S(1)}, u32[]{:S(2)}, u32[]{:S(2)}) collective-permute-start(bf16[272,256]{1,0:T(8,128)(2,1)S(1)} %get-tuple-element.57), channel_id=1, source_target_pairs={{0,5},{1,4},{2,7},{3,6},{4,0},{5,1},{6,2},{7,3},{8,13},{9,12},{10,... | collective-permute-start | bytes 417800 | tf_op jit(solution)/shard_map/ppermute | solution.py:394
  21.9 3.4 %collective-permute-start.10 = (bf16[272,256]{1,0:T(8,128)(2,1)S(1)}, bf16[272,256]{1,0:T(8,128)(2,1)S(1)}, u32[]{:S(2)}, u32[]{:S(2)}) collective-permute-start(bf16[272,256]{1,0:T(8,128)(2,1)S(1)} %get-tuple-element.58), channel_id=1, source_target_pairs={{0,4},{1,6},{2,5},{3,7},{4,0},{5,1},{6,2},{7,3},{8,12},{9,14},{10,... | collective-permute-start | bytes 417800 | tf_op jit(solution)/shard_map/ppermute | solution.py:394
  21.9 1.5 %collective-permute-start.8 = (bf16[2,128,256]{2,1,0:T(8,128)(2,1)S(1)}, bf16[2,128,256]{2,1,0:T(8,128)(2,1)S(1)}, u32[]{:S(2)}, u32[]{:S(2)}) collective-permute-start(bf16[2,128,256]{2,1,0:T(8,128)(2,1)S(1)} %get-tuple-element.56), channel_id=1, source_target_pairs={{0,4},{4,0},{8,12},{12,8},{16,20},{20,16},{24,28},{28,24},{1,5},{5... | collective-permute-start | bytes 393224 | tf_op jit(solution)/shard_map/ppermute | solution.py:433
  22.4 6.2 %collective-permute-start.15 = (bf16[256,256]{1,0:T(8,128)(2,1)S(1)}, bf16[256,256]{1,0:T(8,128)(2,1)S(1)}, u32[]{:S(2)}, u32[]{:S(2)}) collective-permute-start(bf16[256,256]{1,0:T(8,128)(2,1)S(1)} %get-tuple-element.65), channel_id=1, source_target_pairs={{0,4},{1,5},{2,6},{3,7},{4,9},{5,8},{6,11},{7,10},{8,12},{9,13},{1... | collective-permute-start | bytes 393224 | tf_op jit(solution)/shard_map/ppermute | solution.py:394
  23.5 5.5 %collective-permute-start.16 = (bf16[256,256]{1,0:T(8,128)(2,1)S(1)}, bf16[256,256]{1,0:T(8,128)(2,1)S(1)}, u32[]{:S(2)}, u32[]{:S(2)}) collective-permute-start(bf16[256,256]{1,0:T(8,128)(2,1)S(1)} %get-tuple-element.66), channel_id=1, source_target_pairs={{0,4},{1,5},{2,6},{3,7},{4,0},{5,10},{6,9},{7,3},{8,12},{9,13},{10... | collective-permute-start | bytes 393224 | tf_op jit(solution)/shard_map/ppermute | solution.py:394
  25.4 10.7 %collective-permute-start.11 = (bf16[512,256]{1,0:T(8,128)(2,1)S(1)}, bf16[512,256]{1,0:T(8,128)(2,1)S(1)}, u32[]{:S(2)}, u32[]{:S(2)}) collective-permute-start(bf16[512,256]{1,0:T(8,128)(2,1)S(1)} %get-tuple-element.59), channel_id=1, source_target_pairs={{0,4},{4,8},{8,12},{12,16},{16,20},{20,24},{24,28},{28,0},{1,5},{5... | collective-permute-start | bytes 786440 | tf_op jit(solution)/shard_map/ppermute | solution.py:429
  26.2 9.9 %collective-permute-start.12 = (bf16[272,256]{1,0:T(8,128)(2,1)S(1)}, bf16[272,256]{1,0:T(8,128)(2,1)S(1)}, u32[]{:S(2)}, u32[]{:S(2)}) collective-permute-start(bf16[272,256]{1,0:T(8,128)(2,1)S(1)} %get-tuple-element.60), channel_id=1, source_target_pairs={{0,4},{1,5},{2,6},{3,7},{4,9},{5,8},{6,11},{7,10},{8,12},{9,13},{1... | collective-permute-start | bytes 417800 | tf_op jit(solution)/shard_map/ppermute | solution.py:394
  28.6 7.4 %collective-permute-start.13 = (bf16[272,256]{1,0:T(8,128)(2,1)S(1)}, bf16[272,256]{1,0:T(8,128)(2,1)S(1)}, u32[]{:S(2)}, u32[]{:S(2)}) collective-permute-start(bf16[272,256]{1,0:T(8,128)(2,1)S(1)} %get-tuple-element.61), channel_id=1, source_target_pairs={{0,4},{1,5},{2,6},{3,7},{4,0},{5,10},{6,9},{7,3},{8,12},{9,13},{10... | collective-permute-start | bytes 417800 | tf_op jit(solution)/shard_map/ppermute | solution.py:394
  29.7 6.2 %collective-permute-start.17 = (bf16[256,256]{1,0:T(8,128)(2,1)S(1)}, bf16[256,256]{1,0:T(8,128)(2,1)S(1)}, u32[]{:S(2)}, u32[]{:S(2)}) collective-permute-start(bf16[256,256]{1,0:T(8,128)(2,1)S(1)} %get-tuple-element.70), channel_id=1, source_target_pairs={{0,5},{1,4},{2,7},{3,6},{4,0},{5,1},{6,2},{7,3},{8,13},{9,12},{10,... | collective-permute-start | bytes 393224 | tf_op jit(solution)/shard_map/ppermute | solution.py:394
  31.8 4.2 %collective-permute-start.18 = (bf16[256,256]{1,0:T(8,128)(2,1)S(1)}, bf16[256,256]{1,0:T(8,128)(2,1)S(1)}, u32[]{:S(2)}, u32[]{:S(2)}) collective-permute-start(bf16[256,256]{1,0:T(8,128)(2,1)S(1)} %get-tuple-element.71), channel_id=1, source_target_pairs={{0,4},{1,6},{2,5},{3,7},{4,0},{5,1},{6,2},{7,3},{8,12},{9,14},{10,... | collective-permute-start | bytes 393224 | tf_op jit(solution)/shard_map/ppermute | solution.py:394

commit v21 on v20

--- a/solution.py
+++ b/solution.py
@@ -412,6 +412,8 @@
             else:
                 to_next = [pair_type] if last_step else half_types if first_step else part_types
             outs = [wave_type, *lists_of(extra), *to_next]
+            if first_step:
+                outs[2] = lists_of(16)[1]
             echo, *lists = grouped_call(
                 functools.partial(tick_kernel, parity, tick, sections),
                 [*fixed, *arrived[parity]],

time: 37.8 us -> 37 us (0.979)
  starting transfers between devices: 17 us -> 15.9 us
    ppermute x10, starting transfers between devices: 10.1 us -> 8.97 us  [exchange(): return [lax.ppermute(a, both, route) for a, route in zip(lists, routes)]]
where the time goes in v21:
time: 37 us; the launch traced here: 36.8 us
  starting transfers between devices  15.9 us (43%)
  waiting for transfers between devices  9.18 us (25%)
  Pallas kernels  6.72 us (18%)
  blocking collectives  4.15 us (11%)
  between operations  0.76 us (2%)
    ppermute x10, starting transfers between devices, exchange(): return [lax.ppermute(a, both, route) for a, route in zip(lists, routes)]  8.97 us
    ppermute x10, waiting for transfers between devices, exchange(): return [lax.ppermute(a, both, route) for a, route in zip(lists, routes)]  6.61 us
    all_to_all x1, blocking collectives, per_device(): lax.all_to_all(onward[0], 'depth', 0, 0, axis_index_groups=pairs)  4.15 us
    ppermute x1, starting transfers between devices, per_device(): first = lax.ppermute(first, both, routes[0])  4.15 us
    pallas_call x8, Pallas kernels, grouped_call(): pl.pallas_call(body, out_shape=tuple(outs), in_specs=[SMEM_SPEC] + [VMEM_...  3.84 us
    pallas_call x1, Pallas kernels, per_device(): pl.pallas_call(load_kernel, out_shape=(pltpu.VMEM(operators.shape, operat...  1.67 us
    ppermute x1, waiting for transfers between devices, per_device(): first = lax.ppermute(first, both, routes[0])  1.52 us
    ppermute x4, starting transfers between devices, per_device(): waves[ODD] = [lax.ppermute(a, 'depth', inside) for a in onward]  1.4 us
  transfers between devices with their start and end apart: 19, of which 4 were waited for; matrix products, arithmetic and copies ran while one was open for 0% of the time, Pallas kernels for 11%

profile of v21, /device:TPU:0, one launch (start us, length us, event | category | flops | bytes accessed | tf_op | source)
XLA Modules:
  0.0 36.8 jit_solution(13597589548180193600)
XLA Ops:
  0.6 1.2 %prepare.1 = (s32[30]{0:T(128)S(4)}, bf16[4,128,256]{2,1,0:T(8,128)(2,1)S(1)}, bf16[256,256]{1,0:T(8,128)(2,1)S(1)}, bf16[256,256]{1,0:T(8,128)(2,1)S(1)}) custom-call(s32[1,2,2]{2,1,0:T(2,128)} %ids_hbm.1, s32[1,2]{1,0:T(1,128)} %count_hbm.1, s32[4,6]{1,0:T(4,128)} %pattern_hbm.1, f32[1,4,128,256]{3,2,1,0:T(8,128)} %inflow_hbm.1), custom_call_target="tpu_custom_call" | custom-call | flops 131072 | bytes 1048576 | tf_op jit(solution)/shard_map/prepare/pallas_call | solution.py:326
  1.8 0.5 %collective-permute-start.1 = (bf16[256,256]{1,0:T(8,128)(2,1)S(1)}, bf16[256,256]{1,0:T(8,128)(2,1)S(1)}, u32[]{:S(2)}, u32[]{:S(2)}) collective-permute-start(bf16[256,256]{1,0:T(8,128)(2,1)S(1)} %get-tuple-element.45), channel_id=1, source_target_pairs={{0,4},{1,2},{2,1},{3,7},{4,0},{5,6},{6,5},{7,3},{8,12},{9,10},{10,... | collective-permute-start | bytes 393224 | tf_op jit(solution)/shard_map/ppermute | solution.py:353
  2.4 4.1 %collective-permute-start = (bf16[256,256]{1,0:T(8,128)(2,1)S(1)}, bf16[256,256]{1,0:T(8,128)(2,1)S(1)}, u32[]{:S(2)}, u32[]{:S(2)}) collective-permute-start(bf16[256,256]{1,0:T(8,128)(2,1)S(1)} %get-tuple-element.39.after_ref), channel_id=1, source_target_pairs={{0,1},{1,0},{2,3},{3,2},{4,5},{5,4},{6,7},{7,6},{8,9},{9,8},{10,11... | collective-permute-start | bytes 393224 | tf_op jit(solution)/shard_map/ppermute | solution.py:352
  6.5 1.7 %load.1 = (bf16[1,4,6,2,128,128]{5,4,3,2,1,0:T(8,128)(2,1)S(1)}, bf16[3,4,128,256]{3,2,1,0:T(8,128)(2,1)S(1)}, f32[4,128,128]{2,1,0:T(8,128)S(1)}, f32[4,128,128]{2,1,0:T(8,128)S(1)}) custom-call(bf16[1,4,6,2,128,128]{5,4,3,2,1,0:T(8,128)(2,1)} %ops_hbm.1, bf16[3,4,128,256]{3,2,1,0:T(8,128)(2,1)} %source_hbm.1, f32[1,4,128]{2,1,0:T(4,128)} %pass_hbm.1, ...), custom_call_target="tpu_custom_call" | custom-call | bytes 4718592 | tf_op jit(solution)/shard_map/load/pallas_call | solution.py:356
  8.2 0.0 collective-permute-done.1.refs_7_
  8.2 1.5 %collective-permute-done.refs_6_ = bf16[256,256]{1,0:T(8,128)(2,1)S(1)} collective-permute-done((bf16[256,256]{1,0:T(8,128)(2,1)S(1)}, bf16[256,256]{1,0:T(8,128)(2,1)S(1)}, u32[]{:S(2)}, u32[]{:S(2)}) %collective-permute-start) | collective-permute-done | bytes 131104 | tf_op jit(solution)/shard_map/ppermute | solution.py:352
  9.7 0.0 collective-permute-start.2
  9.7 0.7 %tick0_even.1 = (bf16[4,128,256]{2,1,0:T(8,128)(2,1)S(1)}, bf16[256,256]{1,0:T(8,128)(2,1)S(1)}, bf16[272,256]{1,0:T(8,128)(2,1)S(1)}, bf16[2,128,256]{2,1,0:T(8,128)(2,1)S(1)}, bf16[2,128,256]{2,1,0:T(8,128)(2,1)S(1)}) custom-call(s32[30]{0:T(128)S(4)} %get-tuple-element.38.refs_0_, ...), custom_call_target="tpu_custom_call", output_to_operand_aliasing={{0}: (8, {}), {1}: (9, {}), {2}: (10, {})} | custom-call | tf_op jit(solution)/shard_map/tick0_even/pallas_call | solution.py:265
  10.5 0.9 %collective-permute-start.4 = (bf16[272,256]{1,0:T(8,128)(2,1)S(1)}, bf16[272,256]{1,0:T(8,128)(2,1)S(1)}, u32[]{:S(2)}, u32[]{:S(2)}) collective-permute-start(bf16[272,256]{1,0:T(8,128)(2,1)S(1)} %get-tuple-element.51), channel_id=1, source_target_pairs={{0,4},{1,6},{2,5},{3,7},{4,0},{5,10},{6,9},{7,3},{8,12},{9,14},{10... | collective-permute-start | bytes 417800 | tf_op jit(solution)/shard_map/ppermute | solution.py:394
  11.3 2.4 %collective-permute-start.3 = (bf16[256,256]{1,0:T(8,128)(2,1)S(1)}, bf16[256,256]{1,0:T(8,128)(2,1)S(1)}, u32[]{:S(2)}, u32[]{:S(2)}) collective-permute-start(bf16[256,256]{1,0:T(8,128)(2,1)S(1)} %get-tuple-element.50), channel_id=1, source_target_pairs={{0,5},{1,4},{2,7},{3,6},{4,9},{5,8},{6,11},{7,10},{8,13},{9,12},{1... | collective-permute-start | bytes 393224 | tf_op jit(solution)/shard_map/ppermute | solution.py:394
  13.7 0.8 %collective-permute-start.5 = (bf16[2,128,256]{2,1,0:T(8,128)(2,1)S(1)}, bf16[2,128,256]{2,1,0:T(8,128)(2,1)S(1)}, u32[]{:S(2)}, u32[]{:S(2)}) collective-permute-start(bf16[2,128,256]{2,1,0:T(8,128)(2,1)S(1)} %get-tuple-element.52), channel_id=1, source_target_pairs={{0,4},{4,0},{8,12},{12,8},{16,20},{20,16},{24,28},{28,24},{1,5},{5... | collective-permute-start | bytes 393224 | tf_op jit(solution)/shard_map/ppermute | solution.py:435
  14.5 0.0 collective-permute-start.6
  14.5 4.4 %collective-permute-done.3.refs_7_.refs_6_ = bf16[256,256]{1,0:T(8,128)(2,1)S(1)} collective-permute-done((bf16[256,256]{1,0:T(8,128)(2,1)S(1)}, bf16[256,256]{1,0:T(8,128)(2,1)S(1)}, u32[]{:S(2)}, u32[]{:S(2)}) %collective-permute-start.3) | collective-permute-done | bytes 131104 | tf_op jit(solution)/shard_map/ppermute | solution.py:394
  18.9 0.0 collective-permute-done.5.refs_5_
  18.9 0.0 collective-permute-done.6.refs_6_
  18.9 0.0 collective-permute-done.4.refs_8_.refs_7_
  18.9 0.1 collective-permute-start.14
  19.0 0.0 collective-permute-done.2.refs_5_
  19.0 0.8 %tick1_even.1 = (bf16[4,128,256]{2,1,0:T(8,128)(2,1)S(1)}, bf16[272,256]{1,0:T(8,128)(2,1)S(1)}, bf16[272,256]{1,0:T(8,128)(2,1)S(1)}, bf16[2,128,256]{2,1,0:T(8,128)(2,1)S(1)}, bf16[2,128,256]{2,1,0:T(8,128)(2,1)S(1)}) custom-call(s32[30]{0:T(128)S(4)} %get-tuple-element.38.refs_0_, ...), custom_call_target="tpu_custom_call", output_to_operand_aliasing={{0}: (8, {})} | custom-call | tf_op jit(solution)/shard_map/tick1_even/pallas_call | solution.py:265
  19.8 0.1 collective-permute-start.7
  19.8 2.2 %collective-permute-start.9 = (bf16[272,256]{1,0:T(8,128)(2,1)S(1)}, bf16[272,256]{1,0:T(8,128)(2,1)S(1)}, u32[]{:S(2)}, u32[]{:S(2)}) collective-permute-start(bf16[272,256]{1,0:T(8,128)(2,1)S(1)} %get-tuple-element.57), channel_id=1, source_target_pairs={{0,5},{1,4},{2,7},{3,6},{4,0},{5,1},{6,2},{7,3},{8,13},{9,12},{10,... | collective-permute-start | bytes 417800 | tf_op jit(solution)/shard_map/ppermute | solution.py:394
  22.0 0.0 collective-permute-start.10
  22.0 0.5 %collective-permute-start.8 = (bf16[2,128,256]{2,1,0:T(8,128)(2,1)S(1)}, bf16[2,128,256]{2,1,0:T(8,128)(2,1)S(1)}, u32[]{:S(2)}, u32[]{:S(2)}) collective-permute-start(bf16[2,128,256]{2,1,0:T(8,128)(2,1)S(1)} %get-tuple-element.56), channel_id=1, source_target_pairs={{0,4},{4,0},{8,12},{12,8},{16,20},{20,16},{24,28},{28,24},{1,5},{5... | collective-permute-start | bytes 393224 | tf_op jit(solution)/shard_map/ppermute | solution.py:435
  22.5 0.0 collective-permute-done.7.refs_5_
  22.5 0.0 collective-permute-start.15
  22.5 1.0 %collective-permute-done.8.refs_6_ = bf16[2,128,256]{2,1,0:T(8,128)(2,1)S(1)} collective-permute-done((bf16[2,128,256]{2,1,0:T(8,128)(2,1)S(1)}, bf16[2,128,256]{2,1,0:T(8,128)(2,1)S(1)}, u32[]{:S(2)}, u32[]{:S(2)}) %collective-permute-start.8) | collective-permute-done | bytes 131104 | tf_op jit(solution)/shard_map/ppermute | solution.py:435
  23.6 1.5 %collective-permute-start.16 = (bf16[256,256]{1,0:T(8,128)(2,1)S(1)}, bf16[256,256]{1,0:T(8,128)(2,1)S(1)}, u32[]{:S(2)}, u32[]{:S(2)}) collective-permute-start(bf16[256,256]{1,0:T(8,128)(2,1)S(1)} %get-tuple-element.66), channel_id=1, source_target_pairs={{0,4},{1,5},{2,6},{3,7},{4,0},{5,10},{6,9},{7,3},{8,12},{9,13},{10... | collective-permute-start | bytes 393224 | tf_op jit(solution)/shard_map/ppermute | solution.py:394
  25.1 0.0 collective-permute-done.9.refs_7_
  25.1 0.0 collective-permute-done.10.refs_8_
  25.1 0.8 %collective-permute-start.11 = (bf16[512,256]{1,0:T(8,128)(2,1)S(1)}, bf16[512,256]{1,0:T(8,128)(2,1)S(1)}, u32[]{:S(2)}, u32[]{:S(2)}) collective-permute-start(bf16[512,256]{1,0:T(8,128)(2,1)S(1)} %get-tuple-element.59), channel_id=1, source_target_pairs={{0,4},{4,8},{8,12},{12,16},{16,20},{20,24},{24,28},{28,0},{1,5},{5... | collective-permute-start | bytes 786440 | tf_op jit(solution)/shard_map/ppermute | solution.py:431
  25.9 0.6 %collective-permute-start.12 = (bf16[272,256]{1,0:T(8,128)(2,1)S(1)}, bf16[272,256]{1,0:T(8,128)(2,1)S(1)}, u32[]{:S(2)}, u32[]{:S(2)}) collective-permute-start(bf16[272,256]{1,0:T(8,128)(2,1)S(1)} %get-tuple-element.60), channel_id=1, source_target_pairs={{0,4},{1,5},{2,6},{3,7},{4,9},{5,8},{6,11},{7,10},{8,12},{9,13},{1... | collective-permute-start | bytes 417800 | tf_op jit(solution)/shard_map/ppermute | solution.py:394
  26.5 2.2 %collective-permute-done.15.refs_6_ = bf16[256,256]{1,0:T(8,128)(2,1)S(1)} collective-permute-done((bf16[256,256]{1,0:T(8,128)(2,1)S(1)}, bf16[256,256]{1,0:T(8,128)(2,1)S(1)}, u32[]{:S(2)}, u32[]{:S(2)}) %collective-permute-start.15) | collective-permute-done | bytes 131104 | tf_op jit(solution)/shard_map/ppermute | solution.py:394
  28.7 0.8 %collective-permute-start.13 = (bf16[272,256]{1,0:T(8,128)(2,1)S(1)}, bf16[272,256]{1,0:T(8,128)(2,1)S(1)}, u32[]{:S(2)}, u32[]{:S(2)}) collective-permute-start(bf16[272,256]{1,0:T(8,128)(2,1)S(1)} %get-tuple-element.61), channel_id=1, source_target_pairs={{0,4},{1,5},{2,6},{3,7},{4,0},{5,10},{6,9},{7,3},{8,12},{9,13},{10... | collective-permute-start | bytes 417800 | tf_op jit(solution)/shard_map/ppermute | solution.py:394
  29.5 0.0 collective-permute-done.16.refs_7_
  29.5 0.0 collective-permute-done.14.refs_5_
  29.5 0.7 %tick2_even.1 = (bf16[4,128,256]{2,1,0:T(8,128)(2,1)S(1)}, bf16[256,256]{1,0:T(8,128)(2,1)S(1)}, bf16[256,256]{1,0:T(8,128)(2,1)S(1)}, bf16[2,4,128,256]{3,2,1,0:T(8,128)(2,1)S(1)}) custom-call(s32[30]{0:T(128)S(4)} %get-tuple-element.38.refs_0_, bf16[1,4,6,2,128,128]{5,4,3,2,1,0:T(8,128)(2,1)S(1)} %get-tuple-element.40.refs_1_, ...), custom_call_target="tpu_custom_call", output_to_operand_aliasing={{0}: (8, {})} | custom-call | tf_op jit(solution)/shard_map/tick2_even/pallas_call | solution.py:265
  30.2 0.7 %collective-permute-start.17 = (bf16[256,256]{1,0:T(8,128)(2,1)S(1)}, bf16[256,256]{1,0:T(8,128)(2,1)S(1)}, u32[]{:S(2)}, u32[]{:S(2)}) collective-permute-start(bf16[256,256]{1,0:T(8,128)(2,1)S(1)} %get-tuple-element.70), channel_id=1, source_target_pairs={{0,5},{1,4},{2,7},{3,6},{4,0},{5,1},{6,2},{7,3},{8,13},{9,12},{10,... | collective-permute-start | bytes 393224 | tf_op jit(solution)/shard_map/ppermute | solution.py:394
  30.9 0.0 collective-permute-start.18
  30.9 4.1 %all_to_all.5.refs_5_ = bf16[2,4,128,256]{3,2,1,0:T(8,128)(2,1)S(1)} all-to-all(bf16[2,4,128,256]{3,2,1,0:T(8,128)(2,1)S(1)} %get-tuple-element.69), channel_id=1, replica_groups={{0,4},{8,12},{16,20},{24,28},{1,5},{9,13},{17,21},{25,29},{2,6},{10,14}..., dimensions={0} | all-to-all | bytes 1048576 | tf_op jit(solution)/shard_map/all_to_all | solution.py:433
  35.1 0.0 collective-permute-done.17.refs_6_
  35.1 0.0 collective-permute-done.18.refs_7_
  35.1 0.1 last_tick_odd.1
  35.2 0.0 collective-permute-done.12.refs_6_
  35.2 0.0 collective-permute-done.13.refs_7_
  35.2 0.0 collective-permute-done.11.refs_5_
  35.2 1.5 %last_tick_even.1 = (bf16[4,1,4,128,256]{4,3,2,1,0:T(8,128)(2,1)}, f32[1,4,128,256]{3,2,1,0:T(8,128)}) custom-call(s32[30]{0:T(128)S(4)} %get-tuple-element.38.refs_0_, bf16[1,4,6,2,128,128]{5,4,3,2,1,0:T(8,128)(2,1)S(1)} %get-tuple-element.40.refs_1_, ...), custom_call_target="tpu_custom_call", output_to_operand_aliasing={{0}: (11, {}), {1}: (12, {})} | custom-call | tf_op jit(solution)/shard_map/last_tick_even/pallas_call | solution.py:265
  (3 shorter events, 0.0 us)
Async XLA Ops:
  1.8 6.3 %collective-permute-start.1 = (bf16[256,256]{1,0:T(8,128)(2,1)S(1)}, bf16[256,256]{1,0:T(8,128)(2,1)S(1)}, u32[]{:S(2)}, u32[]{:S(2)}) collective-permute-start(bf16[256,256]{1,0:T(8,128)(2,1)S(1)} %get-tuple-element.45), channel_id=1, source_target_pairs={{0,4},{1,2},{2,1},{3,7},{4,0},{5,6},{6,5},{7,3},{8,12},{9,10},{10,... | collective-permute-start | bytes 393224 | tf_op jit(solution)/shard_map/ppermute | solution.py:353
  2.4 7.4 %collective-permute-start = (bf16[256,256]{1,0:T(8,128)(2,1)S(1)}, bf16[256,256]{1,0:T(8,128)(2,1)S(1)}, u32[]{:S(2)}, u32[]{:S(2)}) collective-permute-start(bf16[256,256]{1,0:T(8,128)(2,1)S(1)} %get-tuple-element.39.after_ref), channel_id=1, source_target_pairs={{0,1},{1,0},{2,3},{3,2},{4,5},{5,4},{6,7},{7,6},{8,9},{9,8},{10,11... | collective-permute-start | bytes 393224 | tf_op jit(solution)/shard_map/ppermute | solution.py:352
  9.7 9.3 %collective-permute-start.2 = (bf16[512,256]{1,0:T(8,128)(2,1)S(1)}, bf16[512,256]{1,0:T(8,128)(2,1)S(1)}, u32[]{:S(2)}, u32[]{:S(2)}) collective-permute-start(bf16[512,256]{1,0:T(8,128)(2,1)S(1)} %get-tuple-element.46), channel_id=1, source_target_pairs={{0,4},{4,8},{8,12},{12,16},{16,20},{20,24},{24,28},{28,0},{1,5},{5... | collective-permute-start | bytes 786440 | tf_op jit(solution)/shard_map/ppermute | solution.py:431
  10.5 8.4 %collective-permute-start.4 = (bf16[272,256]{1,0:T(8,128)(2,1)S(1)}, bf16[272,256]{1,0:T(8,128)(2,1)S(1)}, u32[]{:S(2)}, u32[]{:S(2)}) collective-permute-start(bf16[272,256]{1,0:T(8,128)(2,1)S(1)} %get-tuple-element.51), channel_id=1, source_target_pairs={{0,4},{1,6},{2,5},{3,7},{4,0},{5,10},{6,9},{7,3},{8,12},{9,14},{10... | collective-permute-start | bytes 417800 | tf_op jit(solution)/shard_map/ppermute | solution.py:394
  11.3 7.5 %collective-permute-start.3 = (bf16[256,256]{1,0:T(8,128)(2,1)S(1)}, bf16[256,256]{1,0:T(8,128)(2,1)S(1)}, u32[]{:S(2)}, u32[]{:S(2)}) collective-permute-start(bf16[256,256]{1,0:T(8,128)(2,1)S(1)} %get-tuple-element.50), channel_id=1, source_target_pairs={{0,5},{1,4},{2,7},{3,6},{4,9},{5,8},{6,11},{7,10},{8,13},{9,12},{1... | collective-permute-start | bytes 393224 | tf_op jit(solution)/shard_map/ppermute | solution.py:394
  13.7 5.2 %collective-permute-start.5 = (bf16[2,128,256]{2,1,0:T(8,128)(2,1)S(1)}, bf16[2,128,256]{2,1,0:T(8,128)(2,1)S(1)}, u32[]{:S(2)}, u32[]{:S(2)}) collective-permute-start(bf16[2,128,256]{2,1,0:T(8,128)(2,1)S(1)} %get-tuple-element.52), channel_id=1, source_target_pairs={{0,4},{4,0},{8,12},{12,8},{16,20},{20,16},{24,28},{28,24},{1,5},{5... | collective-permute-start | bytes 393224 | tf_op jit(solution)/shard_map/ppermute | solution.py:435
  14.5 4.4 %collective-permute-start.6 = (bf16[2,128,256]{2,1,0:T(8,128)(2,1)S(1)}, bf16[2,128,256]{2,1,0:T(8,128)(2,1)S(1)}, u32[]{:S(2)}, u32[]{:S(2)}) collective-permute-start(bf16[2,128,256]{2,1,0:T(8,128)(2,1)S(1)} %get-tuple-element.53), channel_id=1, source_target_pairs={{0,4},{4,0},{8,12},{12,8},{16,20},{20,16},{24,28},{28,24},{1,5},{5... | collective-permute-start | bytes 393224 | tf_op jit(solution)/shard_map/ppermute | solution.py:435
  18.9 10.6 %collective-permute-start.14 = (bf16[528,256]{1,0:T(8,128)(2,1)S(1)}, bf16[528,256]{1,0:T(8,128)(2,1)S(1)}, u32[]{:S(2)}, u32[]{:S(2)}) collective-permute-start(bf16[528,256]{1,0:T(8,128)(2,1)S(1)} %get-tuple-element.64), channel_id=1, source_target_pairs={{0,4},{4,8},{8,12},{12,16},{16,20},{20,24},{24,28},{28,0},{1,5},{5... | collective-permute-start | bytes 811016 | tf_op jit(solution)/shard_map/ppermute | solution.py:431
  19.8 2.8 %collective-permute-start.7 = (bf16[2,128,256]{2,1,0:T(8,128)(2,1)S(1)}, bf16[2,128,256]{2,1,0:T(8,128)(2,1)S(1)}, u32[]{:S(2)}, u32[]{:S(2)}) collective-permute-start(bf16[2,128,256]{2,1,0:T(8,128)(2,1)S(1)} %get-tuple-element.55), channel_id=1, source_target_pairs={{0,4},{4,0},{8,12},{12,8},{16,20},{20,16},{24,28},{28,24},{1,5},{5... | collective-permute-start | bytes 393224 | tf_op jit(solution)/shard_map/ppermute | solution.py:435
  19.8 5.2 %collective-permute-start.9 = (bf16[272,256]{1,0:T(8,128)(2,1)S(1)}, bf16[272,256]{1,0:T(8,128)(2,1)S(1)}, u32[]{:S(2)}, u32[]{:S(2)}) collective-permute-start(bf16[272,256]{1,0:T(8,128)(2,1)S(1)} %get-tuple-element.57), channel_id=1, source_target_pairs={{0,5},{1,4},{2,7},{3,6},{4,0},{5,1},{6,2},{7,3},{8,13},{9,12},{10,... | collective-permute-start | bytes 417800 | tf_op jit(solution)/shard_map/ppermute | solution.py:394
  22.0 3.1 %collective-permute-start.10 = (bf16[272,256]{1,0:T(8,128)(2,1)S(1)}, bf16[272,256]{1,0:T(8,128)(2,1)S(1)}, u32[]{:S(2)}, u32[]{:S(2)}) collective-permute-start(bf16[272,256]{1,0:T(8,128)(2,1)S(1)} %get-tuple-element.58), channel_id=1, source_target_pairs={{0,4},{1,6},{2,5},{3,7},{4,0},{5,1},{6,2},{7,3},{8,12},{9,14},{10,... | collective-permute-start | bytes 417800 | tf_op jit(solution)/shard_map/ppermute | solution.py:394
  22.0 1.5 %collective-permute-start.8 = (bf16[2,128,256]{2,1,0:T(8,128)(2,1)S(1)}, bf16[2,128,256]{2,1,0:T(8,128)(2,1)S(1)}, u32[]{:S(2)}, u32[]{:S(2)}) collective-permute-start(bf16[2,128,256]{2,1,0:T(8,128)(2,1)S(1)} %get-tuple-element.56), channel_id=1, source_target_pairs={{0,4},{4,0},{8,12},{12,8},{16,20},{20,16},{24,28},{28,24},{1,5},{5... | collective-permute-start | bytes 393224 | tf_op jit(solution)/shard_map/ppermute | solution.py:435
  22.5 6.2 %collective-permute-start.15 = (bf16[256,256]{1,0:T(8,128)(2,1)S(1)}, bf16[256,256]{1,0:T(8,128)(2,1)S(1)}, u32[]{:S(2)}, u32[]{:S(2)}) collective-permute-start(bf16[256,256]{1,0:T(8,128)(2,1)S(1)} %get-tuple-element.65), channel_id=1, source_target_pairs={{0,4},{1,5},{2,6},{3,7},{4,9},{5,8},{6,11},{7,10},{8,12},{9,13},{1... | collective-permute-start | bytes 393224 | tf_op jit(solution)/shard_map/ppermute | solution.py:394
  23.6 5.9 %collective-permute-start.16 = (bf16[256,256]{1,0:T(8,128)(2,1)S(1)}, bf16[256,256]{1,0:T(8,128)(2,1)S(1)}, u32[]{:S(2)}, u32[]{:S(2)}) collective-permute-start(bf16[256,256]{1,0:T(8,128)(2,1)S(1)} %get-tuple-element.66), channel_id=1, source_target_pairs={{0,4},{1,5},{2,6},{3,7},{4,0},{5,10},{6,9},{7,3},{8,12},{9,13},{10... | collective-permute-start | bytes 393224 | tf_op jit(solution)/shard_map/ppermute | solution.py:394
  25.1 10.2 %collective-permute-start.11 = (bf16[512,256]{1,0:T(8,128)(2,1)S(1)}, bf16[512,256]{1,0:T(8,128)(2,1)S(1)}, u32[]{:S(2)}, u32[]{:S(2)}) collective-permute-start(bf16[512,256]{1,0:T(8,128)(2,1)S(1)} %get-tuple-element.59), channel_id=1, source_target_pairs={{0,4},{4,8},{8,12},{12,16},{16,20},{20,24},{24,28},{28,0},{1,5},{5... | collective-permute-start | bytes 786440 | tf_op jit(solution)/shard_map/ppermute | solution.py:431
  25.9 9.3 %collective-permute-start.12 = (bf16[272,256]{1,0:T(8,128)(2,1)S(1)}, bf16[272,256]{1,0:T(8,128)(2,1)S(1)}, u32[]{:S(2)}, u32[]{:S(2)}) collective-permute-start(bf16[272,256]{1,0:T(8,128)(2,1)S(1)} %get-tuple-element.60), channel_id=1, source_target_pairs={{0,4},{1,5},{2,6},{3,7},{4,9},{5,8},{6,11},{7,10},{8,12},{9,13},{1... | collective-permute-start | bytes 417800 | tf_op jit(solution)/shard_map/ppermute | solution.py:394
  28.7 6.5 %collective-permute-start.13 = (bf16[272,256]{1,0:T(8,128)(2,1)S(1)}, bf16[272,256]{1,0:T(8,128)(2,1)S(1)}, u32[]{:S(2)}, u32[]{:S(2)}) collective-permute-start(bf16[272,256]{1,0:T(8,128)(2,1)S(1)} %get-tuple-element.61), channel_id=1, source_target_pairs={{0,4},{1,5},{2,6},{3,7},{4,0},{5,10},{6,9},{7,3},{8,12},{9,13},{10... | collective-permute-start | bytes 417800 | tf_op jit(solution)/shard_map/ppermute | solution.py:394
  30.2 4.9 %collective-permute-start.17 = (bf16[256,256]{1,0:T(8,128)(2,1)S(1)}, bf16[256,256]{1,0:T(8,128)(2,1)S(1)}, u32[]{:S(2)}, u32[]{:S(2)}) collective-permute-start(bf16[256,256]{1,0:T(8,128)(2,1)S(1)} %get-tuple-element.70), channel_id=1, source_target_pairs={{0,5},{1,4},{2,7},{3,6},{4,0},{5,1},{6,2},{7,3},{8,13},{9,12},{10,... | collective-permute-start | bytes 393224 | tf_op jit(solution)/shard_map/ppermute | solution.py:394
  30.9 4.2 %collective-permute-start.18 = (bf16[256,256]{1,0:T(8,128)(2,1)S(1)}, bf16[256,256]{1,0:T(8,128)(2,1)S(1)}, u32[]{:S(2)}, u32[]{:S(2)}) collective-permute-start(bf16[256,256]{1,0:T(8,128)(2,1)S(1)} %get-tuple-element.71), channel_id=1, source_target_pairs={{0,4},{1,6},{2,5},{3,7},{4,0},{5,1},{6,2},{7,3},{8,12},{9,14},{10,... | collective-permute-start | bytes 393224 | tf_op jit(solution)/shard_map/ppermute | solution.py:394
